TPU v7x, 32 devices: a whole 2x2x4 slice. The times are simulated.
32 devices in a mesh: dp: 4 (over y, core), expert: 8 (over z, x).
Axes of the slice: x: 2, y: 2, z: 4, core: 2. Of those that a mesh axis runs over, the one named last changes fastest.
Arguments:
- tokens: bfloat16 [8192, 2048], P(('dp', 'expert')), parts along dimension 0, may hold values from -6 to 6
- target: int32 [8192, 8], P(('dp', 'expert')), parts along dimension 0, may hold values from 0 to 23, as said below
- router_weight: float32 [8192, 8], P(('dp', 'expert')), parts along dimension 0, may hold values from 0.1 to 1
- replica_pick: int32 [32], P(('dp', 'expert')), parts along dimension 0, may hold values from 0 to 1
- w_gate: bfloat16 [16, 2048, 768], P('expert'), may hold values from -0.125 to 0.125
- w_up: bfloat16 [16, 2048, 768], P('expert'), may hold values from -0.125 to 0.125
- w_down: bfloat16 [16, 768, 2048], P('expert'), may hold values from -0.21875 to 0.21875
Outputs:
- mixed: bfloat16 [8192, 2048], P(('dp', 'expert')), parts along dimension 0
There are 4 independent parts, one for each index of `dp`. A program takes and returns all parts, laid end to end along the dimension named above; an argument that names none is the same for every part. Nothing has to cross between parts.
Inputs may be any that keep to these rules, and one draw needn't show every extreme that they name: `target`: within each aligned block of 256 rows (one device's tokens) no slot is named more than 128 times, and at least one slot, the same one in every block, is named exactly 128 times in every block (other slots may also reach 128); the 8 slots of a row name 8 different experts.
All inputs are finite; a program needn't handle non-finite values.
Results may differ from a plain program's by a relative error of at most 0.008.
Values may be sent and summed in bfloat16 or wider, within the bound.
No kernel may reach another device: no remote copies, remote signals or barrier semaphores. Data moves between devices by JAX's collectives and lax.ppermute only.
A program may use at most 192 MiB of HBM per device.

v0:
```python
import functools

import jax
import jax.numpy as jnp
from jax import lax
from jax.experimental import pallas as pl
from jax.experimental.pallas import tpu as pltpu
from jax.sharding import PartitionSpec as P

VMEM_LIMIT = 12 * 1024 * 1024
PACK_LIMIT = 56 * 1024 * 1024


def ring_order(groups):
    columns = 1 << ((groups.bit_length() - 1) // 2)
    rows = groups // columns
    walk = [z * columns for z in range(rows)]
    for turn, z in enumerate(reversed(range(rows))):
        row = [z * columns + x for x in range(1, columns)]
        walk += row if turn % 2 == 0 else row[::-1]
    return walk


def table_rows(slots, height, width):
    one = -(-slots * height // width)
    return one, -(-2 * one // 8) * 8


def pack_kernel(slots, tokens_ref, target_ref, weight_ref, *refs):
    tabled, plain = refs[:2], refs[2:4]
    target_buf, weight_buf, sems = refs[4:]
    height, width = tokens_ref.shape
    half = height // 2
    one, extra = table_rows(slots, height, width)
    per_row = width // height
    copies = [
        pltpu.make_async_copy(target_ref, target_buf, sems.at[0]),
        pltpu.make_async_copy(weight_ref, weight_buf, sems.at[1]),
    ]
    for i in range(2):
        rows = tokens_ref.at[pl.ds(i * half, half)]
        copies.append(pltpu.make_async_copy(rows, tabled[i].at[pl.ds(0, half)], sems.at[2 + i]))
        copies.append(pltpu.make_async_copy(rows, plain[i], sems.at[4 + i]))
    for copy in copies:
        copy.start()
    copies[0].wait()
    copies[1].wait()
    weight = weight_buf[...]
    share = weight / jnp.sum(weight, axis=0, keepdims=True)
    target = target_buf[...]
    row = lax.broadcasted_iota(jnp.int32, (extra, height), 0)
    for lane in range(per_row):
        block = jnp.zeros((extra, height), jnp.float32)
        for r in range(one):
            slot = r * per_row + lane
            if slot < slots:
                value = jnp.sum(jnp.where(target == slot, share, 0.0), axis=0, keepdims=True)
                high = value.astype(jnp.bfloat16).astype(jnp.float32)
                block = jnp.where(row == r, high, block)
                block = jnp.where(row == one + r, value - high, block)
        for ref in tabled:
            ref[half:, lane * height:(lane + 1) * height] = block.astype(jnp.bfloat16)
    for copy in copies[2:]:
        copy.wait()


def pack(tokens, target, router_weight, slots):
    height, width = tokens.shape
    half, top = height // 2, target.shape[1]
    extra = table_rows(slots, height, width)[1]
    vmem = pl.BlockSpec(memory_space=pltpu.VMEM)
    return pl.pallas_call(
        functools.partial(pack_kernel, slots),
        in_specs=[pl.BlockSpec(memory_space=pl.ANY)] * 3,
        out_specs=[vmem] * 4,
        out_shape=[jax.ShapeDtypeStruct((half + extra, width), jnp.bfloat16)] * 2
        + [jax.ShapeDtypeStruct((half, width), jnp.bfloat16)] * 2,
        scratch_shapes=[
            pltpu.VMEM((top, height), jnp.int32),
            pltpu.VMEM((top, height), jnp.float32),
            pltpu.SemaphoreType.DMA((6,)),
        ],
        compiler_params=pltpu.CompilerParams(vmem_limit_bytes=PACK_LIMIT),
        cost_estimate=pl.CostEstimate(flops=0, bytes_accessed=4 * height * width, transcendentals=0),
    )(tokens, target.T, router_weight.T)


def columns(place_ref, table_ref, first, slots, height, owned):
    half = height // 2
    width = table_ref.shape[1]
    one, extra = table_rows(slots, height, width)
    per_row = width // height
    me, after, pick = place_ref[0], place_ref[1], place_ref[2]

    def column(slot):
        lane = pl.multiple_of(lax.rem(slot, per_row) * height + first, half)
        block = table_ref[half:half + extra, pl.ds(lane, half)].astype(jnp.float32)
        row = lax.broadcasted_iota(jnp.int32, block.shape, 0)
        line = lax.div(slot, per_row)
        return jnp.sum(jnp.where((row == line) | (row == one + line), block, 0.0), axis=0, keepdims=True)

    lent = column(after * (owned + 1) + owned)
    row = lax.broadcasted_iota(jnp.int32, (128, half), 0)
    shares = jnp.zeros((128, half), jnp.float32)
    for e in range(owned):
        line = column(me * (owned + 1) + e) + jnp.where(pick == e, lent, 0.0)
        shares = jnp.where(row == e, line, shares)
    return shares.T


def evaluate(chunk_ref, share_ref, gate_ref, up_ref, down_ref, out_ref, hidden_ref):
    half, width = out_ref.shape
    owned, _, units = gate_ref.shape
    tile = 256 if units % 256 == 0 else units
    tiles = units // tile
    wide = 512 if width % 512 == 0 else width

    def project(j, carry):
        e = lax.div(j, tiles)
        at = pl.ds(pl.multiple_of(lax.rem(j, tiles) * tile, tile), tile)
        x = chunk_ref[:half, :]
        gate = jnp.dot(x, gate_ref[e, :, at], preferred_element_type=jnp.float32)
        upper = jnp.dot(x, up_ref[e, :, at], preferred_element_type=jnp.float32)
        shares = share_ref[...]
        lane = lax.broadcasted_iota(jnp.int32, shares.shape, 1)
        share = jnp.sum(jnp.where(lane == e, shares, 0.0), axis=1, keepdims=True)
        hidden = gate / (1.0 + jnp.exp(-gate)) * upper * share
        hidden_ref[:, pl.ds(pl.multiple_of(j * tile, tile), tile)] = hidden.astype(jnp.bfloat16)
        return carry

    lax.fori_loop(0, owned * tiles, project, 0)

    def fold(j, carry):
        at = pl.ds(pl.multiple_of(j * wide, wide), wide)
        part = jnp.dot(hidden_ref[...], down_ref[:, at], preferred_element_type=jnp.float32)
        out_ref[:, at] = part.astype(jnp.bfloat16)
        return carry

    lax.fori_loop(0, width // wide, fold, 0)


def tabled_kernel(firsts, slots, height, place_ref, chunk_ref, gate_ref, up_ref, down_ref, out_ref, other_ref,
                  share_ref, hidden_ref):
    owned = gate_ref.shape[0]
    share_ref[...] = columns(place_ref, chunk_ref, firsts[0], slots, height, owned)
    other_ref[...] = columns(place_ref, chunk_ref, firsts[1], slots, height, owned)
    evaluate(chunk_ref, share_ref, gate_ref, up_ref, down_ref, out_ref, hidden_ref)


def plain_kernel(chunk_ref, share_ref, gate_ref, up_ref, down_ref, out_ref, same_ref, hidden_ref):
    del same_ref
    evaluate(chunk_ref, share_ref, gate_ref, up_ref, down_ref, out_ref, hidden_ref)


def cost(half, w_gate):
    owned, width, units = w_gate.shape
    return pl.CostEstimate(
        flops=6 * half * width * units * owned, bytes_accessed=8 * half * width, transcendentals=half * units * owned
    )


def tabled(place, weights, slots, height, firsts, chunk):
    half, (owned, width, units) = height // 2, weights[0].shape
    vmem = pl.BlockSpec(memory_space=pltpu.VMEM)
    return pl.pallas_call(
        functools.partial(tabled_kernel, firsts, slots, height),
        in_specs=[pl.BlockSpec(memory_space=pltpu.SMEM)] + [vmem] * 4,
        out_specs=[vmem, vmem],
        out_shape=[jax.ShapeDtypeStruct((half, width), jnp.bfloat16), jax.ShapeDtypeStruct((half, 128), jnp.float32)],
        scratch_shapes=[pltpu.VMEM((half, 128), jnp.float32), pltpu.VMEM((half, owned * units), jnp.bfloat16)],
        compiler_params=pltpu.CompilerParams(vmem_limit_bytes=VMEM_LIMIT),
        cost_estimate=cost(half, weights[0]),
    )(place, chunk, *weights)


def plain(weights, chunk, shares):
    (half, width), (owned, _, units) = chunk.shape, weights[0].shape
    vmem = pl.BlockSpec(memory_space=pltpu.VMEM)
    return pl.pallas_call(
        plain_kernel,
        in_specs=[vmem] * 5,
        out_specs=[vmem, vmem],
        out_shape=[jax.ShapeDtypeStruct((half, width), jnp.bfloat16)] * 2,
        scratch_shapes=[pltpu.VMEM((half, owned * units), jnp.bfloat16)],
        input_output_aliases={0: 1},
        compiler_params=pltpu.CompilerParams(vmem_limit_bytes=VMEM_LIMIT),
        cost_estimate=cost(half, weights[0]),
    )(chunk, shares, *weights)


def finish_kernel(*refs):
    out_ref = refs[-1]
    half = refs[0].shape[0]
    for i in range(2):
        total = sum(ref[...].astype(jnp.float32) for ref in refs[3 * i:3 * i + 3])
        out_ref[i * half:(i + 1) * half, :] = total.astype(out_ref.dtype)


def finish(a, b):
    half, width = a[0].shape
    vmem = pl.BlockSpec(memory_space=pltpu.VMEM)
    return pl.pallas_call(
        finish_kernel,
        in_specs=[vmem] * 6,
        out_specs=vmem,
        out_shape=jax.ShapeDtypeStruct((2 * half, width), a[0].dtype),
        compiler_params=pltpu.CompilerParams(vmem_limit_bytes=VMEM_LIMIT),
    )(*a, *b)


def add(a, b):
    return (a.astype(jnp.float32) + b.astype(jnp.float32)).astype(jnp.bfloat16)


def body(tokens, target, router_weight, replica_pick, w_gate, w_up, w_down):
    height, width = tokens.shape
    half = height // 2
    groups = lax.axis_size("expert")
    slots = groups * (w_gate.shape[0] + 1)
    walk = ring_order(groups)
    ahead = [(walk[i], walk[(i + 1) % groups]) for i in range(groups)]
    back = [(b, a) for a, b in ahead]
    me = lax.axis_index("expert").astype(jnp.int32)
    after = jnp.where(me == groups - 1, 0, me + 1)
    place = jnp.stack([me, after, replica_pick[0]])
    weights = w_gate, w_up, w_down.reshape(-1, width)
    far = groups // 2

    lead_a, lead_b, a, b = pack(tokens, target, router_weight, slots)
    run_a = functools.partial(tabled, place, weights, slots, height, (0, half))
    run_b = functools.partial(tabled, place, weights, slots, height, (half, 0))
    own_a, shares_b = run_a(lead_a)
    own_b, _ = plain(weights, b, shares_b)
    parts = {}
    for s in range(1, far):
        lead_a = lax.ppermute(lead_a, "expert", ahead)
        lead_b = lax.ppermute(lead_b, "expert", back)
        b = lax.ppermute(b, "expert", ahead)
        a = lax.ppermute(a, "expert", back)
        lead_part_a, shares_b = run_a(lead_a)
        lead_part_b, shares_a = run_b(lead_b)
        part_b, b = plain(weights, b, shares_b)
        part_a, a = plain(weights, a, shares_a)
        parts[s] = lead_part_a, lead_part_b, part_b, part_a
    far_a = run_a(lax.ppermute(lead_a, "expert", ahead))[0]
    far_b = run_b(lax.ppermute(lead_b, "expert", back))[0]

    lead_a, lead_b, a, b = lax.ppermute(far_a, "expert", back), lax.ppermute(far_b, "expert", ahead), None, None
    for s in range(far - 1, 0, -1):
        lead_part_a, lead_part_b, part_b, part_a = parts[s]
        b = lax.ppermute(part_b if b is None else add(part_b, b), "expert", back)
        a = lax.ppermute(part_a if a is None else add(part_a, a), "expert", ahead)
        lead_a = lax.ppermute(add(lead_part_a, lead_a), "expert", back)
        lead_b = lax.ppermute(add(lead_part_b, lead_b), "expert", ahead)
    return finish((own_a, a, lead_a), (own_b, b, lead_b))


def solution(mesh):
    in_specs = (
        P(("dp", "expert"), None),
        P(("dp", "expert"), None),
        P(("dp", "expert"), None),
        P(("dp", "expert")),
        P("expert", None, None),
        P("expert", None, None),
        P("expert", None, None),
    )
    out_specs = P(("dp", "expert"), None)
    return jax.shard_map(body, mesh=mesh, in_specs=in_specs, out_specs=out_specs, check_vma=False)
```

profile of v0, /device:TPU:0, one launch (start us, length us, event | category | flops | bytes accessed | tf_op | source)
XLA Modules:
  0.0 191.1 jit_solution(2453689447519172219)
XLA Ops:
  0.0 3.2 %shard_map.73 = (bf16[136,2048]{1,0:T(8,128)(2,1)}, bf16[136,2048]{1,0:T(8,128)(2,1)}, bf16[128,2048]{1,0:T(8,128)(2,1)}, bf16[128,2048]{1,0:T(8,128)(2,1)}) custom-call(bf16[256,2048]{1,0:T(8,128)(2,1)} %tokens_ref.1, s32[8,256]{1,0:T(8,128)} %bitcast.21, f32[8,256]{1,0:T(8,128)} %bitcast.22), custom_call_target="tpu_custom_call" | custom-call | bytes 2097152 | tf_op jit(solution)/shard_map/pallas_call | solution.py:72
  3.2 3.0 %collective-permute-start.1 = (bf16[136,2048]{1,0:T(8,128)(2,1)}, bf16[136,2048]{1,0:T(8,128)(2,1)S(1)}, u32[]{:S(2)}, u32[]{:S(2)}) collective-permute-start(bf16[136,2048]{1,0:T(8,128)(2,1)} %get-tuple-element.39), channel_id=1, source_target_pairs={{2,0},{4,2},{6,4},{7,6},{5,7},{3,5},{1,3},{0,1},{10,8},{12,10},{14... | collective-permute-start | bytes 1671176 | tf_op jit(solution)/shard_map/ppermute | solution.py:237
  9.1 10.8 %collective-permute-done.1.chunk_ref = bf16[136,2048]{1,0:T(8,128)(2,1)S(1)} collective-permute-done((bf16[136,2048]{1,0:T(8,128)(2,1)}, bf16[136,2048]{1,0:T(8,128)(2,1)S(1)}, u32[]{:S(2)}, u32[]{:S(2)}) %collective-permute-start.1) | collective-permute-done | bytes 557088 | tf_op jit(solution)/shard_map/ppermute | solution.py:237
  21.9 2.8 %copy-done = bf16[2,2048,768]{2,1,0:T(8,128)(2,1)S(1)} copy-done((bf16[2,2048,768]{2,1,0:T(8,128)(2,1)S(1)}, bf16[2,2048,768]{2,1,0:T(8,128)(2,1)}, u32[]{:S(2)}) %copy-start) | copy-done | bytes 6291480
  24.7 2.8 %copy-done.2 = bf16[2,2048,768]{2,1,0:T(8,128)(2,1)S(1)} copy-done((bf16[2,2048,768]{2,1,0:T(8,128)(2,1)S(1)}, bf16[2,2048,768]{2,1,0:T(8,128)(2,1)}, u32[]{:S(2)}) %copy-start.2) | copy-done | bytes 6291480
  27.5 2.8 %copy-done.4 = bf16[2,768,2048]{2,1,0:T(8,128)(2,1)S(1)} copy-done((bf16[2,768,2048]{2,1,0:T(8,128)(2,1)S(1)}, bf16[2,768,2048]{2,1,0:T(8,128)(2,1)}, u32[]{:S(2)}) %copy-start.4) | copy-done | bytes 6291480
  30.3 5.3 %shard_map.75 = (bf16[128,2048]{1,0:T(8,128)(2,1)S(1)}, f32[128,128]{1,0:T(8,128)S(1)}) custom-call(s32[3]{0:T(128)S(1)} %pad_add_fusion.place_ref, bf16[136,2048]{1,0:T(8,128)(2,1)S(1)} %collective-permute-done.1.chunk_ref, bf16[2,2048,768]{2,1,0:T(8,128)(2,1)S(1)} %copy-done, bf16[2,2048,768]{2,1,0:T(8,128)(2,1)S(1)} %copy-done.2, ...), custom_call_target="tpu_custom_call" | custom-call | flops 2415919104 | bytes 2097152 | tf_op jit(solution)/shard_map/pallas_call | solution.py:165
  36.7 4.5 %shard_map.76 = (bf16[128,2048]{1,0:T(8,128)(2,1)S(1)}, bf16[128,2048]{1,0:T(8,128)(2,1)S(1)}) custom-call(bf16[128,2048]{1,0:T(8,128)(2,1)S(1)} %collective-permute-done.chunk_ref, f32[128,128]{1,0:T(8,128)S(1)} %get-tuple-element.40.share_ref, bf16[2,2048,768]{2,1,0:T(8,128)(2,1)S(1)} %copy-done.1, ...), custom_call_target="tpu_custom_call", output_to_operand_aliasing={{1}: (0, {})} | custom-call | flops 2415919104 | bytes 2097152 | tf_op jit(solution)/shard_map/pallas_call | solution.py:179
  43.3 5.2 %shard_map.81 = (bf16[128,2048]{1,0:T(8,128)(2,1)S(1)}, f32[128,128]{1,0:T(8,128)S(1)}) custom-call(s32[3]{0:T(128)S(1)} %pad_add_fusion.place_ref, bf16[136,2048]{1,0:T(8,128)(2,1)S(1)} %collective-permute-done.9.chunk_ref, bf16[2,2048,768]{2,1,0:T(8,128)(2,1)S(1)} %copy-done.1, bf16[2,2048,768]{2,1,0:T(8,128)(2,1)S(1)} %copy-done.3, ...), custom_call_target="tpu_custom_call" | custom-call | flops 2415919104 | bytes 2097152 | tf_op jit(solution)/shard_map/pallas_call | solution.py:165
  48.5 4.5 %shard_map.86 = (bf16[128,2048]{1,0:T(8,128)(2,1)S(1)}, bf16[128,2048]{1,0:T(8,128)(2,1)S(1)}) custom-call(bf16[128,2048]{1,0:T(8,128)(2,1)S(1)} %collective-permute-done.17.chunk_ref, f32[128,128]{1,0:T(8,128)S(1)} %get-tuple-element.55.share_ref, bf16[2,2048,768]{2,1,0:T(8,128)(2,1)S(1)} %copy-done.1, ...), custom_call_target="tpu_custom_call", output_to_operand_aliasing={{1}: (0, {})} | custom-call | flops 2415919104 | bytes 2097152 | tf_op jit(solution)/shard_map/pallas_call | solution.py:179
  53.3 5.2 %shard_map.77 = (bf16[128,2048]{1,0:T(8,128)(2,1)S(1)}, f32[128,128]{1,0:T(8,128)S(1)}) custom-call(s32[3]{0:T(128)S(1)} %pad_add_fusion.place_ref, bf16[136,2048]{1,0:T(8,128)(2,1)S(1)} %collective-permute-done.3.chunk_ref, bf16[2,2048,768]{2,1,0:T(8,128)(2,1)S(1)} %copy-done.1, bf16[2,2048,768]{2,1,0:T(8,128)(2,1)S(1)} %copy-done.3, ...), custom_call_target="tpu_custom_call" | custom-call | flops 2415919104 | bytes 2097152 | tf_op jit(solution)/shard_map/pallas_call | solution.py:165
  60.4 4.5 %shard_map.78 = (bf16[128,2048]{1,0:T(8,128)(2,1)S(1)}, bf16[128,2048]{1,0:T(8,128)(2,1)S(1)}) custom-call(bf16[128,2048]{1,0:T(8,128)(2,1)S(1)} %collective-permute-done.2.chunk_ref, f32[128,128]{1,0:T(8,128)S(1)} %get-tuple-element.43.share_ref, bf16[2,2048,768]{2,1,0:T(8,128)(2,1)S(1)} %copy-done.1, ...), custom_call_target="tpu_custom_call", output_to_operand_aliasing={{1}: (0, {})} | custom-call | flops 2415919104 | bytes 2097152 | tf_op jit(solution)/shard_map/pallas_call | solution.py:179
  67.0 5.2 %shard_map.82 = (bf16[128,2048]{1,0:T(8,128)(2,1)S(1)}, f32[128,128]{1,0:T(8,128)S(1)}) custom-call(s32[3]{0:T(128)S(1)} %pad_add_fusion.place_ref, bf16[136,2048]{1,0:T(8,128)(2,1)S(1)} %collective-permute-done.10.chunk_ref, bf16[2,2048,768]{2,1,0:T(8,128)(2,1)S(1)} %copy-done.1, bf16[2,2048,768]{2,1,0:T(8,128)(2,1)S(1)} %copy-done.3, ...), custom_call_target="tpu_custom_call" | custom-call | flops 2415919104 | bytes 2097152 | tf_op jit(solution)/shard_map/pallas_call | solution.py:165
  72.2 4.5 %shard_map.87 = (bf16[128,2048]{1,0:T(8,128)(2,1)S(1)}, bf16[128,2048]{1,0:T(8,128)(2,1)S(1)}) custom-call(bf16[128,2048]{1,0:T(8,128)(2,1)S(1)} %collective-permute-done.18.chunk_ref, f32[128,128]{1,0:T(8,128)S(1)} %get-tuple-element.58.share_ref, bf16[2,2048,768]{2,1,0:T(8,128)(2,1)S(1)} %copy-done.1, ...), custom_call_target="tpu_custom_call", output_to_operand_aliasing={{1}: (0, {})} | custom-call | flops 2415919104 | bytes 2097152 | tf_op jit(solution)/shard_map/pallas_call | solution.py:179
  77.0 5.2 %shard_map.79 = (bf16[128,2048]{1,0:T(8,128)(2,1)S(1)}, f32[128,128]{1,0:T(8,128)S(1)}) custom-call(s32[3]{0:T(128)S(1)} %pad_add_fusion.place_ref, bf16[136,2048]{1,0:T(8,128)(2,1)S(1)} %collective-permute-done.5.chunk_ref, bf16[2,2048,768]{2,1,0:T(8,128)(2,1)S(1)} %copy-done.1, bf16[2,2048,768]{2,1,0:T(8,128)(2,1)S(1)} %copy-done.3, ...), custom_call_target="tpu_custom_call" | custom-call | flops 2415919104 | bytes 2097152 | tf_op jit(solution)/shard_map/pallas_call | solution.py:165
  82.2 4.5 %shard_map.80 = (bf16[128,2048]{1,0:T(8,128)(2,1)S(1)}, bf16[128,2048]{1,0:T(8,128)(2,1)S(1)}) custom-call(bf16[128,2048]{1,0:T(8,128)(2,1)S(1)} %collective-permute-done.4.chunk_ref, f32[128,128]{1,0:T(8,128)S(1)} %get-tuple-element.46.share_ref, bf16[2,2048,768]{2,1,0:T(8,128)(2,1)S(1)} %copy-done.1, ...), custom_call_target="tpu_custom_call", output_to_operand_aliasing={{1}: (0, {})} | custom-call | flops 2415919104 | bytes 2097152 | tf_op jit(solution)/shard_map/pallas_call | solution.py:179
  90.3 5.2 %shard_map.83 = (bf16[128,2048]{1,0:T(8,128)(2,1)S(1)}, f32[128,128]{1,0:T(8,128)S(1)}) custom-call(s32[3]{0:T(128)S(1)} %pad_add_fusion.place_ref, bf16[136,2048]{1,0:T(8,128)(2,1)S(1)} %collective-permute-done.11.chunk_ref, bf16[2,2048,768]{2,1,0:T(8,128)(2,1)S(1)} %copy-done.1, bf16[2,2048,768]{2,1,0:T(8,128)(2,1)S(1)} %copy-done.3, ...), custom_call_target="tpu_custom_call" | custom-call | flops 2415919104 | bytes 2097152 | tf_op jit(solution)/shard_map/pallas_call | solution.py:165
  95.5 4.5 %shard_map.88 = (bf16[128,2048]{1,0:T(8,128)(2,1)S(1)}, bf16[128,2048]{1,0:T(8,128)(2,1)S(1)}) custom-call(bf16[128,2048]{1,0:T(8,128)(2,1)S(1)} %collective-permute-done.19.chunk_ref, f32[128,128]{1,0:T(8,128)S(1)} %get-tuple-element.61.share_ref, bf16[2,2048,768]{2,1,0:T(8,128)(2,1)S(1)} %copy-done.1, ...), custom_call_target="tpu_custom_call", output_to_operand_aliasing={{1}: (0, {})} | custom-call | flops 2415919104 | bytes 2097152 | tf_op jit(solution)/shard_map/pallas_call | solution.py:179
  103.8 11.1 %collective-permute-done.12.chunk_ref = bf16[136,2048]{1,0:T(8,128)(2,1)S(1)} collective-permute-done((bf16[136,2048]{1,0:T(8,128)(2,1)S(1)}, bf16[136,2048]{1,0:T(8,128)(2,1)S(1)}, u32[]{:S(2)}, u32[]{:S(2)}) %collective-permute-start.12) | collective-permute-done | bytes 557088 | tf_op jit(solution)/shard_map/ppermute | solution.py:245
  114.9 5.5 %shard_map.84 = (bf16[128,2048]{1,0:T(8,128)(2,1)S(1)}, f32[128,128]{1,0:T(8,128)}) custom-call(s32[3]{0:T(128)S(1)} %pad_add_fusion.place_ref, bf16[136,2048]{1,0:T(8,128)(2,1)S(1)} %collective-permute-done.12.chunk_ref, bf16[2,2048,768]{2,1,0:T(8,128)(2,1)S(1)} %copy-done.1, bf16[2,2048,768]{2,1,0:T(8,128)(2,1)S(1)} %copy-done.3, ...), custom_call_target="tpu_custom_call" | custom-call | flops 2415919104 | bytes 2097152 | tf_op jit(solution)/shard_map/pallas_call | solution.py:165
  124.0 5.5 %shard_map.89 = (bf16[128,2048]{1,0:T(8,128)(2,1)S(1)}, f32[128,128]{1,0:T(8,128)}) custom-call(s32[3]{0:T(128)S(1)} %pad_add_fusion.place_ref, bf16[136,2048]{1,0:T(8,128)(2,1)S(1)} %collective-permute-done.23.chunk_ref, bf16[2,2048,768]{2,1,0:T(8,128)(2,1)S(1)} %copy-done.1, bf16[2,2048,768]{2,1,0:T(8,128)(2,1)S(1)} %copy-done.3, ...), custom_call_target="tpu_custom_call" | custom-call | flops 2415919104 | bytes 2097152 | tf_op jit(solution)/shard_map/pallas_call | solution.py:165
  129.5 3.0 %collective-permute-start.24 = (bf16[128,2048]{1,0:T(8,128)(2,1)S(1)}, bf16[128,2048]{1,0:T(8,128)(2,1)S(1)}, u32[]{:S(2)}, u32[]{:S(2)}) collective-permute-start(bf16[128,2048]{1,0:T(8,128)(2,1)S(1)} %get-tuple-element.66), channel_id=1, source_target_pairs={{0,2},{2,4},{4,6},{6,7},{7,5},{5,3},{3,1},{1,0},{8,10},{10,12},{12... | collective-permute-start | bytes 1572872 | tf_op jit(solution)/shard_map/ppermute | solution.py:248
  137.2 7.7 %collective-permute-done.24 = bf16[128,2048]{1,0:T(8,128)(2,1)S(1)} collective-permute-done((bf16[128,2048]{1,0:T(8,128)(2,1)S(1)}, bf16[128,2048]{1,0:T(8,128)(2,1)S(1)}, u32[]{:S(2)}, u32[]{:S(2)}) %collective-permute-start.24) | collective-permute-done | bytes 524320 | tf_op jit(solution)/shard_map/ppermute | solution.py:248
  145.0 3.0 %collective-permute-start.25 = (bf16[128,2048]{1,0:T(8,128)(2,1)S(1)}, bf16[128,2048]{1,0:T(8,128)(2,1)S(1)}, u32[]{:S(2)}, u32[]{:S(2)}) collective-permute-start(bf16[128,2048]{1,0:T(8,128)(2,1)S(1)} %add_convert_fusion.2), channel_id=1, source_target_pairs={{0,2},{2,4},{4,6},{6,7},{7,5},{5,3},{3,1},{1,0},{8,10},{10,12},{12... | collective-permute-start | bytes 1572872 | tf_op jit(solution)/shard_map/ppermute | solution.py:254
  148.2 2.5 %collective-permute-start.8 = (bf16[128,2048]{1,0:T(8,128)(2,1)S(1)}, bf16[128,2048]{1,0:T(8,128)(2,1)S(1)}, u32[]{:S(2)}, u32[]{:S(2)}) collective-permute-start(bf16[128,2048]{1,0:T(8,128)(2,1)S(1)} %add_convert_fusion.8), channel_id=1, source_target_pairs={{0,2},{2,4},{4,6},{6,7},{7,5},{5,3},{3,1},{1,0},{8,10},{10,12},{12... | collective-permute-start | bytes 1572872 | tf_op jit(solution)/shard_map/ppermute | solution.py:252
  150.7 6.1 %collective-permute-done.14 = bf16[128,2048]{1,0:T(8,128)(2,1)S(1)} collective-permute-done((bf16[128,2048]{1,0:T(8,128)(2,1)S(1)}, bf16[128,2048]{1,0:T(8,128)(2,1)S(1)}, u32[]{:S(2)}, u32[]{:S(2)}) %collective-permute-start.14) | collective-permute-done | bytes 524320 | tf_op jit(solution)/shard_map/ppermute | solution.py:253
  157.8 3.8 %collective-permute-start.26 = (bf16[128,2048]{1,0:T(8,128)(2,1)S(1)}, bf16[128,2048]{1,0:T(8,128)(2,1)S(1)}, u32[]{:S(2)}, u32[]{:S(2)}) collective-permute-start(bf16[128,2048]{1,0:T(8,128)(2,1)S(1)} %add_convert_fusion.1), channel_id=1, source_target_pairs={{0,2},{2,4},{4,6},{6,7},{7,5},{5,3},{3,1},{1,0},{8,10},{10,12},{12... | collective-permute-start | bytes 1572872 | tf_op jit(solution)/shard_map/ppermute | solution.py:254
  161.8 10.0 %collective-permute-done.15 = bf16[128,2048]{1,0:T(8,128)(2,1)S(1)} collective-permute-done((bf16[128,2048]{1,0:T(8,128)(2,1)S(1)}, bf16[128,2048]{1,0:T(8,128)(2,1)S(1)}, u32[]{:S(2)}, u32[]{:S(2)}) %collective-permute-start.15) | collective-permute-done | bytes 524320 | tf_op jit(solution)/shard_map/ppermute | solution.py:253
  172.0 5.1 %collective-permute-done.26 = bf16[128,2048]{1,0:T(8,128)(2,1)S(1)} collective-permute-done((bf16[128,2048]{1,0:T(8,128)(2,1)S(1)}, bf16[128,2048]{1,0:T(8,128)(2,1)S(1)}, u32[]{:S(2)}, u32[]{:S(2)}) %collective-permute-start.26) | collective-permute-done | bytes 524320 | tf_op jit(solution)/shard_map/ppermute | solution.py:254
  177.3 2.6 %collective-permute-start.27 = (bf16[128,2048]{1,0:T(8,128)(2,1)S(1)}, bf16[128,2048]{1,0:T(8,128)(2,1)S(1)}, u32[]{:S(2)}, u32[]{:S(2)}) collective-permute-start(bf16[128,2048]{1,0:T(8,128)(2,1)S(1)} %add_convert_fusion), channel_id=1, source_target_pairs={{0,2},{2,4},{4,6},{6,7},{7,5},{5,3},{3,1},{1,0},{8,10},{10,12},{12... | collective-permute-start | bytes 1572872 | tf_op jit(solution)/shard_map/ppermute | solution.py:254
  179.9 5.2 %shard_map.74 = (bf16[128,2048]{1,0:T(8,128)(2,1)S(1)}, f32[128,128]{1,0:T(8,128)S(1)}) custom-call(s32[3]{0:T(128)S(1)} %pad_add_fusion.place_ref, bf16[136,2048]{1,0:T(8,128)(2,1)S(1)} %copy-done.6, bf16[2,2048,768]{2,1,0:T(8,128)(2,1)S(1)} %copy-done.1, bf16[2,2048,768]{2,1,0:T(8,128)(2,1)S(1)} %copy-done.3, bf16[1536,2048]{1,0:T(8,128)(2,1)S(1)} %bitcast.19), custom_call_target="tpu_custom_call" | custom-call | flops 2415919104 | bytes 2097152 | tf_op jit(solution)/shard_map/pallas_call | solution.py:165
  185.1 4.5 %shard_map.85 = (bf16[128,2048]{1,0:T(8,128)(2,1)S(1)}, bf16[128,2048]{1,0:T(8,128)(2,1)S(1)}) custom-call(bf16[128,2048]{1,0:T(8,128)(2,1)S(1)} %copy-done.7, f32[128,128]{1,0:T(8,128)S(1)} %get-tuple-element.53.share_ref, bf16[2,2048,768]{2,1,0:T(8,128)(2,1)S(1)} %copy-done.1, ...), custom_call_target="tpu_custom_call", output_to_operand_aliasing={{1}: (0, {})} | custom-call | flops 2415919104 | bytes 2097152 | tf_op jit(solution)/shard_map/pallas_call | solution.py:179
  (69 shorter events, 30.5 us)
Async XLA Ops:
  3.2 16.7 %collective-permute-start.1 = (bf16[136,2048]{1,0:T(8,128)(2,1)}, bf16[136,2048]{1,0:T(8,128)(2,1)S(1)}, u32[]{:S(2)}, u32[]{:S(2)}) collective-permute-start(bf16[136,2048]{1,0:T(8,128)(2,1)} %get-tuple-element.39), channel_id=1, source_target_pairs={{2,0},{4,2},{6,4},{7,6},{5,7},{3,5},{1,3},{0,1},{10,8},{12,10},{14... | collective-permute-start | bytes 1671176 | tf_op jit(solution)/shard_map/ppermute | solution.py:237
  6.2 29.4 %collective-permute-start = (bf16[128,2048]{1,0:T(8,128)(2,1)}, bf16[128,2048]{1,0:T(8,128)(2,1)S(1)}, u32[]{:S(2)}, u32[]{:S(2)}) collective-permute-start(bf16[128,2048]{1,0:T(8,128)(2,1)} %get-tuple-element.38), channel_id=1, source_target_pairs={{2,0},{4,2},{6,4},{7,6},{5,7},{3,5},{1,3},{0,1},{10,8},{12,10},{14... | collective-permute-start | bytes 1572872 | tf_op jit(solution)/shard_map/ppermute | solution.py:239
  7.8 35.0 %collective-permute-start.9 = (bf16[136,2048]{1,0:T(8,128)(2,1)}, bf16[136,2048]{1,0:T(8,128)(2,1)S(1)}, u32[]{:S(2)}, u32[]{:S(2)}) collective-permute-start(bf16[136,2048]{1,0:T(8,128)(2,1)} %get-tuple-element.36.chunk_ref), channel_id=1, source_target_pairs={{0,2},{2,4},{4,6},{6,7},{7,5},{5,3},{3,1},{1,0},{8,10},{10,12},{12... | collective-permute-start | bytes 1671176 | tf_op jit(solution)/shard_map/ppermute | solution.py:236
  8.2 40.3 %collective-permute-start.17 = (bf16[128,2048]{1,0:T(8,128)(2,1)}, bf16[128,2048]{1,0:T(8,128)(2,1)S(1)}, u32[]{:S(2)}, u32[]{:S(2)}) collective-permute-start(bf16[128,2048]{1,0:T(8,128)(2,1)} %get-tuple-element.52.chunk_ref), channel_id=1, source_target_pairs={{0,2},{2,4},{4,6},{6,7},{7,5},{5,3},{3,1},{1,0},{8,10},{10,12},{12... | collective-permute-start | bytes 1572872 | tf_op jit(solution)/shard_map/ppermute | solution.py:238
  19.9 33.3 %collective-permute-start.3 = (bf16[136,2048]{1,0:T(8,128)(2,1)S(1)}, bf16[136,2048]{1,0:T(8,128)(2,1)S(1)}, u32[]{:S(2)}, u32[]{:S(2)}) collective-permute-start(bf16[136,2048]{1,0:T(8,128)(2,1)S(1)} %collective-permute-done.1.chunk_ref), channel_id=1, source_target_pairs={{2,0},{4,2},{6,4},{7,6},{5,7},{3,5},{1,3},{0,1},{10,8},{12,10},{14... | collective-permute-start | bytes 1671176 | tf_op jit(solution)/shard_map/ppermute | solution.py:237
  30.3 5.3 %copy-start.3 = (bf16[2,2048,768]{2,1,0:T(8,128)(2,1)S(1)}, bf16[2,2048,768]{2,1,0:T(8,128)(2,1)}, u32[]{:S(2)}) copy-start(bf16[2,2048,768]{2,1,0:T(8,128)(2,1)} %up_ref.31) | copy-start | bytes 18874372
  30.3 6.4 %copy-start.5 = (bf16[2,768,2048]{2,1,0:T(8,128)(2,1)S(1)}, bf16[2,768,2048]{2,1,0:T(8,128)(2,1)}, u32[]{:S(2)}) copy-start(bf16[2,768,2048]{2,1,0:T(8,128)(2,1)} %param.13) | copy-start | bytes 18874372
  41.2 19.2 %collective-permute-start.2 = (bf16[128,2048]{1,0:T(8,128)(2,1)S(1)}, bf16[128,2048]{1,0:T(8,128)(2,1)S(1)}, u32[]{:S(2)}, u32[]{:S(2)}) collective-permute-start(bf16[128,2048]{1,0:T(8,128)(2,1)S(1)} %get-tuple-element.42), channel_id=1, source_target_pairs={{2,0},{4,2},{6,4},{7,6},{5,7},{3,5},{1,3},{0,1},{10,8},{12,10},{14... | collective-permute-start | bytes 1572872 | tf_op jit(solution)/shard_map/ppermute | solution.py:239
  42.8 23.7 %collective-permute-start.10 = (bf16[136,2048]{1,0:T(8,128)(2,1)S(1)}, bf16[136,2048]{1,0:T(8,128)(2,1)S(1)}, u32[]{:S(2)}, u32[]{:S(2)}) collective-permute-start(bf16[136,2048]{1,0:T(8,128)(2,1)S(1)} %collective-permute-done.9.chunk_ref), channel_id=1, source_target_pairs={{0,2},{2,4},{4,6},{6,7},{7,5},{5,3},{3,1},{1,0},{8,10},{10,12},{12... | collective-permute-start | bytes 1671176 | tf_op jit(solution)/shard_map/ppermute | solution.py:236
  53.0 19.2 %collective-permute-start.18 = (bf16[128,2048]{1,0:T(8,128)(2,1)S(1)}, bf16[128,2048]{1,0:T(8,128)(2,1)S(1)}, u32[]{:S(2)}, u32[]{:S(2)}) collective-permute-start(bf16[128,2048]{1,0:T(8,128)(2,1)S(1)} %get-tuple-element.57), channel_id=1, source_target_pairs={{0,2},{2,4},{4,6},{6,7},{7,5},{5,3},{3,1},{1,0},{8,10},{10,12},{12... | collective-permute-start | bytes 1572872 | tf_op jit(solution)/shard_map/ppermute | solution.py:238
  58.5 18.5 %collective-permute-start.5 = (bf16[136,2048]{1,0:T(8,128)(2,1)S(1)}, bf16[136,2048]{1,0:T(8,128)(2,1)S(1)}, u32[]{:S(2)}, u32[]{:S(2)}) collective-permute-start(bf16[136,2048]{1,0:T(8,128)(2,1)S(1)} %collective-permute-done.3.chunk_ref), channel_id=1, source_target_pairs={{2,0},{4,2},{6,4},{7,6},{5,7},{3,5},{1,3},{0,1},{10,8},{12,10},{14... | collective-permute-start | bytes 1671176 | tf_op jit(solution)/shard_map/ppermute | solution.py:237
  64.9 17.3 %collective-permute-start.4 = (bf16[128,2048]{1,0:T(8,128)(2,1)S(1)}, bf16[128,2048]{1,0:T(8,128)(2,1)S(1)}, u32[]{:S(2)}, u32[]{:S(2)}) collective-permute-start(bf16[128,2048]{1,0:T(8,128)(2,1)S(1)} %get-tuple-element.45), channel_id=1, source_target_pairs={{2,0},{4,2},{6,4},{7,6},{5,7},{3,5},{1,3},{0,1},{10,8},{12,10},{14... | collective-permute-start | bytes 1572872 | tf_op jit(solution)/shard_map/ppermute | solution.py:239
  66.6 22.2 %collective-permute-start.11 = (bf16[136,2048]{1,0:T(8,128)(2,1)S(1)}, bf16[136,2048]{1,0:T(8,128)(2,1)S(1)}, u32[]{:S(2)}, u32[]{:S(2)}) collective-permute-start(bf16[136,2048]{1,0:T(8,128)(2,1)S(1)} %collective-permute-done.10.chunk_ref), channel_id=1, source_target_pairs={{0,2},{2,4},{4,6},{6,7},{7,5},{5,3},{3,1},{1,0},{8,10},{10,12},{12... | collective-permute-start | bytes 1671176 | tf_op jit(solution)/shard_map/ppermute | solution.py:236
  76.8 18.8 %collective-permute-start.19 = (bf16[128,2048]{1,0:T(8,128)(2,1)S(1)}, bf16[128,2048]{1,0:T(8,128)(2,1)S(1)}, u32[]{:S(2)}, u32[]{:S(2)}) collective-permute-start(bf16[128,2048]{1,0:T(8,128)(2,1)S(1)} %get-tuple-element.60), channel_id=1, source_target_pairs={{0,2},{2,4},{4,6},{6,7},{7,5},{5,3},{3,1},{1,0},{8,10},{10,12},{12... | collective-permute-start | bytes 1572872 | tf_op jit(solution)/shard_map/ppermute | solution.py:238
  86.8 16.2 %collective-permute-start.6 = (bf16[128,2048]{1,0:T(8,128)(2,1)S(1)}, bf16[128,2048]{1,0:T(8,128)(2,1)S(1)}, u32[]{:S(2)}, u32[]{:S(2)}) collective-permute-start(bf16[128,2048]{1,0:T(8,128)(2,1)S(1)} %get-tuple-element.47), channel_id=1, source_target_pairs={{0,2},{2,4},{4,6},{6,7},{7,5},{5,3},{3,1},{1,0},{8,10},{10,12},{12... | collective-permute-start | bytes 1572872 | tf_op jit(solution)/shard_map/ppermute | solution.py:252
  88.7 26.1 %collective-permute-start.12 = (bf16[136,2048]{1,0:T(8,128)(2,1)S(1)}, bf16[136,2048]{1,0:T(8,128)(2,1)S(1)}, u32[]{:S(2)}, u32[]{:S(2)}) collective-permute-start(bf16[136,2048]{1,0:T(8,128)(2,1)S(1)} %collective-permute-done.11.chunk_ref), channel_id=1, source_target_pairs={{0,2},{2,4},{4,6},{6,7},{7,5},{5,3},{3,1},{1,0},{8,10},{10,12},{12... | collective-permute-start | bytes 1671176 | tf_op jit(solution)/shard_map/ppermute | solution.py:245
  100.0 32.5 %collective-permute-start.20 = (bf16[128,2048]{1,0:T(8,128)(2,1)S(1)}, bf16[128,2048]{1,0:T(8,128)(2,1)S(1)}, u32[]{:S(2)}, u32[]{:S(2)}) collective-permute-start(bf16[128,2048]{1,0:T(8,128)(2,1)S(1)} %get-tuple-element.62), channel_id=1, source_target_pairs={{2,0},{4,2},{6,4},{7,6},{5,7},{3,5},{1,3},{0,1},{10,8},{12,10},{14... | collective-permute-start | bytes 1572872 | tf_op jit(solution)/shard_map/ppermute | solution.py:251
  100.5 23.4 %collective-permute-start.23 = (bf16[136,2048]{1,0:T(8,128)(2,1)S(1)}, bf16[136,2048]{1,0:T(8,128)(2,1)S(1)}, u32[]{:S(2)}, u32[]{:S(2)}) collective-permute-start(bf16[136,2048]{1,0:T(8,128)(2,1)S(1)} %collective-permute-done.5.chunk_ref), channel_id=1, source_target_pairs={{2,0},{4,2},{6,4},{7,6},{5,7},{3,5},{1,3},{0,1},{10,8},{12,10},{14... | collective-permute-start | bytes 1671176 | tf_op jit(solution)/shard_map/ppermute | solution.py:246
  103.0 45.0 %collective-permute-start.7 = (bf16[128,2048]{1,0:T(8,128)(2,1)S(1)}, bf16[128,2048]{1,0:T(8,128)(2,1)S(1)}, u32[]{:S(2)}, u32[]{:S(2)}) collective-permute-start(bf16[128,2048]{1,0:T(8,128)(2,1)S(1)} %add_convert_fusion.9), channel_id=1, source_target_pairs={{0,2},{2,4},{4,6},{6,7},{7,5},{5,3},{3,1},{1,0},{8,10},{10,12},{12... | collective-permute-start | bytes 1572872 | tf_op jit(solution)/shard_map/ppermute | solution.py:252
  120.3 14.9 %collective-permute-start.13 = (bf16[128,2048]{1,0:T(8,128)(2,1)S(1)}, bf16[128,2048]{1,0:T(8,128)(2,1)S(1)}, u32[]{:S(2)}, u32[]{:S(2)}) collective-permute-start(bf16[128,2048]{1,0:T(8,128)(2,1)S(1)} %get-tuple-element.51), channel_id=1, source_target_pairs={{2,0},{4,2},{6,4},{7,6},{5,7},{3,5},{1,3},{0,1},{10,8},{12,10},{14... | collective-permute-start | bytes 1572872 | tf_op jit(solution)/shard_map/ppermute | solution.py:248
  129.5 15.4 %collective-permute-start.24 = (bf16[128,2048]{1,0:T(8,128)(2,1)S(1)}, bf16[128,2048]{1,0:T(8,128)(2,1)S(1)}, u32[]{:S(2)}, u32[]{:S(2)}) collective-permute-start(bf16[128,2048]{1,0:T(8,128)(2,1)S(1)} %get-tuple-element.66), channel_id=1, source_target_pairs={{0,2},{2,4},{4,6},{6,7},{7,5},{5,3},{3,1},{1,0},{8,10},{10,12},{12... | collective-permute-start | bytes 1572872 | tf_op jit(solution)/shard_map/ppermute | solution.py:248
  132.6 29.0 %collective-permute-start.21 = (bf16[128,2048]{1,0:T(8,128)(2,1)S(1)}, bf16[128,2048]{1,0:T(8,128)(2,1)S(1)}, u32[]{:S(2)}, u32[]{:S(2)}) collective-permute-start(bf16[128,2048]{1,0:T(8,128)(2,1)S(1)} %add_convert_fusion.4), channel_id=1, source_target_pairs={{2,0},{4,2},{6,4},{7,6},{5,7},{3,5},{1,3},{0,1},{10,8},{12,10},{14... | collective-permute-start | bytes 1572872 | tf_op jit(solution)/shard_map/ppermute | solution.py:251
  135.2 44.7 %copy-start.6 = (bf16[136,2048]{1,0:T(8,128)(2,1)S(1)}, bf16[136,2048]{1,0:T(8,128)(2,1)}, u32[]{:S(2)}) copy-start(bf16[136,2048]{1,0:T(8,128)(2,1)} %get-tuple-element.36.chunk_ref) | copy-start | bytes 1671172
  135.3 21.4 %collective-permute-start.14 = (bf16[128,2048]{1,0:T(8,128)(2,1)S(1)}, bf16[128,2048]{1,0:T(8,128)(2,1)S(1)}, u32[]{:S(2)}, u32[]{:S(2)}) collective-permute-start(bf16[128,2048]{1,0:T(8,128)(2,1)S(1)} %add_convert_fusion.7), channel_id=1, source_target_pairs={{2,0},{4,2},{6,4},{7,6},{5,7},{3,5},{1,3},{0,1},{10,8},{12,10},{14... | collective-permute-start | bytes 1572872 | tf_op jit(solution)/shard_map/ppermute | solution.py:253
  145.0 12.7 %collective-permute-start.25 = (bf16[128,2048]{1,0:T(8,128)(2,1)S(1)}, bf16[128,2048]{1,0:T(8,128)(2,1)S(1)}, u32[]{:S(2)}, u32[]{:S(2)}) collective-permute-start(bf16[128,2048]{1,0:T(8,128)(2,1)S(1)} %add_convert_fusion.2), channel_id=1, source_target_pairs={{0,2},{2,4},{4,6},{6,7},{7,5},{5,3},{3,1},{1,0},{8,10},{10,12},{12... | collective-permute-start | bytes 1572872 | tf_op jit(solution)/shard_map/ppermute | solution.py:254
  148.2 41.5 %collective-permute-start.8 = (bf16[128,2048]{1,0:T(8,128)(2,1)S(1)}, bf16[128,2048]{1,0:T(8,128)(2,1)S(1)}, u32[]{:S(2)}, u32[]{:S(2)}) collective-permute-start(bf16[128,2048]{1,0:T(8,128)(2,1)S(1)} %add_convert_fusion.8), channel_id=1, source_target_pairs={{0,2},{2,4},{4,6},{6,7},{7,5},{5,3},{3,1},{1,0},{8,10},{10,12},{12... | collective-permute-start | bytes 1572872 | tf_op jit(solution)/shard_map/ppermute | solution.py:252
  156.9 14.9 %collective-permute-start.15 = (bf16[128,2048]{1,0:T(8,128)(2,1)S(1)}, bf16[128,2048]{1,0:T(8,128)(2,1)S(1)}, u32[]{:S(2)}, u32[]{:S(2)}) collective-permute-start(bf16[128,2048]{1,0:T(8,128)(2,1)S(1)} %add_convert_fusion.6), channel_id=1, source_target_pairs={{2,0},{4,2},{6,4},{7,6},{5,7},{3,5},{1,3},{0,1},{10,8},{12,10},{14... | collective-permute-start | bytes 1572872 | tf_op jit(solution)/shard_map/ppermute | solution.py:253
  157.8 19.4 %collective-permute-start.26 = (bf16[128,2048]{1,0:T(8,128)(2,1)S(1)}, bf16[128,2048]{1,0:T(8,128)(2,1)S(1)}, u32[]{:S(2)}, u32[]{:S(2)}) collective-permute-start(bf16[128,2048]{1,0:T(8,128)(2,1)S(1)} %add_convert_fusion.1), channel_id=1, source_target_pairs={{0,2},{2,4},{4,6},{6,7},{7,5},{5,3},{3,1},{1,0},{8,10},{10,12},{12... | collective-permute-start | bytes 1572872 | tf_op jit(solution)/shard_map/ppermute | solution.py:254
  161.8 27.9 %collective-permute-start.22 = (bf16[128,2048]{1,0:T(8,128)(2,1)S(1)}, bf16[128,2048]{1,0:T(8,128)(2,1)S(1)}, u32[]{:S(2)}, u32[]{:S(2)}) collective-permute-start(bf16[128,2048]{1,0:T(8,128)(2,1)S(1)} %add_convert_fusion.3), channel_id=1, source_target_pairs={{2,0},{4,2},{6,4},{7,6},{5,7},{3,5},{1,3},{0,1},{10,8},{12,10},{14... | collective-permute-start | bytes 1572872 | tf_op jit(solution)/shard_map/ppermute | solution.py:251
  172.0 17.7 %collective-permute-start.16 = (bf16[128,2048]{1,0:T(8,128)(2,1)S(1)}, bf16[128,2048]{1,0:T(8,128)(2,1)S(1)}, u32[]{:S(2)}, u32[]{:S(2)}) collective-permute-start(bf16[128,2048]{1,0:T(8,128)(2,1)S(1)} %add_convert_fusion.5), channel_id=1, source_target_pairs={{2,0},{4,2},{6,4},{7,6},{5,7},{3,5},{1,3},{0,1},{10,8},{12,10},{14... | collective-permute-start | bytes 1572872 | tf_op jit(solution)/shard_map/ppermute | solution.py:253
  177.3 7.8 %copy-start.7 = (bf16[128,2048]{1,0:T(8,128)(2,1)S(1)}, bf16[128,2048]{1,0:T(8,128)(2,1)}, u32[]{:S(2)}) copy-start(bf16[128,2048]{1,0:T(8,128)(2,1)} %get-tuple-element.52.chunk_ref) | copy-start | bytes 1572868
  177.3 12.4 %collective-permute-start.27 = (bf16[128,2048]{1,0:T(8,128)(2,1)S(1)}, bf16[128,2048]{1,0:T(8,128)(2,1)S(1)}, u32[]{:S(2)}, u32[]{:S(2)}) collective-permute-start(bf16[128,2048]{1,0:T(8,128)(2,1)S(1)} %add_convert_fusion), channel_id=1, source_target_pairs={{0,2},{2,4},{4,6},{6,7},{7,5},{5,3},{3,1},{1,0},{8,10},{10,12},{12... | collective-permute-start | bytes 1572872 | tf_op jit(solution)/shard_map/ppermute | solution.py:254
  (4 other events, 13.6 us)
where the time goes:
time: 191 us
  Pallas kernels  83.7 us (44%)
  waiting for transfers between devices  58.4 us (31%)
  starting transfers between devices  37.2 us (19%)
  local copies, waits for them, and re-layouts  9.47 us (5%)
    pallas_call x9, Pallas kernels, tabled(): pl.pallas_call(functools.partial(tabled_kernel, firsts, slots, height), i...  47.6 us
    pallas_call x7, Pallas kernels, plain(): pl.pallas_call(plain_kernel, in_specs=[vmem] * 5, out_specs=[vmem, vmem],...  31.5 us
    ppermute x3, waiting for transfers between devices, body(): lead_a = lax.ppermute(add(lead_part_a, lead_a), 'expert', back)  16.1 us
    ppermute x1, waiting for transfers between devices, body(): far_a = run_a(lax.ppermute(lead_a, 'expert', ahead))[0]  11.1 us
    ppermute x3, waiting for transfers between devices, body(): lead_b = lax.ppermute(lead_b, 'expert', back)  10.8 us
    ppermute x3, starting transfers between devices, body(): lead_b = lax.ppermute(add(lead_part_b, lead_b), 'expert', ahead)  9.47 us
    unnamed x16, local copies, waits for them, and re-layouts  9.47 us
    ppermute x1, waiting for transfers between devices, body(): lax.ppermute(far_b, 'expert', ahead)  7.71 us
  transfers between devices with their start and end apart: 28, of which 10 were waited for; matrix products, arithmetic and copies ran while one was open for 1% of the time, Pallas kernels for 41%

commit v1 on v0

--- a/solution.py
+++ b/solution.py
@@ -108,84 +108,97 @@
     return shares.T
 
 
-def evaluate(chunk_ref, share_ref, gate_ref, up_ref, down_ref, out_ref, hidden_ref):
-    half, width = out_ref.shape
+def evaluate(rows_ref, share_ref, gate_ref, up_ref, down_ref, outs, hidden_ref):
+    half, width = outs[0].shape
     owned, _, units = gate_ref.shape
-    tile = 256 if units % 256 == 0 else units
-    tiles = units // tile
-    wide = 512 if width % 512 == 0 else width
-
-    def project(j, carry):
-        e = lax.div(j, tiles)
-        at = pl.ds(pl.multiple_of(lax.rem(j, tiles) * tile, tile), tile)
-        x = chunk_ref[:half, :]
-        gate = jnp.dot(x, gate_ref[e, :, at], preferred_element_type=jnp.float32)
-        upper = jnp.dot(x, up_ref[e, :, at], preferred_element_type=jnp.float32)
+    wide = width // 2 if width % 256 == 0 else width
+
+    def project(e, carry):
+        x = rows_ref[...]
+        gate = jnp.dot(x, gate_ref[e], preferred_element_type=jnp.float32)
+        upper = jnp.dot(x, up_ref[e], preferred_element_type=jnp.float32)
         shares = share_ref[...]
         lane = lax.broadcasted_iota(jnp.int32, shares.shape, 1)
         share = jnp.sum(jnp.where(lane == e, shares, 0.0), axis=1, keepdims=True)
         hidden = gate / (1.0 + jnp.exp(-gate)) * upper * share
-        hidden_ref[:, pl.ds(pl.multiple_of(j * tile, tile), tile)] = hidden.astype(jnp.bfloat16)
+        hidden_ref[:, pl.ds(pl.multiple_of(e * units, units), units)] = hidden.astype(jnp.bfloat16)
         return carry
 
-    lax.fori_loop(0, owned * tiles, project, 0)
+    lax.fori_loop(0, owned, project, 0)
 
     def fold(j, carry):
         at = pl.ds(pl.multiple_of(j * wide, wide), wide)
         part = jnp.dot(hidden_ref[...], down_ref[:, at], preferred_element_type=jnp.float32)
-        out_ref[:, at] = part.astype(jnp.bfloat16)
+        for i, out_ref in enumerate(outs):
+            out_ref[:, at] = part[i * half:(i + 1) * half].astype(jnp.bfloat16)
         return carry
 
     lax.fori_loop(0, width // wide, fold, 0)
 
 
-def tabled_kernel(firsts, slots, height, place_ref, chunk_ref, gate_ref, up_ref, down_ref, out_ref, other_ref,
-                  share_ref, hidden_ref):
+def lead_kernel(slots, height, place_ref, a_ref, b_ref, gate_ref, up_ref, down_ref, *refs):
+    out_a_ref, out_b_ref, other_ref, rows_ref, share_ref, hidden_ref = refs[-6:]
     owned = gate_ref.shape[0]
-    share_ref[...] = columns(place_ref, chunk_ref, firsts[0], slots, height, owned)
-    other_ref[...] = columns(place_ref, chunk_ref, firsts[1], slots, height, owned)
-    evaluate(chunk_ref, share_ref, gate_ref, up_ref, down_ref, out_ref, hidden_ref)
-
-
-def plain_kernel(chunk_ref, share_ref, gate_ref, up_ref, down_ref, out_ref, same_ref, hidden_ref):
-    del same_ref
-    evaluate(chunk_ref, share_ref, gate_ref, up_ref, down_ref, out_ref, hidden_ref)
-
-
-def cost(half, w_gate):
+    half = height // 2
+    for i, (ref, first) in enumerate(((a_ref, 0), (b_ref, half))):
+        at = slice(i * half, (i + 1) * half)
+        rows_ref[at, :] = ref[:half, :]
+        share_ref[at, :] = columns(place_ref, ref, first, slots, height, owned)
+        other_ref[at, :] = columns(place_ref, ref, half - first, slots, height, owned)
+    evaluate(rows_ref, share_ref, gate_ref, up_ref, down_ref, (out_a_ref, out_b_ref), hidden_ref)
+
+
+def plain_kernel(b_ref, a_ref, share_ref, gate_ref, up_ref, down_ref, out_b_ref, out_a_ref, same_b_ref, same_a_ref,
+                 rows_ref, hidden_ref):
+    del same_b_ref, same_a_ref
+    half = b_ref.shape[0]
+    rows_ref[:half, :] = b_ref[...]
+    rows_ref[half:, :] = a_ref[...]
+    evaluate(rows_ref, share_ref, gate_ref, up_ref, down_ref, (out_b_ref, out_a_ref), hidden_ref)
+
+
+def cost(rows, w_gate):
     owned, width, units = w_gate.shape
     return pl.CostEstimate(
-        flops=6 * half * width * units * owned, bytes_accessed=8 * half * width, transcendentals=half * units * owned
+        flops=6 * rows * width * units * owned, bytes_accessed=8 * rows * width, transcendentals=rows * units * owned
     )
 
 
-def tabled(place, weights, slots, height, firsts, chunk):
+def lead(place, weights, slots, height, a, b, earlier=()):
     half, (owned, width, units) = height // 2, weights[0].shape
     vmem = pl.BlockSpec(memory_space=pltpu.VMEM)
     return pl.pallas_call(
-        functools.partial(tabled_kernel, firsts, slots, height),
-        in_specs=[pl.BlockSpec(memory_space=pltpu.SMEM)] + [vmem] * 4,
-        out_specs=[vmem, vmem],
-        out_shape=[jax.ShapeDtypeStruct((half, width), jnp.bfloat16), jax.ShapeDtypeStruct((half, 128), jnp.float32)],
-        scratch_shapes=[pltpu.VMEM((half, 128), jnp.float32), pltpu.VMEM((half, owned * units), jnp.bfloat16)],
+        functools.partial(lead_kernel, slots, height),
+        in_specs=[pl.BlockSpec(memory_space=pltpu.SMEM)] + [vmem] * 5 + [pl.BlockSpec(memory_space=pl.ANY)] * len(earlier),
+        out_specs=[vmem] * 3,
+        out_shape=[jax.ShapeDtypeStruct((half, width), jnp.bfloat16)] * 2
+        + [jax.ShapeDtypeStruct((height, 128), jnp.float32)],
+        scratch_shapes=[
+            pltpu.VMEM((height, width), jnp.bfloat16),
+            pltpu.VMEM((height, 128), jnp.float32),
+            pltpu.VMEM((height, owned * units), jnp.bfloat16),
+        ],
         compiler_params=pltpu.CompilerParams(vmem_limit_bytes=VMEM_LIMIT),
-        cost_estimate=cost(half, weights[0]),
-    )(place, chunk, *weights)
-
-
-def plain(weights, chunk, shares):
-    (half, width), (owned, _, units) = chunk.shape, weights[0].shape
+        cost_estimate=cost(height, weights[0]),
+    )(place, a, b, *weights, *earlier)
+
+
+def plain(weights, b, a, shares):
+    (half, width), (owned, _, units) = b.shape, weights[0].shape
     vmem = pl.BlockSpec(memory_space=pltpu.VMEM)
     return pl.pallas_call(
         plain_kernel,
-        in_specs=[vmem] * 5,
-        out_specs=[vmem, vmem],
-        out_shape=[jax.ShapeDtypeStruct((half, width), jnp.bfloat16)] * 2,
-        scratch_shapes=[pltpu.VMEM((half, owned * units), jnp.bfloat16)],
-        input_output_aliases={0: 1},
+        in_specs=[vmem] * 6,
+        out_specs=[vmem] * 4,
+        out_shape=[jax.ShapeDtypeStruct((half, width), jnp.bfloat16)] * 4,
+        scratch_shapes=[
+            pltpu.VMEM((2 * half, width), jnp.bfloat16),
+            pltpu.VMEM((2 * half, owned * units), jnp.bfloat16),
+        ],
+        input_output_aliases={0: 2, 1: 3},
         compiler_params=pltpu.CompilerParams(vmem_limit_bytes=VMEM_LIMIT),
-        cost_estimate=cost(half, weights[0]),
-    )(chunk, shares, *weights)
+        cost_estimate=cost(2 * half, weights[0]),
+    )(b, a, shares, *weights)
 
 
 def finish_kernel(*refs):
@@ -227,23 +240,20 @@
     far = groups // 2
 
     lead_a, lead_b, a, b = pack(tokens, target, router_weight, slots)
-    run_a = functools.partial(tabled, place, weights, slots, height, (0, half))
-    run_b = functools.partial(tabled, place, weights, slots, height, (half, 0))
-    own_a, shares_b = run_a(lead_a)
-    own_b, _ = plain(weights, b, shares_b)
+    run = functools.partial(lead, place, weights, slots, height)
+    own_a, own_b, shares = run(lead_a, lead_b)
+    earlier = (shares,)
     parts = {}
     for s in range(1, far):
         lead_a = lax.ppermute(lead_a, "expert", ahead)
         lead_b = lax.ppermute(lead_b, "expert", back)
         b = lax.ppermute(b, "expert", ahead)
         a = lax.ppermute(a, "expert", back)
-        lead_part_a, shares_b = run_a(lead_a)
-        lead_part_b, shares_a = run_b(lead_b)
-        part_b, b = plain(weights, b, shares_b)
-        part_a, a = plain(weights, a, shares_a)
+        lead_part_a, lead_part_b, shares = run(lead_a, lead_b, earlier)
+        part_b, part_a, b, a = plain(weights, b, a, shares)
+        earlier = ()
         parts[s] = lead_part_a, lead_part_b, part_b, part_a
-    far_a = run_a(lax.ppermute(lead_a, "expert", ahead))[0]
-    far_b = run_b(lax.ppermute(lead_b, "expert", back))[0]
+    far_a, far_b, _ = run(lax.ppermute(lead_a, "expert", ahead), lax.ppermute(lead_b, "expert", back))
 
     lead_a, lead_b, a, b = lax.ppermute(far_a, "expert", back), lax.ppermute(far_b, "expert", ahead), None, None
     for s in range(far - 1, 0, -1):
@@ -252,7 +262,7 @@
         a = lax.ppermute(part_a if a is None else add(part_a, a), "expert", ahead)
         lead_a = lax.ppermute(add(lead_part_a, lead_a), "expert", back)
         lead_b = lax.ppermute(add(lead_part_b, lead_b), "expert", ahead)
-    return finish((own_a, a, lead_a), (own_b, b, lead_b))
+    return finish((own_a, lead_a, a), (own_b, lead_b, b))
 
 
 def solution(mesh):

time: 191 us -> 174 us (0.911)
  Pallas kernels: 83.7 us -> 54 us
  waiting for transfers between devices: 58.4 us -> 77.6 us
  starting transfers between devices: 37.2 us -> 29.3 us
    pallas_call x16 -> x8, Pallas kernels: 79.1 us -> 49.4 us  [the longest x5 32.1 us: lead(): pl.pallas_call(functools.partial(lead_kernel, slots, height), in_specs=[p...]
    ppermute x3, waiting for transfers between devices: 10.8 us -> 0.01 us  [body(): lead_b = lax.ppermute(lead_b, 'expert', back)]
    ppermute x2, waiting for transfers between devices: 13.1 us -> 4.08 us  [the longest x1 2.24 us: body(): lax.ppermute(lead_a, 'expert', ahead)]
    ppermute x3, waiting for transfers between devices: 16.1 us -> 24.8 us  [body(): lead_a = lax.ppermute(add(lead_part_a, lead_a), 'expert', back)]
    ppermute x1, waiting for transfers between devices: 2.52 us -> 10.9 us  [body(): lax.ppermute(far_a, 'expert', back)]
    ppermute x3, waiting for transfers between devices: 0.01 us -> 7.16 us  [body(): b = lax.ppermute(b, 'expert', ahead)]
    ppermute x3, waiting for transfers between devices: 0.01 us -> 6.57 us  [body(): lead_a = lax.ppermute(lead_a, 'expert', ahead)]
    ppermute x3, starting transfers between devices: 6.87 us -> 0.39 us  [body(): lead_b = lax.ppermute(lead_b, 'expert', back)]
  transfers between devices with their start and end apart: 28 -> 28, of which waited for: 10 -> 18; matrix products, arithmetic and copies ran while one was open for 1% -> 1% of each run, Pallas kernels for 41% -> 28%
where the time goes in v1:
time: 174 us; the launch traced here: 173 us
  waiting for transfers between devices  77.6 us (45%)
  Pallas kernels  54 us (31%)
  starting transfers between devices  29.3 us (17%)
  local copies, waits for them, and re-layouts  10.5 us (6%)
    pallas_call x5, Pallas kernels, lead(): pl.pallas_call(functools.partial(lead_kernel, slots, height), in_specs=[p...  32.1 us
    ppermute x3, waiting for transfers between devices, body(): lead_a = lax.ppermute(add(lead_part_a, lead_a), 'expert', back)  24.8 us
    pallas_call x3, Pallas kernels, plain(): pl.pallas_call(plain_kernel, in_specs=[vmem] * 6, out_specs=[vmem] * 4, o...  17.3 us
    ppermute x1, waiting for transfers between devices, body(): lax.ppermute(far_a, 'expert', back)  10.9 us
    unnamed x16, local copies, waits for them, and re-layouts  10.5 us
    ppermute x3, waiting for transfers between devices, body(): lead_b = lax.ppermute(add(lead_part_b, lead_b), 'expert', ahead)  9.94 us
    ppermute x1, waiting for transfers between devices, body(): lax.ppermute(far_b, 'expert', ahead)  7.57 us
    ppermute x3, waiting for transfers between devices, body(): b = lax.ppermute(b, 'expert', ahead)  7.16 us
  transfers between devices with their start and end apart: 28, of which 18 were waited for; matrix products, arithmetic and copies ran while one was open for 1% of the time, Pallas kernels for 28%

profile of v1, /device:TPU:0, one launch (start us, length us, event | category | flops | bytes accessed | tf_op | source)
XLA Modules:
  0.0 173.5 jit_solution(9649090946954242626)
XLA Ops:
  0.0 3.2 %shard_map.73 = (bf16[136,2048]{1,0:T(8,128)(2,1)}, bf16[136,2048]{1,0:T(8,128)(2,1)}, bf16[128,2048]{1,0:T(8,128)(2,1)}, bf16[128,2048]{1,0:T(8,128)(2,1)}) custom-call(bf16[256,2048]{1,0:T(8,128)(2,1)} %tokens_ref.1, s32[8,256]{1,0:T(8,128)} %bitcast.13, f32[8,256]{1,0:T(8,128)} %bitcast.14), custom_call_target="tpu_custom_call" | custom-call | bytes 2097152 | tf_op jit(solution)/shard_map/pallas_call | solution.py:72
  3.2 3.1 %collective-permute-start.12 = (bf16[128,2048]{1,0:T(8,128)(2,1)}, bf16[128,2048]{1,0:T(8,128)(2,1)S(1)}, u32[]{:S(2)}, u32[]{:S(2)}) collective-permute-start(bf16[128,2048]{1,0:T(8,128)(2,1)} %get-tuple-element.41), channel_id=1, source_target_pairs={{0,2},{2,4},{4,6},{6,7},{7,5},{5,3},{3,1},{1,0},{8,10},{10,12},{12... | collective-permute-start | bytes 1572872 | tf_op jit(solution)/shard_map/ppermute | solution.py:250
  6.3 2.0 %collective-permute-start = (bf16[136,2048]{1,0:T(8,128)(2,1)}, bf16[136,2048]{1,0:T(8,128)(2,1)S(1)}, u32[]{:S(2)}, u32[]{:S(2)}) collective-permute-start(bf16[136,2048]{1,0:T(8,128)(2,1)} %get-tuple-element.33.a_ref), channel_id=1, source_target_pairs={{0,2},{2,4},{4,6},{6,7},{7,5},{5,3},{3,1},{1,0},{8,10},{10,12},{12... | collective-permute-start | bytes 1671176 | tf_op jit(solution)/shard_map/ppermute | solution.py:248
  9.1 2.8 %copy-done = bf16[2,2048,768]{2,1,0:T(8,128)(2,1)S(1)} copy-done((bf16[2,2048,768]{2,1,0:T(8,128)(2,1)S(1)}, bf16[2,2048,768]{2,1,0:T(8,128)(2,1)}, u32[]{:S(2)}) %copy-start) | copy-done | bytes 6291480
  11.8 2.8 %copy-done.2 = bf16[2,2048,768]{2,1,0:T(8,128)(2,1)S(1)} copy-done((bf16[2,2048,768]{2,1,0:T(8,128)(2,1)S(1)}, bf16[2,2048,768]{2,1,0:T(8,128)(2,1)}, u32[]{:S(2)}) %copy-start.2) | copy-done | bytes 6291480
  14.6 2.8 %copy-done.4 = bf16[2,768,2048]{2,1,0:T(8,128)(2,1)S(1)} copy-done((bf16[2,768,2048]{2,1,0:T(8,128)(2,1)S(1)}, bf16[2,768,2048]{2,1,0:T(8,128)(2,1)}, u32[]{:S(2)}) %copy-start.4) | copy-done | bytes 6291480
  19.5 6.4 %shard_map.74 = (bf16[128,2048]{1,0:T(8,128)(2,1)S(1)}, bf16[128,2048]{1,0:T(8,128)(2,1)S(1)}, f32[256,128]{1,0:T(8,128)S(1)}) custom-call(s32[3]{0:T(128)S(1)} %pad_add_fusion.place_ref, bf16[136,2048]{1,0:T(8,128)(2,1)S(1)} %copy-done.7, bf16[136,2048]{1,0:T(8,128)(2,1)S(1)} %copy-done.6, bf16[2,2048,768]{2,1,0:T(8,128)(2,1)S(1)} %copy-done, ...), custom_call_target="tpu_custom_call" | custom-call | flops 4831838208 | bytes 4194304 | tf_op jit(solution)/shard_map/pallas_call | solution.py:170
  25.9 4.3 %collective-permute-done.a_ref = bf16[136,2048]{1,0:T(8,128)(2,1)S(1)} collective-permute-done((bf16[136,2048]{1,0:T(8,128)(2,1)}, bf16[136,2048]{1,0:T(8,128)(2,1)S(1)}, u32[]{:S(2)}, u32[]{:S(2)}) %collective-permute-start) | collective-permute-done | bytes 557088 | tf_op jit(solution)/shard_map/ppermute | solution.py:248
  32.3 6.4 %shard_map.75 = (bf16[128,2048]{1,0:T(8,128)(2,1)S(1)}, bf16[128,2048]{1,0:T(8,128)(2,1)S(1)}, f32[256,128]{1,0:T(8,128)S(1)}) custom-call(s32[3]{0:T(128)S(1)} %pad_add_fusion.place_ref, bf16[136,2048]{1,0:T(8,128)(2,1)S(1)} %collective-permute-done.a_ref, bf16[136,2048]{1,0:T(8,128)(2,1)S(1)} %collective-permute-done.1.b_ref, ...), custom_call_target="tpu_custom_call" | custom-call | flops 4831838208 | bytes 4194304 | tf_op jit(solution)/shard_map/pallas_call | solution.py:170
  38.7 5.8 %shard_map.79 = (bf16[128,2048]{1,0:T(8,128)(2,1)S(1)}, bf16[128,2048]{1,0:T(8,128)(2,1)S(1)}, bf16[128,2048]{1,0:T(8,128)(2,1)S(1)}, bf16[128,2048]{1,0:T(8,128)(2,1)S(1)}) custom-call(bf16[128,2048]{1,0:T(8,128)(2,1)S(1)} %collective-permute-done.12.b_ref, ...), custom_call_target="tpu_custom_call", output_to_operand_aliasing={{2}: (0, {}), {3}: (1, {})} | custom-call | flops 4831838208 | bytes 4194304 | tf_op jit(solution)/shard_map/pallas_call | solution.py:189
  44.5 1.9 %collective-permute-start.14 = (bf16[128,2048]{1,0:T(8,128)(2,1)S(1)}, bf16[128,2048]{1,0:T(8,128)(2,1)S(1)}, u32[]{:S(2)}, u32[]{:S(2)}) collective-permute-start(bf16[128,2048]{1,0:T(8,128)(2,1)S(1)} %get-tuple-element.45), channel_id=1, source_target_pairs={{0,2},{2,4},{4,6},{6,7},{7,5},{5,3},{3,1},{1,0},{8,10},{10,12},{12... | collective-permute-start | bytes 1572872 | tf_op jit(solution)/shard_map/ppermute | solution.py:250
  46.6 1.8 %collective-permute-start.4 = (bf16[136,2048]{1,0:T(8,128)(2,1)S(1)}, bf16[136,2048]{1,0:T(8,128)(2,1)S(1)}, u32[]{:S(2)}, u32[]{:S(2)}) collective-permute-start(bf16[136,2048]{1,0:T(8,128)(2,1)S(1)} %collective-permute-done.2.a_ref), channel_id=1, source_target_pairs={{0,2},{2,4},{4,6},{6,7},{7,5},{5,3},{3,1},{1,0},{8,10},{10,12},{12... | collective-permute-start | bytes 1671176 | tf_op jit(solution)/shard_map/ppermute | solution.py:248
  48.6 6.4 %shard_map.76 = (bf16[128,2048]{1,0:T(8,128)(2,1)S(1)}, bf16[128,2048]{1,0:T(8,128)(2,1)S(1)}, f32[256,128]{1,0:T(8,128)S(1)}) custom-call(s32[3]{0:T(128)S(1)} %pad_add_fusion.place_ref, bf16[136,2048]{1,0:T(8,128)(2,1)S(1)} %collective-permute-done.2.a_ref, bf16[136,2048]{1,0:T(8,128)(2,1)S(1)} %collective-permute-done.3.b_ref, ...), custom_call_target="tpu_custom_call" | custom-call | flops 4831838208 | bytes 4194304 | tf_op jit(solution)/shard_map/pallas_call | solution.py:170
  55.1 4.4 %collective-permute-done.14.b_ref = bf16[128,2048]{1,0:T(8,128)(2,1)S(1)} collective-permute-done((bf16[128,2048]{1,0:T(8,128)(2,1)S(1)}, bf16[128,2048]{1,0:T(8,128)(2,1)S(1)}, u32[]{:S(2)}, u32[]{:S(2)}) %collective-permute-start.14) | collective-permute-done | bytes 524320 | tf_op jit(solution)/shard_map/ppermute | solution.py:250
  59.4 1.8 %collective-permute-done.15.a_ref = bf16[128,2048]{1,0:T(8,128)(2,1)S(1)} collective-permute-done((bf16[128,2048]{1,0:T(8,128)(2,1)S(1)}, bf16[128,2048]{1,0:T(8,128)(2,1)S(1)}, u32[]{:S(2)}, u32[]{:S(2)}) %collective-permute-start.15) | collective-permute-done | bytes 524320 | tf_op jit(solution)/shard_map/ppermute | solution.py:251
  61.3 5.8 %shard_map.80 = (bf16[128,2048]{1,0:T(8,128)(2,1)S(1)}, bf16[128,2048]{1,0:T(8,128)(2,1)S(1)}, bf16[128,2048]{1,0:T(8,128)(2,1)S(1)}, bf16[128,2048]{1,0:T(8,128)(2,1)S(1)}) custom-call(bf16[128,2048]{1,0:T(8,128)(2,1)S(1)} %collective-permute-done.14.b_ref, ...), custom_call_target="tpu_custom_call", output_to_operand_aliasing={{2}: (0, {}), {3}: (1, {})} | custom-call | flops 4831838208 | bytes 4194304 | tf_op jit(solution)/shard_map/pallas_call | solution.py:189
  69.2 2.2 %collective-permute-done.4.a_ref = bf16[136,2048]{1,0:T(8,128)(2,1)S(1)} collective-permute-done((bf16[136,2048]{1,0:T(8,128)(2,1)S(1)}, bf16[136,2048]{1,0:T(8,128)(2,1)S(1)}, u32[]{:S(2)}, u32[]{:S(2)}) %collective-permute-start.4) | collective-permute-done | bytes 557088 | tf_op jit(solution)/shard_map/ppermute | solution.py:248
  71.4 1.8 %collective-permute-start.6 = (bf16[136,2048]{1,0:T(8,128)(2,1)S(1)}, bf16[136,2048]{1,0:T(8,128)(2,1)S(1)}, u32[]{:S(2)}, u32[]{:S(2)}) collective-permute-start(bf16[136,2048]{1,0:T(8,128)(2,1)S(1)} %collective-permute-done.4.a_ref), channel_id=1, source_target_pairs={{0,2},{2,4},{4,6},{6,7},{7,5},{5,3},{3,1},{1,0},{8,10},{10,12},{12... | collective-permute-start | bytes 1671176 | tf_op jit(solution)/shard_map/ppermute | solution.py:256
  73.4 6.4 %shard_map.77 = (bf16[128,2048]{1,0:T(8,128)(2,1)S(1)}, bf16[128,2048]{1,0:T(8,128)(2,1)S(1)}, f32[256,128]{1,0:T(8,128)S(1)}) custom-call(s32[3]{0:T(128)S(1)} %pad_add_fusion.place_ref, bf16[136,2048]{1,0:T(8,128)(2,1)S(1)} %collective-permute-done.4.a_ref, bf16[136,2048]{1,0:T(8,128)(2,1)S(1)} %collective-permute-done.5.b_ref, ...), custom_call_target="tpu_custom_call" | custom-call | flops 4831838208 | bytes 4194304 | tf_op jit(solution)/shard_map/pallas_call | solution.py:170
  79.8 2.8 %collective-permute-done.16.b_ref = bf16[128,2048]{1,0:T(8,128)(2,1)S(1)} collective-permute-done((bf16[128,2048]{1,0:T(8,128)(2,1)S(1)}, bf16[128,2048]{1,0:T(8,128)(2,1)S(1)}, u32[]{:S(2)}, u32[]{:S(2)}) %collective-permute-start.16) | collective-permute-done | bytes 524320 | tf_op jit(solution)/shard_map/ppermute | solution.py:250
  82.6 1.8 %collective-permute-done.17.a_ref = bf16[128,2048]{1,0:T(8,128)(2,1)S(1)} collective-permute-done((bf16[128,2048]{1,0:T(8,128)(2,1)S(1)}, bf16[128,2048]{1,0:T(8,128)(2,1)S(1)}, u32[]{:S(2)}, u32[]{:S(2)}) %collective-permute-start.17) | collective-permute-done | bytes 524320 | tf_op jit(solution)/shard_map/ppermute | solution.py:251
  84.5 5.8 %shard_map.81 = (bf16[128,2048]{1,0:T(8,128)(2,1)S(1)}, bf16[128,2048]{1,0:T(8,128)(2,1)S(1)}, bf16[128,2048]{1,0:T(8,128)(2,1)S(1)}, bf16[128,2048]{1,0:T(8,128)(2,1)S(1)}) custom-call(bf16[128,2048]{1,0:T(8,128)(2,1)S(1)} %collective-permute-done.16.b_ref, ...), custom_call_target="tpu_custom_call", output_to_operand_aliasing={{2}: (0, {}), {3}: (1, {})} | custom-call | flops 4831838208 | bytes 4194304 | tf_op jit(solution)/shard_map/pallas_call | solution.py:189
  92.3 2.2 %collective-permute-done.6.a_ref = bf16[136,2048]{1,0:T(8,128)(2,1)S(1)} collective-permute-done((bf16[136,2048]{1,0:T(8,128)(2,1)S(1)}, bf16[136,2048]{1,0:T(8,128)(2,1)S(1)}, u32[]{:S(2)}, u32[]{:S(2)}) %collective-permute-start.6) | collective-permute-done | bytes 557088 | tf_op jit(solution)/shard_map/ppermute | solution.py:256
  94.6 1.8 %collective-permute-done.7.b_ref = bf16[136,2048]{1,0:T(8,128)(2,1)S(1)} collective-permute-done((bf16[136,2048]{1,0:T(8,128)(2,1)S(1)}, bf16[136,2048]{1,0:T(8,128)(2,1)S(1)}, u32[]{:S(2)}, u32[]{:S(2)}) %collective-permute-start.7) | collective-permute-done | bytes 557088 | tf_op jit(solution)/shard_map/ppermute | solution.py:256
  96.4 6.4 %shard_map.78 = (bf16[128,2048]{1,0:T(8,128)(2,1)S(1)}, bf16[128,2048]{1,0:T(8,128)(2,1)S(1)}, f32[256,128]{1,0:T(8,128)}) custom-call(s32[3]{0:T(128)S(1)} %pad_add_fusion.place_ref, bf16[136,2048]{1,0:T(8,128)(2,1)S(1)} %collective-permute-done.6.a_ref, bf16[136,2048]{1,0:T(8,128)(2,1)S(1)} %collective-permute-done.7.b_ref, ...), custom_call_target="tpu_custom_call" | custom-call | flops 4831838208 | bytes 4194304 | tf_op jit(solution)/shard_map/pallas_call | solution.py:170
  108.0 10.9 %collective-permute-done.8 = bf16[128,2048]{1,0:T(8,128)(2,1)S(1)} collective-permute-done((bf16[128,2048]{1,0:T(8,128)(2,1)S(1)}, bf16[128,2048]{1,0:T(8,128)(2,1)S(1)}, u32[]{:S(2)}, u32[]{:S(2)}) %collective-permute-start.8) | collective-permute-done | bytes 524320 | tf_op jit(solution)/shard_map/ppermute | solution.py:258
  119.2 7.6 %collective-permute-done.21 = bf16[128,2048]{1,0:T(8,128)(2,1)S(1)} collective-permute-done((bf16[128,2048]{1,0:T(8,128)(2,1)S(1)}, bf16[128,2048]{1,0:T(8,128)(2,1)S(1)}, u32[]{:S(2)}, u32[]{:S(2)}) %collective-permute-start.21) | collective-permute-done | bytes 524320 | tf_op jit(solution)/shard_map/ppermute | solution.py:258
  130.3 8.1 %collective-permute-done.9 = bf16[128,2048]{1,0:T(8,128)(2,1)S(1)} collective-permute-done((bf16[128,2048]{1,0:T(8,128)(2,1)S(1)}, bf16[128,2048]{1,0:T(8,128)(2,1)S(1)}, u32[]{:S(2)}, u32[]{:S(2)}) %collective-permute-start.9) | collective-permute-done | bytes 524320 | tf_op jit(solution)/shard_map/ppermute | solution.py:263
  139.1 2.7 %collective-permute-done.22 = bf16[128,2048]{1,0:T(8,128)(2,1)S(1)} collective-permute-done((bf16[128,2048]{1,0:T(8,128)(2,1)S(1)}, bf16[128,2048]{1,0:T(8,128)(2,1)S(1)}, u32[]{:S(2)}, u32[]{:S(2)}) %collective-permute-start.22) | collective-permute-done | bytes 524320 | tf_op jit(solution)/shard_map/ppermute | solution.py:264
  144.3 9.2 %collective-permute-done.10 = bf16[128,2048]{1,0:T(8,128)(2,1)S(1)} collective-permute-done((bf16[128,2048]{1,0:T(8,128)(2,1)S(1)}, bf16[128,2048]{1,0:T(8,128)(2,1)S(1)}, u32[]{:S(2)}, u32[]{:S(2)}) %collective-permute-start.10) | collective-permute-done | bytes 524320 | tf_op jit(solution)/shard_map/ppermute | solution.py:263
  154.2 7.2 %collective-permute-done.23 = bf16[128,2048]{1,0:T(8,128)(2,1)S(1)} collective-permute-done((bf16[128,2048]{1,0:T(8,128)(2,1)S(1)}, bf16[128,2048]{1,0:T(8,128)(2,1)S(1)}, u32[]{:S(2)}, u32[]{:S(2)}) %collective-permute-start.23) | collective-permute-done | bytes 524320 | tf_op jit(solution)/shard_map/ppermute | solution.py:264
  164.7 7.4 %collective-permute-done.11.refs_1_ = bf16[128,2048]{1,0:T(8,128)(2,1)S(1)} collective-permute-done((bf16[128,2048]{1,0:T(8,128)(2,1)S(1)}, bf16[128,2048]{1,0:T(8,128)(2,1)S(1)}, u32[]{:S(2)}, u32[]{:S(2)}) %collective-permute-start.11) | collective-permute-done | bytes 524320 | tf_op jit(solution)/shard_map/ppermute | solution.py:263
  (61 shorter events, 26.4 us)
Async XLA Ops:
  3.2 35.5 %collective-permute-start.12 = (bf16[128,2048]{1,0:T(8,128)(2,1)}, bf16[128,2048]{1,0:T(8,128)(2,1)S(1)}, u32[]{:S(2)}, u32[]{:S(2)}) collective-permute-start(bf16[128,2048]{1,0:T(8,128)(2,1)} %get-tuple-element.41), channel_id=1, source_target_pairs={{0,2},{2,4},{4,6},{6,7},{7,5},{5,3},{3,1},{1,0},{8,10},{10,12},{12... | collective-permute-start | bytes 1572872 | tf_op jit(solution)/shard_map/ppermute | solution.py:250
  6.3 32.4 %collective-permute-start.13 = (bf16[128,2048]{1,0:T(8,128)(2,1)}, bf16[128,2048]{1,0:T(8,128)(2,1)S(1)}, u32[]{:S(2)}, u32[]{:S(2)}) collective-permute-start(bf16[128,2048]{1,0:T(8,128)(2,1)} %get-tuple-element.42), channel_id=1, source_target_pairs={{2,0},{4,2},{6,4},{7,6},{5,7},{3,5},{1,3},{0,1},{10,8},{12,10},{14... | collective-permute-start | bytes 1572872 | tf_op jit(solution)/shard_map/ppermute | solution.py:251
  6.3 24.0 %collective-permute-start = (bf16[136,2048]{1,0:T(8,128)(2,1)}, bf16[136,2048]{1,0:T(8,128)(2,1)S(1)}, u32[]{:S(2)}, u32[]{:S(2)}) collective-permute-start(bf16[136,2048]{1,0:T(8,128)(2,1)} %get-tuple-element.33.a_ref), channel_id=1, source_target_pairs={{0,2},{2,4},{4,6},{6,7},{7,5},{5,3},{3,1},{1,0},{8,10},{10,12},{12... | collective-permute-start | bytes 1671176 | tf_op jit(solution)/shard_map/ppermute | solution.py:248
  8.3 23.8 %collective-permute-start.1 = (bf16[136,2048]{1,0:T(8,128)(2,1)}, bf16[136,2048]{1,0:T(8,128)(2,1)S(1)}, u32[]{:S(2)}, u32[]{:S(2)}) collective-permute-start(bf16[136,2048]{1,0:T(8,128)(2,1)} %get-tuple-element.34.b_ref), channel_id=1, source_target_pairs={{2,0},{4,2},{6,4},{7,6},{5,7},{3,5},{1,3},{0,1},{10,8},{12,10},{14... | collective-permute-start | bytes 1671176 | tf_op jit(solution)/shard_map/ppermute | solution.py:249
  9.0 2.8 %copy-start = (bf16[2,2048,768]{2,1,0:T(8,128)(2,1)S(1)}, bf16[2,2048,768]{2,1,0:T(8,128)(2,1)}, u32[]{:S(2)}) copy-start(bf16[2,2048,768]{2,1,0:T(8,128)(2,1)} %gate_ref.15) | copy-start | bytes 18874372
  19.5 12.8 %copy-start.1 = (bf16[2,2048,768]{2,1,0:T(8,128)(2,1)S(1)}, bf16[2,2048,768]{2,1,0:T(8,128)(2,1)}, u32[]{:S(2)}) copy-start(bf16[2,2048,768]{2,1,0:T(8,128)(2,1)} %gate_ref.15) | copy-start | bytes 18874372
  19.5 12.8 %copy-start.3 = (bf16[2,2048,768]{2,1,0:T(8,128)(2,1)S(1)}, bf16[2,2048,768]{2,1,0:T(8,128)(2,1)}, u32[]{:S(2)}) copy-start(bf16[2,2048,768]{2,1,0:T(8,128)(2,1)} %up_ref.15) | copy-start | bytes 18874372
  19.5 12.8 %copy-start.5 = (bf16[2,768,2048]{2,1,0:T(8,128)(2,1)S(1)}, bf16[2,768,2048]{2,1,0:T(8,128)(2,1)}, u32[]{:S(2)}) copy-start(bf16[2,768,2048]{2,1,0:T(8,128)(2,1)} %param.13) | copy-start | bytes 18874372
  30.3 16.3 %collective-permute-start.2 = (bf16[136,2048]{1,0:T(8,128)(2,1)S(1)}, bf16[136,2048]{1,0:T(8,128)(2,1)S(1)}, u32[]{:S(2)}, u32[]{:S(2)}) collective-permute-start(bf16[136,2048]{1,0:T(8,128)(2,1)S(1)} %collective-permute-done.a_ref), channel_id=1, source_target_pairs={{0,2},{2,4},{4,6},{6,7},{7,5},{5,3},{3,1},{1,0},{8,10},{10,12},{12... | collective-permute-start | bytes 1671176 | tf_op jit(solution)/shard_map/ppermute | solution.py:248
  32.1 16.3 %collective-permute-start.3 = (bf16[136,2048]{1,0:T(8,128)(2,1)S(1)}, bf16[136,2048]{1,0:T(8,128)(2,1)S(1)}, u32[]{:S(2)}, u32[]{:S(2)}) collective-permute-start(bf16[136,2048]{1,0:T(8,128)(2,1)S(1)} %collective-permute-done.1.b_ref), channel_id=1, source_target_pairs={{2,0},{4,2},{6,4},{7,6},{5,7},{3,5},{1,3},{0,1},{10,8},{12,10},{14... | collective-permute-start | bytes 1671176 | tf_op jit(solution)/shard_map/ppermute | solution.py:249
  44.5 14.9 %collective-permute-start.14 = (bf16[128,2048]{1,0:T(8,128)(2,1)S(1)}, bf16[128,2048]{1,0:T(8,128)(2,1)S(1)}, u32[]{:S(2)}, u32[]{:S(2)}) collective-permute-start(bf16[128,2048]{1,0:T(8,128)(2,1)S(1)} %get-tuple-element.45), channel_id=1, source_target_pairs={{0,2},{2,4},{4,6},{6,7},{7,5},{5,3},{3,1},{1,0},{8,10},{10,12},{12... | collective-permute-start | bytes 1572872 | tf_op jit(solution)/shard_map/ppermute | solution.py:250
  46.4 14.9 %collective-permute-start.15 = (bf16[128,2048]{1,0:T(8,128)(2,1)S(1)}, bf16[128,2048]{1,0:T(8,128)(2,1)S(1)}, u32[]{:S(2)}, u32[]{:S(2)}) collective-permute-start(bf16[128,2048]{1,0:T(8,128)(2,1)S(1)} %get-tuple-element.46), channel_id=1, source_target_pairs={{2,0},{4,2},{6,4},{7,6},{5,7},{3,5},{1,3},{0,1},{10,8},{12,10},{14... | collective-permute-start | bytes 1572872 | tf_op jit(solution)/shard_map/ppermute | solution.py:251
  46.6 24.8 %collective-permute-start.4 = (bf16[136,2048]{1,0:T(8,128)(2,1)S(1)}, bf16[136,2048]{1,0:T(8,128)(2,1)S(1)}, u32[]{:S(2)}, u32[]{:S(2)}) collective-permute-start(bf16[136,2048]{1,0:T(8,128)(2,1)S(1)} %collective-permute-done.2.a_ref), channel_id=1, source_target_pairs={{0,2},{2,4},{4,6},{6,7},{7,5},{5,3},{3,1},{1,0},{8,10},{10,12},{12... | collective-permute-start | bytes 1671176 | tf_op jit(solution)/shard_map/ppermute | solution.py:248
  48.4 24.8 %collective-permute-start.5 = (bf16[136,2048]{1,0:T(8,128)(2,1)S(1)}, bf16[136,2048]{1,0:T(8,128)(2,1)S(1)}, u32[]{:S(2)}, u32[]{:S(2)}) collective-permute-start(bf16[136,2048]{1,0:T(8,128)(2,1)S(1)} %collective-permute-done.3.b_ref), channel_id=1, source_target_pairs={{2,0},{4,2},{6,4},{7,6},{5,7},{3,5},{1,3},{0,1},{10,8},{12,10},{14... | collective-permute-start | bytes 1671176 | tf_op jit(solution)/shard_map/ppermute | solution.py:249
  67.1 15.5 %collective-permute-start.16 = (bf16[128,2048]{1,0:T(8,128)(2,1)S(1)}, bf16[128,2048]{1,0:T(8,128)(2,1)S(1)}, u32[]{:S(2)}, u32[]{:S(2)}) collective-permute-start(bf16[128,2048]{1,0:T(8,128)(2,1)S(1)} %get-tuple-element.49), channel_id=1, source_target_pairs={{0,2},{2,4},{4,6},{6,7},{7,5},{5,3},{3,1},{1,0},{8,10},{10,12},{12... | collective-permute-start | bytes 1572872 | tf_op jit(solution)/shard_map/ppermute | solution.py:250
  68.7 15.7 %collective-permute-start.17 = (bf16[128,2048]{1,0:T(8,128)(2,1)S(1)}, bf16[128,2048]{1,0:T(8,128)(2,1)S(1)}, u32[]{:S(2)}, u32[]{:S(2)}) collective-permute-start(bf16[128,2048]{1,0:T(8,128)(2,1)S(1)} %get-tuple-element.50), channel_id=1, source_target_pairs={{2,0},{4,2},{6,4},{7,6},{5,7},{3,5},{1,3},{0,1},{10,8},{12,10},{14... | collective-permute-start | bytes 1572872 | tf_op jit(solution)/shard_map/ppermute | solution.py:251
  71.4 23.2 %collective-permute-start.6 = (bf16[136,2048]{1,0:T(8,128)(2,1)S(1)}, bf16[136,2048]{1,0:T(8,128)(2,1)S(1)}, u32[]{:S(2)}, u32[]{:S(2)}) collective-permute-start(bf16[136,2048]{1,0:T(8,128)(2,1)S(1)} %collective-permute-done.4.a_ref), channel_id=1, source_target_pairs={{0,2},{2,4},{4,6},{6,7},{7,5},{5,3},{3,1},{1,0},{8,10},{10,12},{12... | collective-permute-start | bytes 1671176 | tf_op jit(solution)/shard_map/ppermute | solution.py:256
  73.2 23.2 %collective-permute-start.7 = (bf16[136,2048]{1,0:T(8,128)(2,1)S(1)}, bf16[136,2048]{1,0:T(8,128)(2,1)S(1)}, u32[]{:S(2)}, u32[]{:S(2)}) collective-permute-start(bf16[136,2048]{1,0:T(8,128)(2,1)S(1)} %collective-permute-done.5.b_ref), channel_id=1, source_target_pairs={{2,0},{4,2},{6,4},{7,6},{5,7},{3,5},{1,3},{0,1},{10,8},{12,10},{14... | collective-permute-start | bytes 1671176 | tf_op jit(solution)/shard_map/ppermute | solution.py:256
  90.2 13.2 %collective-permute-start.18 = (bf16[128,2048]{1,0:T(8,128)(2,1)S(1)}, bf16[128,2048]{1,0:T(8,128)(2,1)S(1)}, u32[]{:S(2)}, u32[]{:S(2)}) collective-permute-start(bf16[128,2048]{1,0:T(8,128)(2,1)S(1)} %get-tuple-element.52), channel_id=1, source_target_pairs={{0,2},{2,4},{4,6},{6,7},{7,5},{5,3},{3,1},{1,0},{8,10},{10,12},{12... | collective-permute-start | bytes 1572872 | tf_op jit(solution)/shard_map/ppermute | solution.py:262
  91.9 15.8 %collective-permute-start.25 = (bf16[128,2048]{1,0:T(8,128)(2,1)S(1)}, bf16[128,2048]{1,0:T(8,128)(2,1)S(1)}, u32[]{:S(2)}, u32[]{:S(2)}) collective-permute-start(bf16[128,2048]{1,0:T(8,128)(2,1)S(1)} %get-tuple-element.60), channel_id=1, source_target_pairs={{2,0},{4,2},{6,4},{7,6},{5,7},{3,5},{1,3},{0,1},{10,8},{12,10},{14... | collective-permute-start | bytes 1572872 | tf_op jit(solution)/shard_map/ppermute | solution.py:261
  102.8 16.0 %collective-permute-start.8 = (bf16[128,2048]{1,0:T(8,128)(2,1)S(1)}, bf16[128,2048]{1,0:T(8,128)(2,1)S(1)}, u32[]{:S(2)}, u32[]{:S(2)}) collective-permute-start(bf16[128,2048]{1,0:T(8,128)(2,1)S(1)} %get-tuple-element.40), channel_id=1, source_target_pairs={{2,0},{4,2},{6,4},{7,6},{5,7},{3,5},{1,3},{0,1},{10,8},{12,10},{14... | collective-permute-start | bytes 1572872 | tf_op jit(solution)/shard_map/ppermute | solution.py:258
  103.6 24.9 %collective-permute-start.19 = (bf16[128,2048]{1,0:T(8,128)(2,1)S(1)}, bf16[128,2048]{1,0:T(8,128)(2,1)S(1)}, u32[]{:S(2)}, u32[]{:S(2)}) collective-permute-start(bf16[128,2048]{1,0:T(8,128)(2,1)S(1)} %add_convert_fusion.6), channel_id=1, source_target_pairs={{0,2},{2,4},{4,6},{6,7},{7,5},{5,3},{3,1},{1,0},{8,10},{10,12},{12... | collective-permute-start | bytes 1572872 | tf_op jit(solution)/shard_map/ppermute | solution.py:262
  105.2 21.6 %collective-permute-start.21 = (bf16[128,2048]{1,0:T(8,128)(2,1)S(1)}, bf16[128,2048]{1,0:T(8,128)(2,1)S(1)}, u32[]{:S(2)}, u32[]{:S(2)}) collective-permute-start(bf16[128,2048]{1,0:T(8,128)(2,1)S(1)} %get-tuple-element.57), channel_id=1, source_target_pairs={{0,2},{2,4},{4,6},{6,7},{7,5},{5,3},{3,1},{1,0},{8,10},{10,12},{12... | collective-permute-start | bytes 1572872 | tf_op jit(solution)/shard_map/ppermute | solution.py:258
  107.8 35.8 %collective-permute-start.26 = (bf16[128,2048]{1,0:T(8,128)(2,1)S(1)}, bf16[128,2048]{1,0:T(8,128)(2,1)S(1)}, u32[]{:S(2)}, u32[]{:S(2)}) collective-permute-start(bf16[128,2048]{1,0:T(8,128)(2,1)S(1)} %add_convert_fusion.1), channel_id=1, source_target_pairs={{2,0},{4,2},{6,4},{7,6},{5,7},{3,5},{1,3},{0,1},{10,8},{12,10},{14... | collective-permute-start | bytes 1572872 | tf_op jit(solution)/shard_map/ppermute | solution.py:261
  119.0 19.4 %collective-permute-start.9 = (bf16[128,2048]{1,0:T(8,128)(2,1)S(1)}, bf16[128,2048]{1,0:T(8,128)(2,1)S(1)}, u32[]{:S(2)}, u32[]{:S(2)}) collective-permute-start(bf16[128,2048]{1,0:T(8,128)(2,1)S(1)} %add_convert_fusion.9), channel_id=1, source_target_pairs={{2,0},{4,2},{6,4},{7,6},{5,7},{3,5},{1,3},{0,1},{10,8},{12,10},{14... | collective-permute-start | bytes 1572872 | tf_op jit(solution)/shard_map/ppermute | solution.py:263
  126.9 14.9 %collective-permute-start.22 = (bf16[128,2048]{1,0:T(8,128)(2,1)S(1)}, bf16[128,2048]{1,0:T(8,128)(2,1)S(1)}, u32[]{:S(2)}, u32[]{:S(2)}) collective-permute-start(bf16[128,2048]{1,0:T(8,128)(2,1)S(1)} %add_convert_fusion.4), channel_id=1, source_target_pairs={{0,2},{2,4},{4,6},{6,7},{7,5},{5,3},{3,1},{1,0},{8,10},{10,12},{12... | collective-permute-start | bytes 1572872 | tf_op jit(solution)/shard_map/ppermute | solution.py:264
  128.6 34.4 %collective-permute-start.20 = (bf16[128,2048]{1,0:T(8,128)(2,1)S(1)}, bf16[128,2048]{1,0:T(8,128)(2,1)S(1)}, u32[]{:S(2)}, u32[]{:S(2)}) collective-permute-start(bf16[128,2048]{1,0:T(8,128)(2,1)S(1)} %add_convert_fusion.5), channel_id=1, source_target_pairs={{0,2},{2,4},{4,6},{6,7},{7,5},{5,3},{3,1},{1,0},{8,10},{10,12},{12... | collective-permute-start | bytes 1572872 | tf_op jit(solution)/shard_map/ppermute | solution.py:262
  138.6 14.9 %collective-permute-start.10 = (bf16[128,2048]{1,0:T(8,128)(2,1)S(1)}, bf16[128,2048]{1,0:T(8,128)(2,1)S(1)}, u32[]{:S(2)}, u32[]{:S(2)}) collective-permute-start(bf16[128,2048]{1,0:T(8,128)(2,1)S(1)} %add_convert_fusion.8), channel_id=1, source_target_pairs={{2,0},{4,2},{6,4},{7,6},{5,7},{3,5},{1,3},{0,1},{10,8},{12,10},{14... | collective-permute-start | bytes 1572872 | tf_op jit(solution)/shard_map/ppermute | solution.py:263
  142.0 19.4 %collective-permute-start.23 = (bf16[128,2048]{1,0:T(8,128)(2,1)S(1)}, bf16[128,2048]{1,0:T(8,128)(2,1)S(1)}, u32[]{:S(2)}, u32[]{:S(2)}) collective-permute-start(bf16[128,2048]{1,0:T(8,128)(2,1)S(1)} %add_convert_fusion.3), channel_id=1, source_target_pairs={{0,2},{2,4},{4,6},{6,7},{7,5},{5,3},{3,1},{1,0},{8,10},{10,12},{12... | collective-permute-start | bytes 1572872 | tf_op jit(solution)/shard_map/ppermute | solution.py:264
  143.7 21.0 %collective-permute-start.27 = (bf16[128,2048]{1,0:T(8,128)(2,1)S(1)}, bf16[128,2048]{1,0:T(8,128)(2,1)S(1)}, u32[]{:S(2)}, u32[]{:S(2)}) collective-permute-start(bf16[128,2048]{1,0:T(8,128)(2,1)S(1)} %add_convert_fusion), channel_id=1, source_target_pairs={{2,0},{4,2},{6,4},{7,6},{5,7},{3,5},{1,3},{0,1},{10,8},{12,10},{14... | collective-permute-start | bytes 1572872 | tf_op jit(solution)/shard_map/ppermute | solution.py:261
  153.6 18.5 %collective-permute-start.11 = (bf16[128,2048]{1,0:T(8,128)(2,1)S(1)}, bf16[128,2048]{1,0:T(8,128)(2,1)S(1)}, u32[]{:S(2)}, u32[]{:S(2)}) collective-permute-start(bf16[128,2048]{1,0:T(8,128)(2,1)S(1)} %add_convert_fusion.7), channel_id=1, source_target_pairs={{2,0},{4,2},{6,4},{7,6},{5,7},{3,5},{1,3},{0,1},{10,8},{12,10},{14... | collective-permute-start | bytes 1572872 | tf_op jit(solution)/shard_map/ppermute | solution.py:263
  161.5 10.6 %collective-permute-start.24 = (bf16[128,2048]{1,0:T(8,128)(2,1)S(1)}, bf16[128,2048]{1,0:T(8,128)(2,1)S(1)}, u32[]{:S(2)}, u32[]{:S(2)}) collective-permute-start(bf16[128,2048]{1,0:T(8,128)(2,1)S(1)} %add_convert_fusion.2), channel_id=1, source_target_pairs={{0,2},{2,4},{4,6},{6,7},{7,5},{5,3},{3,1},{1,0},{8,10},{10,12},{12... | collective-permute-start | bytes 1572872 | tf_op jit(solution)/shard_map/ppermute | solution.py:264
  (4 other events, 7.7 us)

commit v2 on v1

--- a/solution.py
+++ b/solution.py
@@ -8,7 +8,8 @@
 from jax.sharding import PartitionSpec as P
 
 VMEM_LIMIT = 12 * 1024 * 1024
-PACK_LIMIT = 56 * 1024 * 1024
+SPLIT_LIMIT = 56 * 1024 * 1024
+PACK_LIMIT = 40 * 1024 * 1024
 
 
 def ring_order(groups):
@@ -26,21 +27,44 @@
     return one, -(-2 * one // 8) * 8
 
 
-def pack_kernel(slots, tokens_ref, target_ref, weight_ref, *refs):
-    tabled, plain = refs[:2], refs[2:4]
-    target_buf, weight_buf, sems = refs[4:]
-    height, width = tokens_ref.shape
-    half = height // 2
+def split_kernel(tokens_ref, a_ref, b_ref, sems):
+    half = a_ref.shape[0]
+    copies = [
+        pltpu.make_async_copy(tokens_ref.at[pl.ds(i * half, half)], ref, sems.at[i]) for i, ref in enumerate((a_ref, b_ref))
+    ]
+    for copy in copies:
+        copy.start()
+    for copy in copies:
+        copy.wait()
+
+
+def split(tokens):
+    height, width = tokens.shape
+    anywhere = pl.BlockSpec(memory_space=pl.ANY)
+    return pl.pallas_call(
+        split_kernel,
+        in_specs=[anywhere],
+        out_specs=[anywhere] * 2,
+        out_shape=[jax.ShapeDtypeStruct((height // 2, width), jnp.bfloat16)] * 2,
+        scratch_shapes=[pltpu.SemaphoreType.DMA((2,))],
+        compiler_params=pltpu.CompilerParams(vmem_limit_bytes=SPLIT_LIMIT),
+        cost_estimate=pl.CostEstimate(flops=0, bytes_accessed=4 * height * width, transcendentals=0),
+    )(tokens)
+
+
+def pack_kernel(slots, a_ref, b_ref, target_ref, weight_ref, *refs):
+    tabled = refs[:2]
+    target_buf, weight_buf, sems = refs[2:]
+    half, width = a_ref.shape
+    height = 2 * half
     one, extra = table_rows(slots, height, width)
     per_row = width // height
     copies = [
         pltpu.make_async_copy(target_ref, target_buf, sems.at[0]),
         pltpu.make_async_copy(weight_ref, weight_buf, sems.at[1]),
+        pltpu.make_async_copy(a_ref, tabled[0].at[pl.ds(0, half)], sems.at[2]),
+        pltpu.make_async_copy(b_ref, tabled[1].at[pl.ds(0, half)], sems.at[3]),
     ]
-    for i in range(2):
-        rows = tokens_ref.at[pl.ds(i * half, half)]
-        copies.append(pltpu.make_async_copy(rows, tabled[i].at[pl.ds(0, half)], sems.at[2 + i]))
-        copies.append(pltpu.make_async_copy(rows, plain[i], sems.at[4 + i]))
     for copy in copies:
         copy.start()
     copies[0].wait()
@@ -64,25 +88,24 @@
         copy.wait()
 
 
-def pack(tokens, target, router_weight, slots):
-    height, width = tokens.shape
-    half, top = height // 2, target.shape[1]
+def pack(a, b, target, router_weight, slots):
+    half, width = a.shape
+    height, top = target.shape
     extra = table_rows(slots, height, width)[1]
     vmem = pl.BlockSpec(memory_space=pltpu.VMEM)
     return pl.pallas_call(
         functools.partial(pack_kernel, slots),
-        in_specs=[pl.BlockSpec(memory_space=pl.ANY)] * 3,
-        out_specs=[vmem] * 4,
-        out_shape=[jax.ShapeDtypeStruct((half + extra, width), jnp.bfloat16)] * 2
-        + [jax.ShapeDtypeStruct((half, width), jnp.bfloat16)] * 2,
+        in_specs=[pl.BlockSpec(memory_space=pl.ANY)] * 4,
+        out_specs=[vmem] * 2,
+        out_shape=[jax.ShapeDtypeStruct((half + extra, width), jnp.bfloat16)] * 2,
         scratch_shapes=[
             pltpu.VMEM((top, height), jnp.int32),
             pltpu.VMEM((top, height), jnp.float32),
-            pltpu.SemaphoreType.DMA((6,)),
+            pltpu.SemaphoreType.DMA((4,)),
         ],
         compiler_params=pltpu.CompilerParams(vmem_limit_bytes=PACK_LIMIT),
         cost_estimate=pl.CostEstimate(flops=0, bytes_accessed=4 * height * width, transcendentals=0),
-    )(tokens, target.T, router_weight.T)
+    )(a, b, target.T, router_weight.T)
 
 
 def columns(place_ref, table_ref, first, slots, height, owned):
@@ -201,24 +224,28 @@
     )(b, a, shares, *weights)
 
 
-def finish_kernel(*refs):
-    out_ref = refs[-1]
-    half = refs[0].shape[0]
-    for i in range(2):
-        total = sum(ref[...].astype(jnp.float32) for ref in refs[3 * i:3 * i + 3])
-        out_ref[i * half:(i + 1) * half, :] = total.astype(out_ref.dtype)
-
-
-def finish(a, b):
-    half, width = a[0].shape
-    vmem = pl.BlockSpec(memory_space=pltpu.VMEM)
-    return pl.pallas_call(
-        finish_kernel,
-        in_specs=[vmem] * 6,
-        out_specs=vmem,
-        out_shape=jax.ShapeDtypeStruct((2 * half, width), a[0].dtype),
+def finish_kernel(index, own_ref, first_ref, last_ref, *refs):
+    out_ref, total_ref, sem = refs[-3:]
+    half = own_ref.shape[0]
+    total = own_ref[...].astype(jnp.float32) + first_ref[...].astype(jnp.float32) + last_ref[...].astype(jnp.float32)
+    total_ref[...] = total.astype(total_ref.dtype)
+    copy = pltpu.make_async_copy(total_ref, out_ref.at[pl.ds(index * half, half)], sem)
+    copy.start()
+    copy.wait()
+
+
+def finish(index, terms, out=()):
+    half, width = terms[0].shape
+    vmem, anywhere = pl.BlockSpec(memory_space=pltpu.VMEM), pl.BlockSpec(memory_space=pl.ANY)
+    return pl.pallas_call(
+        functools.partial(finish_kernel, index),
+        in_specs=[vmem] * 3 + [anywhere] * len(out),
+        out_specs=anywhere,
+        out_shape=jax.ShapeDtypeStruct((2 * half, width), terms[0].dtype),
+        scratch_shapes=[pltpu.VMEM((half, width), terms[0].dtype), pltpu.SemaphoreType.DMA],
+        input_output_aliases={3: 0} if out else {},
         compiler_params=pltpu.CompilerParams(vmem_limit_bytes=VMEM_LIMIT),
-    )(*a, *b)
+    )(*terms, *out)
 
 
 def add(a, b):
@@ -239,7 +266,8 @@
     weights = w_gate, w_up, w_down.reshape(-1, width)
     far = groups // 2
 
-    lead_a, lead_b, a, b = pack(tokens, target, router_weight, slots)
+    a, b = split(tokens)
+    lead_a, lead_b = pack(a, b, target, router_weight, slots)
     run = functools.partial(lead, place, weights, slots, height)
     own_a, own_b, shares = run(lead_a, lead_b)
     earlier = (shares,)
@@ -262,7 +290,8 @@
         a = lax.ppermute(part_a if a is None else add(part_a, a), "expert", ahead)
         lead_a = lax.ppermute(add(lead_part_a, lead_a), "expert", back)
         lead_b = lax.ppermute(add(lead_part_b, lead_b), "expert", ahead)
-    return finish((own_a, lead_a, a), (own_b, lead_b, b))
+    out = finish(0, (own_a, lead_a, a))
+    return finish(1, (own_b, lead_b, b), (out,))
 
 
 def solution(mesh):

time: 174 us -> 204 us (1.17)
  Pallas kernels: 54 us -> 84.5 us
  waiting for transfers between devices: 77.6 us -> 72.6 us
  starting transfers between devices: 29.3 us -> 32.7 us
    pallas_call x1 -> x3, Pallas kernels: 1.34 us -> 34.9 us  [the longest x1 32.9 us: split(): pl.pallas_call(split_kernel, in_specs=[anywhere], out_specs=[anywhere] *...]
    ppermute x3, waiting for transfers between devices: 9.94 us -> 0.01 us  [body(): lead_b = lax.ppermute(add(lead_part_b, lead_b), 'expert', ahead)]
    ppermute x3, waiting for transfers between devices: 24.8 us -> 33.6 us  [body(): lead_a = lax.ppermute(add(lead_part_a, lead_a), 'expert', back)]
    ppermute x3, waiting for transfers between devices: 2.5 us -> 8.39 us  [body(): b = lax.ppermute(part_b if b is None else add(part_b, b), 'expert', back)]
    ppermute x3, starting transfers between devices: 0.64 us -> 4.95 us  [body(): a = lax.ppermute(a, 'expert', back)]
    ppermute x3, starting transfers between devices: 6.59 us -> 2.35 us  [body(): b = lax.ppermute(b, 'expert', ahead)]
    ppermute x1, waiting for transfers between devices: 7.57 us -> 3.63 us  [body(): lax.ppermute(far_b, 'expert', ahead)]
    ppermute x1, waiting for transfers between devices: 10.9 us -> 7.16 us  [body(): lax.ppermute(far_a, 'expert', back)]
  transfers between devices with their start and end apart: 28 -> 28, of which waited for: 18 -> 15; matrix products, arithmetic and copies ran while one was open for 1% -> 1% of each run, Pallas kernels for 28% -> 25%
where the time goes in v2:
time: 204 us
  Pallas kernels  84.5 us (41%)
  waiting for transfers between devices  72.6 us (36%)
  starting transfers between devices  32.7 us (16%)
  local copies, waits for them, and re-layouts  11.9 us (6%)
    ppermute x3, waiting for transfers between devices, body(): lead_a = lax.ppermute(add(lead_part_a, lead_a), 'expert', back)  33.6 us
    pallas_call x1, Pallas kernels, split(): pl.pallas_call(split_kernel, in_specs=[anywhere], out_specs=[anywhere] *...  32.9 us
    pallas_call x5, Pallas kernels, lead(): pl.pallas_call(functools.partial(lead_kernel, slots, height), in_specs=[p...  32 us
    pallas_call x3, Pallas kernels, plain(): pl.pallas_call(plain_kernel, in_specs=[vmem] * 6, out_specs=[vmem] * 4, o...  17.4 us
    unnamed x20, local copies, waits for them, and re-layouts  11.9 us
    ppermute x3, waiting for transfers between devices, body(): b = lax.ppermute(part_b if b is None else add(part_b, b), 'expert', back)  8.39 us
    ppermute x3, waiting for transfers between devices, body(): lead_a = lax.ppermute(lead_a, 'expert', ahead)  7.69 us
    ppermute x1, waiting for transfers between devices, body(): lax.ppermute(far_a, 'expert', back)  7.16 us
  transfers between devices with their start and end apart: 28, of which 15 were waited for; matrix products, arithmetic and copies ran while one was open for 1% of the time, Pallas kernels for 25%

profile of v2, /device:TPU:0, one launch (start us, length us, event | category | flops | bytes accessed | tf_op | source)
XLA Modules:
  0.0 204.1 jit_solution(11951101296468910952)
XLA Ops:
  0.0 32.9 %shard_map.73 = (bf16[128,2048]{1,0:T(8,128)(2,1)}, bf16[128,2048]{1,0:T(8,128)(2,1)}) custom-call(bf16[256,2048]{1,0:T(8,128)(2,1)} %tokens_ref.1), custom_call_target="tpu_custom_call" | custom-call | bytes 2097152 | tf_op jit(solution)/shard_map/pallas_call | solution.py:44
  32.9 3.0 %collective-permute-start.13 = (bf16[128,2048]{1,0:T(8,128)(2,1)}, bf16[128,2048]{1,0:T(8,128)(2,1)S(1)}, u32[]{:S(2)}, u32[]{:S(2)}) collective-permute-start(bf16[128,2048]{1,0:T(8,128)(2,1)} %get-tuple-element.33.a_ref), channel_id=1, source_target_pairs={{2,0},{4,2},{6,4},{7,6},{5,7},{3,5},{1,3},{0,1},{10,8},{12,10},{14... | collective-permute-start | bytes 1572872 | tf_op jit(solution)/shard_map/ppermute | solution.py:279
  39.8 2.0 collective-permute-start
  42.6 2.8 %copy-done = bf16[2,2048,768]{2,1,0:T(8,128)(2,1)S(1)} copy-done((bf16[2,2048,768]{2,1,0:T(8,128)(2,1)S(1)}, bf16[2,2048,768]{2,1,0:T(8,128)(2,1)}, u32[]{:S(2)}) %copy-start) | copy-done | bytes 6291480
  45.4 2.8 %copy-done.2 = bf16[2,2048,768]{2,1,0:T(8,128)(2,1)S(1)} copy-done((bf16[2,2048,768]{2,1,0:T(8,128)(2,1)S(1)}, bf16[2,2048,768]{2,1,0:T(8,128)(2,1)}, u32[]{:S(2)}) %copy-start.2) | copy-done | bytes 6291480
  48.2 2.8 %copy-done.4 = bf16[2,768,2048]{2,1,0:T(8,128)(2,1)S(1)} copy-done((bf16[2,768,2048]{2,1,0:T(8,128)(2,1)S(1)}, bf16[2,768,2048]{2,1,0:T(8,128)(2,1)}, u32[]{:S(2)}) %copy-start.4) | copy-done | bytes 6291480
  50.9 6.4 %shard_map.75 = (bf16[128,2048]{1,0:T(8,128)(2,1)S(1)}, bf16[128,2048]{1,0:T(8,128)(2,1)S(1)}, f32[256,128]{1,0:T(8,128)S(1)}) custom-call(s32[3]{0:T(128)S(1)} %pad_add_fusion.place_ref, bf16[136,2048]{1,0:T(8,128)(2,1)S(1)} %get-tuple-element.35.a_ref, bf16[136,2048]{1,0:T(8,128)(2,1)S(1)} %get-tuple-element.36.b_ref, bf16[2,2048,768]{2,1,0:T(8,128)(2,1)S(1)} %copy-done, ...), custom_call_target="tpu_custom_call" | custom-call | flops 4831838208 | bytes 4194304 | tf_op jit(solution)/shard_map/pallas_call | solution.py:193
  57.4 4.1 %collective-permute-done.a_ref = bf16[136,2048]{1,0:T(8,128)(2,1)S(1)} collective-permute-done((bf16[136,2048]{1,0:T(8,128)(2,1)S(1)}, bf16[136,2048]{1,0:T(8,128)(2,1)S(1)}, u32[]{:S(2)}, u32[]{:S(2)}) %collective-permute-start) | collective-permute-done | bytes 557088 | tf_op jit(solution)/shard_map/ppermute | solution.py:276
  63.5 6.4 %shard_map.76 = (bf16[128,2048]{1,0:T(8,128)(2,1)S(1)}, bf16[128,2048]{1,0:T(8,128)(2,1)S(1)}, f32[256,128]{1,0:T(8,128)S(1)}) custom-call(s32[3]{0:T(128)S(1)} %pad_add_fusion.place_ref, bf16[136,2048]{1,0:T(8,128)(2,1)S(1)} %collective-permute-done.a_ref, bf16[136,2048]{1,0:T(8,128)(2,1)S(1)} %collective-permute-done.1.b_ref, ...), custom_call_target="tpu_custom_call" | custom-call | flops 4831838208 | bytes 4194304 | tf_op jit(solution)/shard_map/pallas_call | solution.py:193
  69.9 5.8 %shard_map.80 = (bf16[128,2048]{1,0:T(8,128)(2,1)S(1)}, bf16[128,2048]{1,0:T(8,128)(2,1)S(1)}, bf16[128,2048]{1,0:T(8,128)(2,1)S(1)}, bf16[128,2048]{1,0:T(8,128)(2,1)S(1)}) custom-call(bf16[128,2048]{1,0:T(8,128)(2,1)S(1)} %collective-permute-done.12.b_ref, ...), custom_call_target="tpu_custom_call", output_to_operand_aliasing={{2}: (0, {}), {3}: (1, {})} | custom-call | flops 4831838208 | bytes 4194304 | tf_op jit(solution)/shard_map/pallas_call | solution.py:212
  79.8 6.4 %shard_map.77 = (bf16[128,2048]{1,0:T(8,128)(2,1)S(1)}, bf16[128,2048]{1,0:T(8,128)(2,1)S(1)}, f32[256,128]{1,0:T(8,128)S(1)}) custom-call(s32[3]{0:T(128)S(1)} %pad_add_fusion.place_ref, bf16[136,2048]{1,0:T(8,128)(2,1)S(1)} %collective-permute-done.2.a_ref, bf16[136,2048]{1,0:T(8,128)(2,1)S(1)} %collective-permute-done.3.b_ref, ...), custom_call_target="tpu_custom_call" | custom-call | flops 4831838208 | bytes 4194304 | tf_op jit(solution)/shard_map/pallas_call | solution.py:193
  86.2 4.4 %collective-permute-done.14.b_ref = bf16[128,2048]{1,0:T(8,128)(2,1)S(1)} collective-permute-done((bf16[128,2048]{1,0:T(8,128)(2,1)S(1)}, bf16[128,2048]{1,0:T(8,128)(2,1)S(1)}, u32[]{:S(2)}, u32[]{:S(2)}) %collective-permute-start.14) | collective-permute-done | bytes 524320 | tf_op jit(solution)/shard_map/ppermute | solution.py:278
  91.0 5.8 %shard_map.81 = (bf16[128,2048]{1,0:T(8,128)(2,1)S(1)}, bf16[128,2048]{1,0:T(8,128)(2,1)S(1)}, bf16[128,2048]{1,0:T(8,128)(2,1)S(1)}, bf16[128,2048]{1,0:T(8,128)(2,1)S(1)}) custom-call(bf16[128,2048]{1,0:T(8,128)(2,1)S(1)} %collective-permute-done.14.b_ref, ...), custom_call_target="tpu_custom_call", output_to_operand_aliasing={{2}: (0, {}), {3}: (1, {})} | custom-call | flops 4831838208 | bytes 4194304 | tf_op jit(solution)/shard_map/pallas_call | solution.py:212
  96.8 1.7 collective-permute-start.16
  98.9 3.6 %collective-permute-done.4.a_ref = bf16[136,2048]{1,0:T(8,128)(2,1)S(1)} collective-permute-done((bf16[136,2048]{1,0:T(8,128)(2,1)S(1)}, bf16[136,2048]{1,0:T(8,128)(2,1)S(1)}, u32[]{:S(2)}, u32[]{:S(2)}) %collective-permute-start.4) | collective-permute-done | bytes 557088 | tf_op jit(solution)/shard_map/ppermute | solution.py:276
  104.6 6.4 %shard_map.78 = (bf16[128,2048]{1,0:T(8,128)(2,1)S(1)}, bf16[128,2048]{1,0:T(8,128)(2,1)S(1)}, f32[256,128]{1,0:T(8,128)S(1)}) custom-call(s32[3]{0:T(128)S(1)} %pad_add_fusion.place_ref, bf16[136,2048]{1,0:T(8,128)(2,1)S(1)} %collective-permute-done.4.a_ref, bf16[136,2048]{1,0:T(8,128)(2,1)S(1)} %collective-permute-done.5.b_ref, ...), custom_call_target="tpu_custom_call" | custom-call | flops 4831838208 | bytes 4194304 | tf_op jit(solution)/shard_map/pallas_call | solution.py:193
  111.0 2.8 %collective-permute-done.16.b_ref = bf16[128,2048]{1,0:T(8,128)(2,1)S(1)} collective-permute-done((bf16[128,2048]{1,0:T(8,128)(2,1)S(1)}, bf16[128,2048]{1,0:T(8,128)(2,1)S(1)}, u32[]{:S(2)}, u32[]{:S(2)}) %collective-permute-start.16) | collective-permute-done | bytes 524320 | tf_op jit(solution)/shard_map/ppermute | solution.py:278
  114.2 5.8 %shard_map.82 = (bf16[128,2048]{1,0:T(8,128)(2,1)S(1)}, bf16[128,2048]{1,0:T(8,128)(2,1)S(1)}, bf16[128,2048]{1,0:T(8,128)(2,1)S(1)}, bf16[128,2048]{1,0:T(8,128)(2,1)S(1)}) custom-call(bf16[128,2048]{1,0:T(8,128)(2,1)S(1)} %collective-permute-done.16.b_ref, ...), custom_call_target="tpu_custom_call", output_to_operand_aliasing={{2}: (0, {}), {3}: (1, {})} | custom-call | flops 4831838208 | bytes 4194304 | tf_op jit(solution)/shard_map/pallas_call | solution.py:212
  122.1 3.6 %collective-permute-done.6.a_ref = bf16[136,2048]{1,0:T(8,128)(2,1)S(1)} collective-permute-done((bf16[136,2048]{1,0:T(8,128)(2,1)S(1)}, bf16[136,2048]{1,0:T(8,128)(2,1)S(1)}, u32[]{:S(2)}, u32[]{:S(2)}) %collective-permute-start.6) | collective-permute-done | bytes 557088 | tf_op jit(solution)/shard_map/ppermute | solution.py:284
  126.1 6.4 %shard_map.79 = (bf16[128,2048]{1,0:T(8,128)(2,1)S(1)}, bf16[128,2048]{1,0:T(8,128)(2,1)S(1)}, f32[256,128]{1,0:T(8,128)}) custom-call(s32[3]{0:T(128)S(1)} %pad_add_fusion.place_ref, bf16[136,2048]{1,0:T(8,128)(2,1)S(1)} %collective-permute-done.6.a_ref, bf16[136,2048]{1,0:T(8,128)(2,1)S(1)} %collective-permute-done.7.b_ref, ...), custom_call_target="tpu_custom_call" | custom-call | flops 4831838208 | bytes 4194304 | tf_op jit(solution)/shard_map/pallas_call | solution.py:193
  132.6 1.6 collective-permute-start.21
  134.2 3.2 %collective-permute-done.18 = bf16[128,2048]{1,0:T(8,128)(2,1)S(1)} collective-permute-done((bf16[128,2048]{1,0:T(8,128)(2,1)S(1)}, bf16[128,2048]{1,0:T(8,128)(2,1)S(1)}, u32[]{:S(2)}, u32[]{:S(2)}) %collective-permute-start.18) | collective-permute-done | bytes 524320 | tf_op jit(solution)/shard_map/ppermute | solution.py:289
  137.5 1.6 collective-permute-start.19
  139.7 1.7 collective-permute-start.26
  141.4 7.2 %collective-permute-done.21 = bf16[128,2048]{1,0:T(8,128)(2,1)S(1)} collective-permute-done((bf16[128,2048]{1,0:T(8,128)(2,1)S(1)}, bf16[128,2048]{1,0:T(8,128)(2,1)S(1)}, u32[]{:S(2)}, u32[]{:S(2)}) %collective-permute-start.21) | collective-permute-done | bytes 524320 | tf_op jit(solution)/shard_map/ppermute | solution.py:286
  150.4 3.6 %collective-permute-done.8 = bf16[128,2048]{1,0:T(8,128)(2,1)S(1)} collective-permute-done((bf16[128,2048]{1,0:T(8,128)(2,1)S(1)}, bf16[128,2048]{1,0:T(8,128)(2,1)S(1)}, u32[]{:S(2)}, u32[]{:S(2)}) %collective-permute-start.8) | collective-permute-done | bytes 524320 | tf_op jit(solution)/shard_map/ppermute | solution.py:286
  154.6 5.2 %collective-permute-done.19 = bf16[128,2048]{1,0:T(8,128)(2,1)S(1)} collective-permute-done((bf16[128,2048]{1,0:T(8,128)(2,1)S(1)}, bf16[128,2048]{1,0:T(8,128)(2,1)S(1)}, u32[]{:S(2)}, u32[]{:S(2)}) %collective-permute-start.19) | collective-permute-done | bytes 524320 | tf_op jit(solution)/shard_map/ppermute | solution.py:289
  160.0 1.6 collective-permute-start.20
  161.6 9.5 %collective-permute-done.22 = bf16[128,2048]{1,0:T(8,128)(2,1)S(1)} collective-permute-done((bf16[128,2048]{1,0:T(8,128)(2,1)S(1)}, bf16[128,2048]{1,0:T(8,128)(2,1)S(1)}, u32[]{:S(2)}, u32[]{:S(2)}) %collective-permute-start.22) | collective-permute-done | bytes 524320 | tf_op jit(solution)/shard_map/ppermute | solution.py:291
  173.6 1.7 collective-permute-start.27
  175.3 15.3 %collective-permute-done.23 = bf16[128,2048]{1,0:T(8,128)(2,1)S(1)} collective-permute-done((bf16[128,2048]{1,0:T(8,128)(2,1)S(1)}, bf16[128,2048]{1,0:T(8,128)(2,1)S(1)}, u32[]{:S(2)}, u32[]{:S(2)}) %collective-permute-start.23) | collective-permute-done | bytes 524320 | tf_op jit(solution)/shard_map/ppermute | solution.py:291
  193.0 8.8 %collective-permute-done.24.first_ref = bf16[128,2048]{1,0:T(8,128)(2,1)S(1)} collective-permute-done((bf16[128,2048]{1,0:T(8,128)(2,1)S(1)}, bf16[128,2048]{1,0:T(8,128)(2,1)S(1)}, u32[]{:S(2)}, u32[]{:S(2)}) %collective-permute-start.24) | collective-permute-done | bytes 524320 | tf_op jit(solution)/shard_map/ppermute | solution.py:291
  (67 shorter events, 26.0 us)
Async XLA Ops:
  32.9 37.0 %collective-permute-start.13 = (bf16[128,2048]{1,0:T(8,128)(2,1)}, bf16[128,2048]{1,0:T(8,128)(2,1)S(1)}, u32[]{:S(2)}, u32[]{:S(2)}) collective-permute-start(bf16[128,2048]{1,0:T(8,128)(2,1)} %get-tuple-element.33.a_ref), channel_id=1, source_target_pairs={{2,0},{4,2},{6,4},{7,6},{5,7},{3,5},{1,3},{0,1},{10,8},{12,10},{14... | collective-permute-start | bytes 1572872 | tf_op jit(solution)/shard_map/ppermute | solution.py:279
  35.9 34.0 %collective-permute-start.12 = (bf16[128,2048]{1,0:T(8,128)(2,1)}, bf16[128,2048]{1,0:T(8,128)(2,1)S(1)}, u32[]{:S(2)}, u32[]{:S(2)}) collective-permute-start(bf16[128,2048]{1,0:T(8,128)(2,1)} %get-tuple-element.34.b_ref), channel_id=1, source_target_pairs={{0,2},{2,4},{4,6},{6,7},{7,5},{5,3},{3,1},{1,0},{8,10},{10,12},{12... | collective-permute-start | bytes 1572872 | tf_op jit(solution)/shard_map/ppermute | solution.py:278
  39.8 21.6 %collective-permute-start = (bf16[136,2048]{1,0:T(8,128)(2,1)S(1)}, bf16[136,2048]{1,0:T(8,128)(2,1)S(1)}, u32[]{:S(2)}, u32[]{:S(2)}) collective-permute-start(bf16[136,2048]{1,0:T(8,128)(2,1)S(1)} %get-tuple-element.35.a_ref), channel_id=1, source_target_pairs={{0,2},{2,4},{4,6},{6,7},{7,5},{5,3},{3,1},{1,0},{8,10},{10,12},{12... | collective-permute-start | bytes 1671176 | tf_op jit(solution)/shard_map/ppermute | solution.py:276
  41.8 20.1 %collective-permute-start.1 = (bf16[136,2048]{1,0:T(8,128)(2,1)S(1)}, bf16[136,2048]{1,0:T(8,128)(2,1)S(1)}, u32[]{:S(2)}, u32[]{:S(2)}) collective-permute-start(bf16[136,2048]{1,0:T(8,128)(2,1)S(1)} %get-tuple-element.36.b_ref), channel_id=1, source_target_pairs={{2,0},{4,2},{6,4},{7,6},{5,7},{3,5},{1,3},{0,1},{10,8},{12,10},{14... | collective-permute-start | bytes 1671176 | tf_op jit(solution)/shard_map/ppermute | solution.py:277
  42.6 2.8 %copy-start = (bf16[2,2048,768]{2,1,0:T(8,128)(2,1)S(1)}, bf16[2,2048,768]{2,1,0:T(8,128)(2,1)}, u32[]{:S(2)}) copy-start(bf16[2,2048,768]{2,1,0:T(8,128)(2,1)} %gate_ref.15) | copy-start | bytes 18874372
  50.9 12.5 %copy-start.1 = (bf16[2,2048,768]{2,1,0:T(8,128)(2,1)S(1)}, bf16[2,2048,768]{2,1,0:T(8,128)(2,1)}, u32[]{:S(2)}) copy-start(bf16[2,2048,768]{2,1,0:T(8,128)(2,1)} %gate_ref.15) | copy-start | bytes 18874372
  50.9 12.5 %copy-start.3 = (bf16[2,2048,768]{2,1,0:T(8,128)(2,1)S(1)}, bf16[2,2048,768]{2,1,0:T(8,128)(2,1)}, u32[]{:S(2)}) copy-start(bf16[2,2048,768]{2,1,0:T(8,128)(2,1)} %up_ref.15) | copy-start | bytes 18874372
  50.9 12.5 %copy-start.5 = (bf16[2,768,2048]{2,1,0:T(8,128)(2,1)S(1)}, bf16[2,768,2048]{2,1,0:T(8,128)(2,1)}, u32[]{:S(2)}) copy-start(bf16[2,768,2048]{2,1,0:T(8,128)(2,1)} %param.13) | copy-start | bytes 18874372
  61.4 16.3 %collective-permute-start.2 = (bf16[136,2048]{1,0:T(8,128)(2,1)S(1)}, bf16[136,2048]{1,0:T(8,128)(2,1)S(1)}, u32[]{:S(2)}, u32[]{:S(2)}) collective-permute-start(bf16[136,2048]{1,0:T(8,128)(2,1)S(1)} %collective-permute-done.a_ref), channel_id=1, source_target_pairs={{0,2},{2,4},{4,6},{6,7},{7,5},{5,3},{3,1},{1,0},{8,10},{10,12},{12... | collective-permute-start | bytes 1671176 | tf_op jit(solution)/shard_map/ppermute | solution.py:276
  61.8 16.3 %collective-permute-start.3 = (bf16[136,2048]{1,0:T(8,128)(2,1)S(1)}, bf16[136,2048]{1,0:T(8,128)(2,1)S(1)}, u32[]{:S(2)}, u32[]{:S(2)}) collective-permute-start(bf16[136,2048]{1,0:T(8,128)(2,1)S(1)} %collective-permute-done.1.b_ref), channel_id=1, source_target_pairs={{2,0},{4,2},{6,4},{7,6},{5,7},{3,5},{1,3},{0,1},{10,8},{12,10},{14... | collective-permute-start | bytes 1671176 | tf_op jit(solution)/shard_map/ppermute | solution.py:277
  75.7 14.9 %collective-permute-start.14 = (bf16[128,2048]{1,0:T(8,128)(2,1)S(1)}, bf16[128,2048]{1,0:T(8,128)(2,1)S(1)}, u32[]{:S(2)}, u32[]{:S(2)}) collective-permute-start(bf16[128,2048]{1,0:T(8,128)(2,1)S(1)} %get-tuple-element.45), channel_id=1, source_target_pairs={{0,2},{2,4},{4,6},{6,7},{7,5},{5,3},{3,1},{1,0},{8,10},{10,12},{12... | collective-permute-start | bytes 1572872 | tf_op jit(solution)/shard_map/ppermute | solution.py:278
  76.2 14.9 %collective-permute-start.15 = (bf16[128,2048]{1,0:T(8,128)(2,1)S(1)}, bf16[128,2048]{1,0:T(8,128)(2,1)S(1)}, u32[]{:S(2)}, u32[]{:S(2)}) collective-permute-start(bf16[128,2048]{1,0:T(8,128)(2,1)S(1)} %get-tuple-element.46), channel_id=1, source_target_pairs={{2,0},{4,2},{6,4},{7,6},{5,7},{3,5},{1,3},{0,1},{10,8},{12,10},{14... | collective-permute-start | bytes 1572872 | tf_op jit(solution)/shard_map/ppermute | solution.py:279
  77.8 24.8 %collective-permute-start.4 = (bf16[136,2048]{1,0:T(8,128)(2,1)S(1)}, bf16[136,2048]{1,0:T(8,128)(2,1)S(1)}, u32[]{:S(2)}, u32[]{:S(2)}) collective-permute-start(bf16[136,2048]{1,0:T(8,128)(2,1)S(1)} %collective-permute-done.2.a_ref), channel_id=1, source_target_pairs={{0,2},{2,4},{4,6},{6,7},{7,5},{5,3},{3,1},{1,0},{8,10},{10,12},{12... | collective-permute-start | bytes 1671176 | tf_op jit(solution)/shard_map/ppermute | solution.py:276
  78.2 24.8 %collective-permute-start.5 = (bf16[136,2048]{1,0:T(8,128)(2,1)S(1)}, bf16[136,2048]{1,0:T(8,128)(2,1)S(1)}, u32[]{:S(2)}, u32[]{:S(2)}) collective-permute-start(bf16[136,2048]{1,0:T(8,128)(2,1)S(1)} %collective-permute-done.3.b_ref), channel_id=1, source_target_pairs={{2,0},{4,2},{6,4},{7,6},{5,7},{3,5},{1,3},{0,1},{10,8},{12,10},{14... | collective-permute-start | bytes 1671176 | tf_op jit(solution)/shard_map/ppermute | solution.py:277
  96.8 16.9 %collective-permute-start.16 = (bf16[128,2048]{1,0:T(8,128)(2,1)S(1)}, bf16[128,2048]{1,0:T(8,128)(2,1)S(1)}, u32[]{:S(2)}, u32[]{:S(2)}) collective-permute-start(bf16[128,2048]{1,0:T(8,128)(2,1)S(1)} %get-tuple-element.49), channel_id=1, source_target_pairs={{0,2},{2,4},{4,6},{6,7},{7,5},{5,3},{3,1},{1,0},{8,10},{10,12},{12... | collective-permute-start | bytes 1572872 | tf_op jit(solution)/shard_map/ppermute | solution.py:278
  98.5 15.7 %collective-permute-start.17 = (bf16[128,2048]{1,0:T(8,128)(2,1)S(1)}, bf16[128,2048]{1,0:T(8,128)(2,1)S(1)}, u32[]{:S(2)}, u32[]{:S(2)}) collective-permute-start(bf16[128,2048]{1,0:T(8,128)(2,1)S(1)} %get-tuple-element.50), channel_id=1, source_target_pairs={{2,0},{4,2},{6,4},{7,6},{5,7},{3,5},{1,3},{0,1},{10,8},{12,10},{14... | collective-permute-start | bytes 1572872 | tf_op jit(solution)/shard_map/ppermute | solution.py:279
  102.5 23.2 %collective-permute-start.6 = (bf16[136,2048]{1,0:T(8,128)(2,1)S(1)}, bf16[136,2048]{1,0:T(8,128)(2,1)S(1)}, u32[]{:S(2)}, u32[]{:S(2)}) collective-permute-start(bf16[136,2048]{1,0:T(8,128)(2,1)S(1)} %collective-permute-done.4.a_ref), channel_id=1, source_target_pairs={{0,2},{2,4},{4,6},{6,7},{7,5},{5,3},{3,1},{1,0},{8,10},{10,12},{12... | collective-permute-start | bytes 1671176 | tf_op jit(solution)/shard_map/ppermute | solution.py:284
  103.0 23.2 %collective-permute-start.7 = (bf16[136,2048]{1,0:T(8,128)(2,1)S(1)}, bf16[136,2048]{1,0:T(8,128)(2,1)S(1)}, u32[]{:S(2)}, u32[]{:S(2)}) collective-permute-start(bf16[136,2048]{1,0:T(8,128)(2,1)S(1)} %collective-permute-done.5.b_ref), channel_id=1, source_target_pairs={{2,0},{4,2},{6,4},{7,6},{5,7},{3,5},{1,3},{0,1},{10,8},{12,10},{14... | collective-permute-start | bytes 1671176 | tf_op jit(solution)/shard_map/ppermute | solution.py:284
  120.0 17.4 %collective-permute-start.18 = (bf16[128,2048]{1,0:T(8,128)(2,1)S(1)}, bf16[128,2048]{1,0:T(8,128)(2,1)S(1)}, u32[]{:S(2)}, u32[]{:S(2)}) collective-permute-start(bf16[128,2048]{1,0:T(8,128)(2,1)S(1)} %get-tuple-element.52), channel_id=1, source_target_pairs={{2,0},{4,2},{6,4},{7,6},{5,7},{3,5},{1,3},{0,1},{10,8},{12,10},{14... | collective-permute-start | bytes 1572872 | tf_op jit(solution)/shard_map/ppermute | solution.py:289
  121.6 18.0 %collective-permute-start.25 = (bf16[128,2048]{1,0:T(8,128)(2,1)S(1)}, bf16[128,2048]{1,0:T(8,128)(2,1)S(1)}, u32[]{:S(2)}, u32[]{:S(2)}) collective-permute-start(bf16[128,2048]{1,0:T(8,128)(2,1)S(1)} %get-tuple-element.60), channel_id=1, source_target_pairs={{0,2},{2,4},{4,6},{6,7},{7,5},{5,3},{3,1},{1,0},{8,10},{10,12},{12... | collective-permute-start | bytes 1572872 | tf_op jit(solution)/shard_map/ppermute | solution.py:290
  132.6 16.1 %collective-permute-start.21 = (bf16[128,2048]{1,0:T(8,128)(2,1)S(1)}, bf16[128,2048]{1,0:T(8,128)(2,1)S(1)}, u32[]{:S(2)}, u32[]{:S(2)}) collective-permute-start(bf16[128,2048]{1,0:T(8,128)(2,1)S(1)} %get-tuple-element.57), channel_id=1, source_target_pairs={{2,0},{4,2},{6,4},{7,6},{5,7},{3,5},{1,3},{0,1},{10,8},{12,10},{14... | collective-permute-start | bytes 1572872 | tf_op jit(solution)/shard_map/ppermute | solution.py:286
  137.5 22.3 %collective-permute-start.19 = (bf16[128,2048]{1,0:T(8,128)(2,1)S(1)}, bf16[128,2048]{1,0:T(8,128)(2,1)S(1)}, u32[]{:S(2)}, u32[]{:S(2)}) collective-permute-start(bf16[128,2048]{1,0:T(8,128)(2,1)S(1)} %add_convert_fusion.6), channel_id=1, source_target_pairs={{2,0},{4,2},{6,4},{7,6},{5,7},{3,5},{1,3},{0,1},{10,8},{12,10},{14... | collective-permute-start | bytes 1572872 | tf_op jit(solution)/shard_map/ppermute | solution.py:289
  139.1 14.9 %collective-permute-start.8 = (bf16[128,2048]{1,0:T(8,128)(2,1)S(1)}, bf16[128,2048]{1,0:T(8,128)(2,1)S(1)}, u32[]{:S(2)}, u32[]{:S(2)}) collective-permute-start(bf16[128,2048]{1,0:T(8,128)(2,1)S(1)} %get-tuple-element.42), channel_id=1, source_target_pairs={{0,2},{2,4},{4,6},{6,7},{7,5},{5,3},{3,1},{1,0},{8,10},{10,12},{12... | collective-permute-start | bytes 1572872 | tf_op jit(solution)/shard_map/ppermute | solution.py:286
  139.7 33.8 %collective-permute-start.26 = (bf16[128,2048]{1,0:T(8,128)(2,1)S(1)}, bf16[128,2048]{1,0:T(8,128)(2,1)S(1)}, u32[]{:S(2)}, u32[]{:S(2)}) collective-permute-start(bf16[128,2048]{1,0:T(8,128)(2,1)S(1)} %add_convert_fusion.1), channel_id=1, source_target_pairs={{0,2},{2,4},{4,6},{6,7},{7,5},{5,3},{3,1},{1,0},{8,10},{10,12},{12... | collective-permute-start | bytes 1572872 | tf_op jit(solution)/shard_map/ppermute | solution.py:290
  148.7 22.3 %collective-permute-start.22 = (bf16[128,2048]{1,0:T(8,128)(2,1)S(1)}, bf16[128,2048]{1,0:T(8,128)(2,1)S(1)}, u32[]{:S(2)}, u32[]{:S(2)}) collective-permute-start(bf16[128,2048]{1,0:T(8,128)(2,1)S(1)} %add_convert_fusion.4), channel_id=1, source_target_pairs={{2,0},{4,2},{6,4},{7,6},{5,7},{3,5},{1,3},{0,1},{10,8},{12,10},{14... | collective-permute-start | bytes 1572872 | tf_op jit(solution)/shard_map/ppermute | solution.py:291
  154.1 18.7 %collective-permute-start.9 = (bf16[128,2048]{1,0:T(8,128)(2,1)S(1)}, bf16[128,2048]{1,0:T(8,128)(2,1)S(1)}, u32[]{:S(2)}, u32[]{:S(2)}) collective-permute-start(bf16[128,2048]{1,0:T(8,128)(2,1)S(1)} %add_convert_fusion.9), channel_id=1, source_target_pairs={{0,2},{2,4},{4,6},{6,7},{7,5},{5,3},{3,1},{1,0},{8,10},{10,12},{12... | collective-permute-start | bytes 1572872 | tf_op jit(solution)/shard_map/ppermute | solution.py:292
  160.0 42.9 %collective-permute-start.20 = (bf16[128,2048]{1,0:T(8,128)(2,1)S(1)}, bf16[128,2048]{1,0:T(8,128)(2,1)S(1)}, u32[]{:S(2)}, u32[]{:S(2)}) collective-permute-start(bf16[128,2048]{1,0:T(8,128)(2,1)S(1)} %add_convert_fusion.5), channel_id=1, source_target_pairs={{2,0},{4,2},{6,4},{7,6},{5,7},{3,5},{1,3},{0,1},{10,8},{12,10},{14... | collective-permute-start | bytes 1572872 | tf_op jit(solution)/shard_map/ppermute | solution.py:289
  171.2 19.4 %collective-permute-start.23 = (bf16[128,2048]{1,0:T(8,128)(2,1)S(1)}, bf16[128,2048]{1,0:T(8,128)(2,1)S(1)}, u32[]{:S(2)}, u32[]{:S(2)}) collective-permute-start(bf16[128,2048]{1,0:T(8,128)(2,1)S(1)} %add_convert_fusion.3), channel_id=1, source_target_pairs={{2,0},{4,2},{6,4},{7,6},{5,7},{3,5},{1,3},{0,1},{10,8},{12,10},{14... | collective-permute-start | bytes 1572872 | tf_op jit(solution)/shard_map/ppermute | solution.py:291
  173.0 19.4 %collective-permute-start.10 = (bf16[128,2048]{1,0:T(8,128)(2,1)S(1)}, bf16[128,2048]{1,0:T(8,128)(2,1)S(1)}, u32[]{:S(2)}, u32[]{:S(2)}) collective-permute-start(bf16[128,2048]{1,0:T(8,128)(2,1)S(1)} %add_convert_fusion.8), channel_id=1, source_target_pairs={{0,2},{2,4},{4,6},{6,7},{7,5},{5,3},{3,1},{1,0},{8,10},{10,12},{12... | collective-permute-start | bytes 1572872 | tf_op jit(solution)/shard_map/ppermute | solution.py:292
  173.6 19.4 %collective-permute-start.27 = (bf16[128,2048]{1,0:T(8,128)(2,1)S(1)}, bf16[128,2048]{1,0:T(8,128)(2,1)S(1)}, u32[]{:S(2)}, u32[]{:S(2)}) collective-permute-start(bf16[128,2048]{1,0:T(8,128)(2,1)S(1)} %add_convert_fusion), channel_id=1, source_target_pairs={{0,2},{2,4},{4,6},{6,7},{7,5},{5,3},{3,1},{1,0},{8,10},{10,12},{12... | collective-permute-start | bytes 1572872 | tf_op jit(solution)/shard_map/ppermute | solution.py:290
  190.8 11.1 %collective-permute-start.24 = (bf16[128,2048]{1,0:T(8,128)(2,1)S(1)}, bf16[128,2048]{1,0:T(8,128)(2,1)S(1)}, u32[]{:S(2)}, u32[]{:S(2)}) collective-permute-start(bf16[128,2048]{1,0:T(8,128)(2,1)S(1)} %add_convert_fusion.2), channel_id=1, source_target_pairs={{2,0},{4,2},{6,4},{7,6},{5,7},{3,5},{1,3},{0,1},{10,8},{12,10},{14... | collective-permute-start | bytes 1572872 | tf_op jit(solution)/shard_map/ppermute | solution.py:291
  192.5 10.4 %collective-permute-start.11 = (bf16[128,2048]{1,0:T(8,128)(2,1)S(1)}, bf16[128,2048]{1,0:T(8,128)(2,1)S(1)}, u32[]{:S(2)}, u32[]{:S(2)}) collective-permute-start(bf16[128,2048]{1,0:T(8,128)(2,1)S(1)} %add_convert_fusion.7), channel_id=1, source_target_pairs={{0,2},{2,4},{4,6},{6,7},{7,5},{5,3},{3,1},{1,0},{8,10},{10,12},{12... | collective-permute-start | bytes 1572872 | tf_op jit(solution)/shard_map/ppermute | solution.py:292
  (6 other events, 9.1 us)

commit v3 on v1

--- a/solution.py
+++ b/solution.py
@@ -8,7 +8,7 @@
 from jax.sharding import PartitionSpec as P
 
 VMEM_LIMIT = 12 * 1024 * 1024
-PACK_LIMIT = 56 * 1024 * 1024
+PACK_LIMIT = 40 * 1024 * 1024
 
 
 def ring_order(groups):
@@ -26,21 +26,19 @@
     return one, -(-2 * one // 8) * 8
 
 
-def pack_kernel(slots, tokens_ref, target_ref, weight_ref, *refs):
-    tabled, plain = refs[:2], refs[2:4]
-    target_buf, weight_buf, sems = refs[4:]
-    height, width = tokens_ref.shape
-    half = height // 2
+def pack_kernel(slots, a_ref, b_ref, target_ref, weight_ref, *refs):
+    tabled = refs[:2]
+    target_buf, weight_buf, sems = refs[2:]
+    half, width = a_ref.shape
+    height = 2 * half
     one, extra = table_rows(slots, height, width)
     per_row = width // height
     copies = [
         pltpu.make_async_copy(target_ref, target_buf, sems.at[0]),
         pltpu.make_async_copy(weight_ref, weight_buf, sems.at[1]),
+        pltpu.make_async_copy(a_ref, tabled[0].at[pl.ds(0, half)], sems.at[2]),
+        pltpu.make_async_copy(b_ref, tabled[1].at[pl.ds(0, half)], sems.at[3]),
     ]
-    for i in range(2):
-        rows = tokens_ref.at[pl.ds(i * half, half)]
-        copies.append(pltpu.make_async_copy(rows, tabled[i].at[pl.ds(0, half)], sems.at[2 + i]))
-        copies.append(pltpu.make_async_copy(rows, plain[i], sems.at[4 + i]))
     for copy in copies:
         copy.start()
     copies[0].wait()
@@ -64,25 +62,24 @@
         copy.wait()
 
 
-def pack(tokens, target, router_weight, slots):
-    height, width = tokens.shape
-    half, top = height // 2, target.shape[1]
+def pack(a, b, target, router_weight, slots):
+    half, width = a.shape
+    height, top = target.shape
     extra = table_rows(slots, height, width)[1]
     vmem = pl.BlockSpec(memory_space=pltpu.VMEM)
     return pl.pallas_call(
         functools.partial(pack_kernel, slots),
-        in_specs=[pl.BlockSpec(memory_space=pl.ANY)] * 3,
-        out_specs=[vmem] * 4,
-        out_shape=[jax.ShapeDtypeStruct((half + extra, width), jnp.bfloat16)] * 2
-        + [jax.ShapeDtypeStruct((half, width), jnp.bfloat16)] * 2,
+        in_specs=[pl.BlockSpec(memory_space=pl.ANY)] * 4,
+        out_specs=[vmem] * 2,
+        out_shape=[jax.ShapeDtypeStruct((half + extra, width), jnp.bfloat16)] * 2,
         scratch_shapes=[
             pltpu.VMEM((top, height), jnp.int32),
             pltpu.VMEM((top, height), jnp.float32),
-            pltpu.SemaphoreType.DMA((6,)),
+            pltpu.SemaphoreType.DMA((4,)),
         ],
         compiler_params=pltpu.CompilerParams(vmem_limit_bytes=PACK_LIMIT),
         cost_estimate=pl.CostEstimate(flops=0, bytes_accessed=4 * height * width, transcendentals=0),
-    )(tokens, target.T, router_weight.T)
+    )(a, b, target.T, router_weight.T)
 
 
 def columns(place_ref, table_ref, first, slots, height, owned):
@@ -150,7 +147,8 @@
 
 def plain_kernel(b_ref, a_ref, share_ref, gate_ref, up_ref, down_ref, out_b_ref, out_a_ref, same_b_ref, same_a_ref,
                  rows_ref, hidden_ref):
-    del same_b_ref, same_a_ref
+    same_b_ref[...] = b_ref[...]
+    same_a_ref[...] = a_ref[...]
     half = b_ref.shape[0]
     rows_ref[:half, :] = b_ref[...]
     rows_ref[half:, :] = a_ref[...]
@@ -195,28 +193,33 @@
             pltpu.VMEM((2 * half, width), jnp.bfloat16),
             pltpu.VMEM((2 * half, owned * units), jnp.bfloat16),
         ],
-        input_output_aliases={0: 2, 1: 3},
         compiler_params=pltpu.CompilerParams(vmem_limit_bytes=VMEM_LIMIT),
         cost_estimate=cost(2 * half, weights[0]),
     )(b, a, shares, *weights)
 
 
 def finish_kernel(*refs):
-    out_ref = refs[-1]
-    half = refs[0].shape[0]
+    terms, (out_ref, total_ref, sems) = refs[:-3], refs[-3:]
+    half = terms[0].shape[0]
+    copies = []
     for i in range(2):
-        total = sum(ref[...].astype(jnp.float32) for ref in refs[3 * i:3 * i + 3])
-        out_ref[i * half:(i + 1) * half, :] = total.astype(out_ref.dtype)
+        rows = pl.ds(i * half, half)
+        total = sum(ref[...].astype(jnp.float32) for ref in terms[3 * i:3 * i + 3])
+        total_ref[rows, :] = total.astype(total_ref.dtype)
+        copies.append(pltpu.make_async_copy(total_ref.at[rows], out_ref.at[rows], sems.at[i]))
+        copies[i].start()
+    for copy in copies:
+        copy.wait()
 
 
 def finish(a, b):
     half, width = a[0].shape
-    vmem = pl.BlockSpec(memory_space=pltpu.VMEM)
     return pl.pallas_call(
         finish_kernel,
-        in_specs=[vmem] * 6,
-        out_specs=vmem,
+        in_specs=[pl.BlockSpec(memory_space=pltpu.VMEM)] * 6,
+        out_specs=pl.BlockSpec(memory_space=pl.ANY),
         out_shape=jax.ShapeDtypeStruct((2 * half, width), a[0].dtype),
+        scratch_shapes=[pltpu.VMEM((2 * half, width), a[0].dtype), pltpu.SemaphoreType.DMA((2,))],
         compiler_params=pltpu.CompilerParams(vmem_limit_bytes=VMEM_LIMIT),
     )(*a, *b)
 
@@ -239,7 +242,8 @@
     weights = w_gate, w_up, w_down.reshape(-1, width)
     far = groups // 2
 
-    lead_a, lead_b, a, b = pack(tokens, target, router_weight, slots)
+    a, b = tokens[:half], tokens[half:]
+    lead_a, lead_b = pack(a, b, target, router_weight, slots)
     run = functools.partial(lead, place, weights, slots, height)
     own_a, own_b, shares = run(lead_a, lead_b)
     earlier = (shares,)

time: 174 us -> 173 us (level)
  Pallas kernels: 54 us -> 51.1 us
    pallas_call x1, Pallas kernels: 3.2 us -> 0.22 us  [pack(): pl.pallas_call(functools.partial(pack_kernel, slots), in_specs=[pl.BlockS...]
  transfers between devices with their start and end apart: 28 -> 28, of which waited for: 18 -> 18; matrix products, arithmetic and copies ran while one was open for 1% -> 1% of each run, Pallas kernels for 28% -> 29%
where the time goes in v3:
time: 173 us; the launch traced here: 172 us
  waiting for transfers between devices  78.3 us (45%)
  Pallas kernels  51.1 us (30%)
  starting transfers between devices  29.6 us (17%)
  local copies, waits for them, and re-layouts  11 us (6%)
    pallas_call x5, Pallas kernels, lead(): pl.pallas_call(functools.partial(lead_kernel, slots, height), in_specs=[p...  31.4 us
    ppermute x3, waiting for transfers between devices, body(): lead_a = lax.ppermute(add(lead_part_a, lead_a), 'expert', back)  24.3 us
    pallas_call x3, Pallas kernels, plain(): pl.pallas_call(plain_kernel, in_specs=[vmem] * 6, out_specs=[vmem] * 4, o...  18.3 us
    ppermute x1, waiting for transfers between devices, body(): lax.ppermute(far_a, 'expert', back)  10.8 us
    ppermute x3, waiting for transfers between devices, body(): lead_b = lax.ppermute(add(lead_part_b, lead_b), 'expert', ahead)  10.4 us
    unnamed x16, local copies, waits for them, and re-layouts  9.76 us
    ppermute x1, waiting for transfers between devices, body(): lax.ppermute(far_b, 'expert', ahead)  7.79 us
    ppermute x3, waiting for transfers between devices, body(): b = lax.ppermute(b, 'expert', ahead)  7.5 us
  transfers between devices with their start and end apart: 28, of which 18 were waited for; matrix products, arithmetic and copies ran while one was open for 1% of the time, Pallas kernels for 29%

profile of v3, /device:TPU:0, one launch (start us, length us, event | category | flops | bytes accessed | tf_op | source)
XLA Modules:
  0.0 172.3 jit_solution(15011100609628047453)
XLA Ops:
  1.3 3.1 %collective-permute-start.12 = (bf16[128,2048]{1,0:T(8,128)(2,1)S(1)}, bf16[128,2048]{1,0:T(8,128)(2,1)}, u32[]{:S(2)}, u32[]{:S(2)}) collective-permute-start(bf16[128,2048]{1,0:T(8,128)(2,1)S(1)} %get-tuple-element.57.b_ref), channel_id=1, source_target_pairs={{0,2},{2,4},{4,6},{6,7},{7,5},{5,3},{3,1},{1,0},{8,10},{10,12},{12... | collective-permute-start | bytes 1572872 | tf_op jit(solution)/shard_map/ppermute | solution.py:254
  6.0 2.1 %collective-permute-start = (bf16[136,2048]{1,0:T(8,128)(2,1)S(1)}, bf16[136,2048]{1,0:T(8,128)(2,1)S(1)}, u32[]{:S(2)}, u32[]{:S(2)}) collective-permute-start(bf16[136,2048]{1,0:T(8,128)(2,1)S(1)} %get-tuple-element.31.a_ref), channel_id=1, source_target_pairs={{0,2},{2,4},{4,6},{6,7},{7,5},{5,3},{3,1},{1,0},{8,10},{10,12},{12... | collective-permute-start | bytes 1671176 | tf_op jit(solution)/shard_map/ppermute | solution.py:252
  8.8 2.8 %copy-done = bf16[2,2048,768]{2,1,0:T(8,128)(2,1)S(1)} copy-done((bf16[2,2048,768]{2,1,0:T(8,128)(2,1)S(1)}, bf16[2,2048,768]{2,1,0:T(8,128)(2,1)}, u32[]{:S(2)}) %copy-start) | copy-done | bytes 6291480
  11.6 2.8 %copy-done.2 = bf16[2,2048,768]{2,1,0:T(8,128)(2,1)S(1)} copy-done((bf16[2,2048,768]{2,1,0:T(8,128)(2,1)S(1)}, bf16[2,2048,768]{2,1,0:T(8,128)(2,1)}, u32[]{:S(2)}) %copy-start.2) | copy-done | bytes 6291480
  14.4 2.8 %copy-done.4 = bf16[2,768,2048]{2,1,0:T(8,128)(2,1)S(1)} copy-done((bf16[2,768,2048]{2,1,0:T(8,128)(2,1)S(1)}, bf16[2,768,2048]{2,1,0:T(8,128)(2,1)}, u32[]{:S(2)}) %copy-start.4) | copy-done | bytes 6291480
  17.1 6.4 %shard_map.74 = (bf16[128,2048]{1,0:T(8,128)(2,1)S(1)}, bf16[128,2048]{1,0:T(8,128)(2,1)S(1)}, f32[256,128]{1,0:T(8,128)S(1)}) custom-call(s32[3]{0:T(128)S(1)} %pad_add_fusion.place_ref, bf16[136,2048]{1,0:T(8,128)(2,1)S(1)} %get-tuple-element.31.a_ref, bf16[136,2048]{1,0:T(8,128)(2,1)S(1)} %get-tuple-element.32.b_ref, bf16[2,2048,768]{2,1,0:T(8,128)(2,1)S(1)} %copy-done, ...), custom_call_target="tpu_custom_call" | custom-call | flops 4831838208 | bytes 4194304 | tf_op jit(solution)/shard_map/pallas_call | solution.py:168
  23.6 4.6 %collective-permute-done.a_ref = bf16[136,2048]{1,0:T(8,128)(2,1)S(1)} collective-permute-done((bf16[136,2048]{1,0:T(8,128)(2,1)S(1)}, bf16[136,2048]{1,0:T(8,128)(2,1)S(1)}, u32[]{:S(2)}, u32[]{:S(2)}) %collective-permute-start) | collective-permute-done | bytes 557088 | tf_op jit(solution)/shard_map/ppermute | solution.py:252
  28.1 1.8 %collective-permute-start.2 = (bf16[136,2048]{1,0:T(8,128)(2,1)S(1)}, bf16[136,2048]{1,0:T(8,128)(2,1)S(1)}, u32[]{:S(2)}, u32[]{:S(2)}) collective-permute-start(bf16[136,2048]{1,0:T(8,128)(2,1)S(1)} %collective-permute-done.a_ref), channel_id=1, source_target_pairs={{0,2},{2,4},{4,6},{6,7},{7,5},{5,3},{3,1},{1,0},{8,10},{10,12},{12... | collective-permute-start | bytes 1671176 | tf_op jit(solution)/shard_map/ppermute | solution.py:252
  30.2 6.2 %shard_map.75 = (bf16[128,2048]{1,0:T(8,128)(2,1)S(1)}, bf16[128,2048]{1,0:T(8,128)(2,1)S(1)}, f32[256,128]{1,0:T(8,128)S(1)}) custom-call(s32[3]{0:T(128)S(1)} %pad_add_fusion.place_ref, bf16[136,2048]{1,0:T(8,128)(2,1)S(1)} %collective-permute-done.a_ref, bf16[136,2048]{1,0:T(8,128)(2,1)S(1)} %collective-permute-done.1.b_ref, ...), custom_call_target="tpu_custom_call" | custom-call | flops 4831838208 | bytes 4194304 | tf_op jit(solution)/shard_map/pallas_call | solution.py:168
  36.4 6.9 %shard_map.79 = (bf16[128,2048]{1,0:T(8,128)(2,1)S(1)}, bf16[128,2048]{1,0:T(8,128)(2,1)S(1)}, bf16[128,2048]{1,0:T(8,128)(2,1)S(1)}, bf16[128,2048]{1,0:T(8,128)(2,1)S(1)}) custom-call(bf16[128,2048]{1,0:T(8,128)(2,1)} %collective-permute-done.12.b_ref, bf16[128,2048]{1,0:T(8,128)(2,1)} %collective-permute-done.13.a_ref, ...), custom_call_target="tpu_custom_call" | custom-call | flops 4831838208 | bytes 4194304 | tf_op jit(solution)/shard_map/pallas_call | solution.py:187
  43.3 1.9 %collective-permute-start.14 = (bf16[128,2048]{1,0:T(8,128)(2,1)S(1)}, bf16[128,2048]{1,0:T(8,128)(2,1)S(1)}, u32[]{:S(2)}, u32[]{:S(2)}) collective-permute-start(bf16[128,2048]{1,0:T(8,128)(2,1)S(1)} %get-tuple-element.41), channel_id=1, source_target_pairs={{0,2},{2,4},{4,6},{6,7},{7,5},{5,3},{3,1},{1,0},{8,10},{10,12},{12... | collective-permute-start | bytes 1572872 | tf_op jit(solution)/shard_map/ppermute | solution.py:254
  45.4 1.8 %collective-permute-start.4 = (bf16[136,2048]{1,0:T(8,128)(2,1)S(1)}, bf16[136,2048]{1,0:T(8,128)(2,1)S(1)}, u32[]{:S(2)}, u32[]{:S(2)}) collective-permute-start(bf16[136,2048]{1,0:T(8,128)(2,1)S(1)} %collective-permute-done.2.a_ref), channel_id=1, source_target_pairs={{0,2},{2,4},{4,6},{6,7},{7,5},{5,3},{3,1},{1,0},{8,10},{10,12},{12... | collective-permute-start | bytes 1671176 | tf_op jit(solution)/shard_map/ppermute | solution.py:252
  47.4 6.2 %shard_map.76 = (bf16[128,2048]{1,0:T(8,128)(2,1)S(1)}, bf16[128,2048]{1,0:T(8,128)(2,1)S(1)}, f32[256,128]{1,0:T(8,128)S(1)}) custom-call(s32[3]{0:T(128)S(1)} %pad_add_fusion.place_ref, bf16[136,2048]{1,0:T(8,128)(2,1)S(1)} %collective-permute-done.2.a_ref, bf16[136,2048]{1,0:T(8,128)(2,1)S(1)} %collective-permute-done.3.b_ref, ...), custom_call_target="tpu_custom_call" | custom-call | flops 4831838208 | bytes 4194304 | tf_op jit(solution)/shard_map/pallas_call | solution.py:168
  53.7 4.5 %collective-permute-done.14.b_ref = bf16[128,2048]{1,0:T(8,128)(2,1)S(1)} collective-permute-done((bf16[128,2048]{1,0:T(8,128)(2,1)S(1)}, bf16[128,2048]{1,0:T(8,128)(2,1)S(1)}, u32[]{:S(2)}, u32[]{:S(2)}) %collective-permute-start.14) | collective-permute-done | bytes 524320 | tf_op jit(solution)/shard_map/ppermute | solution.py:254
  58.2 1.8 %collective-permute-done.15.a_ref = bf16[128,2048]{1,0:T(8,128)(2,1)S(1)} collective-permute-done((bf16[128,2048]{1,0:T(8,128)(2,1)S(1)}, bf16[128,2048]{1,0:T(8,128)(2,1)S(1)}, u32[]{:S(2)}, u32[]{:S(2)}) %collective-permute-start.15) | collective-permute-done | bytes 524320 | tf_op jit(solution)/shard_map/ppermute | solution.py:255
  60.1 5.7 %shard_map.80 = (bf16[128,2048]{1,0:T(8,128)(2,1)S(1)}, bf16[128,2048]{1,0:T(8,128)(2,1)S(1)}, bf16[128,2048]{1,0:T(8,128)(2,1)S(1)}, bf16[128,2048]{1,0:T(8,128)(2,1)S(1)}) custom-call(bf16[128,2048]{1,0:T(8,128)(2,1)S(1)} %collective-permute-done.14.b_ref, bf16[128,2048]{1,0:T(8,128)(2,1)S(1)} %collective-permute-done.15.a_ref, ...), custom_call_target="tpu_custom_call" | custom-call | flops 4831838208 | bytes 4194304 | tf_op jit(solution)/shard_map/pallas_call | solution.py:187
  67.8 2.3 %collective-permute-done.4.a_ref = bf16[136,2048]{1,0:T(8,128)(2,1)S(1)} collective-permute-done((bf16[136,2048]{1,0:T(8,128)(2,1)S(1)}, bf16[136,2048]{1,0:T(8,128)(2,1)S(1)}, u32[]{:S(2)}, u32[]{:S(2)}) %collective-permute-start.4) | collective-permute-done | bytes 557088 | tf_op jit(solution)/shard_map/ppermute | solution.py:252
  70.2 1.8 %collective-permute-start.6 = (bf16[136,2048]{1,0:T(8,128)(2,1)S(1)}, bf16[136,2048]{1,0:T(8,128)(2,1)S(1)}, u32[]{:S(2)}, u32[]{:S(2)}) collective-permute-start(bf16[136,2048]{1,0:T(8,128)(2,1)S(1)} %collective-permute-done.4.a_ref), channel_id=1, source_target_pairs={{0,2},{2,4},{4,6},{6,7},{7,5},{5,3},{3,1},{1,0},{8,10},{10,12},{12... | collective-permute-start | bytes 1671176 | tf_op jit(solution)/shard_map/ppermute | solution.py:260
  72.2 6.2 %shard_map.77 = (bf16[128,2048]{1,0:T(8,128)(2,1)S(1)}, bf16[128,2048]{1,0:T(8,128)(2,1)S(1)}, f32[256,128]{1,0:T(8,128)S(1)}) custom-call(s32[3]{0:T(128)S(1)} %pad_add_fusion.place_ref, bf16[136,2048]{1,0:T(8,128)(2,1)S(1)} %collective-permute-done.4.a_ref, bf16[136,2048]{1,0:T(8,128)(2,1)S(1)} %collective-permute-done.5.b_ref, ...), custom_call_target="tpu_custom_call" | custom-call | flops 4831838208 | bytes 4194304 | tf_op jit(solution)/shard_map/pallas_call | solution.py:168
  78.5 3.0 %collective-permute-done.16.b_ref = bf16[128,2048]{1,0:T(8,128)(2,1)S(1)} collective-permute-done((bf16[128,2048]{1,0:T(8,128)(2,1)S(1)}, bf16[128,2048]{1,0:T(8,128)(2,1)S(1)}, u32[]{:S(2)}, u32[]{:S(2)}) %collective-permute-start.16) | collective-permute-done | bytes 524320 | tf_op jit(solution)/shard_map/ppermute | solution.py:254
  81.4 1.8 %collective-permute-done.17.a_ref = bf16[128,2048]{1,0:T(8,128)(2,1)S(1)} collective-permute-done((bf16[128,2048]{1,0:T(8,128)(2,1)S(1)}, bf16[128,2048]{1,0:T(8,128)(2,1)S(1)}, u32[]{:S(2)}, u32[]{:S(2)}) %collective-permute-start.17) | collective-permute-done | bytes 524320 | tf_op jit(solution)/shard_map/ppermute | solution.py:255
  83.2 5.7 %shard_map.81 = (bf16[128,2048]{1,0:T(8,128)(2,1)S(1)}, bf16[128,2048]{1,0:T(8,128)(2,1)S(1)}, bf16[128,2048]{1,0:T(8,128)(2,1)}, bf16[128,2048]{1,0:T(8,128)(2,1)}) custom-call(bf16[128,2048]{1,0:T(8,128)(2,1)S(1)} %collective-permute-done.16.b_ref, bf16[128,2048]{1,0:T(8,128)(2,1)S(1)} %collective-permute-done.17.a_ref, ...), custom_call_target="tpu_custom_call" | custom-call | flops 4831838208 | bytes 4194304 | tf_op jit(solution)/shard_map/pallas_call | solution.py:187
  91.0 2.3 %collective-permute-done.6.a_ref = bf16[136,2048]{1,0:T(8,128)(2,1)S(1)} collective-permute-done((bf16[136,2048]{1,0:T(8,128)(2,1)S(1)}, bf16[136,2048]{1,0:T(8,128)(2,1)S(1)}, u32[]{:S(2)}, u32[]{:S(2)}) %collective-permute-start.6) | collective-permute-done | bytes 557088 | tf_op jit(solution)/shard_map/ppermute | solution.py:260
  93.4 1.8 %collective-permute-done.7.b_ref = bf16[136,2048]{1,0:T(8,128)(2,1)S(1)} collective-permute-done((bf16[136,2048]{1,0:T(8,128)(2,1)S(1)}, bf16[136,2048]{1,0:T(8,128)(2,1)S(1)}, u32[]{:S(2)}, u32[]{:S(2)}) %collective-permute-start.7) | collective-permute-done | bytes 557088 | tf_op jit(solution)/shard_map/ppermute | solution.py:260
  95.2 6.2 %shard_map.78 = (bf16[128,2048]{1,0:T(8,128)(2,1)S(1)}, bf16[128,2048]{1,0:T(8,128)(2,1)S(1)}, f32[256,128]{1,0:T(8,128)}) custom-call(s32[3]{0:T(128)S(1)} %pad_add_fusion.place_ref, bf16[136,2048]{1,0:T(8,128)(2,1)S(1)} %collective-permute-done.6.a_ref, bf16[136,2048]{1,0:T(8,128)(2,1)S(1)} %collective-permute-done.7.b_ref, ...), custom_call_target="tpu_custom_call" | custom-call | flops 4831838208 | bytes 4194304 | tf_op jit(solution)/shard_map/pallas_call | solution.py:168
  106.8 10.8 %collective-permute-done.8 = bf16[128,2048]{1,0:T(8,128)(2,1)S(1)} collective-permute-done((bf16[128,2048]{1,0:T(8,128)(2,1)S(1)}, bf16[128,2048]{1,0:T(8,128)(2,1)S(1)}, u32[]{:S(2)}, u32[]{:S(2)}) %collective-permute-start.8) | collective-permute-done | bytes 524320 | tf_op jit(solution)/shard_map/ppermute | solution.py:262
  118.0 7.8 %collective-permute-done.21 = bf16[128,2048]{1,0:T(8,128)(2,1)S(1)} collective-permute-done((bf16[128,2048]{1,0:T(8,128)(2,1)S(1)}, bf16[128,2048]{1,0:T(8,128)(2,1)S(1)}, u32[]{:S(2)}, u32[]{:S(2)}) %collective-permute-start.21) | collective-permute-done | bytes 524320 | tf_op jit(solution)/shard_map/ppermute | solution.py:262
  129.3 7.9 %collective-permute-done.9 = bf16[128,2048]{1,0:T(8,128)(2,1)S(1)} collective-permute-done((bf16[128,2048]{1,0:T(8,128)(2,1)S(1)}, bf16[128,2048]{1,0:T(8,128)(2,1)S(1)}, u32[]{:S(2)}, u32[]{:S(2)}) %collective-permute-start.9) | collective-permute-done | bytes 524320 | tf_op jit(solution)/shard_map/ppermute | solution.py:267
  137.9 3.0 %collective-permute-done.22 = bf16[128,2048]{1,0:T(8,128)(2,1)S(1)} collective-permute-done((bf16[128,2048]{1,0:T(8,128)(2,1)S(1)}, bf16[128,2048]{1,0:T(8,128)(2,1)S(1)}, u32[]{:S(2)}, u32[]{:S(2)}) %collective-permute-start.22) | collective-permute-done | bytes 524320 | tf_op jit(solution)/shard_map/ppermute | solution.py:268
  143.3 9.0 %collective-permute-done.10 = bf16[128,2048]{1,0:T(8,128)(2,1)S(1)} collective-permute-done((bf16[128,2048]{1,0:T(8,128)(2,1)S(1)}, bf16[128,2048]{1,0:T(8,128)(2,1)S(1)}, u32[]{:S(2)}, u32[]{:S(2)}) %collective-permute-start.10) | collective-permute-done | bytes 524320 | tf_op jit(solution)/shard_map/ppermute | solution.py:267
  153.0 7.4 %collective-permute-done.23 = bf16[128,2048]{1,0:T(8,128)(2,1)S(1)} collective-permute-done((bf16[128,2048]{1,0:T(8,128)(2,1)S(1)}, bf16[128,2048]{1,0:T(8,128)(2,1)S(1)}, u32[]{:S(2)}, u32[]{:S(2)}) %collective-permute-start.23) | collective-permute-done | bytes 524320 | tf_op jit(solution)/shard_map/ppermute | solution.py:268
  163.5 7.4 %collective-permute-done.11.refs_1_ = bf16[128,2048]{1,0:T(8,128)(2,1)S(1)} collective-permute-done((bf16[128,2048]{1,0:T(8,128)(2,1)S(1)}, bf16[128,2048]{1,0:T(8,128)(2,1)S(1)}, u32[]{:S(2)}, u32[]{:S(2)}) %collective-permute-start.11) | collective-permute-done | bytes 524320 | tf_op jit(solution)/shard_map/ppermute | solution.py:267
  (62 shorter events, 25.2 us)
Async XLA Ops:
  1.3 35.2 %collective-permute-start.12 = (bf16[128,2048]{1,0:T(8,128)(2,1)S(1)}, bf16[128,2048]{1,0:T(8,128)(2,1)}, u32[]{:S(2)}, u32[]{:S(2)}) collective-permute-start(bf16[128,2048]{1,0:T(8,128)(2,1)S(1)} %get-tuple-element.57.b_ref), channel_id=1, source_target_pairs={{0,2},{2,4},{4,6},{6,7},{7,5},{5,3},{3,1},{1,0},{8,10},{10,12},{12... | collective-permute-start | bytes 1572872 | tf_op jit(solution)/shard_map/ppermute | solution.py:254
  4.4 32.1 %collective-permute-start.13 = (bf16[128,2048]{1,0:T(8,128)(2,1)S(1)}, bf16[128,2048]{1,0:T(8,128)(2,1)}, u32[]{:S(2)}, u32[]{:S(2)}) collective-permute-start(bf16[128,2048]{1,0:T(8,128)(2,1)S(1)} %get-tuple-element.58.a_ref), channel_id=1, source_target_pairs={{2,0},{4,2},{6,4},{7,6},{5,7},{3,5},{1,3},{0,1},{10,8},{12,10},{14... | collective-permute-start | bytes 1572872 | tf_op jit(solution)/shard_map/ppermute | solution.py:255
  6.0 22.2 %collective-permute-start = (bf16[136,2048]{1,0:T(8,128)(2,1)S(1)}, bf16[136,2048]{1,0:T(8,128)(2,1)S(1)}, u32[]{:S(2)}, u32[]{:S(2)}) collective-permute-start(bf16[136,2048]{1,0:T(8,128)(2,1)S(1)} %get-tuple-element.31.a_ref), channel_id=1, source_target_pairs={{0,2},{2,4},{4,6},{6,7},{7,5},{5,3},{3,1},{1,0},{8,10},{10,12},{12... | collective-permute-start | bytes 1671176 | tf_op jit(solution)/shard_map/ppermute | solution.py:252
  8.1 21.9 %collective-permute-start.1 = (bf16[136,2048]{1,0:T(8,128)(2,1)S(1)}, bf16[136,2048]{1,0:T(8,128)(2,1)S(1)}, u32[]{:S(2)}, u32[]{:S(2)}) collective-permute-start(bf16[136,2048]{1,0:T(8,128)(2,1)S(1)} %get-tuple-element.32.b_ref), channel_id=1, source_target_pairs={{2,0},{4,2},{6,4},{7,6},{5,7},{3,5},{1,3},{0,1},{10,8},{12,10},{14... | collective-permute-start | bytes 1671176 | tf_op jit(solution)/shard_map/ppermute | solution.py:253
  8.8 2.8 %copy-start = (bf16[2,2048,768]{2,1,0:T(8,128)(2,1)S(1)}, bf16[2,2048,768]{2,1,0:T(8,128)(2,1)}, u32[]{:S(2)}) copy-start(bf16[2,2048,768]{2,1,0:T(8,128)(2,1)} %gate_ref.15) | copy-start | bytes 18874372
  17.1 13.0 %copy-start.1 = (bf16[2,2048,768]{2,1,0:T(8,128)(2,1)S(1)}, bf16[2,2048,768]{2,1,0:T(8,128)(2,1)}, u32[]{:S(2)}) copy-start(bf16[2,2048,768]{2,1,0:T(8,128)(2,1)} %gate_ref.15) | copy-start | bytes 18874372
  17.1 13.0 %copy-start.3 = (bf16[2,2048,768]{2,1,0:T(8,128)(2,1)S(1)}, bf16[2,2048,768]{2,1,0:T(8,128)(2,1)}, u32[]{:S(2)}) copy-start(bf16[2,2048,768]{2,1,0:T(8,128)(2,1)} %up_ref.15) | copy-start | bytes 18874372
  17.1 13.0 %copy-start.5 = (bf16[2,768,2048]{2,1,0:T(8,128)(2,1)S(1)}, bf16[2,768,2048]{2,1,0:T(8,128)(2,1)}, u32[]{:S(2)}) copy-start(bf16[2,768,2048]{2,1,0:T(8,128)(2,1)} %param.13) | copy-start | bytes 18874372
  28.1 17.3 %collective-permute-start.2 = (bf16[136,2048]{1,0:T(8,128)(2,1)S(1)}, bf16[136,2048]{1,0:T(8,128)(2,1)S(1)}, u32[]{:S(2)}, u32[]{:S(2)}) collective-permute-start(bf16[136,2048]{1,0:T(8,128)(2,1)S(1)} %collective-permute-done.a_ref), channel_id=1, source_target_pairs={{0,2},{2,4},{4,6},{6,7},{7,5},{5,3},{3,1},{1,0},{8,10},{10,12},{12... | collective-permute-start | bytes 1671176 | tf_op jit(solution)/shard_map/ppermute | solution.py:252
  30.0 17.3 %collective-permute-start.3 = (bf16[136,2048]{1,0:T(8,128)(2,1)S(1)}, bf16[136,2048]{1,0:T(8,128)(2,1)S(1)}, u32[]{:S(2)}, u32[]{:S(2)}) collective-permute-start(bf16[136,2048]{1,0:T(8,128)(2,1)S(1)} %collective-permute-done.1.b_ref), channel_id=1, source_target_pairs={{2,0},{4,2},{6,4},{7,6},{5,7},{3,5},{1,3},{0,1},{10,8},{12,10},{14... | collective-permute-start | bytes 1671176 | tf_op jit(solution)/shard_map/ppermute | solution.py:253
  43.3 14.9 %collective-permute-start.14 = (bf16[128,2048]{1,0:T(8,128)(2,1)S(1)}, bf16[128,2048]{1,0:T(8,128)(2,1)S(1)}, u32[]{:S(2)}, u32[]{:S(2)}) collective-permute-start(bf16[128,2048]{1,0:T(8,128)(2,1)S(1)} %get-tuple-element.41), channel_id=1, source_target_pairs={{0,2},{2,4},{4,6},{6,7},{7,5},{5,3},{3,1},{1,0},{8,10},{10,12},{12... | collective-permute-start | bytes 1572872 | tf_op jit(solution)/shard_map/ppermute | solution.py:254
  45.2 14.9 %collective-permute-start.15 = (bf16[128,2048]{1,0:T(8,128)(2,1)S(1)}, bf16[128,2048]{1,0:T(8,128)(2,1)S(1)}, u32[]{:S(2)}, u32[]{:S(2)}) collective-permute-start(bf16[128,2048]{1,0:T(8,128)(2,1)S(1)} %get-tuple-element.42), channel_id=1, source_target_pairs={{2,0},{4,2},{6,4},{7,6},{5,7},{3,5},{1,3},{0,1},{10,8},{12,10},{14... | collective-permute-start | bytes 1572872 | tf_op jit(solution)/shard_map/ppermute | solution.py:255
  45.4 24.8 %collective-permute-start.4 = (bf16[136,2048]{1,0:T(8,128)(2,1)S(1)}, bf16[136,2048]{1,0:T(8,128)(2,1)S(1)}, u32[]{:S(2)}, u32[]{:S(2)}) collective-permute-start(bf16[136,2048]{1,0:T(8,128)(2,1)S(1)} %collective-permute-done.2.a_ref), channel_id=1, source_target_pairs={{0,2},{2,4},{4,6},{6,7},{7,5},{5,3},{3,1},{1,0},{8,10},{10,12},{12... | collective-permute-start | bytes 1671176 | tf_op jit(solution)/shard_map/ppermute | solution.py:252
  47.2 24.8 %collective-permute-start.5 = (bf16[136,2048]{1,0:T(8,128)(2,1)S(1)}, bf16[136,2048]{1,0:T(8,128)(2,1)S(1)}, u32[]{:S(2)}, u32[]{:S(2)}) collective-permute-start(bf16[136,2048]{1,0:T(8,128)(2,1)S(1)} %collective-permute-done.3.b_ref), channel_id=1, source_target_pairs={{2,0},{4,2},{6,4},{7,6},{5,7},{3,5},{1,3},{0,1},{10,8},{12,10},{14... | collective-permute-start | bytes 1671176 | tf_op jit(solution)/shard_map/ppermute | solution.py:253
  65.8 15.7 %collective-permute-start.16 = (bf16[128,2048]{1,0:T(8,128)(2,1)S(1)}, bf16[128,2048]{1,0:T(8,128)(2,1)S(1)}, u32[]{:S(2)}, u32[]{:S(2)}) collective-permute-start(bf16[128,2048]{1,0:T(8,128)(2,1)S(1)} %get-tuple-element.45), channel_id=1, source_target_pairs={{0,2},{2,4},{4,6},{6,7},{7,5},{5,3},{3,1},{1,0},{8,10},{10,12},{12... | collective-permute-start | bytes 1572872 | tf_op jit(solution)/shard_map/ppermute | solution.py:254
  67.4 15.8 %collective-permute-start.17 = (bf16[128,2048]{1,0:T(8,128)(2,1)S(1)}, bf16[128,2048]{1,0:T(8,128)(2,1)S(1)}, u32[]{:S(2)}, u32[]{:S(2)}) collective-permute-start(bf16[128,2048]{1,0:T(8,128)(2,1)S(1)} %get-tuple-element.46), channel_id=1, source_target_pairs={{2,0},{4,2},{6,4},{7,6},{5,7},{3,5},{1,3},{0,1},{10,8},{12,10},{14... | collective-permute-start | bytes 1572872 | tf_op jit(solution)/shard_map/ppermute | solution.py:255
  70.2 23.2 %collective-permute-start.6 = (bf16[136,2048]{1,0:T(8,128)(2,1)S(1)}, bf16[136,2048]{1,0:T(8,128)(2,1)S(1)}, u32[]{:S(2)}, u32[]{:S(2)}) collective-permute-start(bf16[136,2048]{1,0:T(8,128)(2,1)S(1)} %collective-permute-done.4.a_ref), channel_id=1, source_target_pairs={{0,2},{2,4},{4,6},{6,7},{7,5},{5,3},{3,1},{1,0},{8,10},{10,12},{12... | collective-permute-start | bytes 1671176 | tf_op jit(solution)/shard_map/ppermute | solution.py:260
  72.0 23.2 %collective-permute-start.7 = (bf16[136,2048]{1,0:T(8,128)(2,1)S(1)}, bf16[136,2048]{1,0:T(8,128)(2,1)S(1)}, u32[]{:S(2)}, u32[]{:S(2)}) collective-permute-start(bf16[136,2048]{1,0:T(8,128)(2,1)S(1)} %collective-permute-done.5.b_ref), channel_id=1, source_target_pairs={{2,0},{4,2},{6,4},{7,6},{5,7},{3,5},{1,3},{0,1},{10,8},{12,10},{14... | collective-permute-start | bytes 1671176 | tf_op jit(solution)/shard_map/ppermute | solution.py:260
  88.9 13.3 %collective-permute-start.18 = (bf16[128,2048]{1,0:T(8,128)(2,1)S(1)}, bf16[128,2048]{1,0:T(8,128)(2,1)S(1)}, u32[]{:S(2)}, u32[]{:S(2)}) collective-permute-start(bf16[128,2048]{1,0:T(8,128)(2,1)S(1)} %get-tuple-element.48), channel_id=1, source_target_pairs={{0,2},{2,4},{4,6},{6,7},{7,5},{5,3},{3,1},{1,0},{8,10},{10,12},{12... | collective-permute-start | bytes 1572872 | tf_op jit(solution)/shard_map/ppermute | solution.py:266
  90.6 15.8 %collective-permute-start.25 = (bf16[128,2048]{1,0:T(8,128)(2,1)S(1)}, bf16[128,2048]{1,0:T(8,128)(2,1)S(1)}, u32[]{:S(2)}, u32[]{:S(2)}) collective-permute-start(bf16[128,2048]{1,0:T(8,128)(2,1)S(1)} %get-tuple-element.56), channel_id=1, source_target_pairs={{2,0},{4,2},{6,4},{7,6},{5,7},{3,5},{1,3},{0,1},{10,8},{12,10},{14... | collective-permute-start | bytes 1572872 | tf_op jit(solution)/shard_map/ppermute | solution.py:265
  101.4 16.2 %collective-permute-start.8 = (bf16[128,2048]{1,0:T(8,128)(2,1)S(1)}, bf16[128,2048]{1,0:T(8,128)(2,1)S(1)}, u32[]{:S(2)}, u32[]{:S(2)}) collective-permute-start(bf16[128,2048]{1,0:T(8,128)(2,1)S(1)} %get-tuple-element.38), channel_id=1, source_target_pairs={{2,0},{4,2},{6,4},{7,6},{5,7},{3,5},{1,3},{0,1},{10,8},{12,10},{14... | collective-permute-start | bytes 1572872 | tf_op jit(solution)/shard_map/ppermute | solution.py:262
  102.4 25.1 %collective-permute-start.19 = (bf16[128,2048]{1,0:T(8,128)(2,1)S(1)}, bf16[128,2048]{1,0:T(8,128)(2,1)S(1)}, u32[]{:S(2)}, u32[]{:S(2)}) collective-permute-start(bf16[128,2048]{1,0:T(8,128)(2,1)S(1)} %add_convert_fusion.6), channel_id=1, source_target_pairs={{0,2},{2,4},{4,6},{6,7},{7,5},{5,3},{3,1},{1,0},{8,10},{10,12},{12... | collective-permute-start | bytes 1572872 | tf_op jit(solution)/shard_map/ppermute | solution.py:266
  104.2 21.6 %collective-permute-start.21 = (bf16[128,2048]{1,0:T(8,128)(2,1)S(1)}, bf16[128,2048]{1,0:T(8,128)(2,1)S(1)}, u32[]{:S(2)}, u32[]{:S(2)}) collective-permute-start(bf16[128,2048]{1,0:T(8,128)(2,1)S(1)} %get-tuple-element.53), channel_id=1, source_target_pairs={{0,2},{2,4},{4,6},{6,7},{7,5},{5,3},{3,1},{1,0},{8,10},{10,12},{12... | collective-permute-start | bytes 1572872 | tf_op jit(solution)/shard_map/ppermute | solution.py:262
  106.5 36.0 %collective-permute-start.26 = (bf16[128,2048]{1,0:T(8,128)(2,1)S(1)}, bf16[128,2048]{1,0:T(8,128)(2,1)S(1)}, u32[]{:S(2)}, u32[]{:S(2)}) collective-permute-start(bf16[128,2048]{1,0:T(8,128)(2,1)S(1)} %add_convert_fusion.1), channel_id=1, source_target_pairs={{2,0},{4,2},{6,4},{7,6},{5,7},{3,5},{1,3},{0,1},{10,8},{12,10},{14... | collective-permute-start | bytes 1572872 | tf_op jit(solution)/shard_map/ppermute | solution.py:265
  117.8 19.4 %collective-permute-start.9 = (bf16[128,2048]{1,0:T(8,128)(2,1)S(1)}, bf16[128,2048]{1,0:T(8,128)(2,1)S(1)}, u32[]{:S(2)}, u32[]{:S(2)}) collective-permute-start(bf16[128,2048]{1,0:T(8,128)(2,1)S(1)} %add_convert_fusion.9), channel_id=1, source_target_pairs={{2,0},{4,2},{6,4},{7,6},{5,7},{3,5},{1,3},{0,1},{10,8},{12,10},{14... | collective-permute-start | bytes 1572872 | tf_op jit(solution)/shard_map/ppermute | solution.py:267
  126.0 14.9 %collective-permute-start.22 = (bf16[128,2048]{1,0:T(8,128)(2,1)S(1)}, bf16[128,2048]{1,0:T(8,128)(2,1)S(1)}, u32[]{:S(2)}, u32[]{:S(2)}) collective-permute-start(bf16[128,2048]{1,0:T(8,128)(2,1)S(1)} %add_convert_fusion.4), channel_id=1, source_target_pairs={{0,2},{2,4},{4,6},{6,7},{7,5},{5,3},{3,1},{1,0},{8,10},{10,12},{12... | collective-permute-start | bytes 1572872 | tf_op jit(solution)/shard_map/ppermute | solution.py:268
  127.7 34.4 %collective-permute-start.20 = (bf16[128,2048]{1,0:T(8,128)(2,1)S(1)}, bf16[128,2048]{1,0:T(8,128)(2,1)S(1)}, u32[]{:S(2)}, u32[]{:S(2)}) collective-permute-start(bf16[128,2048]{1,0:T(8,128)(2,1)S(1)} %add_convert_fusion.5), channel_id=1, source_target_pairs={{0,2},{2,4},{4,6},{6,7},{7,5},{5,3},{3,1},{1,0},{8,10},{10,12},{12... | collective-permute-start | bytes 1572872 | tf_op jit(solution)/shard_map/ppermute | solution.py:266
  137.3 14.9 %collective-permute-start.10 = (bf16[128,2048]{1,0:T(8,128)(2,1)S(1)}, bf16[128,2048]{1,0:T(8,128)(2,1)S(1)}, u32[]{:S(2)}, u32[]{:S(2)}) collective-permute-start(bf16[128,2048]{1,0:T(8,128)(2,1)S(1)} %add_convert_fusion.8), channel_id=1, source_target_pairs={{2,0},{4,2},{6,4},{7,6},{5,7},{3,5},{1,3},{0,1},{10,8},{12,10},{14... | collective-permute-start | bytes 1572872 | tf_op jit(solution)/shard_map/ppermute | solution.py:267
  141.0 19.4 %collective-permute-start.23 = (bf16[128,2048]{1,0:T(8,128)(2,1)S(1)}, bf16[128,2048]{1,0:T(8,128)(2,1)S(1)}, u32[]{:S(2)}, u32[]{:S(2)}) collective-permute-start(bf16[128,2048]{1,0:T(8,128)(2,1)S(1)} %add_convert_fusion.3), channel_id=1, source_target_pairs={{0,2},{2,4},{4,6},{6,7},{7,5},{5,3},{3,1},{1,0},{8,10},{10,12},{12... | collective-permute-start | bytes 1572872 | tf_op jit(solution)/shard_map/ppermute | solution.py:268
  142.7 20.8 %collective-permute-start.27 = (bf16[128,2048]{1,0:T(8,128)(2,1)S(1)}, bf16[128,2048]{1,0:T(8,128)(2,1)S(1)}, u32[]{:S(2)}, u32[]{:S(2)}) collective-permute-start(bf16[128,2048]{1,0:T(8,128)(2,1)S(1)} %add_convert_fusion), channel_id=1, source_target_pairs={{2,0},{4,2},{6,4},{7,6},{5,7},{3,5},{1,3},{0,1},{10,8},{12,10},{14... | collective-permute-start | bytes 1572872 | tf_op jit(solution)/shard_map/ppermute | solution.py:265
  152.4 18.5 %collective-permute-start.11 = (bf16[128,2048]{1,0:T(8,128)(2,1)S(1)}, bf16[128,2048]{1,0:T(8,128)(2,1)S(1)}, u32[]{:S(2)}, u32[]{:S(2)}) collective-permute-start(bf16[128,2048]{1,0:T(8,128)(2,1)S(1)} %add_convert_fusion.7), channel_id=1, source_target_pairs={{2,0},{4,2},{6,4},{7,6},{5,7},{3,5},{1,3},{0,1},{10,8},{12,10},{14... | collective-permute-start | bytes 1572872 | tf_op jit(solution)/shard_map/ppermute | solution.py:267
  160.5 10.4 %collective-permute-start.24 = (bf16[128,2048]{1,0:T(8,128)(2,1)S(1)}, bf16[128,2048]{1,0:T(8,128)(2,1)S(1)}, u32[]{:S(2)}, u32[]{:S(2)}) collective-permute-start(bf16[128,2048]{1,0:T(8,128)(2,1)S(1)} %add_convert_fusion.2), channel_id=1, source_target_pairs={{0,2},{2,4},{4,6},{6,7},{7,5},{5,3},{3,1},{1,0},{8,10},{10,12},{12... | collective-permute-start | bytes 1572872 | tf_op jit(solution)/shard_map/ppermute | solution.py:268
  (4 other events, 7.0 us)

commit v4 on v3

--- a/solution.py
+++ b/solution.py
@@ -8,7 +8,6 @@
 from jax.sharding import PartitionSpec as P
 
 VMEM_LIMIT = 12 * 1024 * 1024
-PACK_LIMIT = 40 * 1024 * 1024
 
 
 def ring_order(groups):
@@ -21,87 +20,65 @@
     return walk
 
 
-def table_rows(slots, height, width):
-    one = -(-slots * height // width)
-    return one, -(-2 * one // 8) * 8
-
-
-def pack_kernel(slots, a_ref, b_ref, target_ref, weight_ref, *refs):
-    tabled = refs[:2]
-    target_buf, weight_buf, sems = refs[2:]
+def table_rows(slots):
+    return -(-2 * slots // 16) * 16
+
+
+def tiles(half, width):
+    across = width // half
+    for i in range(half // 16):
+        for j in range(across):
+            at = (i * across + j) * 16
+            yield slice(i * 16, i * 16 + 16), slice(j * half, (j + 1) * half), slice(at, at + 16)
+
+
+def pack_kernel(slots, a_ref, b_ref, target_ref, weight_ref, out_a_ref, out_b_ref):
     half, width = a_ref.shape
-    height = 2 * half
-    one, extra = table_rows(slots, height, width)
-    per_row = width // height
-    copies = [
-        pltpu.make_async_copy(target_ref, target_buf, sems.at[0]),
-        pltpu.make_async_copy(weight_ref, weight_buf, sems.at[1]),
-        pltpu.make_async_copy(a_ref, tabled[0].at[pl.ds(0, half)], sems.at[2]),
-        pltpu.make_async_copy(b_ref, tabled[1].at[pl.ds(0, half)], sems.at[3]),
-    ]
-    for copy in copies:
-        copy.start()
-    copies[0].wait()
-    copies[1].wait()
-    weight = weight_buf[...]
+    for rows, columns, packed in tiles(half, width):
+        out_a_ref[packed, :] = a_ref[rows, columns]
+        out_b_ref[packed, :] = b_ref[rows, columns]
+    weight = weight_ref[...]
     share = weight / jnp.sum(weight, axis=0, keepdims=True)
-    target = target_buf[...]
-    row = lax.broadcasted_iota(jnp.int32, (extra, height), 0)
-    for lane in range(per_row):
-        block = jnp.zeros((extra, height), jnp.float32)
-        for r in range(one):
-            slot = r * per_row + lane
-            if slot < slots:
-                value = jnp.sum(jnp.where(target == slot, share, 0.0), axis=0, keepdims=True)
-                high = value.astype(jnp.bfloat16).astype(jnp.float32)
-                block = jnp.where(row == r, high, block)
-                block = jnp.where(row == one + r, value - high, block)
-        for ref in tabled:
-            ref[half:, lane * height:(lane + 1) * height] = block.astype(jnp.bfloat16)
-    for copy in copies[2:]:
-        copy.wait()
+    target = target_ref[...]
+    row = lax.broadcasted_iota(jnp.int32, (table_rows(slots), half), 0)
+    block = jnp.zeros(row.shape, jnp.float32)
+    for slot in range(slots):
+        value = jnp.sum(jnp.where(target == slot, share, 0.0), axis=0, keepdims=True)
+        block = jnp.where(row == slot, value[:, :half], block)
+        block = jnp.where(row == slots + slot, value[:, half:], block)
+    out_a_ref[width:, :] = block.astype(jnp.bfloat16)
+    out_b_ref[width:, :] = block.astype(jnp.bfloat16)
 
 
 def pack(a, b, target, router_weight, slots):
     half, width = a.shape
-    height, top = target.shape
-    extra = table_rows(slots, height, width)[1]
     vmem = pl.BlockSpec(memory_space=pltpu.VMEM)
     return pl.pallas_call(
         functools.partial(pack_kernel, slots),
-        in_specs=[pl.BlockSpec(memory_space=pl.ANY)] * 4,
+        in_specs=[vmem] * 4,
         out_specs=[vmem] * 2,
-        out_shape=[jax.ShapeDtypeStruct((half + extra, width), jnp.bfloat16)] * 2,
-        scratch_shapes=[
-            pltpu.VMEM((top, height), jnp.int32),
-            pltpu.VMEM((top, height), jnp.float32),
-            pltpu.SemaphoreType.DMA((4,)),
-        ],
-        compiler_params=pltpu.CompilerParams(vmem_limit_bytes=PACK_LIMIT),
-        cost_estimate=pl.CostEstimate(flops=0, bytes_accessed=4 * height * width, transcendentals=0),
+        out_shape=[jax.ShapeDtypeStruct((width + table_rows(slots), half), jnp.bfloat16)] * 2,
+        compiler_params=pltpu.CompilerParams(vmem_limit_bytes=VMEM_LIMIT),
+        cost_estimate=pl.CostEstimate(flops=0, bytes_accessed=8 * half * width, transcendentals=0),
     )(a, b, target.T, router_weight.T)
 
 
-def columns(place_ref, table_ref, first, slots, height, owned):
-    half = height // 2
-    width = table_ref.shape[1]
-    one, extra = table_rows(slots, height, width)
-    per_row = width // height
+def columns(place_ref, lead_ref, index, slots, owned):
+    rows, half = lead_ref.shape
+    extra = table_rows(slots)
     me, after, pick = place_ref[0], place_ref[1], place_ref[2]
+    block = lead_ref[rows - extra:, :].astype(jnp.float32)
+    row = lax.broadcasted_iota(jnp.int32, block.shape, 0)
 
     def column(slot):
-        lane = pl.multiple_of(lax.rem(slot, per_row) * height + first, half)
-        block = table_ref[half:half + extra, pl.ds(lane, half)].astype(jnp.float32)
-        row = lax.broadcasted_iota(jnp.int32, block.shape, 0)
-        line = lax.div(slot, per_row)
-        return jnp.sum(jnp.where((row == line) | (row == one + line), block, 0.0), axis=0, keepdims=True)
+        return jnp.sum(jnp.where(row == index * slots + slot, block, 0.0), axis=0, keepdims=True)
 
     lent = column(after * (owned + 1) + owned)
-    row = lax.broadcasted_iota(jnp.int32, (128, half), 0)
+    line_of = lax.broadcasted_iota(jnp.int32, (128, half), 0)
     shares = jnp.zeros((128, half), jnp.float32)
     for e in range(owned):
         line = column(me * (owned + 1) + e) + jnp.where(pick == e, lent, 0.0)
-        shares = jnp.where(row == e, line, shares)
+        shares = jnp.where(line_of == e, line, shares)
     return shares.T
 
 
@@ -133,15 +110,16 @@
     lax.fori_loop(0, width // wide, fold, 0)
 
 
-def lead_kernel(slots, height, place_ref, a_ref, b_ref, gate_ref, up_ref, down_ref, *refs):
+def lead_kernel(slots, place_ref, a_ref, b_ref, gate_ref, up_ref, down_ref, *refs):
     out_a_ref, out_b_ref, other_ref, rows_ref, share_ref, hidden_ref = refs[-6:]
     owned = gate_ref.shape[0]
-    half = height // 2
-    for i, (ref, first) in enumerate(((a_ref, 0), (b_ref, half))):
+    half, width = out_a_ref.shape
+    for i, ref in enumerate((a_ref, b_ref)):
         at = slice(i * half, (i + 1) * half)
-        rows_ref[at, :] = ref[:half, :]
-        share_ref[at, :] = columns(place_ref, ref, first, slots, height, owned)
-        other_ref[at, :] = columns(place_ref, ref, half - first, slots, height, owned)
+        for rows, across, packed in tiles(half, width):
+            rows_ref[i * half + rows.start:i * half + rows.stop, across] = ref[packed, :]
+        share_ref[at, :] = columns(place_ref, ref, i, slots, owned)
+        other_ref[at, :] = columns(place_ref, ref, 1 - i, slots, owned)
     evaluate(rows_ref, share_ref, gate_ref, up_ref, down_ref, (out_a_ref, out_b_ref), hidden_ref)
 
 
@@ -162,11 +140,12 @@
     )
 
 
-def lead(place, weights, slots, height, a, b, earlier=()):
-    half, (owned, width, units) = height // 2, weights[0].shape
+def lead(place, weights, slots, a, b, earlier=()):
+    half, (owned, width, units) = a.shape[1], weights[0].shape
+    height = 2 * half
     vmem = pl.BlockSpec(memory_space=pltpu.VMEM)
     return pl.pallas_call(
-        functools.partial(lead_kernel, slots, height),
+        functools.partial(lead_kernel, slots),
         in_specs=[pl.BlockSpec(memory_space=pltpu.SMEM)] + [vmem] * 5 + [pl.BlockSpec(memory_space=pl.ANY)] * len(earlier),
         out_specs=[vmem] * 3,
         out_shape=[jax.ShapeDtypeStruct((half, width), jnp.bfloat16)] * 2
@@ -244,7 +223,7 @@
 
     a, b = tokens[:half], tokens[half:]
     lead_a, lead_b = pack(a, b, target, router_weight, slots)
-    run = functools.partial(lead, place, weights, slots, height)
+    run = functools.partial(lead, place, weights, slots)
     own_a, own_b, shares = run(lead_a, lead_b)
     earlier = (shares,)
     parts = {}

time: 173 us -> 171 us (0.988)
  no operation moved by 1% of the time
where the time goes in v4:
time: 171 us
  waiting for transfers between devices  76.6 us (45%)
  Pallas kernels  51.4 us (30%)
  starting transfers between devices  29.7 us (17%)
  local copies, waits for them, and re-layouts  11 us (6%)
    pallas_call x5, Pallas kernels, lead(): pl.pallas_call(functools.partial(lead_kernel, slots), in_specs=[pl.BlockS...  31.7 us
    ppermute x3, waiting for transfers between devices, body(): lead_a = lax.ppermute(add(lead_part_a, lead_a), 'expert', back)  24.8 us
    pallas_call x3, Pallas kernels, plain(): pl.pallas_call(plain_kernel, in_specs=[vmem] * 6, out_specs=[vmem] * 4, o...  18.3 us
    ppermute x1, waiting for transfers between devices, body(): lax.ppermute(far_a, 'expert', back)  10.8 us
    ppermute x3, waiting for transfers between devices, body(): lead_b = lax.ppermute(add(lead_part_b, lead_b), 'expert', ahead)  9.94 us
    unnamed x16, local copies, waits for them, and re-layouts  9.76 us
    ppermute x1, waiting for transfers between devices, body(): lax.ppermute(far_b, 'expert', ahead)  7.56 us
    ppermute x3, waiting for transfers between devices, body(): b = lax.ppermute(b, 'expert', ahead)  7.37 us
  transfers between devices with their start and end apart: 28, of which 18 were waited for; matrix products, arithmetic and copies ran while one was open for 1% of the time, Pallas kernels for 29%

profile of v4, /device:TPU:0, one launch (start us, length us, event | category | flops | bytes accessed | tf_op | source)
XLA Modules:
  0.0 171.0 jit_solution(3895218343082660667)
XLA Ops:
  1.3 3.1 %collective-permute-start.12 = (bf16[128,2048]{1,0:T(8,128)(2,1)S(1)}, bf16[128,2048]{1,0:T(8,128)(2,1)}, u32[]{:S(2)}, u32[]{:S(2)}) collective-permute-start(bf16[128,2048]{1,0:T(8,128)(2,1)S(1)} %get-tuple-element.57.b_ref), channel_id=1, source_target_pairs={{0,2},{2,4},{4,6},{6,7},{7,5},{5,3},{3,1},{1,0},{8,10},{10,12},{12... | collective-permute-start | bytes 1572872 | tf_op jit(solution)/shard_map/ppermute | solution.py:233
  6.0 2.1 %collective-permute-start = (bf16[2096,128]{1,0:T(8,128)(2,1)S(1)}, bf16[2096,128]{1,0:T(8,128)(2,1)S(1)}, u32[]{:S(2)}, u32[]{:S(2)}) collective-permute-start(bf16[2096,128]{1,0:T(8,128)(2,1)S(1)} %get-tuple-element.31.a_ref), channel_id=1, source_target_pairs={{0,2},{2,4},{4,6},{6,7},{7,5},{5,3},{3,1},{1,0},{8,10},{10,12},{12... | collective-permute-start | bytes 1609736 | tf_op jit(solution)/shard_map/ppermute | solution.py:231
  8.8 2.8 %copy-done = bf16[2,2048,768]{2,1,0:T(8,128)(2,1)S(1)} copy-done((bf16[2,2048,768]{2,1,0:T(8,128)(2,1)S(1)}, bf16[2,2048,768]{2,1,0:T(8,128)(2,1)}, u32[]{:S(2)}) %copy-start) | copy-done | bytes 6291480
  11.6 2.8 %copy-done.2 = bf16[2,2048,768]{2,1,0:T(8,128)(2,1)S(1)} copy-done((bf16[2,2048,768]{2,1,0:T(8,128)(2,1)S(1)}, bf16[2,2048,768]{2,1,0:T(8,128)(2,1)}, u32[]{:S(2)}) %copy-start.2) | copy-done | bytes 6291480
  14.4 2.8 %copy-done.4 = bf16[2,768,2048]{2,1,0:T(8,128)(2,1)S(1)} copy-done((bf16[2,768,2048]{2,1,0:T(8,128)(2,1)S(1)}, bf16[2,768,2048]{2,1,0:T(8,128)(2,1)}, u32[]{:S(2)}) %copy-start.4) | copy-done | bytes 6291480
  17.2 6.5 %shard_map.74 = (bf16[128,2048]{1,0:T(8,128)(2,1)S(1)}, bf16[128,2048]{1,0:T(8,128)(2,1)S(1)}, f32[256,128]{1,0:T(8,128)S(1)}) custom-call(s32[3]{0:T(128)S(1)} %pad_add_fusion.place_ref, bf16[2096,128]{1,0:T(8,128)(2,1)S(1)} %get-tuple-element.31.a_ref, bf16[2096,128]{1,0:T(8,128)(2,1)S(1)} %get-tuple-element.32.b_ref, bf16[2,2048,768]{2,1,0:T(8,128)(2,1)S(1)} %copy-done, ...), custom_call_target="tpu_custom_call" | custom-call | flops 4831838208 | bytes 4194304 | tf_op jit(solution)/shard_map/pallas_call | solution.py:147
  23.7 4.0 %collective-permute-done.a_ref = bf16[2096,128]{1,0:T(8,128)(2,1)S(1)} collective-permute-done((bf16[2096,128]{1,0:T(8,128)(2,1)S(1)}, bf16[2096,128]{1,0:T(8,128)(2,1)S(1)}, u32[]{:S(2)}, u32[]{:S(2)}) %collective-permute-start) | collective-permute-done | bytes 536608 | tf_op jit(solution)/shard_map/ppermute | solution.py:231
  27.7 1.8 %collective-permute-start.2 = (bf16[2096,128]{1,0:T(8,128)(2,1)S(1)}, bf16[2096,128]{1,0:T(8,128)(2,1)S(1)}, u32[]{:S(2)}, u32[]{:S(2)}) collective-permute-start(bf16[2096,128]{1,0:T(8,128)(2,1)S(1)} %collective-permute-done.a_ref), channel_id=1, source_target_pairs={{0,2},{2,4},{4,6},{6,7},{7,5},{5,3},{3,1},{1,0},{8,10},{10,12},{12... | collective-permute-start | bytes 1609736 | tf_op jit(solution)/shard_map/ppermute | solution.py:231
  29.7 6.3 %shard_map.75 = (bf16[128,2048]{1,0:T(8,128)(2,1)S(1)}, bf16[128,2048]{1,0:T(8,128)(2,1)S(1)}, f32[256,128]{1,0:T(8,128)S(1)}) custom-call(s32[3]{0:T(128)S(1)} %pad_add_fusion.place_ref, bf16[2096,128]{1,0:T(8,128)(2,1)S(1)} %collective-permute-done.a_ref, bf16[2096,128]{1,0:T(8,128)(2,1)S(1)} %collective-permute-done.1.b_ref, ...), custom_call_target="tpu_custom_call" | custom-call | flops 4831838208 | bytes 4194304 | tf_op jit(solution)/shard_map/pallas_call | solution.py:147
  36.1 6.9 %shard_map.79 = (bf16[128,2048]{1,0:T(8,128)(2,1)S(1)}, bf16[128,2048]{1,0:T(8,128)(2,1)S(1)}, bf16[128,2048]{1,0:T(8,128)(2,1)S(1)}, bf16[128,2048]{1,0:T(8,128)(2,1)S(1)}) custom-call(bf16[128,2048]{1,0:T(8,128)(2,1)} %collective-permute-done.12.b_ref, bf16[128,2048]{1,0:T(8,128)(2,1)} %collective-permute-done.13.a_ref, ...), custom_call_target="tpu_custom_call" | custom-call | flops 4831838208 | bytes 4194304 | tf_op jit(solution)/shard_map/pallas_call | solution.py:166
  43.0 1.9 %collective-permute-start.14 = (bf16[128,2048]{1,0:T(8,128)(2,1)S(1)}, bf16[128,2048]{1,0:T(8,128)(2,1)S(1)}, u32[]{:S(2)}, u32[]{:S(2)}) collective-permute-start(bf16[128,2048]{1,0:T(8,128)(2,1)S(1)} %get-tuple-element.41), channel_id=1, source_target_pairs={{0,2},{2,4},{4,6},{6,7},{7,5},{5,3},{3,1},{1,0},{8,10},{10,12},{12... | collective-permute-start | bytes 1572872 | tf_op jit(solution)/shard_map/ppermute | solution.py:233
  45.0 1.8 %collective-permute-start.4 = (bf16[2096,128]{1,0:T(8,128)(2,1)S(1)}, bf16[2096,128]{1,0:T(8,128)(2,1)S(1)}, u32[]{:S(2)}, u32[]{:S(2)}) collective-permute-start(bf16[2096,128]{1,0:T(8,128)(2,1)S(1)} %collective-permute-done.2.a_ref), channel_id=1, source_target_pairs={{0,2},{2,4},{4,6},{6,7},{7,5},{5,3},{3,1},{1,0},{8,10},{10,12},{12... | collective-permute-start | bytes 1609736 | tf_op jit(solution)/shard_map/ppermute | solution.py:231
  47.1 6.3 %shard_map.76 = (bf16[128,2048]{1,0:T(8,128)(2,1)S(1)}, bf16[128,2048]{1,0:T(8,128)(2,1)S(1)}, f32[256,128]{1,0:T(8,128)S(1)}) custom-call(s32[3]{0:T(128)S(1)} %pad_add_fusion.place_ref, bf16[2096,128]{1,0:T(8,128)(2,1)S(1)} %collective-permute-done.2.a_ref, bf16[2096,128]{1,0:T(8,128)(2,1)S(1)} %collective-permute-done.3.b_ref, ...), custom_call_target="tpu_custom_call" | custom-call | flops 4831838208 | bytes 4194304 | tf_op jit(solution)/shard_map/pallas_call | solution.py:147
  53.4 4.5 %collective-permute-done.14.b_ref = bf16[128,2048]{1,0:T(8,128)(2,1)S(1)} collective-permute-done((bf16[128,2048]{1,0:T(8,128)(2,1)S(1)}, bf16[128,2048]{1,0:T(8,128)(2,1)S(1)}, u32[]{:S(2)}, u32[]{:S(2)}) %collective-permute-start.14) | collective-permute-done | bytes 524320 | tf_op jit(solution)/shard_map/ppermute | solution.py:233
  57.9 1.8 %collective-permute-done.15.a_ref = bf16[128,2048]{1,0:T(8,128)(2,1)S(1)} collective-permute-done((bf16[128,2048]{1,0:T(8,128)(2,1)S(1)}, bf16[128,2048]{1,0:T(8,128)(2,1)S(1)}, u32[]{:S(2)}, u32[]{:S(2)}) %collective-permute-start.15) | collective-permute-done | bytes 524320 | tf_op jit(solution)/shard_map/ppermute | solution.py:234
  59.7 5.7 %shard_map.80 = (bf16[128,2048]{1,0:T(8,128)(2,1)S(1)}, bf16[128,2048]{1,0:T(8,128)(2,1)S(1)}, bf16[128,2048]{1,0:T(8,128)(2,1)S(1)}, bf16[128,2048]{1,0:T(8,128)(2,1)S(1)}) custom-call(bf16[128,2048]{1,0:T(8,128)(2,1)S(1)} %collective-permute-done.14.b_ref, bf16[128,2048]{1,0:T(8,128)(2,1)S(1)} %collective-permute-done.15.a_ref, ...), custom_call_target="tpu_custom_call" | custom-call | flops 4831838208 | bytes 4194304 | tf_op jit(solution)/shard_map/pallas_call | solution.py:166
  67.5 1.9 %collective-permute-done.4.a_ref = bf16[2096,128]{1,0:T(8,128)(2,1)S(1)} collective-permute-done((bf16[2096,128]{1,0:T(8,128)(2,1)S(1)}, bf16[2096,128]{1,0:T(8,128)(2,1)S(1)}, u32[]{:S(2)}, u32[]{:S(2)}) %collective-permute-start.4) | collective-permute-done | bytes 536608 | tf_op jit(solution)/shard_map/ppermute | solution.py:231
  69.4 1.8 %collective-permute-start.6 = (bf16[2096,128]{1,0:T(8,128)(2,1)S(1)}, bf16[2096,128]{1,0:T(8,128)(2,1)S(1)}, u32[]{:S(2)}, u32[]{:S(2)}) collective-permute-start(bf16[2096,128]{1,0:T(8,128)(2,1)S(1)} %collective-permute-done.4.a_ref), channel_id=1, source_target_pairs={{0,2},{2,4},{4,6},{6,7},{7,5},{5,3},{3,1},{1,0},{8,10},{10,12},{12... | collective-permute-start | bytes 1609736 | tf_op jit(solution)/shard_map/ppermute | solution.py:239
  71.4 6.3 %shard_map.77 = (bf16[128,2048]{1,0:T(8,128)(2,1)S(1)}, bf16[128,2048]{1,0:T(8,128)(2,1)S(1)}, f32[256,128]{1,0:T(8,128)S(1)}) custom-call(s32[3]{0:T(128)S(1)} %pad_add_fusion.place_ref, bf16[2096,128]{1,0:T(8,128)(2,1)S(1)} %collective-permute-done.4.a_ref, bf16[2096,128]{1,0:T(8,128)(2,1)S(1)} %collective-permute-done.5.b_ref, ...), custom_call_target="tpu_custom_call" | custom-call | flops 4831838208 | bytes 4194304 | tf_op jit(solution)/shard_map/pallas_call | solution.py:147
  77.7 2.9 %collective-permute-done.16.b_ref = bf16[128,2048]{1,0:T(8,128)(2,1)S(1)} collective-permute-done((bf16[128,2048]{1,0:T(8,128)(2,1)S(1)}, bf16[128,2048]{1,0:T(8,128)(2,1)S(1)}, u32[]{:S(2)}, u32[]{:S(2)}) %collective-permute-start.16) | collective-permute-done | bytes 524320 | tf_op jit(solution)/shard_map/ppermute | solution.py:233
  80.6 1.8 %collective-permute-done.17.a_ref = bf16[128,2048]{1,0:T(8,128)(2,1)S(1)} collective-permute-done((bf16[128,2048]{1,0:T(8,128)(2,1)S(1)}, bf16[128,2048]{1,0:T(8,128)(2,1)S(1)}, u32[]{:S(2)}, u32[]{:S(2)}) %collective-permute-start.17) | collective-permute-done | bytes 524320 | tf_op jit(solution)/shard_map/ppermute | solution.py:234
  82.4 5.7 %shard_map.81 = (bf16[128,2048]{1,0:T(8,128)(2,1)S(1)}, bf16[128,2048]{1,0:T(8,128)(2,1)S(1)}, bf16[128,2048]{1,0:T(8,128)(2,1)}, bf16[128,2048]{1,0:T(8,128)(2,1)}) custom-call(bf16[128,2048]{1,0:T(8,128)(2,1)S(1)} %collective-permute-done.16.b_ref, bf16[128,2048]{1,0:T(8,128)(2,1)S(1)} %collective-permute-done.17.a_ref, ...), custom_call_target="tpu_custom_call" | custom-call | flops 4831838208 | bytes 4194304 | tf_op jit(solution)/shard_map/pallas_call | solution.py:166
  90.2 1.9 %collective-permute-done.6.a_ref = bf16[2096,128]{1,0:T(8,128)(2,1)S(1)} collective-permute-done((bf16[2096,128]{1,0:T(8,128)(2,1)S(1)}, bf16[2096,128]{1,0:T(8,128)(2,1)S(1)}, u32[]{:S(2)}, u32[]{:S(2)}) %collective-permute-start.6) | collective-permute-done | bytes 536608 | tf_op jit(solution)/shard_map/ppermute | solution.py:239
  92.1 1.8 %collective-permute-done.7.b_ref = bf16[2096,128]{1,0:T(8,128)(2,1)S(1)} collective-permute-done((bf16[2096,128]{1,0:T(8,128)(2,1)S(1)}, bf16[2096,128]{1,0:T(8,128)(2,1)S(1)}, u32[]{:S(2)}, u32[]{:S(2)}) %collective-permute-start.7) | collective-permute-done | bytes 536608 | tf_op jit(solution)/shard_map/ppermute | solution.py:239
  93.9 6.3 %shard_map.78 = (bf16[128,2048]{1,0:T(8,128)(2,1)S(1)}, bf16[128,2048]{1,0:T(8,128)(2,1)S(1)}, f32[256,128]{1,0:T(8,128)}) custom-call(s32[3]{0:T(128)S(1)} %pad_add_fusion.place_ref, bf16[2096,128]{1,0:T(8,128)(2,1)S(1)} %collective-permute-done.6.a_ref, bf16[2096,128]{1,0:T(8,128)(2,1)S(1)} %collective-permute-done.7.b_ref, ...), custom_call_target="tpu_custom_call" | custom-call | flops 4831838208 | bytes 4194304 | tf_op jit(solution)/shard_map/pallas_call | solution.py:147
  105.6 10.8 %collective-permute-done.8 = bf16[128,2048]{1,0:T(8,128)(2,1)S(1)} collective-permute-done((bf16[128,2048]{1,0:T(8,128)(2,1)S(1)}, bf16[128,2048]{1,0:T(8,128)(2,1)S(1)}, u32[]{:S(2)}, u32[]{:S(2)}) %collective-permute-start.8) | collective-permute-done | bytes 524320 | tf_op jit(solution)/shard_map/ppermute | solution.py:241
  116.8 7.6 %collective-permute-done.21 = bf16[128,2048]{1,0:T(8,128)(2,1)S(1)} collective-permute-done((bf16[128,2048]{1,0:T(8,128)(2,1)S(1)}, bf16[128,2048]{1,0:T(8,128)(2,1)S(1)}, u32[]{:S(2)}, u32[]{:S(2)}) %collective-permute-start.21) | collective-permute-done | bytes 524320 | tf_op jit(solution)/shard_map/ppermute | solution.py:241
  127.8 8.1 %collective-permute-done.9 = bf16[128,2048]{1,0:T(8,128)(2,1)S(1)} collective-permute-done((bf16[128,2048]{1,0:T(8,128)(2,1)S(1)}, bf16[128,2048]{1,0:T(8,128)(2,1)S(1)}, u32[]{:S(2)}, u32[]{:S(2)}) %collective-permute-start.9) | collective-permute-done | bytes 524320 | tf_op jit(solution)/shard_map/ppermute | solution.py:246
  136.7 2.7 %collective-permute-done.22 = bf16[128,2048]{1,0:T(8,128)(2,1)S(1)} collective-permute-done((bf16[128,2048]{1,0:T(8,128)(2,1)S(1)}, bf16[128,2048]{1,0:T(8,128)(2,1)S(1)}, u32[]{:S(2)}, u32[]{:S(2)}) %collective-permute-start.22) | collective-permute-done | bytes 524320 | tf_op jit(solution)/shard_map/ppermute | solution.py:247
  141.8 9.2 %collective-permute-done.10 = bf16[128,2048]{1,0:T(8,128)(2,1)S(1)} collective-permute-done((bf16[128,2048]{1,0:T(8,128)(2,1)S(1)}, bf16[128,2048]{1,0:T(8,128)(2,1)S(1)}, u32[]{:S(2)}, u32[]{:S(2)}) %collective-permute-start.10) | collective-permute-done | bytes 524320 | tf_op jit(solution)/shard_map/ppermute | solution.py:246
  151.7 7.2 %collective-permute-done.23 = bf16[128,2048]{1,0:T(8,128)(2,1)S(1)} collective-permute-done((bf16[128,2048]{1,0:T(8,128)(2,1)S(1)}, bf16[128,2048]{1,0:T(8,128)(2,1)S(1)}, u32[]{:S(2)}, u32[]{:S(2)}) %collective-permute-start.23) | collective-permute-done | bytes 524320 | tf_op jit(solution)/shard_map/ppermute | solution.py:247
  162.2 7.4 %collective-permute-done.11.refs_1_ = bf16[128,2048]{1,0:T(8,128)(2,1)S(1)} collective-permute-done((bf16[128,2048]{1,0:T(8,128)(2,1)S(1)}, bf16[128,2048]{1,0:T(8,128)(2,1)S(1)}, u32[]{:S(2)}, u32[]{:S(2)}) %collective-permute-start.11) | collective-permute-done | bytes 524320 | tf_op jit(solution)/shard_map/ppermute | solution.py:246
  (62 shorter events, 25.4 us)
Async XLA Ops:
  1.3 34.8 %collective-permute-start.12 = (bf16[128,2048]{1,0:T(8,128)(2,1)S(1)}, bf16[128,2048]{1,0:T(8,128)(2,1)}, u32[]{:S(2)}, u32[]{:S(2)}) collective-permute-start(bf16[128,2048]{1,0:T(8,128)(2,1)S(1)} %get-tuple-element.57.b_ref), channel_id=1, source_target_pairs={{0,2},{2,4},{4,6},{6,7},{7,5},{5,3},{3,1},{1,0},{8,10},{10,12},{12... | collective-permute-start | bytes 1572872 | tf_op jit(solution)/shard_map/ppermute | solution.py:233
  4.4 31.7 %collective-permute-start.13 = (bf16[128,2048]{1,0:T(8,128)(2,1)S(1)}, bf16[128,2048]{1,0:T(8,128)(2,1)}, u32[]{:S(2)}, u32[]{:S(2)}) collective-permute-start(bf16[128,2048]{1,0:T(8,128)(2,1)S(1)} %get-tuple-element.58.a_ref), channel_id=1, source_target_pairs={{2,0},{4,2},{6,4},{7,6},{5,7},{3,5},{1,3},{0,1},{10,8},{12,10},{14... | collective-permute-start | bytes 1572872 | tf_op jit(solution)/shard_map/ppermute | solution.py:234
  6.0 21.7 %collective-permute-start = (bf16[2096,128]{1,0:T(8,128)(2,1)S(1)}, bf16[2096,128]{1,0:T(8,128)(2,1)S(1)}, u32[]{:S(2)}, u32[]{:S(2)}) collective-permute-start(bf16[2096,128]{1,0:T(8,128)(2,1)S(1)} %get-tuple-element.31.a_ref), channel_id=1, source_target_pairs={{0,2},{2,4},{4,6},{6,7},{7,5},{5,3},{3,1},{1,0},{8,10},{10,12},{12... | collective-permute-start | bytes 1609736 | tf_op jit(solution)/shard_map/ppermute | solution.py:231
  8.1 21.4 %collective-permute-start.1 = (bf16[2096,128]{1,0:T(8,128)(2,1)S(1)}, bf16[2096,128]{1,0:T(8,128)(2,1)S(1)}, u32[]{:S(2)}, u32[]{:S(2)}) collective-permute-start(bf16[2096,128]{1,0:T(8,128)(2,1)S(1)} %get-tuple-element.32.b_ref), channel_id=1, source_target_pairs={{2,0},{4,2},{6,4},{7,6},{5,7},{3,5},{1,3},{0,1},{10,8},{12,10},{14... | collective-permute-start | bytes 1609736 | tf_op jit(solution)/shard_map/ppermute | solution.py:232
  8.8 2.8 %copy-start = (bf16[2,2048,768]{2,1,0:T(8,128)(2,1)S(1)}, bf16[2,2048,768]{2,1,0:T(8,128)(2,1)}, u32[]{:S(2)}) copy-start(bf16[2,2048,768]{2,1,0:T(8,128)(2,1)} %gate_ref.15) | copy-start | bytes 18874372
  17.2 12.6 %copy-start.1 = (bf16[2,2048,768]{2,1,0:T(8,128)(2,1)S(1)}, bf16[2,2048,768]{2,1,0:T(8,128)(2,1)}, u32[]{:S(2)}) copy-start(bf16[2,2048,768]{2,1,0:T(8,128)(2,1)} %gate_ref.15) | copy-start | bytes 18874372
  17.2 12.6 %copy-start.3 = (bf16[2,2048,768]{2,1,0:T(8,128)(2,1)S(1)}, bf16[2,2048,768]{2,1,0:T(8,128)(2,1)}, u32[]{:S(2)}) copy-start(bf16[2,2048,768]{2,1,0:T(8,128)(2,1)} %up_ref.15) | copy-start | bytes 18874372
  17.2 12.6 %copy-start.5 = (bf16[2,768,2048]{2,1,0:T(8,128)(2,1)S(1)}, bf16[2,768,2048]{2,1,0:T(8,128)(2,1)}, u32[]{:S(2)}) copy-start(bf16[2,768,2048]{2,1,0:T(8,128)(2,1)} %param.13) | copy-start | bytes 18874372
  27.7 17.4 %collective-permute-start.2 = (bf16[2096,128]{1,0:T(8,128)(2,1)S(1)}, bf16[2096,128]{1,0:T(8,128)(2,1)S(1)}, u32[]{:S(2)}, u32[]{:S(2)}) collective-permute-start(bf16[2096,128]{1,0:T(8,128)(2,1)S(1)} %collective-permute-done.a_ref), channel_id=1, source_target_pairs={{0,2},{2,4},{4,6},{6,7},{7,5},{5,3},{3,1},{1,0},{8,10},{10,12},{12... | collective-permute-start | bytes 1609736 | tf_op jit(solution)/shard_map/ppermute | solution.py:231
  29.5 17.3 %collective-permute-start.3 = (bf16[2096,128]{1,0:T(8,128)(2,1)S(1)}, bf16[2096,128]{1,0:T(8,128)(2,1)S(1)}, u32[]{:S(2)}, u32[]{:S(2)}) collective-permute-start(bf16[2096,128]{1,0:T(8,128)(2,1)S(1)} %collective-permute-done.1.b_ref), channel_id=1, source_target_pairs={{2,0},{4,2},{6,4},{7,6},{5,7},{3,5},{1,3},{0,1},{10,8},{12,10},{14... | collective-permute-start | bytes 1609736 | tf_op jit(solution)/shard_map/ppermute | solution.py:232
  43.0 14.9 %collective-permute-start.14 = (bf16[128,2048]{1,0:T(8,128)(2,1)S(1)}, bf16[128,2048]{1,0:T(8,128)(2,1)S(1)}, u32[]{:S(2)}, u32[]{:S(2)}) collective-permute-start(bf16[128,2048]{1,0:T(8,128)(2,1)S(1)} %get-tuple-element.41), channel_id=1, source_target_pairs={{0,2},{2,4},{4,6},{6,7},{7,5},{5,3},{3,1},{1,0},{8,10},{10,12},{12... | collective-permute-start | bytes 1572872 | tf_op jit(solution)/shard_map/ppermute | solution.py:233
  44.8 14.9 %collective-permute-start.15 = (bf16[128,2048]{1,0:T(8,128)(2,1)S(1)}, bf16[128,2048]{1,0:T(8,128)(2,1)S(1)}, u32[]{:S(2)}, u32[]{:S(2)}) collective-permute-start(bf16[128,2048]{1,0:T(8,128)(2,1)S(1)} %get-tuple-element.42), channel_id=1, source_target_pairs={{2,0},{4,2},{6,4},{7,6},{5,7},{3,5},{1,3},{0,1},{10,8},{12,10},{14... | collective-permute-start | bytes 1572872 | tf_op jit(solution)/shard_map/ppermute | solution.py:234
  45.0 24.3 %collective-permute-start.4 = (bf16[2096,128]{1,0:T(8,128)(2,1)S(1)}, bf16[2096,128]{1,0:T(8,128)(2,1)S(1)}, u32[]{:S(2)}, u32[]{:S(2)}) collective-permute-start(bf16[2096,128]{1,0:T(8,128)(2,1)S(1)} %collective-permute-done.2.a_ref), channel_id=1, source_target_pairs={{0,2},{2,4},{4,6},{6,7},{7,5},{5,3},{3,1},{1,0},{8,10},{10,12},{12... | collective-permute-start | bytes 1609736 | tf_op jit(solution)/shard_map/ppermute | solution.py:231
  46.9 24.3 %collective-permute-start.5 = (bf16[2096,128]{1,0:T(8,128)(2,1)S(1)}, bf16[2096,128]{1,0:T(8,128)(2,1)S(1)}, u32[]{:S(2)}, u32[]{:S(2)}) collective-permute-start(bf16[2096,128]{1,0:T(8,128)(2,1)S(1)} %collective-permute-done.3.b_ref), channel_id=1, source_target_pairs={{2,0},{4,2},{6,4},{7,6},{5,7},{3,5},{1,3},{0,1},{10,8},{12,10},{14... | collective-permute-start | bytes 1609736 | tf_op jit(solution)/shard_map/ppermute | solution.py:232
  65.4 15.2 %collective-permute-start.16 = (bf16[128,2048]{1,0:T(8,128)(2,1)S(1)}, bf16[128,2048]{1,0:T(8,128)(2,1)S(1)}, u32[]{:S(2)}, u32[]{:S(2)}) collective-permute-start(bf16[128,2048]{1,0:T(8,128)(2,1)S(1)} %get-tuple-element.45), channel_id=1, source_target_pairs={{0,2},{2,4},{4,6},{6,7},{7,5},{5,3},{3,1},{1,0},{8,10},{10,12},{12... | collective-permute-start | bytes 1572872 | tf_op jit(solution)/shard_map/ppermute | solution.py:233
  67.0 15.4 %collective-permute-start.17 = (bf16[128,2048]{1,0:T(8,128)(2,1)S(1)}, bf16[128,2048]{1,0:T(8,128)(2,1)S(1)}, u32[]{:S(2)}, u32[]{:S(2)}) collective-permute-start(bf16[128,2048]{1,0:T(8,128)(2,1)S(1)} %get-tuple-element.46), channel_id=1, source_target_pairs={{2,0},{4,2},{6,4},{7,6},{5,7},{3,5},{1,3},{0,1},{10,8},{12,10},{14... | collective-permute-start | bytes 1572872 | tf_op jit(solution)/shard_map/ppermute | solution.py:234
  69.4 22.7 %collective-permute-start.6 = (bf16[2096,128]{1,0:T(8,128)(2,1)S(1)}, bf16[2096,128]{1,0:T(8,128)(2,1)S(1)}, u32[]{:S(2)}, u32[]{:S(2)}) collective-permute-start(bf16[2096,128]{1,0:T(8,128)(2,1)S(1)} %collective-permute-done.4.a_ref), channel_id=1, source_target_pairs={{0,2},{2,4},{4,6},{6,7},{7,5},{5,3},{3,1},{1,0},{8,10},{10,12},{12... | collective-permute-start | bytes 1609736 | tf_op jit(solution)/shard_map/ppermute | solution.py:239
  71.2 22.7 %collective-permute-start.7 = (bf16[2096,128]{1,0:T(8,128)(2,1)S(1)}, bf16[2096,128]{1,0:T(8,128)(2,1)S(1)}, u32[]{:S(2)}, u32[]{:S(2)}) collective-permute-start(bf16[2096,128]{1,0:T(8,128)(2,1)S(1)} %collective-permute-done.5.b_ref), channel_id=1, source_target_pairs={{2,0},{4,2},{6,4},{7,6},{5,7},{3,5},{1,3},{0,1},{10,8},{12,10},{14... | collective-permute-start | bytes 1609736 | tf_op jit(solution)/shard_map/ppermute | solution.py:239
  88.1 12.9 %collective-permute-start.18 = (bf16[128,2048]{1,0:T(8,128)(2,1)S(1)}, bf16[128,2048]{1,0:T(8,128)(2,1)S(1)}, u32[]{:S(2)}, u32[]{:S(2)}) collective-permute-start(bf16[128,2048]{1,0:T(8,128)(2,1)S(1)} %get-tuple-element.48), channel_id=1, source_target_pairs={{0,2},{2,4},{4,6},{6,7},{7,5},{5,3},{3,1},{1,0},{8,10},{10,12},{12... | collective-permute-start | bytes 1572872 | tf_op jit(solution)/shard_map/ppermute | solution.py:245
  89.7 15.4 %collective-permute-start.25 = (bf16[128,2048]{1,0:T(8,128)(2,1)S(1)}, bf16[128,2048]{1,0:T(8,128)(2,1)S(1)}, u32[]{:S(2)}, u32[]{:S(2)}) collective-permute-start(bf16[128,2048]{1,0:T(8,128)(2,1)S(1)} %get-tuple-element.56), channel_id=1, source_target_pairs={{2,0},{4,2},{6,4},{7,6},{5,7},{3,5},{1,3},{0,1},{10,8},{12,10},{14... | collective-permute-start | bytes 1572872 | tf_op jit(solution)/shard_map/ppermute | solution.py:244
  100.2 16.2 %collective-permute-start.8 = (bf16[128,2048]{1,0:T(8,128)(2,1)S(1)}, bf16[128,2048]{1,0:T(8,128)(2,1)S(1)}, u32[]{:S(2)}, u32[]{:S(2)}) collective-permute-start(bf16[128,2048]{1,0:T(8,128)(2,1)S(1)} %get-tuple-element.38), channel_id=1, source_target_pairs={{2,0},{4,2},{6,4},{7,6},{5,7},{3,5},{1,3},{0,1},{10,8},{12,10},{14... | collective-permute-start | bytes 1572872 | tf_op jit(solution)/shard_map/ppermute | solution.py:241
  101.2 24.9 %collective-permute-start.19 = (bf16[128,2048]{1,0:T(8,128)(2,1)S(1)}, bf16[128,2048]{1,0:T(8,128)(2,1)S(1)}, u32[]{:S(2)}, u32[]{:S(2)}) collective-permute-start(bf16[128,2048]{1,0:T(8,128)(2,1)S(1)} %add_convert_fusion.6), channel_id=1, source_target_pairs={{0,2},{2,4},{4,6},{6,7},{7,5},{5,3},{3,1},{1,0},{8,10},{10,12},{12... | collective-permute-start | bytes 1572872 | tf_op jit(solution)/shard_map/ppermute | solution.py:245
  102.7 21.6 %collective-permute-start.21 = (bf16[128,2048]{1,0:T(8,128)(2,1)S(1)}, bf16[128,2048]{1,0:T(8,128)(2,1)S(1)}, u32[]{:S(2)}, u32[]{:S(2)}) collective-permute-start(bf16[128,2048]{1,0:T(8,128)(2,1)S(1)} %get-tuple-element.53), channel_id=1, source_target_pairs={{0,2},{2,4},{4,6},{6,7},{7,5},{5,3},{3,1},{1,0},{8,10},{10,12},{12... | collective-permute-start | bytes 1572872 | tf_op jit(solution)/shard_map/ppermute | solution.py:241
  105.3 35.8 %collective-permute-start.26 = (bf16[128,2048]{1,0:T(8,128)(2,1)S(1)}, bf16[128,2048]{1,0:T(8,128)(2,1)S(1)}, u32[]{:S(2)}, u32[]{:S(2)}) collective-permute-start(bf16[128,2048]{1,0:T(8,128)(2,1)S(1)} %add_convert_fusion.1), channel_id=1, source_target_pairs={{2,0},{4,2},{6,4},{7,6},{5,7},{3,5},{1,3},{0,1},{10,8},{12,10},{14... | collective-permute-start | bytes 1572872 | tf_op jit(solution)/shard_map/ppermute | solution.py:244
  116.5 19.4 %collective-permute-start.9 = (bf16[128,2048]{1,0:T(8,128)(2,1)S(1)}, bf16[128,2048]{1,0:T(8,128)(2,1)S(1)}, u32[]{:S(2)}, u32[]{:S(2)}) collective-permute-start(bf16[128,2048]{1,0:T(8,128)(2,1)S(1)} %add_convert_fusion.9), channel_id=1, source_target_pairs={{2,0},{4,2},{6,4},{7,6},{5,7},{3,5},{1,3},{0,1},{10,8},{12,10},{14... | collective-permute-start | bytes 1572872 | tf_op jit(solution)/shard_map/ppermute | solution.py:246
  124.5 14.9 %collective-permute-start.22 = (bf16[128,2048]{1,0:T(8,128)(2,1)S(1)}, bf16[128,2048]{1,0:T(8,128)(2,1)S(1)}, u32[]{:S(2)}, u32[]{:S(2)}) collective-permute-start(bf16[128,2048]{1,0:T(8,128)(2,1)S(1)} %add_convert_fusion.4), channel_id=1, source_target_pairs={{0,2},{2,4},{4,6},{6,7},{7,5},{5,3},{3,1},{1,0},{8,10},{10,12},{12... | collective-permute-start | bytes 1572872 | tf_op jit(solution)/shard_map/ppermute | solution.py:247
  126.2 34.4 %collective-permute-start.20 = (bf16[128,2048]{1,0:T(8,128)(2,1)S(1)}, bf16[128,2048]{1,0:T(8,128)(2,1)S(1)}, u32[]{:S(2)}, u32[]{:S(2)}) collective-permute-start(bf16[128,2048]{1,0:T(8,128)(2,1)S(1)} %add_convert_fusion.5), channel_id=1, source_target_pairs={{0,2},{2,4},{4,6},{6,7},{7,5},{5,3},{3,1},{1,0},{8,10},{10,12},{12... | collective-permute-start | bytes 1572872 | tf_op jit(solution)/shard_map/ppermute | solution.py:245
  136.1 14.9 %collective-permute-start.10 = (bf16[128,2048]{1,0:T(8,128)(2,1)S(1)}, bf16[128,2048]{1,0:T(8,128)(2,1)S(1)}, u32[]{:S(2)}, u32[]{:S(2)}) collective-permute-start(bf16[128,2048]{1,0:T(8,128)(2,1)S(1)} %add_convert_fusion.8), channel_id=1, source_target_pairs={{2,0},{4,2},{6,4},{7,6},{5,7},{3,5},{1,3},{0,1},{10,8},{12,10},{14... | collective-permute-start | bytes 1572872 | tf_op jit(solution)/shard_map/ppermute | solution.py:246
  139.5 19.4 %collective-permute-start.23 = (bf16[128,2048]{1,0:T(8,128)(2,1)S(1)}, bf16[128,2048]{1,0:T(8,128)(2,1)S(1)}, u32[]{:S(2)}, u32[]{:S(2)}) collective-permute-start(bf16[128,2048]{1,0:T(8,128)(2,1)S(1)} %add_convert_fusion.3), channel_id=1, source_target_pairs={{0,2},{2,4},{4,6},{6,7},{7,5},{5,3},{3,1},{1,0},{8,10},{10,12},{12... | collective-permute-start | bytes 1572872 | tf_op jit(solution)/shard_map/ppermute | solution.py:247
  141.2 21.0 %collective-permute-start.27 = (bf16[128,2048]{1,0:T(8,128)(2,1)S(1)}, bf16[128,2048]{1,0:T(8,128)(2,1)S(1)}, u32[]{:S(2)}, u32[]{:S(2)}) collective-permute-start(bf16[128,2048]{1,0:T(8,128)(2,1)S(1)} %add_convert_fusion), channel_id=1, source_target_pairs={{2,0},{4,2},{6,4},{7,6},{5,7},{3,5},{1,3},{0,1},{10,8},{12,10},{14... | collective-permute-start | bytes 1572872 | tf_op jit(solution)/shard_map/ppermute | solution.py:244
  151.1 18.5 %collective-permute-start.11 = (bf16[128,2048]{1,0:T(8,128)(2,1)S(1)}, bf16[128,2048]{1,0:T(8,128)(2,1)S(1)}, u32[]{:S(2)}, u32[]{:S(2)}) collective-permute-start(bf16[128,2048]{1,0:T(8,128)(2,1)S(1)} %add_convert_fusion.7), channel_id=1, source_target_pairs={{2,0},{4,2},{6,4},{7,6},{5,7},{3,5},{1,3},{0,1},{10,8},{12,10},{14... | collective-permute-start | bytes 1572872 | tf_op jit(solution)/shard_map/ppermute | solution.py:246
  159.0 10.6 %collective-permute-start.24 = (bf16[128,2048]{1,0:T(8,128)(2,1)S(1)}, bf16[128,2048]{1,0:T(8,128)(2,1)S(1)}, u32[]{:S(2)}, u32[]{:S(2)}) collective-permute-start(bf16[128,2048]{1,0:T(8,128)(2,1)S(1)} %add_convert_fusion.2), channel_id=1, source_target_pairs={{0,2},{2,4},{4,6},{6,7},{7,5},{5,3},{3,1},{1,0},{8,10},{10,12},{12... | collective-permute-start | bytes 1572872 | tf_op jit(solution)/shard_map/ppermute | solution.py:247
  (4 other events, 7.0 us)

commit v5 on v4

v5 whole, which is shorter than its diff:
```python
import functools

import jax
import jax.numpy as jnp
import numpy as np
from jax import lax
from jax.experimental import pallas as pl
from jax.experimental.pallas import tpu as pltpu
from jax.sharding import PartitionSpec as P

VMEM_LIMIT = 12 * 1024 * 1024


def grid_of(groups):
    columns = 1 << ((groups.bit_length() - 1) // 2)
    return groups // columns, columns


def ring_order(groups):
    rows, columns = grid_of(groups)
    walk = [z * columns for z in range(rows)]
    for turn, z in enumerate(reversed(range(rows))):
        row = [z * columns + x for x in range(1, columns)]
        walk += row if turn % 2 == 0 else row[::-1]
    return walk


def table_rows(slots):
    return -(-slots // 16) * 16


def pack_kernel(slots, tokens_ref, target_ref, weight_ref, *outs):
    height, width = tokens_ref.shape
    half = height // 2
    across = width // half
    weight = weight_ref[...]
    share = weight / jnp.sum(weight, axis=0, keepdims=True)
    target = target_ref[...]
    row = lax.broadcasted_iota(jnp.int32, (table_rows(slots), height), 0)
    block = jnp.zeros(row.shape, jnp.float32)
    for slot in range(slots):
        value = jnp.sum(jnp.where(target == slot, share, 0.0), axis=0, keepdims=True)
        block = jnp.where(row == slot, value, block)
    for k, out_ref in enumerate(outs):
        for i in range(half // 16):
            for j in range(across):
                tile = tokens_ref[k * half + i * 16:k * half + i * 16 + 16, j * half:(j + 1) * half]
                out_ref[(i * across + j) * 16:(i * across + j) * 16 + 16, :] = tile
        out_ref[width:, :] = block[:, k * half:(k + 1) * half].astype(jnp.bfloat16)


def pack(tokens, target, router_weight, slots):
    height, width = tokens.shape
    half = height // 2
    vmem = pl.BlockSpec(memory_space=pltpu.VMEM)
    return pl.pallas_call(
        functools.partial(pack_kernel, slots),
        in_specs=[vmem] * 3,
        out_specs=[vmem] * 2,
        out_shape=[jax.ShapeDtypeStruct((width + table_rows(slots), half), jnp.bfloat16)] * 2,
        compiler_params=pltpu.CompilerParams(vmem_limit_bytes=VMEM_LIMIT),
        cost_estimate=pl.CostEstimate(flops=0, bytes_accessed=4 * height * width, transcendentals=0),
    )(tokens, target.T, router_weight.T)


def columns(place_ref, chunk_ref, slots, owned):
    rows, half = chunk_ref.shape
    me, after, pick = place_ref[0], place_ref[1], place_ref[2]
    block = chunk_ref[rows - table_rows(slots):, :].astype(jnp.float32)
    row = lax.broadcasted_iota(jnp.int32, block.shape, 0)

    def column(slot):
        return jnp.sum(jnp.where(row == slot, block, 0.0), axis=0, keepdims=True)

    lent = column(after * (owned + 1) + owned)
    line_of = lax.broadcasted_iota(jnp.int32, (128, half), 0)
    shares = jnp.zeros((128, half), jnp.float32)
    for e in range(owned):
        line = column(me * (owned + 1) + e) + jnp.where(pick == e, lent, 0.0)
        shares = jnp.where(line_of == e, line, shares)
    return shares.T


def evaluate(rows_ref, share_ref, gate_ref, up_ref, down_ref, outs, hidden_ref):
    half, width = outs[0].shape
    owned, _, units = gate_ref.shape
    wide = width // 2 if width % 256 == 0 else width

    def project(e, carry):
        x = rows_ref[...]
        gate = jnp.dot(x, gate_ref[e], preferred_element_type=jnp.float32)
        upper = jnp.dot(x, up_ref[e], preferred_element_type=jnp.float32)
        shares = share_ref[...]
        lane = lax.broadcasted_iota(jnp.int32, shares.shape, 1)
        share = jnp.sum(jnp.where(lane == e, shares, 0.0), axis=1, keepdims=True)
        hidden = gate / (1.0 + jnp.exp(-gate)) * upper * share
        hidden_ref[:, pl.ds(pl.multiple_of(e * units, units), units)] = hidden.astype(jnp.bfloat16)
        return carry

    lax.fori_loop(0, owned, project, 0)

    def fold(j, carry):
        at = pl.ds(pl.multiple_of(j * wide, wide), wide)
        part = jnp.dot(hidden_ref[...], down_ref[:, at], preferred_element_type=jnp.float32)
        for i, out_ref in enumerate(outs):
            out_ref[:, at] = part[i * half:(i + 1) * half].astype(jnp.bfloat16)
        return carry

    lax.fori_loop(0, width // wide, fold, 0)


def cost(rows, w_gate):
    owned, width, units = w_gate.shape
    return pl.CostEstimate(
        flops=6 * rows * width * units * owned, bytes_accessed=8 * rows * width, transcendentals=rows * units * owned
    )


def pair_kernel(slots, count, first, place_ref, *refs):
    chunks = refs[:count]
    gate_ref, up_ref, down_ref = refs[count:count + 3]
    outs = refs[count + 3:count + 5]
    picked_ref, rows_ref, share_ref, hidden_ref, sems = refs[count + 5:]
    owned = gate_ref.shape[0]
    half, width = outs[0].shape
    across = width // half
    for k in range(2):
        for i, chunk in enumerate(chunks):
            @pl.when(place_ref[first + k] == i)
            def _(k=k, chunk=chunk):
                pltpu.make_async_copy(chunk, picked_ref.at[k], sems.at[k]).start()
    for k in range(2):
        pltpu.make_async_copy(chunks[0], picked_ref.at[k], sems.at[k]).wait()
        for i in range(half // 16):
            for j in range(across):
                tile = picked_ref[k, (i * across + j) * 16:(i * across + j) * 16 + 16, :]
                rows_ref[k * half + i * 16:k * half + i * 16 + 16, j * half:(j + 1) * half] = tile
        share_ref[k * half:(k + 1) * half, :] = columns(place_ref, picked_ref.at[k], slots, owned)
    evaluate(rows_ref, share_ref, gate_ref, up_ref, down_ref, outs, hidden_ref)


def pair(place, weights, slots, chunks, first):
    (packed, half), (owned, width, units) = chunks[0].shape, weights[0].shape
    vmem, anywhere = pl.BlockSpec(memory_space=pltpu.VMEM), pl.BlockSpec(memory_space=pl.ANY)
    return pl.pallas_call(
        functools.partial(pair_kernel, slots, len(chunks), first),
        in_specs=[pl.BlockSpec(memory_space=pltpu.SMEM)] + [anywhere] * len(chunks) + [vmem] * 3,
        out_specs=[vmem] * 2,
        out_shape=[jax.ShapeDtypeStruct((half, width), jnp.bfloat16)] * 2,
        scratch_shapes=[
            pltpu.VMEM((2, packed, half), jnp.bfloat16),
            pltpu.VMEM((2 * half, width), jnp.bfloat16),
            pltpu.VMEM((2 * half, 128), jnp.float32),
            pltpu.VMEM((2 * half, owned * units), jnp.bfloat16),
            pltpu.SemaphoreType.DMA((2,)),
        ],
        compiler_params=pltpu.CompilerParams(vmem_limit_bytes=VMEM_LIMIT),
        cost_estimate=cost(2 * half, weights[0]),
    )(place, *chunks, *weights)


def finish_kernel(counts, *refs):
    terms, (out_ref, total_ref, sems) = refs[:-3], refs[-3:]
    half = terms[0].shape[0]
    copies = []
    for i, group in enumerate((terms[:counts[0]], terms[counts[0]:])):
        rows = pl.ds(i * half, half)
        total = sum(ref[...].astype(jnp.float32) for ref in group)
        total_ref[rows, :] = total.astype(total_ref.dtype)
        copies.append(pltpu.make_async_copy(total_ref.at[rows], out_ref.at[rows], sems.at[i]))
        copies[i].start()
    for copy in copies:
        copy.wait()


def finish(a, b):
    half, width = a[0].shape
    return pl.pallas_call(
        functools.partial(finish_kernel, (len(a), len(b))),
        in_specs=[pl.BlockSpec(memory_space=pltpu.VMEM)] * (len(a) + len(b)),
        out_specs=pl.BlockSpec(memory_space=pl.ANY),
        out_shape=jax.ShapeDtypeStruct((2 * half, width), a[0].dtype),
        scratch_shapes=[pltpu.VMEM((2 * half, width), a[0].dtype), pltpu.SemaphoreType.DMA((2,))],
        compiler_params=pltpu.CompilerParams(vmem_limit_bytes=VMEM_LIMIT),
    )(*a, *b)


def add(*terms):
    return sum(term.astype(jnp.float32) for term in terms).astype(jnp.bfloat16)


def ring_gather(own, groups, move, select, back_first):
    walk = ring_order(groups)
    ahead = [(walk[i], walk[(i + 1) % groups]) for i in range(groups)]
    back = [(j, i) for i, j in ahead]
    far = groups // 2
    chains = []
    for pairs, steps in ((ahead, far - back_first), (back, far - 1 + back_first)):
        chain = [own]
        for _ in range(steps):
            chain.append(move(chain[-1], pairs))
        chains.append(chain[1:])
    return [own] + chains[0] + chains[1]


def ring_scatter(parts, groups, move, back_first):
    walk = ring_order(groups)
    ahead = [(walk[i], walk[(i + 1) % groups]) for i in range(groups)]
    back = [(j, i) for i, j in ahead]
    far = groups // 2
    counts = far - back_first, far - 1 + back_first
    sums = [None, None]
    for step in range(far, 0, -1):
        for k, pairs in ((0, back), (1, ahead)):
            if step <= counts[k]:
                part = parts(step if k == 0 else counts[0] + step)
                sums[k] = move(part if sums[k] is None else add(part, sums[k]), pairs)
    return [parts(0)] + sums


def grid_pairs(groups):
    rows, columns = grid_of(groups)
    at = lambda z, x: z * columns + x
    swap = [(at(z, x), at(z, 1 - x)) for z in range(rows) for x in range(columns)]
    end = [(at(z, x), at(z ^ 1, x)) for z in range(rows) for x in range(columns)]
    middle = [(at(z, x), at(rows - 1 - z, x)) for z in (1, 2) for x in range(columns)]
    out = [(at(z, x), at(z ^ 1, x)) for z in (0, 3) for x in range(columns)]
    return swap, end, middle, out, [(j, i) for i, j in out]


def grid_gather(own, groups, move, select):
    swap, end, middle, _, inward = grid_pairs(groups)
    v1, v2, m4 = move(own, swap), move(own, end), move(own, middle)
    m6, m5, v3 = move(v2, middle), move(v1, middle), move(v2, swap)
    v6 = select(m6, move(m6, inward))
    v4 = select(m4, move(m4, inward))
    v5 = select(m5, move(m5, inward))
    v7 = move(v6, swap)
    return [own, v1, v2, v3, v4, v5, v6, v7]


def grid_scatter(parts, groups, move):
    swap, end, middle, outward, _ = grid_pairs(groups)
    s6 = add(parts(6), move(parts(7), swap))
    s6 = add(s6, move(s6, outward))
    s5 = add(parts(5), move(parts(5), outward))
    s4 = add(parts(4), move(parts(4), outward))
    s2 = add(parts(2), move(parts(3), swap), move(s6, middle))
    s1 = add(parts(1), move(s5, middle))
    return [parts(0), move(s4, middle), move(s2, end), move(s1, swap)]


def body(tokens, target, router_weight, replica_pick, w_gate, w_up, w_down):
    width = tokens.shape[1]
    groups = lax.axis_size("expert")
    slots = groups * (w_gate.shape[0] + 1)
    rows, columns_of = grid_of(groups)
    gridded = (rows, columns_of) == (4, 2)
    me = lax.axis_index("expert").astype(jnp.int32)
    inner = (me // columns_of) % (rows - 1) != 0

    def move(value, pairs):
        return lax.ppermute(value, "expert", pairs)

    def select(mine, other):
        return jnp.where(inner, mine, other)

    def move_index(value, pairs):
        result = np.zeros_like(value)
        for i, j in pairs:
            result[j] = value[i]
        return result

    is_inner = np.array([(i // columns_of) % (rows - 1) != 0 for i in range(groups)])
    ring = [functools.partial(ring_gather, back_first=k) for k in range(2)]
    gathers = [ring[0], grid_gather if gridded else ring[1]]
    scatter_maps = [grid_gather if gridded else ring[0], ring[0]]
    scatters = [grid_scatter if gridded else functools.partial(ring_scatter, back_first=0),
                functools.partial(ring_scatter, back_first=0)]
    far = groups // 2
    ring_calls = [(far - i, far + far - 1 - i) for i in range(far - 1)] + [(1, 0)]
    calls = [[(7, 6), (5, 4), (3, 2), (1, 0)] if gridded else ring_calls, ring_calls]

    entries = [np.arange(groups), (np.arange(groups) + 1) % groups, np.zeros(groups, int)]
    plans = []
    for k in range(2):
        owners = [f(np.arange(groups), groups, move_index, lambda a, b: np.where(is_inner, a, b))
                  for f in (gathers[k], scatter_maps[k])]
        plan = {}
        for call in calls[k]:
            held = [[next(i for i in range(groups) if owners[0][i][d] == owners[1][slot][d]) for d in range(groups)]
                    for slot in call]
            used = sorted(set(held[0] + held[1]))
            plan[call] = used, len(entries)
            entries += [np.array([used.index(i) for i in line]) for line in held]
        plans.append(plan)
    table = jnp.asarray(np.stack(entries, axis=1), jnp.int32)
    place = lax.dynamic_index_in_dim(table, me, 0, keepdims=False)
    place = lax.dynamic_update_slice(place, replica_pick, (2,))

    weights = w_gate, w_up, w_down.reshape(-1, width)
    totals = []
    for k, own in enumerate(pack(tokens, target, router_weight, slots)):
        chunks = gathers[k](own, groups, move, select)
        done = {}

        def parts(slot, k=k, chunks=chunks, done=done):
            if slot not in done:
                call = next(c for c in calls[k] if slot in c)
                used, first = plans[k][call]
                done.update(zip(call, pair(place, weights, slots, [chunks[i] for i in used], first)))
            return done[slot]

        totals.append(scatters[k](parts, groups, move))
    return finish(*totals)


def solution(mesh):
    in_specs = (
        P(("dp", "expert"), None),
        P(("dp", "expert"), None),
        P(("dp", "expert"), None),
        P(("dp", "expert")),
        P("expert", None, None),
        P("expert", None, None),
        P("expert", None, None),
    )
    out_specs = P(("dp", "expert"), None)
    return jax.shard_map(body, mesh=mesh, in_specs=in_specs, out_specs=out_specs, check_vma=False)
```

time: 171 us -> 225 us (1.32)
  starting transfers between devices: 29.7 us -> 56.1 us
  waiting for transfers between devices: 76.6 us -> 94.8 us
  Pallas kernels: 51.4 us -> 58 us
    ppermute x28 -> x34, starting transfers between devices: 29.7 us -> 56.1 us  [move(): return lax.ppermute(value, 'expert', pairs)]
    ppermute x28 -> x34, waiting for transfers between devices: 76.6 us -> 94.8 us  [move(): return lax.ppermute(value, 'expert', pairs)]
    pallas_call x10, Pallas kernels: 51.4 us -> 58 us  [the longest x8 55.8 us: pair(): pl.pallas_call(functools.partial(pair_kernel, slots, len(chunks), first),...]
    unnamed x16 -> x22, local copies, waits for them, and re-layouts: 9.76 us -> 11.8 us
  transfers between devices with their start and end apart: 28 -> 34, of which waited for: 18 -> 14; matrix products, arithmetic and copies ran while one was open for 1% -> 1% of each run, Pallas kernels for 29% -> 25%
where the time goes in v5:
time: 225 us; the launch traced here: 224 us
  waiting for transfers between devices  94.8 us (42%)
  Pallas kernels  58 us (26%)
  starting transfers between devices  56.1 us (25%)
  local copies, waits for them, and re-layouts  12.5 us (6%)
    ppermute x34, waiting for transfers between devices, move(): return lax.ppermute(value, 'expert', pairs)  94.8 us
    ppermute x34, starting transfers between devices, move(): return lax.ppermute(value, 'expert', pairs)  56.1 us
    pallas_call x8, Pallas kernels, pair(): pl.pallas_call(functools.partial(pair_kernel, slots, len(chunks), first),...  55.8 us
    unnamed x22, local copies, waits for them, and re-layouts  11.8 us
  transfers between devices with their start and end apart: 34, of which 14 were waited for; matrix products, arithmetic and copies ran while one was open for 1% of the time, Pallas kernels for 25%

profile of v5, /device:TPU:0, one launch (start us, length us, event | category | flops | bytes accessed | tf_op | source)
XLA Modules:
  0.0 224.5 jit_solution(603766212202880368)
XLA Ops:
  3.6 3.0 %collective-permute-start = (bf16[2080,128]{1,0:T(8,128)(2,1)S(1)}, bf16[2080,128]{1,0:T(8,128)(2,1)S(1)}, u32[]{:S(2)}, u32[]{:S(2)}) collective-permute-start(bf16[2080,128]{1,0:T(8,128)(2,1)S(1)} %get-tuple-element.23.refs_0_), channel_id=1, source_target_pairs={{0,2},{2,4},{4,6},{6,7},{7,5},{5,3},{3,1},{1,0},{8,10},{10,12},{12... | collective-permute-start | bytes 1597448 | tf_op jit(solution)/shard_map/ppermute | solution.py:263
  7.4 2.0 collective-permute-start.18
  12.4 7.1 %collective-permute-done.refs_1_.refs_0_ = bf16[2080,128]{1,0:T(8,128)(2,1)S(1)} collective-permute-done((bf16[2080,128]{1,0:T(8,128)(2,1)S(1)}, bf16[2080,128]{1,0:T(8,128)(2,1)S(1)}, u32[]{:S(2)}, u32[]{:S(2)}) %collective-permute-start) | collective-permute-done | bytes 532512 | tf_op jit(solution)/shard_map/ppermute | solution.py:263
  19.5 2.1 collective-permute-start.1
  22.3 10.8 %collective-permute-done.18.refs_2_.refs_1_ = bf16[2080,128]{1,0:T(8,128)(2,1)S(1)} collective-permute-done((bf16[2080,128]{1,0:T(8,128)(2,1)}, bf16[2080,128]{1,0:T(8,128)(2,1)S(1)}, u32[]{:S(2)}, u32[]{:S(2)}) %collective-permute-start.18) | collective-permute-done | bytes 532512 | tf_op jit(solution)/shard_map/ppermute | solution.py:263
  35.9 6.4 %collective-permute-done.1.refs_1_.refs_0_ = bf16[2080,128]{1,0:T(8,128)(2,1)S(1)} collective-permute-done((bf16[2080,128]{1,0:T(8,128)(2,1)S(1)}, bf16[2080,128]{1,0:T(8,128)(2,1)S(1)}, u32[]{:S(2)}, u32[]{:S(2)}) %collective-permute-start.1) | collective-permute-done | bytes 532512 | tf_op jit(solution)/shard_map/ppermute | solution.py:263
  44.5 2.8 %copy-done = bf16[2,2048,768]{2,1,0:T(8,128)(2,1)S(1)} copy-done((bf16[2,2048,768]{2,1,0:T(8,128)(2,1)S(1)}, bf16[2,2048,768]{2,1,0:T(8,128)(2,1)}, u32[]{:S(2)}) %copy-start) | copy-done | bytes 6291480
  47.3 2.8 %copy-done.2 = bf16[2,2048,768]{2,1,0:T(8,128)(2,1)S(1)} copy-done((bf16[2,2048,768]{2,1,0:T(8,128)(2,1)S(1)}, bf16[2,2048,768]{2,1,0:T(8,128)(2,1)}, u32[]{:S(2)}) %copy-start.2) | copy-done | bytes 6291480
  50.1 2.8 %copy-done.4 = bf16[2,768,2048]{2,1,0:T(8,128)(2,1)S(1)} copy-done((bf16[2,768,2048]{2,1,0:T(8,128)(2,1)S(1)}, bf16[2,768,2048]{2,1,0:T(8,128)(2,1)}, u32[]{:S(2)}) %copy-start.4) | copy-done | bytes 6291480
  52.9 6.8 %shard_map.85 = (bf16[128,2048]{1,0:T(8,128)(2,1)S(1)}, bf16[128,2048]{1,0:T(8,128)(2,1)S(1)}) custom-call(s32[19]{0:T(128)S(1)} %constant_dynamic-update-slice_fusion.place_ref, bf16[2080,128]{1,0:T(8,128)(2,1)S(1)} %collective-permute-done.refs_1_.refs_0_, bf16[2080,128]{1,0:T(8,128)(2,1)S(1)} %collective-permute-done.1.refs_1_.refs_0_, ...), custom_call_target="tpu_custom_call" | custom-call | flops 4831838208 | bytes 4194304 | tf_op jit(solution)/shard_map/pallas_call | solution.py:145
  60.3 3.2 %collective-permute-start.2 = (bf16[2080,128]{1,0:T(8,128)(2,1)S(1)}, bf16[2080,128]{1,0:T(8,128)(2,1)S(1)}, u32[]{:S(2)}, u32[]{:S(2)}) collective-permute-start(bf16[2080,128]{1,0:T(8,128)(2,1)S(1)} %collective-permute-done.1.refs_1_.refs_0_), channel_id=1, source_target_pairs={{0,2},{2,4},{4,6},{6,7},{7,5},{5,3},{3,1},{1,0},{8,10},{10,12},{12... | collective-permute-start | bytes 1597448 | tf_op jit(solution)/shard_map/ppermute | solution.py:263
  64.9 7.6 %shard_map.87 = (bf16[128,2048]{1,0:T(8,128)(2,1)S(1)}, bf16[128,2048]{1,0:T(8,128)(2,1)S(1)}) custom-call(s32[19]{0:T(128)S(1)} %constant_dynamic-update-slice_fusion.place_ref, bf16[2080,128]{1,0:T(8,128)(2,1)} %get-tuple-element.32.refs_0_, bf16[2080,128]{1,0:T(8,128)(2,1)S(1)} %collective-permute-done.17.refs_1_.refs_0_, ...), custom_call_target="tpu_custom_call" | custom-call | flops 4831838208 | bytes 4194304 | tf_op jit(solution)/shard_map/pallas_call | solution.py:145
  72.6 7.4 %collective-permute-done.23 = bf16[2080,128]{1,0:T(8,128)(2,1)S(1)} collective-permute-done((bf16[2080,128]{1,0:T(8,128)(2,1)S(1)}, bf16[2080,128]{1,0:T(8,128)(2,1)S(1)}, u32[]{:S(2)}, u32[]{:S(2)}) %collective-permute-start.23) | collective-permute-done | bytes 532512 | tf_op jit(solution)/shard_map/ppermute | solution.py:263
  81.4 19.0 %collective-permute-done.25 = bf16[2080,128]{1,0:T(8,128)(2,1)S(1)} collective-permute-done((bf16[2080,128]{1,0:T(8,128)(2,1)S(1)}, bf16[2080,128]{1,0:T(8,128)(2,1)S(1)}, u32[]{:S(2)}, u32[]{:S(2)}) %collective-permute-start.25) | collective-permute-done | bytes 532512 | tf_op jit(solution)/shard_map/ppermute | solution.py:263
  100.5 6.8 %shard_map.88 = (bf16[128,2048]{1,0:T(8,128)(2,1)S(1)}, bf16[128,2048]{1,0:T(8,128)(2,1)S(1)}) custom-call(s32[19]{0:T(128)S(1)} %constant_dynamic-update-slice_fusion.place_ref, bf16[2080,128]{1,0:T(8,128)(2,1)S(1)} %collective-permute-done.17.refs_1_.refs_0_, bf16[2080,128]{1,0:T(8,128)(2,1)S(1)} %collective-permute-done.18.refs_2_.refs_1_, ...), custom_call_target="tpu_custom_call" | custom-call | flops 4831838208 | bytes 4194304 | tf_op jit(solution)/shard_map/pallas_call | solution.py:145
  107.4 7.0 %shard_map.83 = (bf16[128,2048]{1,0:T(8,128)(2,1)S(1)}, bf16[128,2048]{1,0:T(8,128)(2,1)S(1)}) custom-call(s32[19]{0:T(128)S(1)} %constant_dynamic-update-slice_fusion.place_ref, bf16[2080,128]{1,0:T(8,128)(2,1)S(1)} %copy-done.8, bf16[2080,128]{1,0:T(8,128)(2,1)S(1)} %collective-permute-done.refs_1_.refs_0_, ...), custom_call_target="tpu_custom_call" | custom-call | flops 4831838208 | bytes 4194304 | tf_op jit(solution)/shard_map/pallas_call | solution.py:145
  115.4 6.8 %shard_map.90 = (bf16[128,2048]{1,0:T(8,128)(2,1)S(1)}, bf16[128,2048]{1,0:T(8,128)(2,1)S(1)}) custom-call(s32[19]{0:T(128)S(1)} %constant_dynamic-update-slice_fusion.place_ref, bf16[2080,128]{1,0:T(8,128)(2,1)S(1)} %collective-permute-done.17.refs_1_.refs_0_, bf16[2080,128]{1,0:T(8,128)(2,1)S(1)} %broadcast_select_fusion.refs_3_.refs_1_, ...), custom_call_target="tpu_custom_call" | custom-call | flops 4831838208 | bytes 4194304 | tf_op jit(solution)/shard_map/pallas_call | solution.py:145
  122.3 2.0 collective-permute-start.27
  125.2 6.9 %shard_map.84 = (bf16[128,2048]{1,0:T(8,128)(2,1)S(1)}, bf16[128,2048]{1,0:T(8,128)(2,1)S(1)}) custom-call(s32[19]{0:T(128)S(1)} %constant_dynamic-update-slice_fusion.place_ref, bf16[2080,128]{1,0:T(8,128)(2,1)S(1)} %collective-permute-done.refs_1_.refs_0_, bf16[2080,128]{1,0:T(8,128)(2,1)S(1)} %collective-permute-done.1.refs_1_.refs_0_, ...), custom_call_target="tpu_custom_call" | custom-call | flops 4831838208 | bytes 4194304 | tf_op jit(solution)/shard_map/pallas_call | solution.py:145
  133.4 6.8 %shard_map.86 = (bf16[128,2048]{1,0:T(8,128)(2,1)S(1)}, bf16[128,2048]{1,0:T(8,128)(2,1)S(1)}) custom-call(s32[19]{0:T(128)S(1)} %constant_dynamic-update-slice_fusion.place_ref, bf16[2080,128]{1,0:T(8,128)(2,1)S(1)} %collective-permute-done.1.refs_1_.refs_0_, bf16[2080,128]{1,0:T(8,128)(2,1)S(1)} %collective-permute-done.2.refs_2_.refs_1_, ...), custom_call_target="tpu_custom_call" | custom-call | flops 4831838208 | bytes 4194304 | tf_op jit(solution)/shard_map/pallas_call | solution.py:145
  140.3 2.8 %collective-permute-start.10 = (bf16[128,2048]{1,0:T(8,128)(2,1)S(1)}, bf16[128,2048]{1,0:T(8,128)(2,1)S(1)}, u32[]{:S(2)}, u32[]{:S(2)}) collective-permute-start(bf16[128,2048]{1,0:T(8,128)(2,1)S(1)} %get-tuple-element.29), channel_id=1, source_target_pairs={{0,1},{1,0},{2,3},{3,2},{4,5},{5,4},{6,7},{7,6},{8,9},{9,8},{10,11... | collective-permute-start | bytes 1572872 | tf_op jit(solution)/shard_map/ppermute | solution.py:263
  143.1 7.1 %shard_map.89 = (bf16[128,2048]{1,0:T(8,128)(2,1)S(1)}, bf16[128,2048]{1,0:T(8,128)(2,1)S(1)}) custom-call(s32[19]{0:T(128)S(1)} %constant_dynamic-update-slice_fusion.place_ref, bf16[2080,128]{1,0:T(8,128)(2,1)S(1)} %collective-permute-done.17.refs_1_.refs_0_, bf16[2080,128]{1,0:T(8,128)(2,1)S(1)} %collective-permute-done.21.refs_2_.refs_1_, ...), custom_call_target="tpu_custom_call" | custom-call | flops 4831838208 | bytes 4194304 | tf_op jit(solution)/shard_map/pallas_call | solution.py:145
  151.8 2.1 collective-permute-start.28
  154.9 8.9 %collective-permute-done.7 = bf16[128,2048]{1,0:T(8,128)(2,1)S(1)} collective-permute-done((bf16[128,2048]{1,0:T(8,128)(2,1)S(1)}, bf16[128,2048]{1,0:T(8,128)(2,1)S(1)}, u32[]{:S(2)}, u32[]{:S(2)}) %collective-permute-start.7) | collective-permute-done | bytes 524320 | tf_op jit(solution)/shard_map/ppermute | solution.py:263
  163.8 4.4 %collective-permute-start.11 = (bf16[128,2048]{1,0:T(8,128)(2,1)S(1)}, bf16[128,2048]{1,0:T(8,128)(2,1)S(1)}, u32[]{:S(2)}, u32[]{:S(2)}) collective-permute-start(bf16[128,2048]{1,0:T(8,128)(2,1)S(1)} %add_convert_fusion.9), channel_id=1, source_target_pairs={{0,2},{1,3},{6,4},{7,5},{8,10},{9,11},{14,12},{15,13},{16,18},{17,... | collective-permute-start | bytes 1572872 | tf_op jit(solution)/shard_map/ppermute | solution.py:263
  168.4 6.7 %collective-permute-done.32 = bf16[128,2048]{1,0:T(8,128)(2,1)S(1)} collective-permute-done((bf16[128,2048]{1,0:T(8,128)(2,1)S(1)}, bf16[128,2048]{1,0:T(8,128)(2,1)S(1)}, u32[]{:S(2)}, u32[]{:S(2)}) %collective-permute-start.32) | collective-permute-done | bytes 524320 | tf_op jit(solution)/shard_map/ppermute | solution.py:263
  175.9 3.8 %collective-permute-start.33 = (bf16[128,2048]{1,0:T(8,128)(2,1)S(1)}, bf16[128,2048]{1,0:T(8,128)(2,1)S(1)}, u32[]{:S(2)}, u32[]{:S(2)}) collective-permute-start(bf16[128,2048]{1,0:T(8,128)(2,1)S(1)} %add_convert_fusion), channel_id=1, source_target_pairs={{0,2},{2,4},{4,6},{6,7},{7,5},{5,3},{3,1},{1,0},{8,10},{10,12},{12... | collective-permute-start | bytes 1572872 | tf_op jit(solution)/shard_map/ppermute | solution.py:263
  179.8 6.5 %collective-permute-done.11 = bf16[128,2048]{1,0:T(8,128)(2,1)S(1)} collective-permute-done((bf16[128,2048]{1,0:T(8,128)(2,1)S(1)}, bf16[128,2048]{1,0:T(8,128)(2,1)S(1)}, u32[]{:S(2)}, u32[]{:S(2)}) %collective-permute-start.11) | collective-permute-done | bytes 524320 | tf_op jit(solution)/shard_map/ppermute | solution.py:263
  187.3 11.4 %collective-permute-done.29 = bf16[128,2048]{1,0:T(8,128)(2,1)S(1)} collective-permute-done((bf16[128,2048]{1,0:T(8,128)(2,1)S(1)}, bf16[128,2048]{1,0:T(8,128)(2,1)S(1)}, u32[]{:S(2)}, u32[]{:S(2)}) %collective-permute-start.29) | collective-permute-done | bytes 524320 | tf_op jit(solution)/shard_map/ppermute | solution.py:263
  198.6 2.1 collective-permute-start.16
  201.2 14.7 %collective-permute-start.13 = (bf16[128,2048]{1,0:T(8,128)(2,1)S(1)}, bf16[128,2048]{1,0:T(8,128)(2,1)S(1)}, u32[]{:S(2)}, u32[]{:S(2)}) collective-permute-start(bf16[128,2048]{1,0:T(8,128)(2,1)S(1)} %add_convert_fusion.7), channel_id=1, source_target_pairs={{0,2},{1,3},{2,0},{3,1},{4,6},{5,7},{6,4},{7,5},{8,10},{9,11},{10,... | collective-permute-start | bytes 1572872 | tf_op jit(solution)/shard_map/ppermute | solution.py:263
  215.9 7.1 %collective-permute-done.13.refs_2_ = bf16[128,2048]{1,0:T(8,128)(2,1)S(1)} collective-permute-done((bf16[128,2048]{1,0:T(8,128)(2,1)S(1)}, bf16[128,2048]{1,0:T(8,128)(2,1)S(1)}, u32[]{:S(2)}, u32[]{:S(2)}) %collective-permute-start.13) | collective-permute-done | bytes 524320 | tf_op jit(solution)/shard_map/ppermute | solution.py:263
  (84 shorter events, 25.5 us)
Async XLA Ops:
  3.6 15.9 %collective-permute-start = (bf16[2080,128]{1,0:T(8,128)(2,1)S(1)}, bf16[2080,128]{1,0:T(8,128)(2,1)S(1)}, u32[]{:S(2)}, u32[]{:S(2)}) collective-permute-start(bf16[2080,128]{1,0:T(8,128)(2,1)S(1)} %get-tuple-element.23.refs_0_), channel_id=1, source_target_pairs={{0,2},{2,4},{4,6},{6,7},{7,5},{5,3},{3,1},{1,0},{8,10},{10,12},{12... | collective-permute-start | bytes 1597448 | tf_op jit(solution)/shard_map/ppermute | solution.py:263
  6.6 15.0 %collective-permute-start.3 = (bf16[2080,128]{1,0:T(8,128)(2,1)S(1)}, bf16[2080,128]{1,0:T(8,128)(2,1)S(1)}, u32[]{:S(2)}, u32[]{:S(2)}) collective-permute-start(bf16[2080,128]{1,0:T(8,128)(2,1)S(1)} %get-tuple-element.23.refs_0_), channel_id=1, source_target_pairs={{2,0},{4,2},{6,4},{7,6},{5,7},{3,5},{1,3},{0,1},{10,8},{12,10},{14... | collective-permute-start | bytes 1597448 | tf_op jit(solution)/shard_map/ppermute | solution.py:263
  7.4 25.6 %collective-permute-start.18 = (bf16[2080,128]{1,0:T(8,128)(2,1)}, bf16[2080,128]{1,0:T(8,128)(2,1)S(1)}, u32[]{:S(2)}, u32[]{:S(2)}) collective-permute-start(bf16[2080,128]{1,0:T(8,128)(2,1)} %get-tuple-element.32.refs_0_), channel_id=1, source_target_pairs={{0,2},{1,3},{2,0},{3,1},{4,6},{5,7},{6,4},{7,5},{8,10},{9,11},{10,... | collective-permute-start | bytes 1597448 | tf_op jit(solution)/shard_map/ppermute | solution.py:263
  9.5 24.3 %collective-permute-start.19 = (bf16[2080,128]{1,0:T(8,128)(2,1)}, bf16[2080,128]{1,0:T(8,128)(2,1)}, u32[]{:S(2)}, u32[]{:S(2)}) collective-permute-start(bf16[2080,128]{1,0:T(8,128)(2,1)} %get-tuple-element.32.refs_0_), channel_id=1, source_target_pairs={{2,4},{3,5},{4,2},{5,3},{10,12},{11,13},{12,10},{13,11},{18,20},{1... | collective-permute-start | bytes 1597448 | tf_op jit(solution)/shard_map/ppermute | solution.py:263
  10.9 24.9 %collective-permute-start.17 = (bf16[2080,128]{1,0:T(8,128)(2,1)}, bf16[2080,128]{1,0:T(8,128)(2,1)S(1)}, u32[]{:S(2)}, u32[]{:S(2)}) collective-permute-start(bf16[2080,128]{1,0:T(8,128)(2,1)} %get-tuple-element.32.refs_0_), channel_id=1, source_target_pairs={{0,1},{1,0},{2,3},{3,2},{4,5},{5,4},{6,7},{7,6},{8,9},{9,8},{10,11... | collective-permute-start | bytes 1597448 | tf_op jit(solution)/shard_map/ppermute | solution.py:263
  19.5 22.8 %collective-permute-start.1 = (bf16[2080,128]{1,0:T(8,128)(2,1)S(1)}, bf16[2080,128]{1,0:T(8,128)(2,1)S(1)}, u32[]{:S(2)}, u32[]{:S(2)}) collective-permute-start(bf16[2080,128]{1,0:T(8,128)(2,1)S(1)} %collective-permute-done.refs_1_.refs_0_), channel_id=1, source_target_pairs={{0,2},{2,4},{4,6},{6,7},{7,5},{5,3},{3,1},{1,0},{8,10},{10,12},{12... | collective-permute-start | bytes 1597448 | tf_op jit(solution)/shard_map/ppermute | solution.py:263
  21.7 22.8 %collective-permute-start.4 = (bf16[2080,128]{1,0:T(8,128)(2,1)S(1)}, bf16[2080,128]{1,0:T(8,128)(2,1)S(1)}, u32[]{:S(2)}, u32[]{:S(2)}) collective-permute-start(bf16[2080,128]{1,0:T(8,128)(2,1)S(1)} %collective-permute-done.3.refs_3_.refs_4_.refs_2_), channel_id=1, source_target_pairs={{2,0},{4,2},{6,4},{7,6},{5,7},{3,5},{1,3},{0,1},{10,8},{12,10},{14... | collective-permute-start | bytes 1597448 | tf_op jit(solution)/shard_map/ppermute | solution.py:263
  33.1 27.2 %collective-permute-start.22 = (bf16[2080,128]{1,0:T(8,128)(2,1)S(1)}, bf16[2080,128]{1,0:T(8,128)(2,1)S(1)}, u32[]{:S(2)}, u32[]{:S(2)}) collective-permute-start(bf16[2080,128]{1,0:T(8,128)(2,1)S(1)} %collective-permute-done.18.refs_2_.refs_1_), channel_id=1, source_target_pairs={{2,4},{3,5},{4,2},{5,3},{10,12},{11,13},{12,10},{13,11},{18,20},{1... | collective-permute-start | bytes 1597448 | tf_op jit(solution)/shard_map/ppermute | solution.py:263
  33.8 29.7 %collective-permute-start.20 = (bf16[2080,128]{1,0:T(8,128)(2,1)}, bf16[2080,128]{1,0:T(8,128)(2,1)S(1)}, u32[]{:S(2)}, u32[]{:S(2)}) collective-permute-start(bf16[2080,128]{1,0:T(8,128)(2,1)} %collective-permute-done.19), channel_id=1, source_target_pairs={{2,0},{3,1},{4,6},{5,7},{10,8},{11,9},{12,14},{13,15},{18,16},{19,... | collective-permute-start | bytes 1597448 | tf_op jit(solution)/shard_map/ppermute | solution.py:263
  35.8 64.7 %collective-permute-start.21 = (bf16[2080,128]{1,0:T(8,128)(2,1)S(1)}, bf16[2080,128]{1,0:T(8,128)(2,1)S(1)}, u32[]{:S(2)}, u32[]{:S(2)}) collective-permute-start(bf16[2080,128]{1,0:T(8,128)(2,1)S(1)} %collective-permute-done.18.refs_2_.refs_1_), channel_id=1, source_target_pairs={{0,1},{1,0},{2,3},{3,2},{4,5},{5,4},{6,7},{7,6},{8,9},{9,8},{10,11... | collective-permute-start | bytes 1597448 | tf_op jit(solution)/shard_map/ppermute | solution.py:263
  42.3 30.2 %collective-permute-start.24 = (bf16[2080,128]{1,0:T(8,128)(2,1)S(1)}, bf16[2080,128]{1,0:T(8,128)(2,1)S(1)}, u32[]{:S(2)}, u32[]{:S(2)}) collective-permute-start(bf16[2080,128]{1,0:T(8,128)(2,1)S(1)} %collective-permute-done.17.refs_1_.refs_0_), channel_id=1, source_target_pairs={{2,4},{3,5},{4,2},{5,3},{10,12},{11,13},{12,10},{13,11},{18,20},{1... | collective-permute-start | bytes 1597448 | tf_op jit(solution)/shard_map/ppermute | solution.py:263
  59.7 141.1 %collective-permute-start.9 = (bf16[128,2048]{1,0:T(8,128)(2,1)S(1)}, bf16[128,2048]{1,0:T(8,128)(2,1)S(1)}, u32[]{:S(2)}, u32[]{:S(2)}) collective-permute-start(bf16[128,2048]{1,0:T(8,128)(2,1)S(1)} %get-tuple-element.27), channel_id=1, source_target_pairs={{0,1},{1,0},{2,3},{3,2},{4,5},{5,4},{6,7},{7,6},{8,9},{9,8},{10,11... | collective-permute-start | bytes 1572872 | tf_op jit(solution)/shard_map/ppermute | solution.py:263
  60.3 47.0 %collective-permute-start.2 = (bf16[2080,128]{1,0:T(8,128)(2,1)S(1)}, bf16[2080,128]{1,0:T(8,128)(2,1)S(1)}, u32[]{:S(2)}, u32[]{:S(2)}) collective-permute-start(bf16[2080,128]{1,0:T(8,128)(2,1)S(1)} %collective-permute-done.1.refs_1_.refs_0_), channel_id=1, source_target_pairs={{0,2},{2,4},{4,6},{6,7},{7,5},{5,3},{3,1},{1,0},{8,10},{10,12},{12... | collective-permute-start | bytes 1597448 | tf_op jit(solution)/shard_map/ppermute | solution.py:263
  63.5 16.5 %collective-permute-start.23 = (bf16[2080,128]{1,0:T(8,128)(2,1)S(1)}, bf16[2080,128]{1,0:T(8,128)(2,1)S(1)}, u32[]{:S(2)}, u32[]{:S(2)}) collective-permute-start(bf16[2080,128]{1,0:T(8,128)(2,1)S(1)} %collective-permute-done.22), channel_id=1, source_target_pairs={{2,0},{3,1},{4,6},{5,7},{10,8},{11,9},{12,14},{13,15},{18,16},{19,... | collective-permute-start | bytes 1597448 | tf_op jit(solution)/shard_map/ppermute | solution.py:263
  72.5 34.9 %collective-permute-start.5 = (bf16[2080,128]{1,0:T(8,128)(2,1)S(1)}, bf16[2080,128]{1,0:T(8,128)(2,1)S(1)}, u32[]{:S(2)}, u32[]{:S(2)}) collective-permute-start(bf16[2080,128]{1,0:T(8,128)(2,1)S(1)} %collective-permute-done.4.refs_5_.refs_3_), channel_id=1, source_target_pairs={{2,0},{4,2},{6,4},{7,6},{5,7},{3,5},{1,3},{0,1},{10,8},{12,10},{14... | collective-permute-start | bytes 1597448 | tf_op jit(solution)/shard_map/ppermute | solution.py:263
  80.0 20.3 %collective-permute-start.25 = (bf16[2080,128]{1,0:T(8,128)(2,1)S(1)}, bf16[2080,128]{1,0:T(8,128)(2,1)S(1)}, u32[]{:S(2)}, u32[]{:S(2)}) collective-permute-start(bf16[2080,128]{1,0:T(8,128)(2,1)S(1)} %collective-permute-done.24), channel_id=1, source_target_pairs={{2,0},{3,1},{4,6},{5,7},{10,8},{11,9},{12,14},{13,15},{18,16},{19,... | collective-permute-start | bytes 1597448 | tf_op jit(solution)/shard_map/ppermute | solution.py:263
  100.4 15.0 %collective-permute-start.26 = (bf16[2080,128]{1,0:T(8,128)(2,1)S(1)}, bf16[2080,128]{1,0:T(8,128)(2,1)S(1)}, u32[]{:S(2)}, u32[]{:S(2)}) collective-permute-start(bf16[2080,128]{1,0:T(8,128)(2,1)S(1)} %broadcast_select_fusion.1.refs_4_.refs_2_), channel_id=1, source_target_pairs={{0,1},{1,0},{2,3},{3,2},{4,5},{5,4},{6,7},{7,6},{8,9},{9,8},{10,11... | collective-permute-start | bytes 1597448 | tf_op jit(solution)/shard_map/ppermute | solution.py:263
  107.3 17.9 %collective-permute-start.6 = (bf16[2080,128]{1,0:T(8,128)(2,1)S(1)}, bf16[2080,128]{1,0:T(8,128)(2,1)S(1)}, u32[]{:S(2)}, u32[]{:S(2)}) collective-permute-start(bf16[2080,128]{1,0:T(8,128)(2,1)S(1)} %collective-permute-done.2.refs_2_.refs_1_), channel_id=1, source_target_pairs={{0,2},{2,4},{4,6},{6,7},{7,5},{5,3},{3,1},{1,0},{8,10},{10,12},{12... | collective-permute-start | bytes 1597448 | tf_op jit(solution)/shard_map/ppermute | solution.py:263
  122.2 27.9 %collective-permute-start.31 = (bf16[128,2048]{1,0:T(8,128)(2,1)S(1)}, bf16[128,2048]{1,0:T(8,128)(2,1)S(1)}, u32[]{:S(2)}, u32[]{:S(2)}) collective-permute-start(bf16[128,2048]{1,0:T(8,128)(2,1)S(1)} %get-tuple-element.40), channel_id=1, source_target_pairs={{0,2},{2,4},{4,6},{6,7},{7,5},{5,3},{3,1},{1,0},{8,10},{10,12},{12... | collective-permute-start | bytes 1572872 | tf_op jit(solution)/shard_map/ppermute | solution.py:263
  122.3 29.3 %collective-permute-start.27 = (bf16[128,2048]{1,0:T(8,128)(2,1)S(1)}, bf16[128,2048]{1,0:T(8,128)(2,1)S(1)}, u32[]{:S(2)}, u32[]{:S(2)}) collective-permute-start(bf16[128,2048]{1,0:T(8,128)(2,1)S(1)} %get-tuple-element.37), channel_id=1, source_target_pairs={{2,0},{4,2},{6,4},{7,6},{5,7},{3,5},{1,3},{0,1},{10,8},{12,10},{14... | collective-permute-start | bytes 1572872 | tf_op jit(solution)/shard_map/ppermute | solution.py:263
  132.1 19.7 %collective-permute-start.14 = (bf16[128,2048]{1,0:T(8,128)(2,1)S(1)}, bf16[128,2048]{1,0:T(8,128)(2,1)S(1)}, u32[]{:S(2)}, u32[]{:S(2)}) collective-permute-start(bf16[128,2048]{1,0:T(8,128)(2,1)S(1)} %get-tuple-element.31), channel_id=1, source_target_pairs={{0,2},{1,3},{6,4},{7,5},{8,10},{9,11},{14,12},{15,13},{16,18},{17,... | collective-permute-start | bytes 1572872 | tf_op jit(solution)/shard_map/ppermute | solution.py:263
  140.3 13.8 %collective-permute-start.10 = (bf16[128,2048]{1,0:T(8,128)(2,1)S(1)}, bf16[128,2048]{1,0:T(8,128)(2,1)S(1)}, u32[]{:S(2)}, u32[]{:S(2)}) collective-permute-start(bf16[128,2048]{1,0:T(8,128)(2,1)S(1)} %get-tuple-element.29), channel_id=1, source_target_pairs={{0,1},{1,0},{2,3},{3,2},{4,5},{5,4},{6,7},{7,6},{8,9},{9,8},{10,11... | collective-permute-start | bytes 1572872 | tf_op jit(solution)/shard_map/ppermute | solution.py:263
  151.6 23.4 %collective-permute-start.32 = (bf16[128,2048]{1,0:T(8,128)(2,1)S(1)}, bf16[128,2048]{1,0:T(8,128)(2,1)S(1)}, u32[]{:S(2)}, u32[]{:S(2)}) collective-permute-start(bf16[128,2048]{1,0:T(8,128)(2,1)S(1)} %add_convert_fusion.1), channel_id=1, source_target_pairs={{0,2},{2,4},{4,6},{6,7},{7,5},{5,3},{3,1},{1,0},{8,10},{10,12},{12... | collective-permute-start | bytes 1572872 | tf_op jit(solution)/shard_map/ppermute | solution.py:263
  151.8 24.0 %collective-permute-start.28 = (bf16[128,2048]{1,0:T(8,128)(2,1)S(1)}, bf16[128,2048]{1,0:T(8,128)(2,1)S(1)}, u32[]{:S(2)}, u32[]{:S(2)}) collective-permute-start(bf16[128,2048]{1,0:T(8,128)(2,1)S(1)} %add_convert_fusion.4), channel_id=1, source_target_pairs={{2,0},{4,2},{6,4},{7,6},{5,7},{3,5},{1,3},{0,1},{10,8},{12,10},{14... | collective-permute-start | bytes 1572872 | tf_op jit(solution)/shard_map/ppermute | solution.py:263
  154.1 32.4 %collective-permute-start.15 = (bf16[128,2048]{1,0:T(8,128)(2,1)S(1)}, bf16[128,2048]{1,0:T(8,128)(2,1)S(1)}, u32[]{:S(2)}, u32[]{:S(2)}) collective-permute-start(bf16[128,2048]{1,0:T(8,128)(2,1)S(1)} %add_convert_fusion.6), channel_id=1, source_target_pairs={{2,4},{3,5},{4,2},{5,3},{10,12},{11,13},{12,10},{13,11},{18,20},{1... | collective-permute-start | bytes 1572872 | tf_op jit(solution)/shard_map/ppermute | solution.py:263
  163.8 22.5 %collective-permute-start.11 = (bf16[128,2048]{1,0:T(8,128)(2,1)S(1)}, bf16[128,2048]{1,0:T(8,128)(2,1)S(1)}, u32[]{:S(2)}, u32[]{:S(2)}) collective-permute-start(bf16[128,2048]{1,0:T(8,128)(2,1)S(1)} %add_convert_fusion.9), channel_id=1, source_target_pairs={{0,2},{1,3},{6,4},{7,5},{8,10},{9,11},{14,12},{15,13},{16,18},{17,... | collective-permute-start | bytes 1572872 | tf_op jit(solution)/shard_map/ppermute | solution.py:263
  175.0 40.8 %collective-permute-start.8 = (bf16[128,2048]{1,0:T(8,128)(2,1)S(1)}, bf16[128,2048]{1,0:T(8,128)(2,1)S(1)}, u32[]{:S(2)}, u32[]{:S(2)}) collective-permute-start(bf16[128,2048]{1,0:T(8,128)(2,1)S(1)} %add_convert_fusion.10), channel_id=1, source_target_pairs={{2,4},{3,5},{4,2},{5,3},{10,12},{11,13},{12,10},{13,11},{18,20},{1... | collective-permute-start | bytes 1572872 | tf_op jit(solution)/shard_map/ppermute | solution.py:263
  175.9 40.0 %collective-permute-start.33 = (bf16[128,2048]{1,0:T(8,128)(2,1)S(1)}, bf16[128,2048]{1,0:T(8,128)(2,1)S(1)}, u32[]{:S(2)}, u32[]{:S(2)}) collective-permute-start(bf16[128,2048]{1,0:T(8,128)(2,1)S(1)} %add_convert_fusion), channel_id=1, source_target_pairs={{0,2},{2,4},{4,6},{6,7},{7,5},{5,3},{3,1},{1,0},{8,10},{10,12},{12... | collective-permute-start | bytes 1572872 | tf_op jit(solution)/shard_map/ppermute | solution.py:263
  186.4 14.5 %collective-permute-start.12 = (bf16[128,2048]{1,0:T(8,128)(2,1)S(1)}, bf16[128,2048]{1,0:T(8,128)(2,1)S(1)}, u32[]{:S(2)}, u32[]{:S(2)}) collective-permute-start(bf16[128,2048]{1,0:T(8,128)(2,1)S(1)} %add_convert_fusion.8), channel_id=1, source_target_pairs={{2,4},{3,5},{4,2},{5,3},{10,12},{11,13},{12,10},{13,11},{18,20},{1... | collective-permute-start | bytes 1572872 | tf_op jit(solution)/shard_map/ppermute | solution.py:263
  198.6 17.3 %collective-permute-start.16 = (bf16[128,2048]{1,0:T(8,128)(2,1)S(1)}, bf16[128,2048]{1,0:T(8,128)(2,1)S(1)}, u32[]{:S(2)}, u32[]{:S(2)}) collective-permute-start(bf16[128,2048]{1,0:T(8,128)(2,1)S(1)} %add_convert_fusion.5), channel_id=1, source_target_pairs={{0,1},{1,0},{2,3},{3,2},{4,5},{5,4},{6,7},{7,6},{8,9},{9,8},{10,11... | collective-permute-start | bytes 1572872 | tf_op jit(solution)/shard_map/ppermute | solution.py:263
  200.8 15.1 %collective-permute-start.30 = (bf16[128,2048]{1,0:T(8,128)(2,1)S(1)}, bf16[128,2048]{1,0:T(8,128)(2,1)S(1)}, u32[]{:S(2)}, u32[]{:S(2)}) collective-permute-start(bf16[128,2048]{1,0:T(8,128)(2,1)S(1)} %add_convert_fusion.2), channel_id=1, source_target_pairs={{2,0},{4,2},{6,4},{7,6},{5,7},{3,5},{1,3},{0,1},{10,8},{12,10},{14... | collective-permute-start | bytes 1572872 | tf_op jit(solution)/shard_map/ppermute | solution.py:263
  201.2 21.9 %collective-permute-start.13 = (bf16[128,2048]{1,0:T(8,128)(2,1)S(1)}, bf16[128,2048]{1,0:T(8,128)(2,1)S(1)}, u32[]{:S(2)}, u32[]{:S(2)}) collective-permute-start(bf16[128,2048]{1,0:T(8,128)(2,1)S(1)} %add_convert_fusion.7), channel_id=1, source_target_pairs={{0,2},{1,3},{2,0},{3,1},{4,6},{5,7},{6,4},{7,5},{8,10},{9,11},{10,... | collective-permute-start | bytes 1572872 | tf_op jit(solution)/shard_map/ppermute | solution.py:263
  (13 other events, 81.0 us)

commit v6 on v4

--- a/solution.py
+++ b/solution.py
@@ -123,10 +123,7 @@
     evaluate(rows_ref, share_ref, gate_ref, up_ref, down_ref, (out_a_ref, out_b_ref), hidden_ref)
 
 
-def plain_kernel(b_ref, a_ref, share_ref, gate_ref, up_ref, down_ref, out_b_ref, out_a_ref, same_b_ref, same_a_ref,
-                 rows_ref, hidden_ref):
-    same_b_ref[...] = b_ref[...]
-    same_a_ref[...] = a_ref[...]
+def plain_kernel(b_ref, a_ref, share_ref, gate_ref, up_ref, down_ref, out_b_ref, out_a_ref, rows_ref, hidden_ref):
     half = b_ref.shape[0]
     rows_ref[:half, :] = b_ref[...]
     rows_ref[half:, :] = a_ref[...]
@@ -166,8 +163,8 @@
     return pl.pallas_call(
         plain_kernel,
         in_specs=[vmem] * 6,
-        out_specs=[vmem] * 4,
-        out_shape=[jax.ShapeDtypeStruct((half, width), jnp.bfloat16)] * 4,
+        out_specs=[vmem] * 2,
+        out_shape=[jax.ShapeDtypeStruct((half, width), jnp.bfloat16)] * 2,
         scratch_shapes=[
             pltpu.VMEM((2 * half, width), jnp.bfloat16),
             pltpu.VMEM((2 * half, owned * units), jnp.bfloat16),
@@ -201,6 +198,10 @@
         scratch_shapes=[pltpu.VMEM((2 * half, width), a[0].dtype), pltpu.SemaphoreType.DMA((2,))],
         compiler_params=pltpu.CompilerParams(vmem_limit_bytes=VMEM_LIMIT),
     )(*a, *b)
+
+
+def after_all(*values):
+    return lax.optimization_barrier(values)
 
 
 def add(a, b):
@@ -224,17 +225,16 @@
     a, b = tokens[:half], tokens[half:]
     lead_a, lead_b = pack(a, b, target, router_weight, slots)
     run = functools.partial(lead, place, weights, slots)
-    own_a, own_b, shares = run(lead_a, lead_b)
-    earlier = (shares,)
+    own_a, own_b, ended = run(lead_a, lead_b)
     parts = {}
     for s in range(1, far):
-        lead_a = lax.ppermute(lead_a, "expert", ahead)
-        lead_b = lax.ppermute(lead_b, "expert", back)
-        b = lax.ppermute(b, "expert", ahead)
-        a = lax.ppermute(a, "expert", back)
-        lead_part_a, lead_part_b, shares = run(lead_a, lead_b, earlier)
-        part_b, part_a, b, a = plain(weights, b, a, shares)
-        earlier = ()
+        b, a = lax.ppermute(b, "expert", ahead), lax.ppermute(a, "expert", back)
+        lead_a, lead_b = lax.ppermute(lead_a, "expert", ahead), lax.ppermute(lead_b, "expert", back)
+        lead_a, lead_b = after_all((lead_a, lead_b), ended)[0]
+        lead_part_a, lead_part_b, shares = run(lead_a, lead_b, (ended,) if s == 1 else ())
+        b, a = after_all((b, a), shares)[0]
+        part_b, part_a = plain(weights, b, a, shares)
+        ended = part_b
         parts[s] = lead_part_a, lead_part_b, part_b, part_a
     far_a, far_b, _ = run(lax.ppermute(lead_a, "expert", ahead), lax.ppermute(lead_b, "expert", back))
 

time: 171 us -> 169 us (0.988)
  waiting for transfers between devices: 76.6 us -> 72.9 us
    ppermute x12 -> x6, waiting for transfers between devices: 17 us -> 4.45 us  [body(): b, a = (lax.ppermute(b, 'expert', ahead), lax.ppermute(a, 'expert', back))]
    ppermute x3, waiting for transfers between devices: 9.94 us -> 21.8 us  [body(): lead_b = lax.ppermute(add(lead_part_b, lead_b), 'expert', ahead)]
    ppermute x3, waiting for transfers between devices: 24.8 us -> 14.4 us  [body(): lead_a = lax.ppermute(add(lead_part_a, lead_a), 'expert', back)]
    ppermute x1 -> x4, waiting for transfers between devices: 1.91 us -> 8.23 us  [body(): lax.ppermute(lead_a, 'expert', ahead)]
    ppermute x12 -> x6, starting transfers between devices: 13.4 us -> 7.18 us  [body(): b, a = (lax.ppermute(b, 'expert', ahead), lax.ppermute(a, 'expert', back))]
    ppermute x1 -> x4, starting transfers between devices: 1.82 us -> 6.83 us  [body(): lax.ppermute(lead_a, 'expert', ahead)]
    ppermute x1 -> x4, waiting for transfers between devices: 1.82 us -> 4.7 us  [body(): lax.ppermute(lead_b, 'expert', back)]
    ppermute x1, waiting for transfers between devices: 7.56 us -> 10 us  [body(): lax.ppermute(far_b, 'expert', ahead)]
  transfers between devices with their start and end apart: 28 -> 28, of which waited for: 18 -> 20; matrix products, arithmetic and copies ran while one was open for 1% -> 1% of each run, Pallas kernels for 29% -> 30%
where the time goes in v6:
time: 169 us
  waiting for transfers between devices  72.9 us (43%)
  Pallas kernels  52.4 us (31%)
  starting transfers between devices  30.3 us (18%)
  local copies, waits for them, and re-layouts  11 us (7%)
    pallas_call x5, Pallas kernels, lead(): pl.pallas_call(functools.partial(lead_kernel, slots), in_specs=[pl.BlockS...  32.4 us
    ppermute x3, waiting for transfers between devices, body(): lead_b = lax.ppermute(add(lead_part_b, lead_b), 'expert', ahead)  21.8 us
    pallas_call x3, Pallas kernels, plain(): pl.pallas_call(plain_kernel, in_specs=[vmem] * 6, out_specs=[vmem] * 2, o...  18.5 us
    ppermute x3, waiting for transfers between devices, body(): lead_a = lax.ppermute(add(lead_part_a, lead_a), 'expert', back)  14.4 us
    ppermute x1, waiting for transfers between devices, body(): lax.ppermute(far_b, 'expert', ahead)  10 us
    unnamed x16, local copies, waits for them, and re-layouts  9.76 us
    ppermute x1, waiting for transfers between devices, body(): lax.ppermute(far_a, 'expert', back)  8.71 us
    ppermute x4, waiting for transfers between devices, body(): lax.ppermute(lead_a, 'expert', ahead)  8.23 us
  transfers between devices with their start and end apart: 28, of which 20 were waited for; matrix products, arithmetic and copies ran while one was open for 1% of the time, Pallas kernels for 30%

profile of v6, /device:TPU:0, one launch (start us, length us, event | category | flops | bytes accessed | tf_op | source)
XLA Modules:
  0.0 169.0 jit_solution(10982799270934455918)
XLA Ops:
  1.3 3.1 %collective-permute-start.4 = (bf16[128,2048]{1,0:T(8,128)(2,1)S(1)}, bf16[128,2048]{1,0:T(8,128)(2,1)}, u32[]{:S(2)}, u32[]{:S(2)}) collective-permute-start(bf16[128,2048]{1,0:T(8,128)(2,1)S(1)} %get-tuple-element.73.b_ref), channel_id=1, source_target_pairs={{0,2},{2,4},{4,6},{6,7},{7,5},{5,3},{3,1},{1,0},{8,10},{10,12},{12... | collective-permute-start | bytes 1572872 | tf_op jit(solution)/shard_map/ppermute | solution.py:231
  6.0 2.1 %collective-permute-start = (bf16[2096,128]{1,0:T(8,128)(2,1)S(1)}, bf16[2096,128]{1,0:T(8,128)(2,1)S(1)}, u32[]{:S(2)}, u32[]{:S(2)}) collective-permute-start(bf16[2096,128]{1,0:T(8,128)(2,1)S(1)} %get-tuple-element.39.a_ref), channel_id=1, source_target_pairs={{0,2},{2,4},{4,6},{6,7},{7,5},{5,3},{3,1},{1,0},{8,10},{10,12},{12... | collective-permute-start | bytes 1609736 | tf_op jit(solution)/shard_map/ppermute | solution.py:232
  8.8 2.8 %copy-done = bf16[2,2048,768]{2,1,0:T(8,128)(2,1)S(1)} copy-done((bf16[2,2048,768]{2,1,0:T(8,128)(2,1)S(1)}, bf16[2,2048,768]{2,1,0:T(8,128)(2,1)}, u32[]{:S(2)}) %copy-start) | copy-done | bytes 6291480
  11.6 2.8 %copy-done.2 = bf16[2,2048,768]{2,1,0:T(8,128)(2,1)S(1)} copy-done((bf16[2,2048,768]{2,1,0:T(8,128)(2,1)S(1)}, bf16[2,2048,768]{2,1,0:T(8,128)(2,1)}, u32[]{:S(2)}) %copy-start.2) | copy-done | bytes 6291480
  14.4 2.8 %copy-done.4 = bf16[2,768,2048]{2,1,0:T(8,128)(2,1)S(1)} copy-done((bf16[2,768,2048]{2,1,0:T(8,128)(2,1)S(1)}, bf16[2,768,2048]{2,1,0:T(8,128)(2,1)}, u32[]{:S(2)}) %copy-start.4) | copy-done | bytes 6291480
  17.2 6.5 %shard_map.74 = (bf16[128,2048]{1,0:T(8,128)(2,1)S(1)}, bf16[128,2048]{1,0:T(8,128)(2,1)S(1)}, f32[256,128]{1,0:T(8,128)S(1)}) custom-call(s32[3]{0:T(128)S(1)} %pad_add_fusion.place_ref, bf16[2096,128]{1,0:T(8,128)(2,1)S(1)} %get-tuple-element.39.a_ref, bf16[2096,128]{1,0:T(8,128)(2,1)S(1)} %get-tuple-element.40.b_ref, bf16[2,2048,768]{2,1,0:T(8,128)(2,1)S(1)} %copy-done, ...), custom_call_target="tpu_custom_call" | custom-call | flops 4831838208 | bytes 4194304 | tf_op jit(solution)/shard_map/pallas_call | solution.py:144
  23.7 4.0 %collective-permute-done.a_ref = bf16[2096,128]{1,0:T(8,128)(2,1)S(1)} collective-permute-done((bf16[2096,128]{1,0:T(8,128)(2,1)S(1)}, bf16[2096,128]{1,0:T(8,128)(2,1)S(1)}, u32[]{:S(2)}, u32[]{:S(2)}) %collective-permute-start) | collective-permute-done | bytes 536608 | tf_op jit(solution)/shard_map/ppermute | solution.py:232
  31.3 6.5 %shard_map.75 = (bf16[128,2048]{1,0:T(8,128)(2,1)S(1)}, bf16[128,2048]{1,0:T(8,128)(2,1)S(1)}, f32[256,128]{1,0:T(8,128)S(1)}) custom-call(s32[3]{0:T(128)S(1)} %pad_add_fusion.place_ref, bf16[2096,128]{1,0:T(8,128)(2,1)S(1)} %collective-permute-done.a_ref, bf16[2096,128]{1,0:T(8,128)(2,1)S(1)} %collective-permute-done.1.b_ref, ...), custom_call_target="tpu_custom_call" | custom-call | flops 4831838208 | bytes 4194304 | tf_op jit(solution)/shard_map/pallas_call | solution.py:144
  37.8 1.6 collective-permute-start.8
  39.9 7.0 %shard_map.76 = (bf16[128,2048]{1,0:T(8,128)(2,1)S(1)}, bf16[128,2048]{1,0:T(8,128)(2,1)S(1)}) custom-call(bf16[128,2048]{1,0:T(8,128)(2,1)} %collective-permute-done.4.b_ref, bf16[128,2048]{1,0:T(8,128)(2,1)} %collective-permute-done.5.a_ref, f32[256,128]{1,0:T(8,128)S(1)} %get-tuple-element.46.share_ref, bf16[2,2048,768]{2,1,0:T(8,128)(2,1)S(1)} %copy-done.1, ...), custom_call_target="tpu_custom_call" | custom-call | flops 4831838208 | bytes 4194304 | tf_op jit(solution)/shard_map/pallas_call | solution.py:163
  46.9 1.6 collective-permute-start.6
  48.9 6.5 %shard_map.77 = (bf16[128,2048]{1,0:T(8,128)(2,1)S(1)}, bf16[128,2048]{1,0:T(8,128)(2,1)S(1)}, f32[256,128]{1,0:T(8,128)S(1)}) custom-call(s32[3]{0:T(128)S(1)} %pad_add_fusion.place_ref, bf16[2096,128]{1,0:T(8,128)(2,1)S(1)} %collective-permute-done.2.a_ref, bf16[2096,128]{1,0:T(8,128)(2,1)S(1)} %collective-permute-done.3.b_ref, ...), custom_call_target="tpu_custom_call" | custom-call | flops 4831838208 | bytes 4194304 | tf_op jit(solution)/shard_map/pallas_call | solution.py:144
  59.2 5.8 %shard_map.78 = (bf16[128,2048]{1,0:T(8,128)(2,1)S(1)}, bf16[128,2048]{1,0:T(8,128)(2,1)S(1)}) custom-call(bf16[128,2048]{1,0:T(8,128)(2,1)S(1)} %collective-permute-done.8.b_ref, bf16[128,2048]{1,0:T(8,128)(2,1)S(1)} %collective-permute-done.9.a_ref, f32[256,128]{1,0:T(8,128)S(1)} %get-tuple-element.53.share_ref, bf16[2,2048,768]{2,1,0:T(8,128)(2,1)S(1)} %copy-done.1, ...), custom_call_target="tpu_custom_call" | custom-call | flops 4831838208 | bytes 4194304 | tf_op jit(solution)/shard_map/pallas_call | solution.py:163
  65.0 2.1 %collective-permute-done.6.a_ref = bf16[2096,128]{1,0:T(8,128)(2,1)S(1)} collective-permute-done((bf16[2096,128]{1,0:T(8,128)(2,1)S(1)}, bf16[2096,128]{1,0:T(8,128)(2,1)S(1)}, u32[]{:S(2)}, u32[]{:S(2)}) %collective-permute-start.6) | collective-permute-done | bytes 536608 | tf_op jit(solution)/shard_map/ppermute | solution.py:232
  67.1 1.6 collective-permute-done.7.b_ref
  70.7 6.5 %shard_map.79 = (bf16[128,2048]{1,0:T(8,128)(2,1)S(1)}, bf16[128,2048]{1,0:T(8,128)(2,1)S(1)}, f32[256,128]{1,0:T(8,128)S(1)}) custom-call(s32[3]{0:T(128)S(1)} %pad_add_fusion.place_ref, bf16[2096,128]{1,0:T(8,128)(2,1)S(1)} %collective-permute-done.6.a_ref, bf16[2096,128]{1,0:T(8,128)(2,1)S(1)} %collective-permute-done.7.b_ref, ...), custom_call_target="tpu_custom_call" | custom-call | flops 4831838208 | bytes 4194304 | tf_op jit(solution)/shard_map/pallas_call | solution.py:144
  79.9 5.8 %shard_map.81 = (bf16[128,2048]{1,0:T(8,128)(2,1)S(1)}, bf16[128,2048]{1,0:T(8,128)(2,1)S(1)}) custom-call(bf16[128,2048]{1,0:T(8,128)(2,1)S(1)} %collective-permute-done.16.b_ref, bf16[128,2048]{1,0:T(8,128)(2,1)S(1)} %collective-permute-done.17.a_ref, f32[256,128]{1,0:T(8,128)S(1)} %get-tuple-element.63.share_ref, bf16[2,2048,768]{2,1,0:T(8,128)(2,1)S(1)} %copy-done.1, ...), custom_call_target="tpu_custom_call" | custom-call | flops 4831838208 | bytes 4194304 | tf_op jit(solution)/shard_map/pallas_call | solution.py:163
  86.2 1.6 collective-permute-start.18
  87.7 2.1 %collective-permute-done.10.a_ref = bf16[2096,128]{1,0:T(8,128)(2,1)S(1)} collective-permute-done((bf16[2096,128]{1,0:T(8,128)(2,1)S(1)}, bf16[2096,128]{1,0:T(8,128)(2,1)S(1)}, u32[]{:S(2)}, u32[]{:S(2)}) %collective-permute-start.10) | collective-permute-done | bytes 536608 | tf_op jit(solution)/shard_map/ppermute | solution.py:239
  91.4 6.5 %shard_map.80 = (bf16[128,2048]{1,0:T(8,128)(2,1)S(1)}, bf16[128,2048]{1,0:T(8,128)(2,1)S(1)}, f32[256,128]{1,0:T(8,128)}) custom-call(s32[3]{0:T(128)S(1)} %pad_add_fusion.place_ref, bf16[2096,128]{1,0:T(8,128)(2,1)S(1)} %collective-permute-done.10.a_ref, bf16[2096,128]{1,0:T(8,128)(2,1)S(1)} %collective-permute-done.11.b_ref, ...), custom_call_target="tpu_custom_call" | custom-call | flops 4831838208 | bytes 4194304 | tf_op jit(solution)/shard_map/pallas_call | solution.py:144
  97.9 1.6 collective-permute-start.21
  102.8 10.0 %collective-permute-done.21 = bf16[128,2048]{1,0:T(8,128)(2,1)S(1)} collective-permute-done((bf16[128,2048]{1,0:T(8,128)(2,1)S(1)}, bf16[128,2048]{1,0:T(8,128)(2,1)S(1)}, u32[]{:S(2)}, u32[]{:S(2)}) %collective-permute-start.21) | collective-permute-done | bytes 524320 | tf_op jit(solution)/shard_map/ppermute | solution.py:241
  113.0 1.6 collective-permute-start.22
  114.6 8.7 %collective-permute-done.12 = bf16[128,2048]{1,0:T(8,128)(2,1)S(1)} collective-permute-done((bf16[128,2048]{1,0:T(8,128)(2,1)S(1)}, bf16[128,2048]{1,0:T(8,128)(2,1)S(1)}, u32[]{:S(2)}, u32[]{:S(2)}) %collective-permute-start.12) | collective-permute-done | bytes 524320 | tf_op jit(solution)/shard_map/ppermute | solution.py:241
  124.7 7.7 %collective-permute-done.22 = bf16[128,2048]{1,0:T(8,128)(2,1)S(1)} collective-permute-done((bf16[128,2048]{1,0:T(8,128)(2,1)S(1)}, bf16[128,2048]{1,0:T(8,128)(2,1)S(1)}, u32[]{:S(2)}, u32[]{:S(2)}) %collective-permute-start.22) | collective-permute-done | bytes 524320 | tf_op jit(solution)/shard_map/ppermute | solution.py:247
  132.5 1.6 collective-permute-start.23
  134.1 4.2 %collective-permute-done.13 = bf16[128,2048]{1,0:T(8,128)(2,1)S(1)} collective-permute-done((bf16[128,2048]{1,0:T(8,128)(2,1)S(1)}, bf16[128,2048]{1,0:T(8,128)(2,1)S(1)}, u32[]{:S(2)}, u32[]{:S(2)}) %collective-permute-start.13) | collective-permute-done | bytes 524320 | tf_op jit(solution)/shard_map/ppermute | solution.py:246
  139.1 1.6 collective-permute-start.20
  140.7 6.7 %collective-permute-done.23 = bf16[128,2048]{1,0:T(8,128)(2,1)S(1)} collective-permute-done((bf16[128,2048]{1,0:T(8,128)(2,1)S(1)}, bf16[128,2048]{1,0:T(8,128)(2,1)S(1)}, u32[]{:S(2)}, u32[]{:S(2)}) %collective-permute-start.23) | collective-permute-done | bytes 524320 | tf_op jit(solution)/shard_map/ppermute | solution.py:247
  147.6 1.6 collective-permute-start.24
  149.2 8.7 %collective-permute-done.14 = bf16[128,2048]{1,0:T(8,128)(2,1)S(1)} collective-permute-done((bf16[128,2048]{1,0:T(8,128)(2,1)S(1)}, bf16[128,2048]{1,0:T(8,128)(2,1)S(1)}, u32[]{:S(2)}, u32[]{:S(2)}) %collective-permute-start.14) | collective-permute-done | bytes 524320 | tf_op jit(solution)/shard_map/ppermute | solution.py:246
  158.7 7.4 %collective-permute-done.24.refs_4_ = bf16[128,2048]{1,0:T(8,128)(2,1)S(1)} collective-permute-done((bf16[128,2048]{1,0:T(8,128)(2,1)S(1)}, bf16[128,2048]{1,0:T(8,128)(2,1)S(1)}, u32[]{:S(2)}, u32[]{:S(2)}) %collective-permute-start.24) | collective-permute-done | bytes 524320 | tf_op jit(solution)/shard_map/ppermute | solution.py:247
  (62 shorter events, 27.4 us)
Async XLA Ops:
  1.3 36.5 %collective-permute-start.4 = (bf16[128,2048]{1,0:T(8,128)(2,1)S(1)}, bf16[128,2048]{1,0:T(8,128)(2,1)}, u32[]{:S(2)}, u32[]{:S(2)}) collective-permute-start(bf16[128,2048]{1,0:T(8,128)(2,1)S(1)} %get-tuple-element.73.b_ref), channel_id=1, source_target_pairs={{0,2},{2,4},{4,6},{6,7},{7,5},{5,3},{3,1},{1,0},{8,10},{10,12},{12... | collective-permute-start | bytes 1572872 | tf_op jit(solution)/shard_map/ppermute | solution.py:231
  4.4 33.4 %collective-permute-start.5 = (bf16[128,2048]{1,0:T(8,128)(2,1)S(1)}, bf16[128,2048]{1,0:T(8,128)(2,1)}, u32[]{:S(2)}, u32[]{:S(2)}) collective-permute-start(bf16[128,2048]{1,0:T(8,128)(2,1)S(1)} %get-tuple-element.74.a_ref), channel_id=1, source_target_pairs={{2,0},{4,2},{6,4},{7,6},{5,7},{3,5},{1,3},{0,1},{10,8},{12,10},{14... | collective-permute-start | bytes 1572872 | tf_op jit(solution)/shard_map/ppermute | solution.py:231
  6.0 21.7 %collective-permute-start = (bf16[2096,128]{1,0:T(8,128)(2,1)S(1)}, bf16[2096,128]{1,0:T(8,128)(2,1)S(1)}, u32[]{:S(2)}, u32[]{:S(2)}) collective-permute-start(bf16[2096,128]{1,0:T(8,128)(2,1)S(1)} %get-tuple-element.39.a_ref), channel_id=1, source_target_pairs={{0,2},{2,4},{4,6},{6,7},{7,5},{5,3},{3,1},{1,0},{8,10},{10,12},{12... | collective-permute-start | bytes 1609736 | tf_op jit(solution)/shard_map/ppermute | solution.py:232
  8.1 21.2 %collective-permute-start.1 = (bf16[2096,128]{1,0:T(8,128)(2,1)S(1)}, bf16[2096,128]{1,0:T(8,128)(2,1)S(1)}, u32[]{:S(2)}, u32[]{:S(2)}) collective-permute-start(bf16[2096,128]{1,0:T(8,128)(2,1)S(1)} %get-tuple-element.40.b_ref), channel_id=1, source_target_pairs={{2,0},{4,2},{6,4},{7,6},{5,7},{3,5},{1,3},{0,1},{10,8},{12,10},{14... | collective-permute-start | bytes 1609736 | tf_op jit(solution)/shard_map/ppermute | solution.py:232
  8.8 2.8 %copy-start = (bf16[2,2048,768]{2,1,0:T(8,128)(2,1)S(1)}, bf16[2,2048,768]{2,1,0:T(8,128)(2,1)}, u32[]{:S(2)}) copy-start(bf16[2,2048,768]{2,1,0:T(8,128)(2,1)} %gate_ref.15) | copy-start | bytes 18874372
  17.2 14.1 %copy-start.1 = (bf16[2,2048,768]{2,1,0:T(8,128)(2,1)S(1)}, bf16[2,2048,768]{2,1,0:T(8,128)(2,1)}, u32[]{:S(2)}) copy-start(bf16[2,2048,768]{2,1,0:T(8,128)(2,1)} %gate_ref.15) | copy-start | bytes 18874372
  17.2 14.1 %copy-start.3 = (bf16[2,2048,768]{2,1,0:T(8,128)(2,1)S(1)}, bf16[2,2048,768]{2,1,0:T(8,128)(2,1)}, u32[]{:S(2)}) copy-start(bf16[2,2048,768]{2,1,0:T(8,128)(2,1)} %up_ref.15) | copy-start | bytes 18874372
  17.2 14.1 %copy-start.5 = (bf16[2,768,2048]{2,1,0:T(8,128)(2,1)S(1)}, bf16[2,768,2048]{2,1,0:T(8,128)(2,1)}, u32[]{:S(2)}) copy-start(bf16[2,768,2048]{2,1,0:T(8,128)(2,1)} %param.13) | copy-start | bytes 18874372
  29.2 17.6 %collective-permute-start.2 = (bf16[2096,128]{1,0:T(8,128)(2,1)S(1)}, bf16[2096,128]{1,0:T(8,128)(2,1)S(1)}, u32[]{:S(2)}, u32[]{:S(2)}) collective-permute-start(bf16[2096,128]{1,0:T(8,128)(2,1)S(1)} %collective-permute-done.a_ref), channel_id=1, source_target_pairs={{0,2},{2,4},{4,6},{6,7},{7,5},{5,3},{3,1},{1,0},{8,10},{10,12},{12... | collective-permute-start | bytes 1609736 | tf_op jit(solution)/shard_map/ppermute | solution.py:232
  30.8 16.0 %collective-permute-start.3 = (bf16[2096,128]{1,0:T(8,128)(2,1)S(1)}, bf16[2096,128]{1,0:T(8,128)(2,1)S(1)}, u32[]{:S(2)}, u32[]{:S(2)}) collective-permute-start(bf16[2096,128]{1,0:T(8,128)(2,1)S(1)} %collective-permute-done.1.b_ref), channel_id=1, source_target_pairs={{2,0},{4,2},{6,4},{7,6},{5,7},{3,5},{1,3},{0,1},{10,8},{12,10},{14... | collective-permute-start | bytes 1609736 | tf_op jit(solution)/shard_map/ppermute | solution.py:232
  37.8 17.8 %collective-permute-start.8 = (bf16[128,2048]{1,0:T(8,128)(2,1)}, bf16[128,2048]{1,0:T(8,128)(2,1)S(1)}, u32[]{:S(2)}, u32[]{:S(2)}) collective-permute-start(bf16[128,2048]{1,0:T(8,128)(2,1)} %collective-permute-done.4.b_ref), channel_id=1, source_target_pairs={{0,2},{2,4},{4,6},{6,7},{7,5},{5,3},{3,1},{1,0},{8,10},{10,12},{12... | collective-permute-start | bytes 1572872 | tf_op jit(solution)/shard_map/ppermute | solution.py:231
  39.4 17.8 %collective-permute-start.9 = (bf16[128,2048]{1,0:T(8,128)(2,1)}, bf16[128,2048]{1,0:T(8,128)(2,1)S(1)}, u32[]{:S(2)}, u32[]{:S(2)}) collective-permute-start(bf16[128,2048]{1,0:T(8,128)(2,1)} %collective-permute-done.5.a_ref), channel_id=1, source_target_pairs={{2,0},{4,2},{6,4},{7,6},{5,7},{3,5},{1,3},{0,1},{10,8},{12,10},{14... | collective-permute-start | bytes 1572872 | tf_op jit(solution)/shard_map/ppermute | solution.py:231
  46.9 20.2 %collective-permute-start.6 = (bf16[2096,128]{1,0:T(8,128)(2,1)S(1)}, bf16[2096,128]{1,0:T(8,128)(2,1)S(1)}, u32[]{:S(2)}, u32[]{:S(2)}) collective-permute-start(bf16[2096,128]{1,0:T(8,128)(2,1)S(1)} %collective-permute-done.2.a_ref), channel_id=1, source_target_pairs={{0,2},{2,4},{4,6},{6,7},{7,5},{5,3},{3,1},{1,0},{8,10},{10,12},{12... | collective-permute-start | bytes 1609736 | tf_op jit(solution)/shard_map/ppermute | solution.py:232
  48.5 20.2 %collective-permute-start.7 = (bf16[2096,128]{1,0:T(8,128)(2,1)S(1)}, bf16[2096,128]{1,0:T(8,128)(2,1)S(1)}, u32[]{:S(2)}, u32[]{:S(2)}) collective-permute-start(bf16[2096,128]{1,0:T(8,128)(2,1)S(1)} %collective-permute-done.3.b_ref), channel_id=1, source_target_pairs={{2,0},{4,2},{6,4},{7,6},{5,7},{3,5},{1,3},{0,1},{10,8},{12,10},{14... | collective-permute-start | bytes 1609736 | tf_op jit(solution)/shard_map/ppermute | solution.py:232
  57.2 21.2 %collective-permute-start.16 = (bf16[128,2048]{1,0:T(8,128)(2,1)S(1)}, bf16[128,2048]{1,0:T(8,128)(2,1)S(1)}, u32[]{:S(2)}, u32[]{:S(2)}) collective-permute-start(bf16[128,2048]{1,0:T(8,128)(2,1)S(1)} %collective-permute-done.8.b_ref), channel_id=1, source_target_pairs={{0,2},{2,4},{4,6},{6,7},{7,5},{5,3},{3,1},{1,0},{8,10},{10,12},{12... | collective-permute-start | bytes 1572872 | tf_op jit(solution)/shard_map/ppermute | solution.py:231
  58.7 21.2 %collective-permute-start.17 = (bf16[128,2048]{1,0:T(8,128)(2,1)S(1)}, bf16[128,2048]{1,0:T(8,128)(2,1)S(1)}, u32[]{:S(2)}, u32[]{:S(2)}) collective-permute-start(bf16[128,2048]{1,0:T(8,128)(2,1)S(1)} %collective-permute-done.9.a_ref), channel_id=1, source_target_pairs={{2,0},{4,2},{6,4},{7,6},{5,7},{3,5},{1,3},{0,1},{10,8},{12,10},{14... | collective-permute-start | bytes 1572872 | tf_op jit(solution)/shard_map/ppermute | solution.py:231
  68.7 21.2 %collective-permute-start.10 = (bf16[2096,128]{1,0:T(8,128)(2,1)S(1)}, bf16[2096,128]{1,0:T(8,128)(2,1)S(1)}, u32[]{:S(2)}, u32[]{:S(2)}) collective-permute-start(bf16[2096,128]{1,0:T(8,128)(2,1)S(1)} %collective-permute-done.6.a_ref), channel_id=1, source_target_pairs={{0,2},{2,4},{4,6},{6,7},{7,5},{5,3},{3,1},{1,0},{8,10},{10,12},{12... | collective-permute-start | bytes 1609736 | tf_op jit(solution)/shard_map/ppermute | solution.py:239
  70.2 21.2 %collective-permute-start.11 = (bf16[2096,128]{1,0:T(8,128)(2,1)S(1)}, bf16[2096,128]{1,0:T(8,128)(2,1)S(1)}, u32[]{:S(2)}, u32[]{:S(2)}) collective-permute-start(bf16[2096,128]{1,0:T(8,128)(2,1)S(1)} %collective-permute-done.7.b_ref), channel_id=1, source_target_pairs={{2,0},{4,2},{6,4},{7,6},{5,7},{3,5},{1,3},{0,1},{10,8},{12,10},{14... | collective-permute-start | bytes 1609736 | tf_op jit(solution)/shard_map/ppermute | solution.py:239
  85.7 14.3 %collective-permute-start.25 = (bf16[128,2048]{1,0:T(8,128)(2,1)S(1)}, bf16[128,2048]{1,0:T(8,128)(2,1)S(1)}, u32[]{:S(2)}, u32[]{:S(2)}) collective-permute-start(bf16[128,2048]{1,0:T(8,128)(2,1)S(1)} %get-tuple-element.72), channel_id=1, source_target_pairs={{2,0},{4,2},{6,4},{7,6},{5,7},{3,5},{1,3},{0,1},{10,8},{12,10},{14... | collective-permute-start | bytes 1572872 | tf_op jit(solution)/shard_map/ppermute | solution.py:244
  86.2 15.0 %collective-permute-start.18 = (bf16[128,2048]{1,0:T(8,128)(2,1)S(1)}, bf16[128,2048]{1,0:T(8,128)(2,1)S(1)}, u32[]{:S(2)}, u32[]{:S(2)}) collective-permute-start(bf16[128,2048]{1,0:T(8,128)(2,1)S(1)} %get-tuple-element.66), channel_id=1, source_target_pairs={{0,2},{2,4},{4,6},{6,7},{7,5},{5,3},{3,1},{1,0},{8,10},{10,12},{12... | collective-permute-start | bytes 1572872 | tf_op jit(solution)/shard_map/ppermute | solution.py:245
  97.9 14.9 %collective-permute-start.21 = (bf16[128,2048]{1,0:T(8,128)(2,1)S(1)}, bf16[128,2048]{1,0:T(8,128)(2,1)S(1)}, u32[]{:S(2)}, u32[]{:S(2)}) collective-permute-start(bf16[128,2048]{1,0:T(8,128)(2,1)S(1)} %get-tuple-element.71), channel_id=1, source_target_pairs={{0,2},{2,4},{4,6},{6,7},{7,5},{5,3},{3,1},{1,0},{8,10},{10,12},{12... | collective-permute-start | bytes 1572872 | tf_op jit(solution)/shard_map/ppermute | solution.py:241
  100.1 23.8 %collective-permute-start.26 = (bf16[128,2048]{1,0:T(8,128)(2,1)S(1)}, bf16[128,2048]{1,0:T(8,128)(2,1)S(1)}, u32[]{:S(2)}, u32[]{:S(2)}) collective-permute-start(bf16[128,2048]{1,0:T(8,128)(2,1)S(1)} %add_convert_fusion.1), channel_id=1, source_target_pairs={{2,0},{4,2},{6,4},{7,6},{5,7},{3,5},{1,3},{0,1},{10,8},{12,10},{14... | collective-permute-start | bytes 1572872 | tf_op jit(solution)/shard_map/ppermute | solution.py:244
  100.6 22.7 %collective-permute-start.12 = (bf16[128,2048]{1,0:T(8,128)(2,1)S(1)}, bf16[128,2048]{1,0:T(8,128)(2,1)S(1)}, u32[]{:S(2)}, u32[]{:S(2)}) collective-permute-start(bf16[128,2048]{1,0:T(8,128)(2,1)S(1)} %get-tuple-element.60), channel_id=1, source_target_pairs={{2,0},{4,2},{6,4},{7,6},{5,7},{3,5},{1,3},{0,1},{10,8},{12,10},{14... | collective-permute-start | bytes 1572872 | tf_op jit(solution)/shard_map/ppermute | solution.py:241
  101.3 37.6 %collective-permute-start.19 = (bf16[128,2048]{1,0:T(8,128)(2,1)S(1)}, bf16[128,2048]{1,0:T(8,128)(2,1)S(1)}, u32[]{:S(2)}, u32[]{:S(2)}) collective-permute-start(bf16[128,2048]{1,0:T(8,128)(2,1)S(1)} %add_convert_fusion.6), channel_id=1, source_target_pairs={{0,2},{2,4},{4,6},{6,7},{7,5},{5,3},{3,1},{1,0},{8,10},{10,12},{12... | collective-permute-start | bytes 1572872 | tf_op jit(solution)/shard_map/ppermute | solution.py:245
  113.0 19.4 %collective-permute-start.22 = (bf16[128,2048]{1,0:T(8,128)(2,1)S(1)}, bf16[128,2048]{1,0:T(8,128)(2,1)S(1)}, u32[]{:S(2)}, u32[]{:S(2)}) collective-permute-start(bf16[128,2048]{1,0:T(8,128)(2,1)S(1)} %add_convert_fusion.4), channel_id=1, source_target_pairs={{0,2},{2,4},{4,6},{6,7},{7,5},{5,3},{3,1},{1,0},{8,10},{10,12},{12... | collective-permute-start | bytes 1572872 | tf_op jit(solution)/shard_map/ppermute | solution.py:247
  123.4 14.9 %collective-permute-start.13 = (bf16[128,2048]{1,0:T(8,128)(2,1)S(1)}, bf16[128,2048]{1,0:T(8,128)(2,1)S(1)}, u32[]{:S(2)}, u32[]{:S(2)}) collective-permute-start(bf16[128,2048]{1,0:T(8,128)(2,1)S(1)} %add_convert_fusion.9), channel_id=1, source_target_pairs={{2,0},{4,2},{6,4},{7,6},{5,7},{3,5},{1,3},{0,1},{10,8},{12,10},{14... | collective-permute-start | bytes 1572872 | tf_op jit(solution)/shard_map/ppermute | solution.py:246
  124.1 34.4 %collective-permute-start.27 = (bf16[128,2048]{1,0:T(8,128)(2,1)S(1)}, bf16[128,2048]{1,0:T(8,128)(2,1)S(1)}, u32[]{:S(2)}, u32[]{:S(2)}) collective-permute-start(bf16[128,2048]{1,0:T(8,128)(2,1)S(1)} %add_convert_fusion), channel_id=1, source_target_pairs={{2,0},{4,2},{6,4},{7,6},{5,7},{3,5},{1,3},{0,1},{10,8},{12,10},{14... | collective-permute-start | bytes 1572872 | tf_op jit(solution)/shard_map/ppermute | solution.py:244
  132.5 14.9 %collective-permute-start.23 = (bf16[128,2048]{1,0:T(8,128)(2,1)S(1)}, bf16[128,2048]{1,0:T(8,128)(2,1)S(1)}, u32[]{:S(2)}, u32[]{:S(2)}) collective-permute-start(bf16[128,2048]{1,0:T(8,128)(2,1)S(1)} %add_convert_fusion.3), channel_id=1, source_target_pairs={{0,2},{2,4},{4,6},{6,7},{7,5},{5,3},{3,1},{1,0},{8,10},{10,12},{12... | collective-permute-start | bytes 1572872 | tf_op jit(solution)/shard_map/ppermute | solution.py:247
  138.5 19.4 %collective-permute-start.14 = (bf16[128,2048]{1,0:T(8,128)(2,1)S(1)}, bf16[128,2048]{1,0:T(8,128)(2,1)S(1)}, u32[]{:S(2)}, u32[]{:S(2)}) collective-permute-start(bf16[128,2048]{1,0:T(8,128)(2,1)S(1)} %add_convert_fusion.8), channel_id=1, source_target_pairs={{2,0},{4,2},{6,4},{7,6},{5,7},{3,5},{1,3},{0,1},{10,8},{12,10},{14... | collective-permute-start | bytes 1572872 | tf_op jit(solution)/shard_map/ppermute | solution.py:246
  139.1 19.6 %collective-permute-start.20 = (bf16[128,2048]{1,0:T(8,128)(2,1)S(1)}, bf16[128,2048]{1,0:T(8,128)(2,1)S(1)}, u32[]{:S(2)}, u32[]{:S(2)}) collective-permute-start(bf16[128,2048]{1,0:T(8,128)(2,1)S(1)} %add_convert_fusion.5), channel_id=1, source_target_pairs={{0,2},{2,4},{4,6},{6,7},{7,5},{5,3},{3,1},{1,0},{8,10},{10,12},{12... | collective-permute-start | bytes 1572872 | tf_op jit(solution)/shard_map/ppermute | solution.py:245
  147.6 18.5 %collective-permute-start.24 = (bf16[128,2048]{1,0:T(8,128)(2,1)S(1)}, bf16[128,2048]{1,0:T(8,128)(2,1)S(1)}, u32[]{:S(2)}, u32[]{:S(2)}) collective-permute-start(bf16[128,2048]{1,0:T(8,128)(2,1)S(1)} %add_convert_fusion.2), channel_id=1, source_target_pairs={{0,2},{2,4},{4,6},{6,7},{7,5},{5,3},{3,1},{1,0},{8,10},{10,12},{12... | collective-permute-start | bytes 1572872 | tf_op jit(solution)/shard_map/ppermute | solution.py:247
  158.0 9.6 %collective-permute-start.15 = (bf16[128,2048]{1,0:T(8,128)(2,1)S(1)}, bf16[128,2048]{1,0:T(8,128)(2,1)S(1)}, u32[]{:S(2)}, u32[]{:S(2)}) collective-permute-start(bf16[128,2048]{1,0:T(8,128)(2,1)S(1)} %add_convert_fusion.7), channel_id=1, source_target_pairs={{2,0},{4,2},{6,4},{7,6},{5,7},{3,5},{1,3},{0,1},{10,8},{12,10},{14... | collective-permute-start | bytes 1572872 | tf_op jit(solution)/shard_map/ppermute | solution.py:246
  (4 other events, 7.0 us)

commit v7 on v6

--- a/solution.py
+++ b/solution.py
@@ -174,13 +174,29 @@
     )(b, a, shares, *weights)
 
 
+def early_kernel(*refs):
+    refs[-1][...] = sum(ref[...].astype(jnp.float32) for ref in refs[:-1])
+
+
+def early(terms):
+    vmem = pl.BlockSpec(memory_space=pltpu.VMEM)
+    return pl.pallas_call(
+        early_kernel,
+        in_specs=[vmem] * len(terms),
+        out_specs=vmem,
+        out_shape=jax.ShapeDtypeStruct(terms[0].shape, jnp.float32),
+        compiler_params=pltpu.CompilerParams(vmem_limit_bytes=VMEM_LIMIT),
+    )(*terms)
+
+
 def finish_kernel(*refs):
     terms, (out_ref, total_ref, sems) = refs[:-3], refs[-3:]
     half = terms[0].shape[0]
+    quarter = half // 2
     copies = []
-    for i in range(2):
-        rows = pl.ds(i * half, half)
-        total = sum(ref[...].astype(jnp.float32) for ref in terms[3 * i:3 * i + 3])
+    for i in range(4):
+        rows, part = pl.ds(i * quarter, quarter), pl.ds(i % 2 * quarter, quarter)
+        total = sum(ref[part, :].astype(jnp.float32) for ref in terms[i // 2 * 2:i // 2 * 2 + 2])
         total_ref[rows, :] = total.astype(total_ref.dtype)
         copies.append(pltpu.make_async_copy(total_ref.at[rows], out_ref.at[rows], sems.at[i]))
         copies[i].start()
@@ -192,10 +208,10 @@
     half, width = a[0].shape
     return pl.pallas_call(
         finish_kernel,
-        in_specs=[pl.BlockSpec(memory_space=pltpu.VMEM)] * 6,
+        in_specs=[pl.BlockSpec(memory_space=pltpu.VMEM)] * 4,
         out_specs=pl.BlockSpec(memory_space=pl.ANY),
-        out_shape=jax.ShapeDtypeStruct((2 * half, width), a[0].dtype),
-        scratch_shapes=[pltpu.VMEM((2 * half, width), a[0].dtype), pltpu.SemaphoreType.DMA((2,))],
+        out_shape=jax.ShapeDtypeStruct((2 * half, width), jnp.bfloat16),
+        scratch_shapes=[pltpu.VMEM((2 * half, width), jnp.bfloat16), pltpu.SemaphoreType.DMA((4,))],
         compiler_params=pltpu.CompilerParams(vmem_limit_bytes=VMEM_LIMIT),
     )(*a, *b)
 
@@ -241,11 +257,11 @@
     lead_a, lead_b, a, b = lax.ppermute(far_a, "expert", back), lax.ppermute(far_b, "expert", ahead), None, None
     for s in range(far - 1, 0, -1):
         lead_part_a, lead_part_b, part_b, part_a = parts[s]
+        lead_b = lax.ppermute(add(lead_part_b, lead_b), "expert", ahead)
+        lead_a = lax.ppermute(add(lead_part_a, lead_a), "expert", back)
+        a = lax.ppermute(part_a if a is None else add(part_a, a), "expert", ahead)
         b = lax.ppermute(part_b if b is None else add(part_b, b), "expert", back)
-        a = lax.ppermute(part_a if a is None else add(part_a, a), "expert", ahead)
-        lead_a = lax.ppermute(add(lead_part_a, lead_a), "expert", back)
-        lead_b = lax.ppermute(add(lead_part_b, lead_b), "expert", ahead)
-    return finish((own_a, lead_a, a), (own_b, lead_b, b))
+    return finish((early((own_a, a)), lead_a), (early((own_b, b)), lead_b))
 
 
 def solution(mesh):

time: 169 us -> 169 us (level)
    ppermute x3, waiting for transfers between devices: 21.8 us -> 9.94 us  [body(): lead_b = lax.ppermute(add(lead_part_b, lead_b), 'expert', ahead)]
    ppermute x3, waiting for transfers between devices: 14.4 us -> 25 us  [body(): lead_a = lax.ppermute(add(lead_part_a, lead_a), 'expert', back)]
    ppermute x1, waiting for transfers between devices: 10 us -> 7.49 us  [body(): lax.ppermute(far_b, 'expert', ahead)]
    ppermute x1, waiting for transfers between devices: 8.71 us -> 10.6 us  [body(): lax.ppermute(far_a, 'expert', back)]
    ppermute x3, waiting for transfers between devices: 0.44 us -> 2.15 us  [body(): b = lax.ppermute(part_b if b is None else add(part_b, b), 'expert', back)]
where the time goes in v7:
time: 169 us
  waiting for transfers between devices  72.8 us (43%)
  Pallas kernels  52.5 us (31%)
  starting transfers between devices  30.2 us (18%)
  local copies, waits for them, and re-layouts  11 us (7%)
    pallas_call x5, Pallas kernels, lead(): pl.pallas_call(functools.partial(lead_kernel, slots), in_specs=[pl.BlockS...  32.4 us
    ppermute x3, waiting for transfers between devices, body(): lead_a = lax.ppermute(add(lead_part_a, lead_a), 'expert', back)  25 us
    pallas_call x3, Pallas kernels, plain(): pl.pallas_call(plain_kernel, in_specs=[vmem] * 6, out_specs=[vmem] * 2, o...  18.5 us
    ppermute x1, waiting for transfers between devices, body(): lax.ppermute(far_a, 'expert', back)  10.6 us
    ppermute x3, waiting for transfers between devices, body(): lead_b = lax.ppermute(add(lead_part_b, lead_b), 'expert', ahead)  9.94 us
    unnamed x16, local copies, waits for them, and re-layouts  9.76 us
    ppermute x4, waiting for transfers between devices, body(): lax.ppermute(lead_a, 'expert', ahead)  8.23 us
    ppermute x1, waiting for transfers between devices, body(): lax.ppermute(far_b, 'expert', ahead)  7.49 us
  transfers between devices with their start and end apart: 28, of which 20 were waited for; matrix products, arithmetic and copies ran while one was open for 1% of the time, Pallas kernels for 30%

profile of v7, /device:TPU:0, one launch (start us, length us, event | category | flops | bytes accessed | tf_op | source)
XLA Modules:
  0.0 168.8 jit_solution(15664796868758434231)
XLA Ops:
  1.3 3.1 %collective-permute-start = (bf16[128,2048]{1,0:T(8,128)(2,1)S(1)}, bf16[128,2048]{1,0:T(8,128)(2,1)}, u32[]{:S(2)}, u32[]{:S(2)}) collective-permute-start(bf16[128,2048]{1,0:T(8,128)(2,1)S(1)} %get-tuple-element.73.b_ref), channel_id=1, source_target_pairs={{0,2},{2,4},{4,6},{6,7},{7,5},{5,3},{3,1},{1,0},{8,10},{10,12},{12... | collective-permute-start | bytes 1572872 | tf_op jit(solution)/shard_map/ppermute | solution.py:247
  6.0 2.1 %collective-permute-start.2 = (bf16[2096,128]{1,0:T(8,128)(2,1)S(1)}, bf16[2096,128]{1,0:T(8,128)(2,1)S(1)}, u32[]{:S(2)}, u32[]{:S(2)}) collective-permute-start(bf16[2096,128]{1,0:T(8,128)(2,1)S(1)} %get-tuple-element.39.a_ref), channel_id=1, source_target_pairs={{0,2},{2,4},{4,6},{6,7},{7,5},{5,3},{3,1},{1,0},{8,10},{10,12},{12... | collective-permute-start | bytes 1609736 | tf_op jit(solution)/shard_map/ppermute | solution.py:248
  8.8 2.8 %copy-done = bf16[2,2048,768]{2,1,0:T(8,128)(2,1)S(1)} copy-done((bf16[2,2048,768]{2,1,0:T(8,128)(2,1)S(1)}, bf16[2,2048,768]{2,1,0:T(8,128)(2,1)}, u32[]{:S(2)}) %copy-start) | copy-done | bytes 6291480
  11.6 2.8 %copy-done.2 = bf16[2,2048,768]{2,1,0:T(8,128)(2,1)S(1)} copy-done((bf16[2,2048,768]{2,1,0:T(8,128)(2,1)S(1)}, bf16[2,2048,768]{2,1,0:T(8,128)(2,1)}, u32[]{:S(2)}) %copy-start.2) | copy-done | bytes 6291480
  14.4 2.8 %copy-done.4 = bf16[2,768,2048]{2,1,0:T(8,128)(2,1)S(1)} copy-done((bf16[2,768,2048]{2,1,0:T(8,128)(2,1)S(1)}, bf16[2,768,2048]{2,1,0:T(8,128)(2,1)}, u32[]{:S(2)}) %copy-start.4) | copy-done | bytes 6291480
  17.2 6.5 %shard_map.74 = (bf16[128,2048]{1,0:T(8,128)(2,1)S(1)}, bf16[128,2048]{1,0:T(8,128)(2,1)S(1)}, f32[256,128]{1,0:T(8,128)S(1)}) custom-call(s32[3]{0:T(128)S(1)} %pad_add_fusion.place_ref, bf16[2096,128]{1,0:T(8,128)(2,1)S(1)} %get-tuple-element.39.a_ref, bf16[2096,128]{1,0:T(8,128)(2,1)S(1)} %get-tuple-element.40.b_ref, bf16[2,2048,768]{2,1,0:T(8,128)(2,1)S(1)} %copy-done, ...), custom_call_target="tpu_custom_call" | custom-call | flops 4831838208 | bytes 4194304 | tf_op jit(solution)/shard_map/pallas_call | solution.py:144
  23.7 4.0 %collective-permute-done.2.a_ref = bf16[2096,128]{1,0:T(8,128)(2,1)S(1)} collective-permute-done((bf16[2096,128]{1,0:T(8,128)(2,1)S(1)}, bf16[2096,128]{1,0:T(8,128)(2,1)S(1)}, u32[]{:S(2)}, u32[]{:S(2)}) %collective-permute-start.2) | collective-permute-done | bytes 536608 | tf_op jit(solution)/shard_map/ppermute | solution.py:248
  31.3 6.5 %shard_map.75 = (bf16[128,2048]{1,0:T(8,128)(2,1)S(1)}, bf16[128,2048]{1,0:T(8,128)(2,1)S(1)}, f32[256,128]{1,0:T(8,128)S(1)}) custom-call(s32[3]{0:T(128)S(1)} %pad_add_fusion.place_ref, bf16[2096,128]{1,0:T(8,128)(2,1)S(1)} %collective-permute-done.2.a_ref, bf16[2096,128]{1,0:T(8,128)(2,1)S(1)} %collective-permute-done.3.b_ref, ...), custom_call_target="tpu_custom_call" | custom-call | flops 4831838208 | bytes 4194304 | tf_op jit(solution)/shard_map/pallas_call | solution.py:144
  37.8 1.6 collective-permute-start.4
  39.9 7.0 %shard_map.76 = (bf16[128,2048]{1,0:T(8,128)(2,1)S(1)}, bf16[128,2048]{1,0:T(8,128)(2,1)S(1)}) custom-call(bf16[128,2048]{1,0:T(8,128)(2,1)} %collective-permute-done.b_ref, bf16[128,2048]{1,0:T(8,128)(2,1)} %collective-permute-done.1.a_ref, f32[256,128]{1,0:T(8,128)S(1)} %get-tuple-element.45.share_ref, bf16[2,2048,768]{2,1,0:T(8,128)(2,1)S(1)} %copy-done.1, ...), custom_call_target="tpu_custom_call" | custom-call | flops 4831838208 | bytes 4194304 | tf_op jit(solution)/shard_map/pallas_call | solution.py:163
  46.9 1.6 collective-permute-start.10
  48.9 6.5 %shard_map.77 = (bf16[128,2048]{1,0:T(8,128)(2,1)S(1)}, bf16[128,2048]{1,0:T(8,128)(2,1)S(1)}, f32[256,128]{1,0:T(8,128)S(1)}) custom-call(s32[3]{0:T(128)S(1)} %pad_add_fusion.place_ref, bf16[2096,128]{1,0:T(8,128)(2,1)S(1)} %collective-permute-done.6.a_ref, bf16[2096,128]{1,0:T(8,128)(2,1)S(1)} %collective-permute-done.7.b_ref, ...), custom_call_target="tpu_custom_call" | custom-call | flops 4831838208 | bytes 4194304 | tf_op jit(solution)/shard_map/pallas_call | solution.py:144
  59.2 5.8 %shard_map.78 = (bf16[128,2048]{1,0:T(8,128)(2,1)S(1)}, bf16[128,2048]{1,0:T(8,128)(2,1)S(1)}) custom-call(bf16[128,2048]{1,0:T(8,128)(2,1)S(1)} %collective-permute-done.4.b_ref, bf16[128,2048]{1,0:T(8,128)(2,1)S(1)} %collective-permute-done.5.a_ref, f32[256,128]{1,0:T(8,128)S(1)} %get-tuple-element.52.share_ref, bf16[2,2048,768]{2,1,0:T(8,128)(2,1)S(1)} %copy-done.1, ...), custom_call_target="tpu_custom_call" | custom-call | flops 4831838208 | bytes 4194304 | tf_op jit(solution)/shard_map/pallas_call | solution.py:163
  65.0 2.1 %collective-permute-done.10.a_ref = bf16[2096,128]{1,0:T(8,128)(2,1)S(1)} collective-permute-done((bf16[2096,128]{1,0:T(8,128)(2,1)S(1)}, bf16[2096,128]{1,0:T(8,128)(2,1)S(1)}, u32[]{:S(2)}, u32[]{:S(2)}) %collective-permute-start.10) | collective-permute-done | bytes 536608 | tf_op jit(solution)/shard_map/ppermute | solution.py:248
  67.1 1.6 collective-permute-done.11.b_ref
  70.7 6.5 %shard_map.79 = (bf16[128,2048]{1,0:T(8,128)(2,1)S(1)}, bf16[128,2048]{1,0:T(8,128)(2,1)S(1)}, f32[256,128]{1,0:T(8,128)S(1)}) custom-call(s32[3]{0:T(128)S(1)} %pad_add_fusion.place_ref, bf16[2096,128]{1,0:T(8,128)(2,1)S(1)} %collective-permute-done.10.a_ref, bf16[2096,128]{1,0:T(8,128)(2,1)S(1)} %collective-permute-done.11.b_ref, ...), custom_call_target="tpu_custom_call" | custom-call | flops 4831838208 | bytes 4194304 | tf_op jit(solution)/shard_map/pallas_call | solution.py:144
  79.9 5.8 %shard_map.80 = (bf16[128,2048]{1,0:T(8,128)(2,1)S(1)}, bf16[128,2048]{1,0:T(8,128)(2,1)S(1)}) custom-call(bf16[128,2048]{1,0:T(8,128)(2,1)S(1)} %collective-permute-done.8.b_ref, bf16[128,2048]{1,0:T(8,128)(2,1)S(1)} %collective-permute-done.9.a_ref, f32[256,128]{1,0:T(8,128)S(1)} %get-tuple-element.59.share_ref, bf16[2,2048,768]{2,1,0:T(8,128)(2,1)S(1)} %copy-done.1, ...), custom_call_target="tpu_custom_call" | custom-call | flops 4831838208 | bytes 4194304 | tf_op jit(solution)/shard_map/pallas_call | solution.py:163
  85.7 1.6 collective-permute-start.12
  87.7 2.1 %collective-permute-done.15.a_ref = bf16[2096,128]{1,0:T(8,128)(2,1)S(1)} collective-permute-done((bf16[2096,128]{1,0:T(8,128)(2,1)S(1)}, bf16[2096,128]{1,0:T(8,128)(2,1)S(1)}, u32[]{:S(2)}, u32[]{:S(2)}) %collective-permute-start.15) | collective-permute-done | bytes 536608 | tf_op jit(solution)/shard_map/ppermute | solution.py:255
  91.4 6.5 %shard_map.82 = (bf16[128,2048]{1,0:T(8,128)(2,1)S(1)}, bf16[128,2048]{1,0:T(8,128)(2,1)S(1)}, f32[256,128]{1,0:T(8,128)}) custom-call(s32[3]{0:T(128)S(1)} %pad_add_fusion.place_ref, bf16[2096,128]{1,0:T(8,128)(2,1)S(1)} %collective-permute-done.15.a_ref, bf16[2096,128]{1,0:T(8,128)(2,1)S(1)} %collective-permute-done.16.b_ref, ...), custom_call_target="tpu_custom_call" | custom-call | flops 4831838208 | bytes 4194304 | tf_op jit(solution)/shard_map/pallas_call | solution.py:144
  98.8 1.6 collective-permute-start.13
  103.3 10.6 %collective-permute-done.17 = bf16[128,2048]{1,0:T(8,128)(2,1)S(1)} collective-permute-done((bf16[128,2048]{1,0:T(8,128)(2,1)S(1)}, bf16[128,2048]{1,0:T(8,128)(2,1)S(1)}, u32[]{:S(2)}, u32[]{:S(2)}) %collective-permute-start.17) | collective-permute-done | bytes 524320 | tf_op jit(solution)/shard_map/ppermute | solution.py:257
  114.5 7.5 %collective-permute-done.24 = bf16[128,2048]{1,0:T(8,128)(2,1)S(1)} collective-permute-done((bf16[128,2048]{1,0:T(8,128)(2,1)S(1)}, bf16[128,2048]{1,0:T(8,128)(2,1)S(1)}, u32[]{:S(2)}, u32[]{:S(2)}) %collective-permute-start.24) | collective-permute-done | bytes 524320 | tf_op jit(solution)/shard_map/ppermute | solution.py:257
  122.1 1.6 collective-permute-start.25
  123.9 1.6 collective-permute-start.14
  125.5 8.2 %collective-permute-done.18 = bf16[128,2048]{1,0:T(8,128)(2,1)S(1)} collective-permute-done((bf16[128,2048]{1,0:T(8,128)(2,1)S(1)}, bf16[128,2048]{1,0:T(8,128)(2,1)S(1)}, u32[]{:S(2)}, u32[]{:S(2)}) %collective-permute-start.18) | collective-permute-done | bytes 524320 | tf_op jit(solution)/shard_map/ppermute | solution.py:261
  134.3 2.7 %collective-permute-done.25 = bf16[128,2048]{1,0:T(8,128)(2,1)S(1)} collective-permute-done((bf16[128,2048]{1,0:T(8,128)(2,1)S(1)}, bf16[128,2048]{1,0:T(8,128)(2,1)S(1)}, u32[]{:S(2)}, u32[]{:S(2)}) %collective-permute-start.25) | collective-permute-done | bytes 524320 | tf_op jit(solution)/shard_map/ppermute | solution.py:260
  137.2 1.6 collective-permute-start.26
  139.4 9.3 %collective-permute-done.19 = bf16[128,2048]{1,0:T(8,128)(2,1)S(1)} collective-permute-done((bf16[128,2048]{1,0:T(8,128)(2,1)S(1)}, bf16[128,2048]{1,0:T(8,128)(2,1)S(1)}, u32[]{:S(2)}, u32[]{:S(2)}) %collective-permute-start.19) | collective-permute-done | bytes 524320 | tf_op jit(solution)/shard_map/ppermute | solution.py:261
  149.4 7.2 %collective-permute-done.26 = bf16[128,2048]{1,0:T(8,128)(2,1)S(1)} collective-permute-done((bf16[128,2048]{1,0:T(8,128)(2,1)S(1)}, bf16[128,2048]{1,0:T(8,128)(2,1)S(1)}, u32[]{:S(2)}, u32[]{:S(2)}) %collective-permute-start.26) | collective-permute-done | bytes 524320 | tf_op jit(solution)/shard_map/ppermute | solution.py:260
  156.7 1.6 collective-permute-start.27
  160.1 7.5 %collective-permute-done.20.refs_1_ = bf16[128,2048]{1,0:T(8,128)(2,1)S(1)} collective-permute-done((bf16[128,2048]{1,0:T(8,128)(2,1)S(1)}, bf16[128,2048]{1,0:T(8,128)(2,1)S(1)}, u32[]{:S(2)}, u32[]{:S(2)}) %collective-permute-start.20) | collective-permute-done | bytes 524320 | tf_op jit(solution)/shard_map/ppermute | solution.py:261
  (64 shorter events, 27.6 us)
Async XLA Ops:
  1.3 36.5 %collective-permute-start = (bf16[128,2048]{1,0:T(8,128)(2,1)S(1)}, bf16[128,2048]{1,0:T(8,128)(2,1)}, u32[]{:S(2)}, u32[]{:S(2)}) collective-permute-start(bf16[128,2048]{1,0:T(8,128)(2,1)S(1)} %get-tuple-element.73.b_ref), channel_id=1, source_target_pairs={{0,2},{2,4},{4,6},{6,7},{7,5},{5,3},{3,1},{1,0},{8,10},{10,12},{12... | collective-permute-start | bytes 1572872 | tf_op jit(solution)/shard_map/ppermute | solution.py:247
  4.4 33.4 %collective-permute-start.1 = (bf16[128,2048]{1,0:T(8,128)(2,1)S(1)}, bf16[128,2048]{1,0:T(8,128)(2,1)}, u32[]{:S(2)}, u32[]{:S(2)}) collective-permute-start(bf16[128,2048]{1,0:T(8,128)(2,1)S(1)} %get-tuple-element.74.a_ref), channel_id=1, source_target_pairs={{2,0},{4,2},{6,4},{7,6},{5,7},{3,5},{1,3},{0,1},{10,8},{12,10},{14... | collective-permute-start | bytes 1572872 | tf_op jit(solution)/shard_map/ppermute | solution.py:247
  6.0 21.7 %collective-permute-start.2 = (bf16[2096,128]{1,0:T(8,128)(2,1)S(1)}, bf16[2096,128]{1,0:T(8,128)(2,1)S(1)}, u32[]{:S(2)}, u32[]{:S(2)}) collective-permute-start(bf16[2096,128]{1,0:T(8,128)(2,1)S(1)} %get-tuple-element.39.a_ref), channel_id=1, source_target_pairs={{0,2},{2,4},{4,6},{6,7},{7,5},{5,3},{3,1},{1,0},{8,10},{10,12},{12... | collective-permute-start | bytes 1609736 | tf_op jit(solution)/shard_map/ppermute | solution.py:248
  8.1 21.2 %collective-permute-start.3 = (bf16[2096,128]{1,0:T(8,128)(2,1)S(1)}, bf16[2096,128]{1,0:T(8,128)(2,1)S(1)}, u32[]{:S(2)}, u32[]{:S(2)}) collective-permute-start(bf16[2096,128]{1,0:T(8,128)(2,1)S(1)} %get-tuple-element.40.b_ref), channel_id=1, source_target_pairs={{2,0},{4,2},{6,4},{7,6},{5,7},{3,5},{1,3},{0,1},{10,8},{12,10},{14... | collective-permute-start | bytes 1609736 | tf_op jit(solution)/shard_map/ppermute | solution.py:248
  8.8 2.8 %copy-start = (bf16[2,2048,768]{2,1,0:T(8,128)(2,1)S(1)}, bf16[2,2048,768]{2,1,0:T(8,128)(2,1)}, u32[]{:S(2)}) copy-start(bf16[2,2048,768]{2,1,0:T(8,128)(2,1)} %gate_ref.15) | copy-start | bytes 18874372
  17.2 14.1 %copy-start.1 = (bf16[2,2048,768]{2,1,0:T(8,128)(2,1)S(1)}, bf16[2,2048,768]{2,1,0:T(8,128)(2,1)}, u32[]{:S(2)}) copy-start(bf16[2,2048,768]{2,1,0:T(8,128)(2,1)} %gate_ref.15) | copy-start | bytes 18874372
  17.2 14.1 %copy-start.3 = (bf16[2,2048,768]{2,1,0:T(8,128)(2,1)S(1)}, bf16[2,2048,768]{2,1,0:T(8,128)(2,1)}, u32[]{:S(2)}) copy-start(bf16[2,2048,768]{2,1,0:T(8,128)(2,1)} %up_ref.15) | copy-start | bytes 18874372
  17.2 14.1 %copy-start.5 = (bf16[2,768,2048]{2,1,0:T(8,128)(2,1)S(1)}, bf16[2,768,2048]{2,1,0:T(8,128)(2,1)}, u32[]{:S(2)}) copy-start(bf16[2,768,2048]{2,1,0:T(8,128)(2,1)} %param.13) | copy-start | bytes 18874372
  29.2 17.6 %collective-permute-start.6 = (bf16[2096,128]{1,0:T(8,128)(2,1)S(1)}, bf16[2096,128]{1,0:T(8,128)(2,1)S(1)}, u32[]{:S(2)}, u32[]{:S(2)}) collective-permute-start(bf16[2096,128]{1,0:T(8,128)(2,1)S(1)} %collective-permute-done.2.a_ref), channel_id=1, source_target_pairs={{0,2},{2,4},{4,6},{6,7},{7,5},{5,3},{3,1},{1,0},{8,10},{10,12},{12... | collective-permute-start | bytes 1609736 | tf_op jit(solution)/shard_map/ppermute | solution.py:248
  30.8 16.0 %collective-permute-start.7 = (bf16[2096,128]{1,0:T(8,128)(2,1)S(1)}, bf16[2096,128]{1,0:T(8,128)(2,1)S(1)}, u32[]{:S(2)}, u32[]{:S(2)}) collective-permute-start(bf16[2096,128]{1,0:T(8,128)(2,1)S(1)} %collective-permute-done.3.b_ref), channel_id=1, source_target_pairs={{2,0},{4,2},{6,4},{7,6},{5,7},{3,5},{1,3},{0,1},{10,8},{12,10},{14... | collective-permute-start | bytes 1609736 | tf_op jit(solution)/shard_map/ppermute | solution.py:248
  37.8 17.8 %collective-permute-start.4 = (bf16[128,2048]{1,0:T(8,128)(2,1)}, bf16[128,2048]{1,0:T(8,128)(2,1)S(1)}, u32[]{:S(2)}, u32[]{:S(2)}) collective-permute-start(bf16[128,2048]{1,0:T(8,128)(2,1)} %collective-permute-done.b_ref), channel_id=1, source_target_pairs={{0,2},{2,4},{4,6},{6,7},{7,5},{5,3},{3,1},{1,0},{8,10},{10,12},{12... | collective-permute-start | bytes 1572872 | tf_op jit(solution)/shard_map/ppermute | solution.py:247
  39.4 17.8 %collective-permute-start.5 = (bf16[128,2048]{1,0:T(8,128)(2,1)}, bf16[128,2048]{1,0:T(8,128)(2,1)S(1)}, u32[]{:S(2)}, u32[]{:S(2)}) collective-permute-start(bf16[128,2048]{1,0:T(8,128)(2,1)} %collective-permute-done.1.a_ref), channel_id=1, source_target_pairs={{2,0},{4,2},{6,4},{7,6},{5,7},{3,5},{1,3},{0,1},{10,8},{12,10},{14... | collective-permute-start | bytes 1572872 | tf_op jit(solution)/shard_map/ppermute | solution.py:247
  46.9 20.2 %collective-permute-start.10 = (bf16[2096,128]{1,0:T(8,128)(2,1)S(1)}, bf16[2096,128]{1,0:T(8,128)(2,1)S(1)}, u32[]{:S(2)}, u32[]{:S(2)}) collective-permute-start(bf16[2096,128]{1,0:T(8,128)(2,1)S(1)} %collective-permute-done.6.a_ref), channel_id=1, source_target_pairs={{0,2},{2,4},{4,6},{6,7},{7,5},{5,3},{3,1},{1,0},{8,10},{10,12},{12... | collective-permute-start | bytes 1609736 | tf_op jit(solution)/shard_map/ppermute | solution.py:248
  48.5 20.2 %collective-permute-start.11 = (bf16[2096,128]{1,0:T(8,128)(2,1)S(1)}, bf16[2096,128]{1,0:T(8,128)(2,1)S(1)}, u32[]{:S(2)}, u32[]{:S(2)}) collective-permute-start(bf16[2096,128]{1,0:T(8,128)(2,1)S(1)} %collective-permute-done.7.b_ref), channel_id=1, source_target_pairs={{2,0},{4,2},{6,4},{7,6},{5,7},{3,5},{1,3},{0,1},{10,8},{12,10},{14... | collective-permute-start | bytes 1609736 | tf_op jit(solution)/shard_map/ppermute | solution.py:248
  57.2 21.2 %collective-permute-start.8 = (bf16[128,2048]{1,0:T(8,128)(2,1)S(1)}, bf16[128,2048]{1,0:T(8,128)(2,1)S(1)}, u32[]{:S(2)}, u32[]{:S(2)}) collective-permute-start(bf16[128,2048]{1,0:T(8,128)(2,1)S(1)} %collective-permute-done.4.b_ref), channel_id=1, source_target_pairs={{0,2},{2,4},{4,6},{6,7},{7,5},{5,3},{3,1},{1,0},{8,10},{10,12},{12... | collective-permute-start | bytes 1572872 | tf_op jit(solution)/shard_map/ppermute | solution.py:247
  58.7 21.2 %collective-permute-start.9 = (bf16[128,2048]{1,0:T(8,128)(2,1)S(1)}, bf16[128,2048]{1,0:T(8,128)(2,1)S(1)}, u32[]{:S(2)}, u32[]{:S(2)}) collective-permute-start(bf16[128,2048]{1,0:T(8,128)(2,1)S(1)} %collective-permute-done.5.a_ref), channel_id=1, source_target_pairs={{2,0},{4,2},{6,4},{7,6},{5,7},{3,5},{1,3},{0,1},{10,8},{12,10},{14... | collective-permute-start | bytes 1572872 | tf_op jit(solution)/shard_map/ppermute | solution.py:247
  68.7 21.2 %collective-permute-start.15 = (bf16[2096,128]{1,0:T(8,128)(2,1)S(1)}, bf16[2096,128]{1,0:T(8,128)(2,1)S(1)}, u32[]{:S(2)}, u32[]{:S(2)}) collective-permute-start(bf16[2096,128]{1,0:T(8,128)(2,1)S(1)} %collective-permute-done.10.a_ref), channel_id=1, source_target_pairs={{0,2},{2,4},{4,6},{6,7},{7,5},{5,3},{3,1},{1,0},{8,10},{10,12},{12... | collective-permute-start | bytes 1609736 | tf_op jit(solution)/shard_map/ppermute | solution.py:255
  70.2 21.2 %collective-permute-start.16 = (bf16[2096,128]{1,0:T(8,128)(2,1)S(1)}, bf16[2096,128]{1,0:T(8,128)(2,1)S(1)}, u32[]{:S(2)}, u32[]{:S(2)}) collective-permute-start(bf16[2096,128]{1,0:T(8,128)(2,1)S(1)} %collective-permute-done.11.b_ref), channel_id=1, source_target_pairs={{2,0},{4,2},{6,4},{7,6},{5,7},{3,5},{1,3},{0,1},{10,8},{12,10},{14... | collective-permute-start | bytes 1609736 | tf_op jit(solution)/shard_map/ppermute | solution.py:255
  85.7 13.0 %collective-permute-start.12 = (bf16[128,2048]{1,0:T(8,128)(2,1)S(1)}, bf16[128,2048]{1,0:T(8,128)(2,1)S(1)}, u32[]{:S(2)}, u32[]{:S(2)}) collective-permute-start(bf16[128,2048]{1,0:T(8,128)(2,1)S(1)} %get-tuple-element.62), channel_id=1, source_target_pairs={{0,2},{2,4},{4,6},{6,7},{7,5},{5,3},{3,1},{1,0},{8,10},{10,12},{12... | collective-permute-start | bytes 1572872 | tf_op jit(solution)/shard_map/ppermute | solution.py:262
  87.3 15.3 %collective-permute-start.21 = (bf16[128,2048]{1,0:T(8,128)(2,1)S(1)}, bf16[128,2048]{1,0:T(8,128)(2,1)S(1)}, u32[]{:S(2)}, u32[]{:S(2)}) collective-permute-start(bf16[128,2048]{1,0:T(8,128)(2,1)S(1)} %get-tuple-element.68), channel_id=1, source_target_pairs={{2,0},{4,2},{6,4},{7,6},{5,7},{3,5},{1,3},{0,1},{10,8},{12,10},{14... | collective-permute-start | bytes 1572872 | tf_op jit(solution)/shard_map/ppermute | solution.py:263
  97.9 16.0 %collective-permute-start.17 = (bf16[128,2048]{1,0:T(8,128)(2,1)S(1)}, bf16[128,2048]{1,0:T(8,128)(2,1)S(1)}, u32[]{:S(2)}, u32[]{:S(2)}) collective-permute-start(bf16[128,2048]{1,0:T(8,128)(2,1)S(1)} %get-tuple-element.66), channel_id=1, source_target_pairs={{2,0},{4,2},{6,4},{7,6},{5,7},{3,5},{1,3},{0,1},{10,8},{12,10},{14... | collective-permute-start | bytes 1572872 | tf_op jit(solution)/shard_map/ppermute | solution.py:257
  98.8 25.0 %collective-permute-start.13 = (bf16[128,2048]{1,0:T(8,128)(2,1)S(1)}, bf16[128,2048]{1,0:T(8,128)(2,1)S(1)}, u32[]{:S(2)}, u32[]{:S(2)}) collective-permute-start(bf16[128,2048]{1,0:T(8,128)(2,1)S(1)} %add_convert_fusion.9), channel_id=1, source_target_pairs={{0,2},{2,4},{4,6},{6,7},{7,5},{5,3},{3,1},{1,0},{8,10},{10,12},{12... | collective-permute-start | bytes 1572872 | tf_op jit(solution)/shard_map/ppermute | solution.py:262
  100.4 21.6 %collective-permute-start.24 = (bf16[128,2048]{1,0:T(8,128)(2,1)S(1)}, bf16[128,2048]{1,0:T(8,128)(2,1)S(1)}, u32[]{:S(2)}, u32[]{:S(2)}) collective-permute-start(bf16[128,2048]{1,0:T(8,128)(2,1)S(1)} %get-tuple-element.72), channel_id=1, source_target_pairs={{0,2},{2,4},{4,6},{6,7},{7,5},{5,3},{3,1},{1,0},{8,10},{10,12},{12... | collective-permute-start | bytes 1572872 | tf_op jit(solution)/shard_map/ppermute | solution.py:257
  102.8 36.0 %collective-permute-start.22 = (bf16[128,2048]{1,0:T(8,128)(2,1)S(1)}, bf16[128,2048]{1,0:T(8,128)(2,1)S(1)}, u32[]{:S(2)}, u32[]{:S(2)}) collective-permute-start(bf16[128,2048]{1,0:T(8,128)(2,1)S(1)} %add_convert_fusion.4), channel_id=1, source_target_pairs={{2,0},{4,2},{6,4},{7,6},{5,7},{3,5},{1,3},{0,1},{10,8},{12,10},{14... | collective-permute-start | bytes 1572872 | tf_op jit(solution)/shard_map/ppermute | solution.py:263
  114.0 19.7 %collective-permute-start.18 = (bf16[128,2048]{1,0:T(8,128)(2,1)S(1)}, bf16[128,2048]{1,0:T(8,128)(2,1)S(1)}, u32[]{:S(2)}, u32[]{:S(2)}) collective-permute-start(bf16[128,2048]{1,0:T(8,128)(2,1)S(1)} %add_convert_fusion.7), channel_id=1, source_target_pairs={{2,0},{4,2},{6,4},{7,6},{5,7},{3,5},{1,3},{0,1},{10,8},{12,10},{14... | collective-permute-start | bytes 1572872 | tf_op jit(solution)/shard_map/ppermute | solution.py:261
  122.1 14.9 %collective-permute-start.25 = (bf16[128,2048]{1,0:T(8,128)(2,1)S(1)}, bf16[128,2048]{1,0:T(8,128)(2,1)S(1)}, u32[]{:S(2)}, u32[]{:S(2)}) collective-permute-start(bf16[128,2048]{1,0:T(8,128)(2,1)S(1)} %add_convert_fusion.2), channel_id=1, source_target_pairs={{0,2},{2,4},{4,6},{6,7},{7,5},{5,3},{3,1},{1,0},{8,10},{10,12},{12... | collective-permute-start | bytes 1572872 | tf_op jit(solution)/shard_map/ppermute | solution.py:260
  123.9 34.4 %collective-permute-start.14 = (bf16[128,2048]{1,0:T(8,128)(2,1)S(1)}, bf16[128,2048]{1,0:T(8,128)(2,1)S(1)}, u32[]{:S(2)}, u32[]{:S(2)}) collective-permute-start(bf16[128,2048]{1,0:T(8,128)(2,1)S(1)} %add_convert_fusion.8), channel_id=1, source_target_pairs={{0,2},{2,4},{4,6},{6,7},{7,5},{5,3},{3,1},{1,0},{8,10},{10,12},{12... | collective-permute-start | bytes 1572872 | tf_op jit(solution)/shard_map/ppermute | solution.py:262
  133.8 14.9 %collective-permute-start.19 = (bf16[128,2048]{1,0:T(8,128)(2,1)S(1)}, bf16[128,2048]{1,0:T(8,128)(2,1)S(1)}, u32[]{:S(2)}, u32[]{:S(2)}) collective-permute-start(bf16[128,2048]{1,0:T(8,128)(2,1)S(1)} %add_convert_fusion.6), channel_id=1, source_target_pairs={{2,0},{4,2},{6,4},{7,6},{5,7},{3,5},{1,3},{0,1},{10,8},{12,10},{14... | collective-permute-start | bytes 1572872 | tf_op jit(solution)/shard_map/ppermute | solution.py:261
  137.2 19.4 %collective-permute-start.26 = (bf16[128,2048]{1,0:T(8,128)(2,1)S(1)}, bf16[128,2048]{1,0:T(8,128)(2,1)S(1)}, u32[]{:S(2)}, u32[]{:S(2)}) collective-permute-start(bf16[128,2048]{1,0:T(8,128)(2,1)S(1)} %add_convert_fusion.1), channel_id=1, source_target_pairs={{0,2},{2,4},{4,6},{6,7},{7,5},{5,3},{3,1},{1,0},{8,10},{10,12},{12... | collective-permute-start | bytes 1572872 | tf_op jit(solution)/shard_map/ppermute | solution.py:260
  138.9 21.0 %collective-permute-start.23 = (bf16[128,2048]{1,0:T(8,128)(2,1)S(1)}, bf16[128,2048]{1,0:T(8,128)(2,1)S(1)}, u32[]{:S(2)}, u32[]{:S(2)}) collective-permute-start(bf16[128,2048]{1,0:T(8,128)(2,1)S(1)} %add_convert_fusion.3), channel_id=1, source_target_pairs={{2,0},{4,2},{6,4},{7,6},{5,7},{3,5},{1,3},{0,1},{10,8},{12,10},{14... | collective-permute-start | bytes 1572872 | tf_op jit(solution)/shard_map/ppermute | solution.py:263
  148.9 18.8 %collective-permute-start.20 = (bf16[128,2048]{1,0:T(8,128)(2,1)S(1)}, bf16[128,2048]{1,0:T(8,128)(2,1)S(1)}, u32[]{:S(2)}, u32[]{:S(2)}) collective-permute-start(bf16[128,2048]{1,0:T(8,128)(2,1)S(1)} %add_convert_fusion.5), channel_id=1, source_target_pairs={{2,0},{4,2},{6,4},{7,6},{5,7},{3,5},{1,3},{0,1},{10,8},{12,10},{14... | collective-permute-start | bytes 1572872 | tf_op jit(solution)/shard_map/ppermute | solution.py:261
  156.7 10.9 %collective-permute-start.27 = (bf16[128,2048]{1,0:T(8,128)(2,1)S(1)}, bf16[128,2048]{1,0:T(8,128)(2,1)S(1)}, u32[]{:S(2)}, u32[]{:S(2)}) collective-permute-start(bf16[128,2048]{1,0:T(8,128)(2,1)S(1)} %add_convert_fusion), channel_id=1, source_target_pairs={{0,2},{2,4},{4,6},{6,7},{7,5},{5,3},{3,1},{1,0},{8,10},{10,12},{12... | collective-permute-start | bytes 1572872 | tf_op jit(solution)/shard_map/ppermute | solution.py:260
  (4 other events, 7.0 us)

commit v8 on v7

--- a/solution.py
+++ b/solution.py
@@ -20,8 +20,8 @@
     return walk
 
 
-def table_rows(slots):
-    return -(-2 * slots // 16) * 16
+def table_rows(top):
+    return -(-4 * top // 16) * 16
 
 
 def tiles(half, width):
@@ -32,7 +32,7 @@
             yield slice(i * 16, i * 16 + 16), slice(j * half, (j + 1) * half), slice(at, at + 16)
 
 
-def pack_kernel(slots, a_ref, b_ref, target_ref, weight_ref, out_a_ref, out_b_ref):
+def pack_kernel(a_ref, b_ref, target_ref, weight_ref, out_a_ref, out_b_ref):
     half, width = a_ref.shape
     for rows, columns, packed in tiles(half, width):
         out_a_ref[packed, :] = a_ref[rows, columns]
@@ -40,38 +40,39 @@
     weight = weight_ref[...]
     share = weight / jnp.sum(weight, axis=0, keepdims=True)
     target = target_ref[...]
-    row = lax.broadcasted_iota(jnp.int32, (table_rows(slots), half), 0)
-    block = jnp.zeros(row.shape, jnp.float32)
-    for slot in range(slots):
-        value = jnp.sum(jnp.where(target == slot, share, 0.0), axis=0, keepdims=True)
-        block = jnp.where(row == slot, value[:, :half], block)
-        block = jnp.where(row == slots + slot, value[:, half:], block)
-    out_a_ref[width:, :] = block.astype(jnp.bfloat16)
-    out_b_ref[width:, :] = block.astype(jnp.bfloat16)
-
-
-def pack(a, b, target, router_weight, slots):
+    top = target.shape[0]
+    slot = target.astype(jnp.float32)
+    lines = [part[:, i * half:(i + 1) * half] for i in range(2) for part in (slot, share)]
+    spare = table_rows(top) - 4 * top
+    if spare:
+        lines.append(jnp.zeros((spare, half), jnp.float32))
+    block = jnp.concatenate(lines, axis=0).astype(jnp.bfloat16)
+    out_a_ref[width:, :] = block
+    out_b_ref[width:, :] = block
+
+
+def pack(a, b, target, router_weight):
     half, width = a.shape
     vmem = pl.BlockSpec(memory_space=pltpu.VMEM)
     return pl.pallas_call(
-        functools.partial(pack_kernel, slots),
+        pack_kernel,
         in_specs=[vmem] * 4,
         out_specs=[vmem] * 2,
-        out_shape=[jax.ShapeDtypeStruct((width + table_rows(slots), half), jnp.bfloat16)] * 2,
+        out_shape=[jax.ShapeDtypeStruct((width + table_rows(target.shape[1]), half), jnp.bfloat16)] * 2,
         compiler_params=pltpu.CompilerParams(vmem_limit_bytes=VMEM_LIMIT),
         cost_estimate=pl.CostEstimate(flops=0, bytes_accessed=8 * half * width, transcendentals=0),
     )(a, b, target.T, router_weight.T)
 
 
-def columns(place_ref, lead_ref, index, slots, owned):
+def columns(place_ref, lead_ref, index, top, owned):
     rows, half = lead_ref.shape
-    extra = table_rows(slots)
     me, after, pick = place_ref[0], place_ref[1], place_ref[2]
-    block = lead_ref[rows - extra:, :].astype(jnp.float32)
-    row = lax.broadcasted_iota(jnp.int32, block.shape, 0)
+    block = lead_ref[rows - table_rows(top):, :].astype(jnp.float32)
+    named = block[2 * index * top:(2 * index + 1) * top, :]
+    share = block[(2 * index + 1) * top:(2 * index + 2) * top, :]
 
     def column(slot):
-        return jnp.sum(jnp.where(row == index * slots + slot, block, 0.0), axis=0, keepdims=True)
+        return jnp.sum(jnp.where(named == slot.astype(jnp.float32), share, 0.0), axis=0, keepdims=True)
 
     lent = column(after * (owned + 1) + owned)
     line_of = lax.broadcasted_iota(jnp.int32, (128, half), 0)
@@ -110,7 +111,7 @@
     lax.fori_loop(0, width // wide, fold, 0)
 
 
-def lead_kernel(slots, place_ref, a_ref, b_ref, gate_ref, up_ref, down_ref, *refs):
+def lead_kernel(top, place_ref, a_ref, b_ref, gate_ref, up_ref, down_ref, *refs):
     out_a_ref, out_b_ref, other_ref, rows_ref, share_ref, hidden_ref = refs[-6:]
     owned = gate_ref.shape[0]
     half, width = out_a_ref.shape
@@ -118,8 +119,8 @@
         at = slice(i * half, (i + 1) * half)
         for rows, across, packed in tiles(half, width):
             rows_ref[i * half + rows.start:i * half + rows.stop, across] = ref[packed, :]
-        share_ref[at, :] = columns(place_ref, ref, i, slots, owned)
-        other_ref[at, :] = columns(place_ref, ref, 1 - i, slots, owned)
+        share_ref[at, :] = columns(place_ref, ref, i, top, owned)
+        other_ref[at, :] = columns(place_ref, ref, 1 - i, top, owned)
     evaluate(rows_ref, share_ref, gate_ref, up_ref, down_ref, (out_a_ref, out_b_ref), hidden_ref)
 
 
@@ -137,12 +138,12 @@
     )
 
 
-def lead(place, weights, slots, a, b, earlier=()):
+def lead(place, weights, top, a, b, earlier=()):
     half, (owned, width, units) = a.shape[1], weights[0].shape
     height = 2 * half
     vmem = pl.BlockSpec(memory_space=pltpu.VMEM)
     return pl.pallas_call(
-        functools.partial(lead_kernel, slots),
+        functools.partial(lead_kernel, top),
         in_specs=[pl.BlockSpec(memory_space=pltpu.SMEM)] + [vmem] * 5 + [pl.BlockSpec(memory_space=pl.ANY)] * len(earlier),
         out_specs=[vmem] * 3,
         out_shape=[jax.ShapeDtypeStruct((half, width), jnp.bfloat16)] * 2
@@ -228,7 +229,6 @@
     height, width = tokens.shape
     half = height // 2
     groups = lax.axis_size("expert")
-    slots = groups * (w_gate.shape[0] + 1)
     walk = ring_order(groups)
     ahead = [(walk[i], walk[(i + 1) % groups]) for i in range(groups)]
     back = [(b, a) for a, b in ahead]
@@ -239,8 +239,8 @@
     far = groups // 2
 
     a, b = tokens[:half], tokens[half:]
-    lead_a, lead_b = pack(a, b, target, router_weight, slots)
-    run = functools.partial(lead, place, weights, slots)
+    lead_a, lead_b = pack(a, b, target, router_weight)
+    run = functools.partial(lead, place, weights, target.shape[1])
     own_a, own_b, ended = run(lead_a, lead_b)
     parts = {}
     for s in range(1, far):

time: 169 us -> 169 us (level)
  no operation moved by 1% of the time
where the time goes in v8:
time: 169 us; the launch traced here: 168 us
  waiting for transfers between devices  72.7 us (43%)
  Pallas kernels  52.2 us (31%)
  starting transfers between devices  30.2 us (18%)
  local copies, waits for them, and re-layouts  11 us (7%)
    pallas_call x5, Pallas kernels, lead(): pl.pallas_call(functools.partial(lead_kernel, top), in_specs=[pl.BlockSpe...  32.2 us
    ppermute x3, waiting for transfers between devices, body(): lead_a = lax.ppermute(add(lead_part_a, lead_a), 'expert', back)  25 us
    pallas_call x3, Pallas kernels, plain(): pl.pallas_call(plain_kernel, in_specs=[vmem] * 6, out_specs=[vmem] * 2, o...  18.5 us
    ppermute x1, waiting for transfers between devices, body(): lax.ppermute(far_a, 'expert', back)  10.6 us
    ppermute x3, waiting for transfers between devices, body(): lead_b = lax.ppermute(add(lead_part_b, lead_b), 'expert', ahead)  9.94 us
    unnamed x16, local copies, waits for them, and re-layouts  9.76 us
    ppermute x4, waiting for transfers between devices, body(): lax.ppermute(lead_a, 'expert', ahead)  8.03 us
    ppermute x1, waiting for transfers between devices, body(): lax.ppermute(far_b, 'expert', ahead)  7.49 us
  transfers between devices with their start and end apart: 28, of which 20 were waited for; matrix products, arithmetic and copies ran while one was open for 1% of the time, Pallas kernels for 30%

profile of v8, /device:TPU:0, one launch (start us, length us, event | category | flops | bytes accessed | tf_op | source)
XLA Modules:
  0.0 168.5 jit_solution(7319168794981468846)
XLA Ops:
  1.3 3.1 %collective-permute-start = (bf16[128,2048]{1,0:T(8,128)(2,1)S(1)}, bf16[128,2048]{1,0:T(8,128)(2,1)}, u32[]{:S(2)}, u32[]{:S(2)}) collective-permute-start(bf16[128,2048]{1,0:T(8,128)(2,1)S(1)} %get-tuple-element.73.b_ref), channel_id=1, source_target_pairs={{0,2},{2,4},{4,6},{6,7},{7,5},{5,3},{3,1},{1,0},{8,10},{10,12},{12... | collective-permute-start | bytes 1572872 | tf_op jit(solution)/shard_map/ppermute | solution.py:247
  5.9 2.1 %collective-permute-start.2 = (bf16[2080,128]{1,0:T(8,128)(2,1)S(1)}, bf16[2080,128]{1,0:T(8,128)(2,1)S(1)}, u32[]{:S(2)}, u32[]{:S(2)}) collective-permute-start(bf16[2080,128]{1,0:T(8,128)(2,1)S(1)} %get-tuple-element.39.a_ref), channel_id=1, source_target_pairs={{0,2},{2,4},{4,6},{6,7},{7,5},{5,3},{3,1},{1,0},{8,10},{10,12},{12... | collective-permute-start | bytes 1597448 | tf_op jit(solution)/shard_map/ppermute | solution.py:248
  8.8 2.8 %copy-done = bf16[2,2048,768]{2,1,0:T(8,128)(2,1)S(1)} copy-done((bf16[2,2048,768]{2,1,0:T(8,128)(2,1)S(1)}, bf16[2,2048,768]{2,1,0:T(8,128)(2,1)}, u32[]{:S(2)}) %copy-start) | copy-done | bytes 6291480
  11.5 2.8 %copy-done.2 = bf16[2,2048,768]{2,1,0:T(8,128)(2,1)S(1)} copy-done((bf16[2,2048,768]{2,1,0:T(8,128)(2,1)S(1)}, bf16[2,2048,768]{2,1,0:T(8,128)(2,1)}, u32[]{:S(2)}) %copy-start.2) | copy-done | bytes 6291480
  14.3 2.8 %copy-done.4 = bf16[2,768,2048]{2,1,0:T(8,128)(2,1)S(1)} copy-done((bf16[2,768,2048]{2,1,0:T(8,128)(2,1)S(1)}, bf16[2,768,2048]{2,1,0:T(8,128)(2,1)}, u32[]{:S(2)}) %copy-start.4) | copy-done | bytes 6291480
  17.1 6.4 %shard_map.74 = (bf16[128,2048]{1,0:T(8,128)(2,1)S(1)}, bf16[128,2048]{1,0:T(8,128)(2,1)S(1)}, f32[256,128]{1,0:T(8,128)S(1)}) custom-call(s32[3]{0:T(128)S(1)} %pad_add_fusion.place_ref, bf16[2080,128]{1,0:T(8,128)(2,1)S(1)} %get-tuple-element.39.a_ref, bf16[2080,128]{1,0:T(8,128)(2,1)S(1)} %get-tuple-element.40.b_ref, bf16[2,2048,768]{2,1,0:T(8,128)(2,1)S(1)} %copy-done, ...), custom_call_target="tpu_custom_call" | custom-call | flops 4831838208 | bytes 4194304 | tf_op jit(solution)/shard_map/pallas_call | solution.py:145
  23.6 4.0 %collective-permute-done.2.a_ref = bf16[2080,128]{1,0:T(8,128)(2,1)S(1)} collective-permute-done((bf16[2080,128]{1,0:T(8,128)(2,1)S(1)}, bf16[2080,128]{1,0:T(8,128)(2,1)S(1)}, u32[]{:S(2)}, u32[]{:S(2)}) %collective-permute-start.2) | collective-permute-done | bytes 532512 | tf_op jit(solution)/shard_map/ppermute | solution.py:248
  29.1 1.6 collective-permute-start.6
  31.2 6.4 %shard_map.75 = (bf16[128,2048]{1,0:T(8,128)(2,1)S(1)}, bf16[128,2048]{1,0:T(8,128)(2,1)S(1)}, f32[256,128]{1,0:T(8,128)S(1)}) custom-call(s32[3]{0:T(128)S(1)} %pad_add_fusion.place_ref, bf16[2080,128]{1,0:T(8,128)(2,1)S(1)} %collective-permute-done.2.a_ref, bf16[2080,128]{1,0:T(8,128)(2,1)S(1)} %collective-permute-done.3.b_ref, ...), custom_call_target="tpu_custom_call" | custom-call | flops 4831838208 | bytes 4194304 | tf_op jit(solution)/shard_map/pallas_call | solution.py:145
  37.6 1.6 collective-permute-start.4
  39.7 7.0 %shard_map.76 = (bf16[128,2048]{1,0:T(8,128)(2,1)S(1)}, bf16[128,2048]{1,0:T(8,128)(2,1)S(1)}) custom-call(bf16[128,2048]{1,0:T(8,128)(2,1)} %collective-permute-done.b_ref, bf16[128,2048]{1,0:T(8,128)(2,1)} %collective-permute-done.1.a_ref, f32[256,128]{1,0:T(8,128)S(1)} %get-tuple-element.45.share_ref, bf16[2,2048,768]{2,1,0:T(8,128)(2,1)S(1)} %copy-done.1, ...), custom_call_target="tpu_custom_call" | custom-call | flops 4831838208 | bytes 4194304 | tf_op jit(solution)/shard_map/pallas_call | solution.py:164
  46.7 1.6 collective-permute-start.10
  48.8 6.4 %shard_map.77 = (bf16[128,2048]{1,0:T(8,128)(2,1)S(1)}, bf16[128,2048]{1,0:T(8,128)(2,1)S(1)}, f32[256,128]{1,0:T(8,128)S(1)}) custom-call(s32[3]{0:T(128)S(1)} %pad_add_fusion.place_ref, bf16[2080,128]{1,0:T(8,128)(2,1)S(1)} %collective-permute-done.6.a_ref, bf16[2080,128]{1,0:T(8,128)(2,1)S(1)} %collective-permute-done.7.b_ref, ...), custom_call_target="tpu_custom_call" | custom-call | flops 4831838208 | bytes 4194304 | tf_op jit(solution)/shard_map/pallas_call | solution.py:145
  59.0 5.8 %shard_map.78 = (bf16[128,2048]{1,0:T(8,128)(2,1)S(1)}, bf16[128,2048]{1,0:T(8,128)(2,1)S(1)}) custom-call(bf16[128,2048]{1,0:T(8,128)(2,1)S(1)} %collective-permute-done.4.b_ref, bf16[128,2048]{1,0:T(8,128)(2,1)S(1)} %collective-permute-done.5.a_ref, f32[256,128]{1,0:T(8,128)S(1)} %get-tuple-element.52.share_ref, bf16[2,2048,768]{2,1,0:T(8,128)(2,1)S(1)} %copy-done.1, ...), custom_call_target="tpu_custom_call" | custom-call | flops 4831838208 | bytes 4194304 | tf_op jit(solution)/shard_map/pallas_call | solution.py:164
  64.8 2.0 %collective-permute-done.10.a_ref = bf16[2080,128]{1,0:T(8,128)(2,1)S(1)} collective-permute-done((bf16[2080,128]{1,0:T(8,128)(2,1)S(1)}, bf16[2080,128]{1,0:T(8,128)(2,1)S(1)}, u32[]{:S(2)}, u32[]{:S(2)}) %collective-permute-start.10) | collective-permute-done | bytes 532512 | tf_op jit(solution)/shard_map/ppermute | solution.py:248
  70.4 6.4 %shard_map.79 = (bf16[128,2048]{1,0:T(8,128)(2,1)S(1)}, bf16[128,2048]{1,0:T(8,128)(2,1)S(1)}, f32[256,128]{1,0:T(8,128)S(1)}) custom-call(s32[3]{0:T(128)S(1)} %pad_add_fusion.place_ref, bf16[2080,128]{1,0:T(8,128)(2,1)S(1)} %collective-permute-done.10.a_ref, bf16[2080,128]{1,0:T(8,128)(2,1)S(1)} %collective-permute-done.11.b_ref, ...), custom_call_target="tpu_custom_call" | custom-call | flops 4831838208 | bytes 4194304 | tf_op jit(solution)/shard_map/pallas_call | solution.py:145
  79.6 5.8 %shard_map.80 = (bf16[128,2048]{1,0:T(8,128)(2,1)S(1)}, bf16[128,2048]{1,0:T(8,128)(2,1)S(1)}) custom-call(bf16[128,2048]{1,0:T(8,128)(2,1)S(1)} %collective-permute-done.8.b_ref, bf16[128,2048]{1,0:T(8,128)(2,1)S(1)} %collective-permute-done.9.a_ref, f32[256,128]{1,0:T(8,128)S(1)} %get-tuple-element.59.share_ref, bf16[2,2048,768]{2,1,0:T(8,128)(2,1)S(1)} %copy-done.1, ...), custom_call_target="tpu_custom_call" | custom-call | flops 4831838208 | bytes 4194304 | tf_op jit(solution)/shard_map/pallas_call | solution.py:164
  85.4 1.6 collective-permute-start.12
  87.5 2.0 %collective-permute-done.15.a_ref = bf16[2080,128]{1,0:T(8,128)(2,1)S(1)} collective-permute-done((bf16[2080,128]{1,0:T(8,128)(2,1)S(1)}, bf16[2080,128]{1,0:T(8,128)(2,1)S(1)}, u32[]{:S(2)}, u32[]{:S(2)}) %collective-permute-start.15) | collective-permute-done | bytes 532512 | tf_op jit(solution)/shard_map/ppermute | solution.py:255
  91.1 6.4 %shard_map.82 = (bf16[128,2048]{1,0:T(8,128)(2,1)S(1)}, bf16[128,2048]{1,0:T(8,128)(2,1)S(1)}, f32[256,128]{1,0:T(8,128)}) custom-call(s32[3]{0:T(128)S(1)} %pad_add_fusion.place_ref, bf16[2080,128]{1,0:T(8,128)(2,1)S(1)} %collective-permute-done.15.a_ref, bf16[2080,128]{1,0:T(8,128)(2,1)S(1)} %collective-permute-done.16.b_ref, ...), custom_call_target="tpu_custom_call" | custom-call | flops 4831838208 | bytes 4194304 | tf_op jit(solution)/shard_map/pallas_call | solution.py:145
  98.5 1.6 collective-permute-start.13
  102.9 10.6 %collective-permute-done.17 = bf16[128,2048]{1,0:T(8,128)(2,1)S(1)} collective-permute-done((bf16[128,2048]{1,0:T(8,128)(2,1)S(1)}, bf16[128,2048]{1,0:T(8,128)(2,1)S(1)}, u32[]{:S(2)}, u32[]{:S(2)}) %collective-permute-start.17) | collective-permute-done | bytes 524320 | tf_op jit(solution)/shard_map/ppermute | solution.py:257
  114.2 7.5 %collective-permute-done.24 = bf16[128,2048]{1,0:T(8,128)(2,1)S(1)} collective-permute-done((bf16[128,2048]{1,0:T(8,128)(2,1)S(1)}, bf16[128,2048]{1,0:T(8,128)(2,1)S(1)}, u32[]{:S(2)}, u32[]{:S(2)}) %collective-permute-start.24) | collective-permute-done | bytes 524320 | tf_op jit(solution)/shard_map/ppermute | solution.py:257
  121.8 1.6 collective-permute-start.25
  123.5 1.6 collective-permute-start.14
  125.2 8.2 %collective-permute-done.18 = bf16[128,2048]{1,0:T(8,128)(2,1)S(1)} collective-permute-done((bf16[128,2048]{1,0:T(8,128)(2,1)S(1)}, bf16[128,2048]{1,0:T(8,128)(2,1)S(1)}, u32[]{:S(2)}, u32[]{:S(2)}) %collective-permute-start.18) | collective-permute-done | bytes 524320 | tf_op jit(solution)/shard_map/ppermute | solution.py:261
  134.0 2.7 %collective-permute-done.25 = bf16[128,2048]{1,0:T(8,128)(2,1)S(1)} collective-permute-done((bf16[128,2048]{1,0:T(8,128)(2,1)S(1)}, bf16[128,2048]{1,0:T(8,128)(2,1)S(1)}, u32[]{:S(2)}, u32[]{:S(2)}) %collective-permute-start.25) | collective-permute-done | bytes 524320 | tf_op jit(solution)/shard_map/ppermute | solution.py:260
  136.8 1.6 collective-permute-start.26
  139.1 9.3 %collective-permute-done.19 = bf16[128,2048]{1,0:T(8,128)(2,1)S(1)} collective-permute-done((bf16[128,2048]{1,0:T(8,128)(2,1)S(1)}, bf16[128,2048]{1,0:T(8,128)(2,1)S(1)}, u32[]{:S(2)}, u32[]{:S(2)}) %collective-permute-start.19) | collective-permute-done | bytes 524320 | tf_op jit(solution)/shard_map/ppermute | solution.py:261
  149.0 7.2 %collective-permute-done.26 = bf16[128,2048]{1,0:T(8,128)(2,1)S(1)} collective-permute-done((bf16[128,2048]{1,0:T(8,128)(2,1)S(1)}, bf16[128,2048]{1,0:T(8,128)(2,1)S(1)}, u32[]{:S(2)}, u32[]{:S(2)}) %collective-permute-start.26) | collective-permute-done | bytes 524320 | tf_op jit(solution)/shard_map/ppermute | solution.py:260
  156.3 1.6 collective-permute-start.27
  159.7 7.5 %collective-permute-done.20.refs_1_ = bf16[128,2048]{1,0:T(8,128)(2,1)S(1)} collective-permute-done((bf16[128,2048]{1,0:T(8,128)(2,1)S(1)}, bf16[128,2048]{1,0:T(8,128)(2,1)S(1)}, u32[]{:S(2)}, u32[]{:S(2)}) %collective-permute-start.20) | collective-permute-done | bytes 524320 | tf_op jit(solution)/shard_map/ppermute | solution.py:261
  (64 shorter events, 27.6 us)
Async XLA Ops:
  1.3 36.3 %collective-permute-start = (bf16[128,2048]{1,0:T(8,128)(2,1)S(1)}, bf16[128,2048]{1,0:T(8,128)(2,1)}, u32[]{:S(2)}, u32[]{:S(2)}) collective-permute-start(bf16[128,2048]{1,0:T(8,128)(2,1)S(1)} %get-tuple-element.73.b_ref), channel_id=1, source_target_pairs={{0,2},{2,4},{4,6},{6,7},{7,5},{5,3},{3,1},{1,0},{8,10},{10,12},{12... | collective-permute-start | bytes 1572872 | tf_op jit(solution)/shard_map/ppermute | solution.py:247
  4.4 33.3 %collective-permute-start.1 = (bf16[128,2048]{1,0:T(8,128)(2,1)S(1)}, bf16[128,2048]{1,0:T(8,128)(2,1)}, u32[]{:S(2)}, u32[]{:S(2)}) collective-permute-start(bf16[128,2048]{1,0:T(8,128)(2,1)S(1)} %get-tuple-element.74.a_ref), channel_id=1, source_target_pairs={{2,0},{4,2},{6,4},{7,6},{5,7},{3,5},{1,3},{0,1},{10,8},{12,10},{14... | collective-permute-start | bytes 1572872 | tf_op jit(solution)/shard_map/ppermute | solution.py:247
  5.9 21.7 %collective-permute-start.2 = (bf16[2080,128]{1,0:T(8,128)(2,1)S(1)}, bf16[2080,128]{1,0:T(8,128)(2,1)S(1)}, u32[]{:S(2)}, u32[]{:S(2)}) collective-permute-start(bf16[2080,128]{1,0:T(8,128)(2,1)S(1)} %get-tuple-element.39.a_ref), channel_id=1, source_target_pairs={{0,2},{2,4},{4,6},{6,7},{7,5},{5,3},{3,1},{1,0},{8,10},{10,12},{12... | collective-permute-start | bytes 1597448 | tf_op jit(solution)/shard_map/ppermute | solution.py:248
  8.0 21.1 %collective-permute-start.3 = (bf16[2080,128]{1,0:T(8,128)(2,1)S(1)}, bf16[2080,128]{1,0:T(8,128)(2,1)S(1)}, u32[]{:S(2)}, u32[]{:S(2)}) collective-permute-start(bf16[2080,128]{1,0:T(8,128)(2,1)S(1)} %get-tuple-element.40.b_ref), channel_id=1, source_target_pairs={{2,0},{4,2},{6,4},{7,6},{5,7},{3,5},{1,3},{0,1},{10,8},{12,10},{14... | collective-permute-start | bytes 1597448 | tf_op jit(solution)/shard_map/ppermute | solution.py:248
  8.7 2.8 %copy-start = (bf16[2,2048,768]{2,1,0:T(8,128)(2,1)S(1)}, bf16[2,2048,768]{2,1,0:T(8,128)(2,1)}, u32[]{:S(2)}) copy-start(bf16[2,2048,768]{2,1,0:T(8,128)(2,1)} %gate_ref.15) | copy-start | bytes 18874372
  17.1 14.1 %copy-start.1 = (bf16[2,2048,768]{2,1,0:T(8,128)(2,1)S(1)}, bf16[2,2048,768]{2,1,0:T(8,128)(2,1)}, u32[]{:S(2)}) copy-start(bf16[2,2048,768]{2,1,0:T(8,128)(2,1)} %gate_ref.15) | copy-start | bytes 18874372
  17.1 14.1 %copy-start.3 = (bf16[2,2048,768]{2,1,0:T(8,128)(2,1)S(1)}, bf16[2,2048,768]{2,1,0:T(8,128)(2,1)}, u32[]{:S(2)}) copy-start(bf16[2,2048,768]{2,1,0:T(8,128)(2,1)} %up_ref.15) | copy-start | bytes 18874372
  17.1 14.1 %copy-start.5 = (bf16[2,768,2048]{2,1,0:T(8,128)(2,1)S(1)}, bf16[2,768,2048]{2,1,0:T(8,128)(2,1)}, u32[]{:S(2)}) copy-start(bf16[2,768,2048]{2,1,0:T(8,128)(2,1)} %param.13) | copy-start | bytes 18874372
  29.1 17.6 %collective-permute-start.6 = (bf16[2080,128]{1,0:T(8,128)(2,1)S(1)}, bf16[2080,128]{1,0:T(8,128)(2,1)S(1)}, u32[]{:S(2)}, u32[]{:S(2)}) collective-permute-start(bf16[2080,128]{1,0:T(8,128)(2,1)S(1)} %collective-permute-done.2.a_ref), channel_id=1, source_target_pairs={{0,2},{2,4},{4,6},{6,7},{7,5},{5,3},{3,1},{1,0},{8,10},{10,12},{12... | collective-permute-start | bytes 1597448 | tf_op jit(solution)/shard_map/ppermute | solution.py:248
  30.7 16.0 %collective-permute-start.7 = (bf16[2080,128]{1,0:T(8,128)(2,1)S(1)}, bf16[2080,128]{1,0:T(8,128)(2,1)S(1)}, u32[]{:S(2)}, u32[]{:S(2)}) collective-permute-start(bf16[2080,128]{1,0:T(8,128)(2,1)S(1)} %collective-permute-done.3.b_ref), channel_id=1, source_target_pairs={{2,0},{4,2},{6,4},{7,6},{5,7},{3,5},{1,3},{0,1},{10,8},{12,10},{14... | collective-permute-start | bytes 1597448 | tf_op jit(solution)/shard_map/ppermute | solution.py:248
  37.6 17.8 %collective-permute-start.4 = (bf16[128,2048]{1,0:T(8,128)(2,1)}, bf16[128,2048]{1,0:T(8,128)(2,1)S(1)}, u32[]{:S(2)}, u32[]{:S(2)}) collective-permute-start(bf16[128,2048]{1,0:T(8,128)(2,1)} %collective-permute-done.b_ref), channel_id=1, source_target_pairs={{0,2},{2,4},{4,6},{6,7},{7,5},{5,3},{3,1},{1,0},{8,10},{10,12},{12... | collective-permute-start | bytes 1572872 | tf_op jit(solution)/shard_map/ppermute | solution.py:247
  39.3 17.7 %collective-permute-start.5 = (bf16[128,2048]{1,0:T(8,128)(2,1)}, bf16[128,2048]{1,0:T(8,128)(2,1)S(1)}, u32[]{:S(2)}, u32[]{:S(2)}) collective-permute-start(bf16[128,2048]{1,0:T(8,128)(2,1)} %collective-permute-done.1.a_ref), channel_id=1, source_target_pairs={{2,0},{4,2},{6,4},{7,6},{5,7},{3,5},{1,3},{0,1},{10,8},{12,10},{14... | collective-permute-start | bytes 1572872 | tf_op jit(solution)/shard_map/ppermute | solution.py:247
  46.7 20.1 %collective-permute-start.10 = (bf16[2080,128]{1,0:T(8,128)(2,1)S(1)}, bf16[2080,128]{1,0:T(8,128)(2,1)S(1)}, u32[]{:S(2)}, u32[]{:S(2)}) collective-permute-start(bf16[2080,128]{1,0:T(8,128)(2,1)S(1)} %collective-permute-done.6.a_ref), channel_id=1, source_target_pairs={{0,2},{2,4},{4,6},{6,7},{7,5},{5,3},{3,1},{1,0},{8,10},{10,12},{12... | collective-permute-start | bytes 1597448 | tf_op jit(solution)/shard_map/ppermute | solution.py:248
  48.4 20.0 %collective-permute-start.11 = (bf16[2080,128]{1,0:T(8,128)(2,1)S(1)}, bf16[2080,128]{1,0:T(8,128)(2,1)S(1)}, u32[]{:S(2)}, u32[]{:S(2)}) collective-permute-start(bf16[2080,128]{1,0:T(8,128)(2,1)S(1)} %collective-permute-done.7.b_ref), channel_id=1, source_target_pairs={{2,0},{4,2},{6,4},{7,6},{5,7},{3,5},{1,3},{0,1},{10,8},{12,10},{14... | collective-permute-start | bytes 1597448 | tf_op jit(solution)/shard_map/ppermute | solution.py:248
  57.0 21.1 %collective-permute-start.8 = (bf16[128,2048]{1,0:T(8,128)(2,1)S(1)}, bf16[128,2048]{1,0:T(8,128)(2,1)S(1)}, u32[]{:S(2)}, u32[]{:S(2)}) collective-permute-start(bf16[128,2048]{1,0:T(8,128)(2,1)S(1)} %collective-permute-done.4.b_ref), channel_id=1, source_target_pairs={{0,2},{2,4},{4,6},{6,7},{7,5},{5,3},{3,1},{1,0},{8,10},{10,12},{12... | collective-permute-start | bytes 1572872 | tf_op jit(solution)/shard_map/ppermute | solution.py:247
  58.6 21.1 %collective-permute-start.9 = (bf16[128,2048]{1,0:T(8,128)(2,1)S(1)}, bf16[128,2048]{1,0:T(8,128)(2,1)S(1)}, u32[]{:S(2)}, u32[]{:S(2)}) collective-permute-start(bf16[128,2048]{1,0:T(8,128)(2,1)S(1)} %collective-permute-done.5.a_ref), channel_id=1, source_target_pairs={{2,0},{4,2},{6,4},{7,6},{5,7},{3,5},{1,3},{0,1},{10,8},{12,10},{14... | collective-permute-start | bytes 1572872 | tf_op jit(solution)/shard_map/ppermute | solution.py:247
  68.4 21.1 %collective-permute-start.15 = (bf16[2080,128]{1,0:T(8,128)(2,1)S(1)}, bf16[2080,128]{1,0:T(8,128)(2,1)S(1)}, u32[]{:S(2)}, u32[]{:S(2)}) collective-permute-start(bf16[2080,128]{1,0:T(8,128)(2,1)S(1)} %collective-permute-done.10.a_ref), channel_id=1, source_target_pairs={{0,2},{2,4},{4,6},{6,7},{7,5},{5,3},{3,1},{1,0},{8,10},{10,12},{12... | collective-permute-start | bytes 1597448 | tf_op jit(solution)/shard_map/ppermute | solution.py:255
  70.0 21.1 %collective-permute-start.16 = (bf16[2080,128]{1,0:T(8,128)(2,1)S(1)}, bf16[2080,128]{1,0:T(8,128)(2,1)S(1)}, u32[]{:S(2)}, u32[]{:S(2)}) collective-permute-start(bf16[2080,128]{1,0:T(8,128)(2,1)S(1)} %collective-permute-done.11.b_ref), channel_id=1, source_target_pairs={{2,0},{4,2},{6,4},{7,6},{5,7},{3,5},{1,3},{0,1},{10,8},{12,10},{14... | collective-permute-start | bytes 1597448 | tf_op jit(solution)/shard_map/ppermute | solution.py:255
  85.4 12.9 %collective-permute-start.12 = (bf16[128,2048]{1,0:T(8,128)(2,1)S(1)}, bf16[128,2048]{1,0:T(8,128)(2,1)S(1)}, u32[]{:S(2)}, u32[]{:S(2)}) collective-permute-start(bf16[128,2048]{1,0:T(8,128)(2,1)S(1)} %get-tuple-element.62), channel_id=1, source_target_pairs={{0,2},{2,4},{4,6},{6,7},{7,5},{5,3},{3,1},{1,0},{8,10},{10,12},{12... | collective-permute-start | bytes 1572872 | tf_op jit(solution)/shard_map/ppermute | solution.py:262
  87.1 15.2 %collective-permute-start.21 = (bf16[128,2048]{1,0:T(8,128)(2,1)S(1)}, bf16[128,2048]{1,0:T(8,128)(2,1)S(1)}, u32[]{:S(2)}, u32[]{:S(2)}) collective-permute-start(bf16[128,2048]{1,0:T(8,128)(2,1)S(1)} %get-tuple-element.68), channel_id=1, source_target_pairs={{2,0},{4,2},{6,4},{7,6},{5,7},{3,5},{1,3},{0,1},{10,8},{12,10},{14... | collective-permute-start | bytes 1572872 | tf_op jit(solution)/shard_map/ppermute | solution.py:263
  97.5 16.0 %collective-permute-start.17 = (bf16[128,2048]{1,0:T(8,128)(2,1)S(1)}, bf16[128,2048]{1,0:T(8,128)(2,1)S(1)}, u32[]{:S(2)}, u32[]{:S(2)}) collective-permute-start(bf16[128,2048]{1,0:T(8,128)(2,1)S(1)} %get-tuple-element.66), channel_id=1, source_target_pairs={{2,0},{4,2},{6,4},{7,6},{5,7},{3,5},{1,3},{0,1},{10,8},{12,10},{14... | collective-permute-start | bytes 1572872 | tf_op jit(solution)/shard_map/ppermute | solution.py:257
  98.5 25.0 %collective-permute-start.13 = (bf16[128,2048]{1,0:T(8,128)(2,1)S(1)}, bf16[128,2048]{1,0:T(8,128)(2,1)S(1)}, u32[]{:S(2)}, u32[]{:S(2)}) collective-permute-start(bf16[128,2048]{1,0:T(8,128)(2,1)S(1)} %add_convert_fusion.9), channel_id=1, source_target_pairs={{0,2},{2,4},{4,6},{6,7},{7,5},{5,3},{3,1},{1,0},{8,10},{10,12},{12... | collective-permute-start | bytes 1572872 | tf_op jit(solution)/shard_map/ppermute | solution.py:262
  100.1 21.6 %collective-permute-start.24 = (bf16[128,2048]{1,0:T(8,128)(2,1)S(1)}, bf16[128,2048]{1,0:T(8,128)(2,1)S(1)}, u32[]{:S(2)}, u32[]{:S(2)}) collective-permute-start(bf16[128,2048]{1,0:T(8,128)(2,1)S(1)} %get-tuple-element.72), channel_id=1, source_target_pairs={{0,2},{2,4},{4,6},{6,7},{7,5},{5,3},{3,1},{1,0},{8,10},{10,12},{12... | collective-permute-start | bytes 1572872 | tf_op jit(solution)/shard_map/ppermute | solution.py:257
  102.4 36.0 %collective-permute-start.22 = (bf16[128,2048]{1,0:T(8,128)(2,1)S(1)}, bf16[128,2048]{1,0:T(8,128)(2,1)S(1)}, u32[]{:S(2)}, u32[]{:S(2)}) collective-permute-start(bf16[128,2048]{1,0:T(8,128)(2,1)S(1)} %add_convert_fusion.4), channel_id=1, source_target_pairs={{2,0},{4,2},{6,4},{7,6},{5,7},{3,5},{1,3},{0,1},{10,8},{12,10},{14... | collective-permute-start | bytes 1572872 | tf_op jit(solution)/shard_map/ppermute | solution.py:263
  113.7 19.7 %collective-permute-start.18 = (bf16[128,2048]{1,0:T(8,128)(2,1)S(1)}, bf16[128,2048]{1,0:T(8,128)(2,1)S(1)}, u32[]{:S(2)}, u32[]{:S(2)}) collective-permute-start(bf16[128,2048]{1,0:T(8,128)(2,1)S(1)} %add_convert_fusion.7), channel_id=1, source_target_pairs={{2,0},{4,2},{6,4},{7,6},{5,7},{3,5},{1,3},{0,1},{10,8},{12,10},{14... | collective-permute-start | bytes 1572872 | tf_op jit(solution)/shard_map/ppermute | solution.py:261
  121.8 14.9 %collective-permute-start.25 = (bf16[128,2048]{1,0:T(8,128)(2,1)S(1)}, bf16[128,2048]{1,0:T(8,128)(2,1)S(1)}, u32[]{:S(2)}, u32[]{:S(2)}) collective-permute-start(bf16[128,2048]{1,0:T(8,128)(2,1)S(1)} %add_convert_fusion.2), channel_id=1, source_target_pairs={{0,2},{2,4},{4,6},{6,7},{7,5},{5,3},{3,1},{1,0},{8,10},{10,12},{12... | collective-permute-start | bytes 1572872 | tf_op jit(solution)/shard_map/ppermute | solution.py:260
  123.5 34.4 %collective-permute-start.14 = (bf16[128,2048]{1,0:T(8,128)(2,1)S(1)}, bf16[128,2048]{1,0:T(8,128)(2,1)S(1)}, u32[]{:S(2)}, u32[]{:S(2)}) collective-permute-start(bf16[128,2048]{1,0:T(8,128)(2,1)S(1)} %add_convert_fusion.8), channel_id=1, source_target_pairs={{0,2},{2,4},{4,6},{6,7},{7,5},{5,3},{3,1},{1,0},{8,10},{10,12},{12... | collective-permute-start | bytes 1572872 | tf_op jit(solution)/shard_map/ppermute | solution.py:262
  133.5 14.9 %collective-permute-start.19 = (bf16[128,2048]{1,0:T(8,128)(2,1)S(1)}, bf16[128,2048]{1,0:T(8,128)(2,1)S(1)}, u32[]{:S(2)}, u32[]{:S(2)}) collective-permute-start(bf16[128,2048]{1,0:T(8,128)(2,1)S(1)} %add_convert_fusion.6), channel_id=1, source_target_pairs={{2,0},{4,2},{6,4},{7,6},{5,7},{3,5},{1,3},{0,1},{10,8},{12,10},{14... | collective-permute-start | bytes 1572872 | tf_op jit(solution)/shard_map/ppermute | solution.py:261
  136.8 19.4 %collective-permute-start.26 = (bf16[128,2048]{1,0:T(8,128)(2,1)S(1)}, bf16[128,2048]{1,0:T(8,128)(2,1)S(1)}, u32[]{:S(2)}, u32[]{:S(2)}) collective-permute-start(bf16[128,2048]{1,0:T(8,128)(2,1)S(1)} %add_convert_fusion.1), channel_id=1, source_target_pairs={{0,2},{2,4},{4,6},{6,7},{7,5},{5,3},{3,1},{1,0},{8,10},{10,12},{12... | collective-permute-start | bytes 1572872 | tf_op jit(solution)/shard_map/ppermute | solution.py:260
  138.6 21.0 %collective-permute-start.23 = (bf16[128,2048]{1,0:T(8,128)(2,1)S(1)}, bf16[128,2048]{1,0:T(8,128)(2,1)S(1)}, u32[]{:S(2)}, u32[]{:S(2)}) collective-permute-start(bf16[128,2048]{1,0:T(8,128)(2,1)S(1)} %add_convert_fusion.3), channel_id=1, source_target_pairs={{2,0},{4,2},{6,4},{7,6},{5,7},{3,5},{1,3},{0,1},{10,8},{12,10},{14... | collective-permute-start | bytes 1572872 | tf_op jit(solution)/shard_map/ppermute | solution.py:263
  148.5 18.8 %collective-permute-start.20 = (bf16[128,2048]{1,0:T(8,128)(2,1)S(1)}, bf16[128,2048]{1,0:T(8,128)(2,1)S(1)}, u32[]{:S(2)}, u32[]{:S(2)}) collective-permute-start(bf16[128,2048]{1,0:T(8,128)(2,1)S(1)} %add_convert_fusion.5), channel_id=1, source_target_pairs={{2,0},{4,2},{6,4},{7,6},{5,7},{3,5},{1,3},{0,1},{10,8},{12,10},{14... | collective-permute-start | bytes 1572872 | tf_op jit(solution)/shard_map/ppermute | solution.py:261
  156.3 10.9 %collective-permute-start.27 = (bf16[128,2048]{1,0:T(8,128)(2,1)S(1)}, bf16[128,2048]{1,0:T(8,128)(2,1)S(1)}, u32[]{:S(2)}, u32[]{:S(2)}) collective-permute-start(bf16[128,2048]{1,0:T(8,128)(2,1)S(1)} %add_convert_fusion), channel_id=1, source_target_pairs={{0,2},{2,4},{4,6},{6,7},{7,5},{5,3},{3,1},{1,0},{8,10},{10,12},{12... | collective-permute-start | bytes 1572872 | tf_op jit(solution)/shard_map/ppermute | solution.py:260
  (4 other events, 7.0 us)
